TPU v7x, 256 devices: a whole 4x4x8 slice. The times are simulated.
256 devices in a mesh: gx: 8 (over x, y_lo), gy: 4 (over y_hi, core), ka: 8 (over z).
Axes of the slice: x: 4, y: 4 (y_hi: 2, y_lo: 2; y = y_hi * 2 + y_lo), z: 8, core: 2. Of those that a mesh axis runs over, the one named last changes fastest.
Arguments:
- fractional_placements: float32 [3, 65536], P(None, ('gx', 'gy', 'ka')), may hold values from 0 to 1, as said below
- particle_speeds: float32 [3, 65536], P(None, ('gx', 'gy', 'ka')), may hold values from -3 to 3
- element_kinds: int32 [65536], P(('gx', 'gy', 'ka')), may hold values from 0 to 5
- adjacent_padded_indices: int32 [65536, 64], P(('gx', 'gy', 'ka')), may hold values from 0 to 4095, as said below
- adjacent_valid_tally: int32 [65536], P(('gx', 'gy', 'ka')), may hold values from 16 to 64, as said below
- border_particle_rows: int32 [16, 8, 128], P('gx', 'gy'), may hold values from 0 to 2047
- reciprocal_integer_triples: int32 [3, 16384], P(None, 'ka'), may hold values from -16 to 16, as said below
- cell_edge_sizes: float32 [3], replicated, may hold values from 20 to 40
- friction_random_kicks: float32 [3, 65536], P(None, ('gx', 'gy', 'ka')), may hold values from -6 to 6
- element_feature_vectors: float32 [6, 128], replicated, may hold values from -5 to 5
- distance_net_initial_weights: float32 [8, 64], replicated, may hold values from -2 to 2
- distance_net_final_weights: float32 [64, 128], replicated, may hold values from -0.75 to 0.75
- message_blend_matrix: float32 [128, 128], replicated, may hold values from -0.5 to 0.5
- energy_head_initial_weights: float32 [128, 16], replicated, may hold values from -0.5 to 0.5
- energy_head_final_weights: float32 [16], replicated, may hold values from -1.5 to 1.5
- hidden_electric_projection: float32 [128, 8], replicated, may hold values from -0.5 to 0.5
Outputs:
- forces: float32 [3, 65536], P(None, ('gx', 'gy', 'ka'))
- new_positions: float32 [3, 65536], P(None, ('gx', 'gy', 'ka'))
- new_velocities: float32 [3, 65536], P(None, ('gx', 'gy', 'ka'))
Inputs may be any that keep to these rules, and one draw needn't show every extreme that they name: `fractional_placements`: domain (X, Y) has first coordinates in [X / 8, (X + 1) / 8) and second ones in [Y / 4, (Y + 1) / 4). `adjacent_padded_indices`: an entry names another atom of the domain or a slot of one of the 12 outer ghost cells, never the atom itself or the 4 inner cells. `adjacent_valid_tally`: on every device some atom has all 64 slots live. `reciprocal_integer_triples`: no triple is all zeros.
All inputs are finite; a program needn't handle non-finite values.
Results may differ from a plain program's by a relative error of at most 0.0003.
Values sent between devices are 32-bit elements; how exact they have to be, the bound alone decides.
No kernel may reach another device: no remote copies, remote signals or barrier semaphores. Data moves between devices by JAX's collectives and lax.ppermute only.
A program may use at most 64 MiB of HBM per device.

v0:
```python
import math

import jax
import jax.numpy as jnp
from jax import lax
from jax.sharding import PartitionSpec as P

highest = lax.Precision.HIGHEST
masses_table = (1.008, 12.011, 15.999, 6.94, 30.974, 18.998)
radial_widths = (2.0, 4.0, 6.0, 8.0, 10.0, 12.0, 14.0, 16.0)
time_step = 0.5
friction = 0.2
gauss_width = 0.3
species_kinds = 6


def with_halo(cells, sides, width):
    for axis, dim in sides:
        count = lax.axis_size(axis)
        head = lax.slice_in_dim(cells, 0, width, axis=dim)
        tail = lax.slice_in_dim(cells, cells.shape[dim] - width, cells.shape[dim], axis=dim)
        cells = jnp.concatenate(
            [
                lax.ppermute(tail, axis, [(i, (i + 1) % count) for i in range(count)]),
                cells,
                lax.ppermute(head, axis, [((i + 1) % count, i) for i in range(count)]),
            ],
            axis=dim,
        )
    return cells


def product(left_side, right_side):
    return jnp.dot(left_side, right_side, precision=highest, preferred_element_type=jnp.float32)


def one_hot_rows(labels):
    levels = jnp.arange(species_kinds).astype(labels.dtype)
    return (labels[None, :] == levels[:, None]).astype(jnp.float32)


def to_blocks(tensor, position_axis, block_rows):
    dims_of = tensor.shape
    pieces = dims_of[position_axis] // block_rows
    divided = tensor.reshape(
        dims_of[:position_axis] + (pieces, block_rows) + dims_of[position_axis + 1 :]
    )
    return jnp.moveaxis(divided, position_axis, 0)


def from_blocks(tensor, position_axis):
    merged = jnp.moveaxis(tensor, 0, position_axis)
    dims_of = merged.shape
    return merged.reshape(
        dims_of[:position_axis]
        + (dims_of[position_axis] * dims_of[position_axis + 1],)
        + dims_of[position_axis + 2 :]
    )


def displacements(extended, listing, centres, cell_edge_sizes):
    nearby = extended[:, listing]
    offsets = nearby[:3] - centres[:, :, None]
    offsets = offsets - jnp.floor(offsets + 0.5)
    return (offsets * cell_edge_sizes[:, None, None], nearby[3])


def pair_messages(
    displace,
    labels,
    live_pairs,
    element_feature_vectors,
    distance_net_initial_weights,
    distance_net_final_weights,
):
    atom_rows = displace.shape[1]
    list_width = displace.shape[2]
    spacing = jnp.sqrt(jnp.sum(displace * displace, axis=0)).reshape(-1)
    scales = jnp.asarray(radial_widths, dtype=jnp.float32)[:, None]
    radial_basis = jnp.exp(-jnp.square(spacing[None, :] / scales))
    hidden = jax.nn.silu(product(distance_net_initial_weights.T, radial_basis))
    radial = product(distance_net_final_weights.T, hidden)
    partner = product(element_feature_vectors.T, one_hot_rows(labels.reshape(-1)))
    weighted = radial * partner * live_pairs.reshape(-1)[None, :]
    return jnp.sum(weighted.reshape(-1, atom_rows, list_width), axis=2) / list_width


def blocked_messages(displace, labels, live_pairs, weights):
    block_rows = min(128, displace.shape[1])

    def one_block(block_items):
        return pair_messages(
            block_items[0], block_items[1], block_items[2], weights[0], weights[1], weights[2]
        )

    outputs = lax.map(
        one_block,
        (
            to_blocks(displace, 1, block_rows),
            to_blocks(labels, 0, block_rows),
            to_blocks(live_pairs, 0, block_rows),
        ),
    )
    return from_blocks(outputs, 1)


def blocked_pullback(displace, labels, live_pairs, upstream, weights):
    block_rows = min(128, displace.shape[1])

    def one_block(block_items):

        def local_map(offsets_in):
            return pair_messages(
                offsets_in, block_items[1], block_items[2], weights[0], weights[1], weights[2]
            )

        _, backward = jax.vjp(local_map, block_items[0])
        return backward(block_items[3])[0]

    gradients = lax.map(
        one_block,
        (
            to_blocks(displace, 1, block_rows),
            to_blocks(labels, 0, block_rows),
            to_blocks(live_pairs, 0, block_rows),
            to_blocks(upstream, 1, block_rows),
        ),
    )
    return from_blocks(gradients, 1)


def phases(kblock, coords):
    phase_angle = (
        kblock[0][:, None] * coords[0][None, :]
        + kblock[1][:, None] * coords[1][None, :]
        + kblock[2][:, None] * coords[2][None, :]
    )
    phase_angle = 2.0 * math.pi * phase_angle
    return (jnp.cos(phase_angle), jnp.sin(phase_angle))


def structure(coords, charges, reciprocal_real_triples, block_cols):

    def one_block(kblock):
        cosine, sine_part = phases(kblock, coords)
        return jnp.stack([product(charges, cosine.T), product(charges, sine_part.T)], 0)

    blockwise = lax.map(one_block, to_blocks(reciprocal_real_triples, 1, block_cols))
    return from_blocks(blockwise, 2)


def kspace_terms(coords, reciprocal_real_triples, cos_weight, sin_weight, block_cols):

    def one_step(running, block_items):
        kblock, first_part, second_part = block_items
        cosine, sine_part = phases(kblock, coords)
        cos_coef = jnp.concatenate(
            [
                first_part,
                kblock[0][None] * second_part,
                kblock[1][None] * second_part,
                kblock[2][None] * second_part,
            ],
            0,
        )
        sin_coef = jnp.concatenate(
            [
                second_part,
                -kblock[0][None] * first_part,
                -kblock[1][None] * first_part,
                -kblock[2][None] * first_part,
            ],
            0,
        )
        return (running + product(cos_coef, cosine) + product(sin_coef, sine_part), None)

    initial = jnp.zeros((4 * cos_weight.shape[0], coords.shape[1]), jnp.float32)
    running, _ = lax.scan(
        one_step,
        initial,
        (
            to_blocks(reciprocal_real_triples, 1, block_cols),
            to_blocks(cos_weight, 1, block_cols),
            to_blocks(sin_weight, 1, block_cols),
        ),
    )
    return running


def kspace_weights(reciprocal_real_triples, cell_edge_sizes, atoms_total):
    wavevector = 2.0 * math.pi * reciprocal_real_triples / cell_edge_sizes[:, None]
    squared = jnp.sum(wavevector * wavevector, axis=0)
    return (
        2.0 * math.pi / atoms_total * jnp.exp(-0.5 * gauss_width * gauss_width * squared) / squared
    )


def feature_gradient(
    features,
    potential,
    energy_head_initial_weights,
    energy_head_final_weights,
    hidden_electric_projection,
):
    activation = product(energy_head_initial_weights.T, features)
    sigmoid_part = jax.nn.sigmoid(activation)
    slope_term = (
        energy_head_final_weights[:, None]
        * sigmoid_part
        * (1.0 + activation * (1.0 - sigmoid_part))
    )
    return product(energy_head_initial_weights, slope_term) + product(
        hidden_electric_projection, potential
    )


def langevin(
    fractional_placements,
    particle_speeds,
    element_kinds,
    forces,
    cell_edge_sizes,
    friction_random_kicks,
):
    masses = jnp.sum(
        jnp.asarray(masses_table, dtype=jnp.float32)[:, None] * one_hot_rows(element_kinds), axis=0
    )
    halfway = particle_speeds + 0.5 * time_step * forces / masses
    retain = math.exp(-friction * time_step)
    updated = retain * halfway + jnp.sqrt((1.0 - retain * retain) / masses) * friction_random_kicks
    new_positions = (
        fractional_placements + 0.5 * time_step * (halfway + updated) / cell_edge_sizes[:, None]
    )
    return (new_positions, updated)


def body(
    fractional_placements,
    particle_speeds,
    element_kinds,
    adjacent_padded_indices,
    adjacent_valid_tally,
    border_particle_rows,
    reciprocal_integer_triples,
    cell_edge_sizes,
    friction_random_kicks,
    element_feature_vectors,
    distance_net_initial_weights,
    distance_net_final_weights,
    message_blend_matrix,
    energy_head_initial_weights,
    energy_head_final_weights,
    hidden_electric_projection,
):
    weights = (element_feature_vectors, distance_net_initial_weights, distance_net_final_weights)
    own_count = fractional_placements.shape[1]
    slot_count = border_particle_rows.shape[2]
    list_width = adjacent_padded_indices.shape[1]
    atoms_total = own_count * lax.axis_size("gx") * lax.axis_size("gy") * lax.axis_size("ka")
    packed = jnp.concatenate([fractional_placements, element_kinds[None, :].astype(jnp.float32)], 0)
    domain_packed = lax.all_gather(packed, "ka", axis=1, tiled=True)
    domain_count = domain_packed.shape[1]
    sending = (
        domain_packed[:, border_particle_rows.reshape(-1)]
        .reshape(4, 2, 2, slot_count)
        .transpose(1, 2, 0, 3)
    )
    received = with_halo(sending, (("gx", 0), ("gy", 1)), 1)
    surround = jnp.concatenate(
        [domain_packed, received.transpose(2, 0, 1, 3).reshape(4, 16 * slot_count)], 1
    )
    live_pairs = (jnp.arange(list_width)[None, :] < adjacent_valid_tally[:, None]).astype(
        jnp.float32
    )
    displace, labels = displacements(
        surround, adjacent_padded_indices, fractional_placements, cell_edge_sizes
    )
    message = blocked_messages(displace, labels, live_pairs, weights)
    features = product(element_feature_vectors.T, one_hot_rows(element_kinds)) + product(
        message_blend_matrix.T, message
    )
    charges = product(hidden_electric_projection.T, features)
    latent = charges.shape[0]
    reciprocal_real_triples = lax.all_gather(
        reciprocal_integer_triples, "ka", axis=1, tiled=True
    ).astype(jnp.float32)
    block_cols = min(512, reciprocal_real_triples.shape[1])
    spectrum = lax.psum(
        structure(fractional_placements, charges, reciprocal_real_triples, block_cols),
        ("gx", "gy", "ka"),
    )
    kweight = kspace_weights(reciprocal_real_triples, cell_edge_sizes, atoms_total)
    kspace_out = kspace_terms(
        fractional_placements,
        reciprocal_real_triples,
        kweight * spectrum[0],
        kweight * spectrum[1],
        block_cols,
    )
    potential = kspace_out[:latent]
    gradient_terms = kspace_out[latent:].reshape(3, latent, own_count)
    long_range = (2.0 * math.pi / cell_edge_sizes)[:, None] * jnp.sum(
        charges[None] * gradient_terms, axis=1
    )
    upstream = product(
        message_blend_matrix,
        feature_gradient(
            features,
            potential,
            energy_head_initial_weights,
            energy_head_final_weights,
            hidden_electric_projection,
        ),
    )
    grad_pairs = blocked_pullback(displace, labels, live_pairs, upstream, weights)
    direct = -jnp.sum(grad_pairs, axis=2)
    scattered = (
        jnp.zeros((3, surround.shape[1]), jnp.float32)
        .at[:, adjacent_padded_indices.reshape(-1)]
        .add(grad_pairs.reshape(3, -1))
    )
    ghost_grad = scattered[:, domain_count:].reshape(3, 4, 4, slot_count).transpose(1, 2, 0, 3)
    echoes = with_halo(ghost_grad, (("gx", 0), ("gy", 1)), 1)
    across = jnp.stack([echoes[0, 2:4], echoes[5, 2:4]], 0)
    sideways = jnp.stack([echoes[2:4, 0], echoes[2:4, 5]], 1)
    corners = jnp.stack(
        [jnp.stack([echoes[0, 0], echoes[0, 5]], 0), jnp.stack([echoes[5, 0], echoes[5, 5]], 0)], 0
    )
    returned = (across + sideways + corners).transpose(2, 0, 1, 3).reshape(3, 4 * slot_count)
    domain_grad = scattered[:, :domain_count].at[:, border_particle_rows.reshape(-1)].add(returned)
    reactions = lax.psum_scatter(domain_grad, "ka", scatter_dimension=1, tiled=True)
    forces = -(direct + reactions + long_range)
    new_positions, updated = langevin(
        fractional_placements,
        particle_speeds,
        element_kinds,
        forces,
        cell_edge_sizes,
        friction_random_kicks,
    )
    return (forces, new_positions, updated)


def solution(mesh):
    return jax.shard_map(
        body,
        mesh=mesh,
        in_specs=(
            P(None, ("gx", "gy", "ka")),
            P(None, ("gx", "gy", "ka")),
            P(("gx", "gy", "ka")),
            P(("gx", "gy", "ka"), None),
            P(("gx", "gy", "ka")),
            P("gx", "gy", None),
            P(None, "ka"),
            P(),
            P(None, ("gx", "gy", "ka")),
            P(),
            P(),
            P(),
            P(),
            P(),
            P(),
            P(),
        ),
        out_specs=(
            P(None, ("gx", "gy", "ka")),
            P(None, ("gx", "gy", "ka")),
            P(None, ("gx", "gy", "ka")),
        ),
        check_vma=False,
    )
```

profile of v0, /device:TPU:14, one launch (start us, length us, event | category | flops | bytes accessed | tf_op | source)
XLA Modules:
  0.0 965.9 jit_solution(17625417360090634864)
XLA Ops:
  8.8 30.6 %all_gather.6 = f32[4,2048]{0,1:T(8,128)S(1)} all-gather(f32[4,256]{0,1:T(8,128)S(1)} %copy.167), channel_id=1, replica_groups=mesh['gx'=8,'gy'=4,'ka'=8] {'ka'}, dimensions={1}, use_global_device_ids=true | all-gather | bytes 36864 | tf_op jit(solution)/shard_map/all_gather | solution.py:261
  45.8 24.9 %all_gather.7 = s32[3,16384]{1,0:T(4,128)S(1)} all-gather(s32[3,2048]{1,0:T(4,128)S(1)} %copy-done.11), channel_id=1, replica_groups=mesh['gx'=8,'gy'=4,'ka'=8] {'ka'}, dimensions={1}, use_global_device_ids=true | all-gather | bytes 221184 | tf_op jit(solution)/shard_map/all_gather | solution.py:284
  72.5 3.7 collective-permute-start.3
  80.6 54.5 %gather_fusion.1 = f32[16384,4]{1,0:T(8,128)} fusion(f32[4,4096]{0,1:T(8,128)S(1)} %pad_maximum_fusion, s32[16384]{0:T(1024)S(1)} %broadcast_clamp_fusion), kind=kCustom, calls=%fused_computation.1 | custom fusion | bytes 589824 | tf_op jit(solution)/shard_map/gather | solution.py:62
  135.2 6.4 copy.171
  142.2 33.4 %while.44 = (s32[]{:T(128)}, f32[2,128,128]{1,2,0:T(8,128)S(1)}, f32[2,3,128,64]{3,2,1,0:T(8,128)S(1)}, f32[8,64]{1,0:T(8,128)S(1)}, f32[64,128]{1,0:T(8,128)S(1...) while((s32[]{:T(128)}, f32[2,128,128]{1,2,0:T(8,128)S(1)}, ...), condition=%wide.region_3.4_spmd.clone, body=%wide.region_0.3_spmd.sunk.clone.sunk | while | flops 936665088 | bytes 13440193 | solution.py:96
  144.2 8.3 fusion.192
  152.6 6.3 bitcast_reduce_fusion.3
  160.9 8.3 fusion.192
  169.3 6.3 bitcast_reduce_fusion.3
  176.1 158.9 %while.43 = (s32[]{:T(128)}, f32[32,2,8,512]{3,2,1,0:T(8,128)S(1)}, f32[32,3,512]{2,1,0:T(4,128)S(1)}, f32[3,256]{1,0:T(4,128)S(1)}, f32[8,256]{1,0:T(8,128)S(1)}, /*index=5*/s32[]{:T(128)}, s32[]{:T(128)}, s32[]{}, s32[]{}) while((s32[]{:T(128)}, f32[32,2,8,512]{3,2,1,0:T(8,128)S(1)}, f32[32,3,512]{2,1,0:T(4,128)S(1)}, ...), condition=%wide.region_6.7_spmd, body=%wide.region_5.6_spmd.sunk | while | flops 26746884 | bytes 151685 | solution.py:148
  178.8 2.5 convolution_bitcast_fusion.14
  183.7 2.5 convolution_bitcast_fusion.14
  188.7 2.5 convolution_bitcast_fusion.14
  193.6 2.5 convolution_bitcast_fusion.14
  198.6 2.5 convolution_bitcast_fusion.14
  203.6 2.5 convolution_bitcast_fusion.14
  208.5 2.5 convolution_bitcast_fusion.14
  213.5 2.5 convolution_bitcast_fusion.14
  218.4 2.5 convolution_bitcast_fusion.14
  223.4 2.5 convolution_bitcast_fusion.14
  228.4 2.5 convolution_bitcast_fusion.14
  233.3 2.5 convolution_bitcast_fusion.14
  238.3 2.5 convolution_bitcast_fusion.14
  243.2 2.5 convolution_bitcast_fusion.14
  253.1 2.5 convolution_bitcast_fusion.14
  263.1 2.5 convolution_bitcast_fusion.14
  268.0 2.5 convolution_bitcast_fusion.14
  277.9 2.5 convolution_bitcast_fusion.14
  292.8 2.5 convolution_bitcast_fusion.14
  307.7 2.5 convolution_bitcast_fusion.14
  317.6 2.5 convolution_bitcast_fusion.14
  332.5 2.5 convolution_bitcast_fusion.14
  337.5 254.7 %all-reduce.2.cloned.1.call-done = f32[2,8,16384]{2,1,0:T(8,128)} async-done(((f32[2,8,16384]{2,1,0:T(8,128)}), f32[2,8,16384]{2,1,0:T(8,128)}) %all-reduce.2.cloned.1.call-update) | async-done | bytes 1048592 | tf_op jit(solution)/shard_map/psum | solution.py:288
  593.6 175.9 %while.46 = (s32[]{:T(128)}, f32[32,256]{1,0:T(8,128)S(1)}, f32[32,8,512]{2,1,0:T(8,128)S(1)}, f32[32,3,512]{2,1,0:T(4,128)}, f32[32,8,512]{2,1,0:T(8,128)S(1)},...) while((s32[]{:T(128)}, f32[32,256]{1,0:T(8,128)S(1)}, ...), condition=%wide.region_9.10_spmd.clone, body=%wide.region_8.9_spmd.clone.sunk | while | flops 102385152 | bytes 520343 | solution.py:178
  770.2 34.1 %while.45 = (s32[]{:T(128)}, f32[2,3,128,64]{3,2,1,0:T(8,128)S(1)}, f32[2,3,128,64]{3,2,1,0:T(8,128)S(1)}, f32[2,128,128]{1,2,0:T(8,128)S(1)}, f32[2,128,64]{2,1...) while((s32[]{:T(128)}, f32[2,3,128,64]{3,2,1,0:T(8,128)S(1)}, ...), condition=%wide.region_13.14_spmd.clone, body=%wide.region_10.13_spmd.sunk.clone.sunk | while | flops 989233152 | bytes 26713324 | solution.py:120
  770.5 2.6 bitcast_multiply_fusion.3
  773.2 5.4 fusion.201
  778.6 4.7 convolution_bitcast_fusion.18
  787.4 2.6 bitcast_multiply_fusion.3
  790.1 5.4 fusion.201
  795.5 4.7 convolution_bitcast_fusion.18
  804.5 5.1 copy.179
  809.6 88.3 %scatter_custom_fusion = f32[3,4096]{0,1:T(8,128)S(1)} fusion(s32[16384]{0:T(1024)} %bitcast.264, f32[16384,3]{1,0:T(8,128)} %copy.179, f32[]{:T(128)} %constant.61.clone.1), kind=kCustom, calls=%fused_computation.146 | custom fusion | flops 49152 | bytes 49664 | tf_op jit(solution)/shard_map/scatter-add | solution.py:320
  904.7 2.9 collective-permute-done.5
  907.9 3.3 collective-permute-start.7
  912.9 5.2 scatter_fusion
  918.1 39.0 %reduce-scatter.4.cloned.1.call-done = f32[256,3]{1,0:T(8,128)} async-done(((f32[2048,3]{1,0:T(8,128)}), f32[256,3]{1,0:T(8,128)}) %reduce-scatter.4.cloned.1.call-update) | async-done | bytes 3088
  (649 shorter events, 319.3 us)
Async XLA Ops:
  7.2 168.5 %copy-start = (f32[128,128]{1,0:T(8,128)S(1)}, f32[128,128]{1,0:T(8,128)}, u32[]{:S(2)}) copy-start(f32[128,128]{1,0:T(8,128)} %param.39) | copy-start | bytes 196612
  7.2 69.1 %copy-start.30 = (f32[6]{0:T(128)S(1)}, f32[6]{0:T(128)}, u32[]{:S(2)}) copy-start(f32[6]{0:T(128)} %constant.106.clone) | copy-start | bytes 76
  7.2 38.3 %copy-start.20 = (s32[256]{0:T(256)S(1)}, s32[256]{0:T(256)}, u32[]{:S(2)}) copy-start(s32[256]{0:T(256)} %param.29) | copy-start | bytes 3076
  7.2 38.1 %copy-start.28 = (s32[256]{0:T(256)S(1)}, s32[256]{0:T(256)}, u32[]{:S(2)}) copy-start(s32[256]{0:T(256)} %param.31) | copy-start | bytes 3076
  7.2 38.2 %copy-start.4 = (f32[6,128]{1,0:T(8,128)S(1)}, f32[6,128]{1,0:T(8,128)}, u32[]{:S(2)}) copy-start(f32[6,128]{1,0:T(8,128)} %param.36) | copy-start | bytes 9220
  7.2 38.5 %copy-start.11 = (s32[3,2048]{1,0:T(4,128)S(1)}, s32[3,2048]{1,0:T(4,128)}, u32[]{:S(2)}) copy-start(s32[3,2048]{1,0:T(4,128)} %param.33) | copy-start | bytes 73732
  7.2 63.4 %copy-start.23 = (f32[3]{0:T(128)S(1)}, f32[3]{0:T(128)}, u32[]{:S(2)}) copy-start(f32[3]{0:T(128)} %param.34) | copy-start | bytes 40
  7.2 584.9 %all-reduce.2.cloned.1.call-start = ((), (), s32[]{:S(2)}) async-start(), calls=%async_computation.1 | async-start | bytes 2097152 | tf_op jit(solution)/shard_map/psum | solution.py:288
  39.4 39.6 %copy-start.1 = (f32[4,2048]{0,1:T(8,128)}, f32[4,2048]{0,1:T(8,128)S(1)}, u32[]{:S(2)}) copy-start(f32[4,2048]{0,1:T(8,128)S(1)} %all_gather.6) | copy-start | bytes 98308
  40.1 38.9 %copy-start.17 = (s32[512,1]{0,1:T(1,128)}, s32[512,1]{0,1:T(1,128)S(1)}, u32[]{:S(2)}) copy-start(s32[512,1]{0,1:T(1,128)S(1)} %compare_select_fusion.2) | copy-start | bytes 6148
  41.3 31.1 %collective-permute-start = (f32[1,2,4,128]{3,2,1,0:T(4,128)S(1)}, f32[1,2,4,128]{3,2,1,0:T(4,128)S(1)}, u32[]{:S(2)}, u32[]{:S(2)}) collective-permute-start(f32[1,2,4,128]{3,2,1,0:T(4,128)S(1)} %get-tuple-element.461), channel_id=1, source_target_pairs={{0,32},{32,64},{64,96},{96,128},{128,160},{160,192},{192,224},{224... | collective-permute-start | bytes 12296 | tf_op jit(solution)/shard_map/ppermute | solution.py:24
  41.7 30.7 %collective-permute-start.1 = (f32[1,2,4,128]{3,2,1,0:T(4,128)S(1)}, f32[1,2,4,128]{3,2,1,0:T(4,128)S(1)}, u32[]{:S(2)}, u32[]{:S(2)}) collective-permute-start(f32[1,2,4,128]{3,2,1,0:T(4,128)S(1)} %get-tuple-element.462), channel_id=1, source_target_pairs={{32,0},{64,32},{96,64},{128,96},{160,128},{192,160},{224,192},{0,2... | collective-permute-start | bytes 12296 | tf_op jit(solution)/shard_map/ppermute | solution.py:26
  72.4 4.7 collective-permute-start.2
  72.5 5.1 collective-permute-start.3
  135.1 6.5 copy-start.5
  135.1 7.0 copy-start.3
  135.1 7.0 copy-start.6
  135.1 7.0 copy-start.9
  135.2 7.0 copy-start.10
  142.2 33.7 %copy-start.19 = (f32[128,8]{0,1:T(8,128)S(1)}, f32[128,8]{0,1:T(8,128)}, u32[]{:S(2)}) copy-start(f32[128,8]{0,1:T(8,128)} %param.42) | copy-start | bytes 12292
  142.2 33.9 %copy-start.2 = (f32[32,2,8,512]{3,2,1,0:T(8,128)S(1)}, f32[32,2,8,512]{3,2,1,0:T(8,128)}, u32[]{:S(2)}) copy-start(f32[32,2,8,512]{3,2,1,0:T(8,128)} %custom-call.5) | copy-start | bytes 3145732
  335.0 1.8 copy-start.7
  335.0 1.8 copy-start.15
  335.0 1.2 copy-start.21
  335.0 1.8 copy-start.12
  335.0 2.0 copy-start.29
  336.1 257.4 %copy-start.8 = (f32[32,512]{1,0:T(8,128)S(1)}, f32[32,512]{1,0:T(8,128)}, u32[]{:S(2)}) copy-start(f32[32,512]{1,0:T(8,128)} %multiply_divide_fusion) | copy-start | bytes 196612
  336.1 621.0 %reduce-scatter.4.cloned.1.call-start = ((), (), s32[]{:S(2)}) async-start(), calls=%async_computation.2 | async-start | bytes 1179648
  769.5 0.7 copy-start.13
  897.9 5.2 copy-start.24
  897.9 14.9 %copy-start.18 = (s32[512,1]{0,1:T(1,128)S(1)}, s32[512,1]{0,1:T(1,128)}, u32[]{:S(2)}) copy-start(s32[512,1]{0,1:T(1,128)} %copy-done.17) | copy-start | bytes 6148
  899.4 18.7 %copy-start.14 = (f32[32,256]{1,0:T(8,128)S(1)}, f32[32,256]{1,0:T(8,128)}, u32[]{:S(2)}) copy-start(f32[32,256]{1,0:T(8,128)} %copy-done.13) | copy-start | bytes 98308
  899.4 18.7 %copy-start.16 = (f32[8,256]{1,0:T(8,128)S(1)}, f32[8,256]{1,0:T(8,128)}, u32[]{:S(2)}) copy-start(f32[8,256]{1,0:T(8,128)} %copy-done.15) | copy-start | bytes 24580
  899.4 58.7 %copy-start.22 = (f32[256]{0:T(256)S(1)}, f32[256]{0:T(256)}, u32[]{:S(2)}) copy-start(f32[256]{0:T(256)} %select_reduce_fusion) | copy-start | bytes 3076
  899.4 58.7 %copy-start.25 = (f32[3,256]{1,0:T(4,128)S(1)}, f32[3,256]{1,0:T(4,128)}, u32[]{:S(2)}) copy-start(f32[3,256]{1,0:T(4,128)} %param.28) | copy-start | bytes 9220
  899.4 58.7 %copy-start.26 = (f32[3,256]{1,0:T(4,128)S(1)}, f32[3,256]{1,0:T(4,128)}, u32[]{:S(2)}) copy-start(f32[3,256]{1,0:T(4,128)} %param.35) | copy-start | bytes 9220
  899.4 58.7 %copy-start.27 = (f32[256]{0:T(256)S(1)}, f32[256]{0:T(256)}, u32[]{:S(2)}) copy-start(f32[256]{0:T(256)} %divide_sqrt_fusion) | copy-start | bytes 3076
  901.1 3.7 collective-permute-start.4
  901.9 5.7 collective-permute-start.5
  907.7 4.7 collective-permute-start.6
  907.9 4.7 collective-permute-start.7
Sparse Core Ops, SparseCore 0:
  336.2 255.8 all-reduce.1
  918.2 38.8 reduce-scatter.3
where the time goes:
time: 972 us; the launch traced here: 966 us
  matrix products  364 us (37%)
  waiting for transfers between devices  300 us (31%)
  other arithmetic  110 us (11%)
  local copies, waits for them, and re-layouts  106 us (11%)
  blocking collectives  55.4 us (6%)
  between operations  15 us (2%)
  starting transfers between devices  11.5 us (1%)
    dot_general x149, matrix products, product(): jnp.dot(left_side, right_side, precision=highest, preferred_element_type=...  364 us
    psum x1, waiting for transfers between devices, body(): lax.psum(structure(fractional_placements, charges, reciprocal_real_triple...  255 us
    scatter-add x1, other arithmetic, body(): scattered = jnp.zeros((3, surround.shape[1]), jnp.float32).at[:, adjacent...  88.3 us
    gather x2, local copies, waits for them, and re-layouts, displacements(): nearby = extended[:, listing]  60.9 us
    unnamed x3, waiting for transfers between devices  39 us
    all_gather x1, blocking collectives, body(): domain_packed = lax.all_gather(packed, 'ka', axis=1, tiled=True)  30.6 us
    slice x32, local copies, waits for them, and re-layouts, one_step(): kblock[0][None] * second_part  26.3 us
    all_gather x1, blocking collectives, body(): lax.all_gather(reciprocal_integer_triples, 'ka', axis=1, tiled=True)  24.9 us
  transfers between devices with their start and end apart: 10, of which 8 were waited for; matrix products, arithmetic and copies ran while one was open for 1% of the time, Pallas kernels for 0%

commit v1 on v0

v1 whole, which is shorter than its diff:
```python
import math

import jax
import jax.numpy as jnp
from jax import lax
from jax.experimental import pallas as pl
from jax.experimental.pallas import tpu as pltpu
from jax.sharding import PartitionSpec as P

f32 = jnp.float32
bf16 = jnp.bfloat16
i32 = jnp.int32
masses_table = (1.008, 12.011, 15.999, 6.94, 30.974, 18.998)
radial_widths = (2.0, 4.0, 6.0, 8.0, 10.0, 12.0, 14.0, 16.0)
time_step = 0.5
friction = 0.2
gauss_width = 0.3
kinds = 6
slots = 64
hidden = 64
chunk = 8
chunks = slots // chunk
own = 256
ranks = 8
atoms_all = 65536
top = 16
span = 2 * top + 1
plane_own = 69
plane_rows = 72
waves = 2 * plane_rows
tau = 2.0 * math.pi
outer = [(u, v) for u in range(4) for v in range(4) if not (u in (1, 2) and v in (1, 2))]
vmem = pl.BlockSpec(memory_space=pltpu.VMEM)
smem = pl.BlockSpec(memory_space=pltpu.SMEM)
params = pltpu.CompilerParams(vmem_limit_bytes=24 * 1024 * 1024)


def call(kernel, outs, specs, scratch=(), cost=None):
    shapes = [jax.ShapeDtypeStruct(s, d) for s, d in outs]
    return pl.pallas_call(
        kernel,
        out_shape=shapes,
        in_specs=specs,
        out_specs=[vmem] * len(shapes),
        scratch_shapes=list(scratch),
        compiler_params=params,
        cost_estimate=cost,
    )


def dot_n(a, b):
    return lax.dot_general(a, b, (((1,), (0,)), ((), ())), preferred_element_type=f32)


def dot_t(a, b):
    return lax.dot_general(a, b, (((1,), (1,)), ((), ())), preferred_element_type=f32)


def dot_c(a, b):
    return lax.dot_general(
        a, b, (((0,), (0,)), ((), ())), precision=lax.Precision.HIGHEST, preferred_element_type=f32
    )


def split(x):
    high = x.astype(bf16)
    return high, (x - high.astype(f32)).astype(bf16)


def dot3(a, b):
    ah, al = split(a)
    bh, bl = split(b)
    return dot_n(ah, bh) + (dot_n(al, bh) + dot_n(ah, bl))


def lane_pick(row, where):
    return jnp.take_along_axis(
        jnp.broadcast_to(row, where.shape), where, axis=1, mode="promise_in_bounds"
    )


def sine_turns(w):
    square = w * w
    total = jnp.full_like(w, -(tau**11) / math.factorial(11))
    for power in (9, 7, 5, 3, 1):
        sign = -1.0 if power % 4 == 3 else 1.0
        total = total * square + sign * tau**power / math.factorial(power)
    return total * w


def circle(turns):
    t = turns - jnp.floor(turns + 0.5)
    cosine = sine_turns(0.25 - jnp.abs(t))
    folded = jnp.where(t > 0.25, 0.5 - t, jnp.where(t < -0.25, -0.5 - t, t))
    return cosine, sine_turns(folded)


def plane_of(rank, shape, axis):
    index = (lax.broadcasted_iota(i32, shape, axis) + rank * plane_own).astype(f32)
    first = jnp.floor((index + (top + 0.5)) * (1.0 / span))
    return first, index - span * first


def pack_kernel(place, kind, out):
    rows = []
    for c in range(3):
        rows += [place[c : c + 1, 0:128], place[c : c + 1, 128:256]]
    species = kind[...].astype(f32)
    rows += [species[:, 0:128], species[:, 128:256]]
    tile = jnp.concatenate(rows, axis=0)
    for z in range(ranks):
        out[z] = tile


def border_kernel(table, rows, cell0, cell1):
    index = jnp.concatenate([rows[0], rows[1], rows[0], rows[1]], axis=0)
    low, high = index & 127, lax.shift_right_logical(index, 7)
    for c in range(4):
        found = jnp.zeros((8, 128), f32)
        for h in range(16):
            row = table[h // 2, 2 * c + h % 2 : 2 * c + h % 2 + 1, :]
            found = jnp.where(high == h, lane_pick(row, low), found)
        for j in range(2):
            cell0[j * 4 + c : j * 4 + c + 1, :] = found[j : j + 1]
            cell1[j * 4 + c : j * 4 + c + 1, :] = found[2 + j : 3 + j]


def columns_kernel(left, cell0, cell1, right, head, tail):
    for u, ref in enumerate((left, cell0, cell1, right)):
        head[u * 4 : u * 4 + 4, :] = ref[0:4, :]
        tail[u * 4 : u * 4 + 4, :] = ref[4:8, :]


def own_gather_kernel(table, listing, near):
    def step(j, carry):
        at = pl.ds(pl.multiple_of(j * chunk, chunk), chunk)
        for half in range(2):
            lanes = slice(half * 128, half * 128 + 128)
            index = listing[at, lanes]
            low, high = index & 127, lax.shift_right_logical(index, 7)
            found = [jnp.zeros((chunk, 128), f32)] * 4
            for h in range(16):
                hit = high == h
                for c in range(4):
                    r = 2 * c + h % 2
                    row = table[h // 2, r : r + 1, :]
                    found[c] = jnp.where(hit, lane_pick(row, low), found[c])
            for c in range(4):
                near[c, at, lanes] = found[c]
        return carry

    lax.fori_loop(0, chunks, step, 0)


def factor_kernel(rank, table, high, low, waves_x):
    shape = (plane_rows, 128)
    ky, kz = plane_of(rank[0], shape, 0)
    kx = (lax.broadcasted_iota(i32, (top, 128), 0) + 1).astype(f32)

    def step(z, carry):
        for half in range(2):
            at = pl.ds(pl.multiple_of(z * own + half * 128, 128), 128)
            x, y, w = (table[z, 2 * c + half : 2 * c + half + 1, :] for c in range(3))
            cosine, sine = circle(ky * y + kz * w)
            both = jnp.concatenate([cosine, sine], axis=0)
            upper, lower = split(both)
            high[:, at] = upper
            low[:, at] = lower
            cosine, sine = circle(kx * x)
            waves_x[0:top, at] = cosine
            waves_x[top : 2 * top, at] = sine
        return carry

    lax.fori_loop(0, ranks, step, 0)


def count_kernel(triples, out):
    kx, ky, kz = (triples[d : d + 1, :].astype(f32) for d in range(3))
    code = span * ky + kz
    flip = jnp.where(code < 0.0, -1.0, 1.0)
    code = code * flip
    kx = kx * flip
    count = kx.shape[1]
    row = lax.broadcasted_iota(i32, (48, count), 0).astype(f32)
    wanted = jnp.where(row < top, row + 1.0, row - (top - 1.0))
    sign = jnp.where(kx < 0.0, -1.0, 1.0)
    value = jnp.where(row < top, 1.0, sign)
    line = jnp.where(row < 2 * top, jnp.where(jnp.abs(kx) == wanted, value, 0.0), 0.0)
    line = jnp.where((row == 2 * top) & (kx == 0.0), 1.0, line).astype(bf16)
    place = lax.broadcasted_iota(i32, (128, count), 0).astype(f32)
    valid = place < plane_own
    for z in range(ranks):
        hit = jnp.where(valid & (code == place + float(z * plane_own)), 1.0, 0.0).astype(bf16)
        out[z] = dot_t(line, hit)[0:40, :]


def message_kernel(
    edges, listing, near, left, right, head, tail, place, kind, tally, counts, first, second_t,
    embed_t, blend_t, project_t, send, feature_out, disp_out, mark_out, slope_out,
    cells, pooled, active,
):
    for u in range(4):
        for c in range(4):
            cells[c * 16 + u * 4 : c * 16 + u * 4 + 1, :] = head[u * 4 + c : u * 4 + c + 1, :]
            cells[c * 16 + u * 4 + 3 : c * 16 + u * 4 + 4, :] = tail[u * 4 + c : u * 4 + c + 1, :]
    for u, ref in ((0, left), (3, right)):
        for j in range(2):
            for c in range(4):
                spot = c * 16 + u * 4 + 1 + j
                cells[spot : spot + 1, :] = ref[j * 4 + c : j * 4 + c + 1, :]
    pooled[...] = jnp.zeros_like(pooled)

    def step(j, carry):
        at = pl.ds(pl.multiple_of(j * chunk, chunk), chunk)
        halves = []
        for half in range(2):
            lanes = slice(half * 128, half * 128 + 128)
            index = listing[at, lanes]
            low, high = index & 127, lax.shift_right_logical(index, 7)
            found = [near[c, at, lanes] for c in range(4)]
            for u, v in outer:
                hit = high == 16 + u * 4 + v
                for c in range(4):
                    spot = c * 16 + u * 4 + v
                    row = cells[spot : spot + 1, :]
                    found[c] = jnp.where(hit, lane_pick(row, low), found[c])
            halves.append(found)
        found = [jnp.concatenate([halves[0][c], halves[1][c]], axis=1) for c in range(4)]
        squared = jnp.zeros((chunk, own), f32)
        for d in range(3):
            offset = found[d] - place[d : d + 1, :]
            offset = offset - jnp.floor(offset + 0.5)
            offset = offset * edges[d]
            disp_out[d, at, :] = offset
            squared = squared + offset * offset
        slot = lax.broadcasted_iota(i32, (chunk, own), 0) + j * chunk
        mark = jnp.where(slot < tally[...], found[3], -1.0)
        mark_out[at, :] = mark
        basis = jnp.concatenate(
            [jnp.exp(squared * (-1.0 / (w * w))) for w in radial_widths], axis=0
        )
        upper, lower = split(basis)
        pre = dot_n(first[...], jnp.concatenate([upper, lower, upper], axis=0))
        gate = 0.5 * jnp.tanh(0.5 * pre) + 0.5
        out = pre * gate
        active[...] = out
        slope_out[j] = gate + out * (1.0 - gate)
        for s in range(kinds):
            total = pooled[s * hidden : (s + 1) * hidden, :]
            for m in range(chunk):
                hit = jnp.broadcast_to(mark[m : m + 1, :], (hidden, own)) == float(s)
                total = total + jnp.where(hit, active[m * hidden : (m + 1) * hidden, :], 0.0)
            pooled[s * hidden : (s + 1) * hidden, :] = total
        return carry

    lax.fori_loop(0, chunks, step, 0)
    message = jnp.zeros((128, own), f32)
    features = jnp.zeros((128, own), f32)
    for s in range(kinds):
        message = message + embed_t[:, s : s + 1] * dot3(
            second_t[...], pooled[s * hidden : (s + 1) * hidden, :]
        )
        features = features + embed_t[:, s : s + 1] * jnp.where(kind[...] == s, 1.0, 0.0)
    features = features + dot3(blend_t[...], message * (1.0 / slots))
    feature_out[...] = features
    charges = dot3(project_t[...], features)
    for z in range(ranks):
        send[z, 0:8, :] = charges[:, 0:128]
        send[z, 8:16, :] = charges[:, 128:256]
        send[z, 16:56, :] = counts[z]


def structure_kernel(core, got, waves_x, high, low, mine, other, total, extra, left_high, left_low):
    total[...] = jnp.zeros_like(total)
    extra[...] = jnp.zeros_like(extra)

    def step(z, carry):
        at = pl.ds(pl.multiple_of(z * own, own), own)
        charge = jnp.concatenate([got[z, 0:8, :], got[z, 8:16, :]], axis=1)
        for f in range(0, 2 * top, 2):
            pair = jnp.concatenate(
                [charge * waves_x[f : f + 1, at], charge * waves_x[f + 1 : f + 2, at]], axis=0
            )
            upper, lower = split(pair)
            left_high[f * 8 : f * 8 + 16, :] = upper
            left_low[f * 8 : f * 8 + 16, :] = lower
        plane_high, plane_low = high[:, at], low[:, at]
        total[...] += dot_t(plane_high, left_high[...]) + (
            dot_t(plane_low, left_high[...]) + dot_t(plane_high, left_low[...])
        )
        upper, lower = split(charge)
        extra[:, 0:waves] += dot_t(upper, plane_high) + (
            dot_t(lower, plane_high) + dot_t(upper, plane_low)
        )
        return carry

    lax.fori_loop(0, ranks, step, 0)
    first = core[0] == 0
    real, imaginary = total[0:plane_rows, :], total[plane_rows:waves, :]
    begin, rest = extra[:, 0:128], extra[:, 128:256]
    for ref, one in ((mine, first), (other, jnp.logical_not(first))):
        ref[0:plane_rows, :] = jnp.where(one, real, imaginary)
        ref[plane_rows : plane_rows + 8, 0:128] = jnp.where(one, begin, rest)
        ref[plane_rows : plane_rows + 8, 128:256] = jnp.zeros((8, 128), f32)


def potential_kernel(
    rank, core, edges, mine, other, got, waves_x, high, low, potential, gradient,
    table, table_high, table_low, result,
):
    first = core[0] == 0
    real = jnp.where(first, mine[0:plane_rows, :], other[0:plane_rows, :])
    imaginary = jnp.where(first, other[0:plane_rows, :], mine[0:plane_rows, :])
    tail = slice(plane_rows, plane_rows + 8)
    begin = jnp.where(first, mine[tail, 0:128], other[tail, 0:128])
    rest = jnp.where(first, other[tail, 0:128], mine[tail, 0:128])
    counts = got[0, 16:56, :]
    for z in range(1, ranks):
        counts = counts + got[z, 16:56, :]
    lane = lax.broadcasted_iota(i32, (top, 128), 1)
    spread = jnp.where(
        lax.shift_right_logical(lane, 3) == lax.broadcasted_iota(i32, (top, 128), 0), 1.0, 0.0
    )
    lane = lax.broadcasted_iota(i32, (8, 128), 1)
    line = lax.broadcasted_iota(i32, (8, 128), 0)
    flat = jnp.where(line == 0, 1.0, 0.0)
    repeat = jnp.where((lane & 7) == line, 1.0, 0.0)
    both = dot_c(counts[0:top], spread)[0:plane_rows]
    apart = dot_c(counts[top : 2 * top], spread)[0:plane_rows]
    zero = dot_c(counts[2 * top : 2 * top + 8], flat)[0:plane_rows]
    lone = dot_c(jnp.concatenate([begin, rest], axis=1), repeat)
    shape = (plane_rows, 128)
    ky, kz = plane_of(rank[0], shape, 0)
    lanes = lax.broadcasted_iota(i32, shape, 1)
    kx = (lax.shift_right_logical(lanes, 3) + 1).astype(f32)
    qx, qy, qz = tau * kx / edges[0], tau * ky / edges[1], tau * kz / edges[2]
    flat_square = qy * qy + qz * qz
    square = qx * qx + flat_square

    def weigh(q):
        return (tau / atoms_all) * jnp.exp((-0.5 * gauss_width * gauss_width) * q) / q

    weight = weigh(square)
    both, apart = both * weight, apart * weight
    zero = zero * jnp.where(flat_square > 0.0, weigh(jnp.maximum(flat_square, 1e-6)), 0.0)
    real_c, real_s = real[:, 0:128], real[:, 128:256]
    imag_c, imag_s = imaginary[:, 0:128], imaginary[:, 128:256]
    pair_c = (both * real_c - apart * imag_s, both * imag_c + apart * real_s)
    pair_s = (both * real_s + apart * imag_c, both * imag_s - apart * real_c)
    ty, tz = tau * ky, tau * kz
    upper, lower = slice(0, plane_rows), slice(plane_rows, waves)
    for part, (re, im) in enumerate((pair_c, pair_s)):
        for form, scale in enumerate((None, ty, tz)):
            at = slice(form * 256 + part * 128, form * 256 + part * 128 + 128)
            table[upper, at] = re if scale is None else scale * im
            table[lower, at] = im if scale is None else -(scale * re)
    re, im = zero * lone[0:plane_rows], zero * lone[plane_rows:waves]
    group = lax.shift_right_logical(lanes, 3)
    turn = jnp.where(group == 1, ty, tz)
    at = slice(768, 896)
    table[upper, at] = jnp.where(group == 0, re, turn * im)
    table[lower, at] = jnp.where(group == 0, im, -(turn * re))
    for block in range(7):
        at = slice(block * 128, block * 128 + 128)
        turned = jnp.transpose(table[:, at])
        table_high[at, 0:waves], table_low[at, 0:waves] = split(turned)

    def step(z, carry):
        at = pl.ds(pl.multiple_of(z * own, own), own)
        plane_high, plane_low = high[:, at], low[:, at]
        weights = table_high[0:800, 0:waves]
        result[...] = dot_n(weights, plane_high) + (
            dot_n(table_low[0:800, 0:waves], plane_high) + dot_n(weights, plane_low)
        )
        total = [result[768:776, :], jnp.zeros((8, own), f32), result[776:784, :], result[784:792, :]]
        for f in range(2 * top):
            wave = waves_x[f : f + 1, at]
            for form, slot in enumerate((0, 2, 3)):
                lines = slice(form * 256 + f * 8, form * 256 + f * 8 + 8)
                total[slot] = total[slot] + wave * result[lines, :]
        for k in range(top):
            cosine, sine = waves_x[k : k + 1, at], waves_x[top + k : top + k + 1, at]
            turn = tau * (k + 1)
            total[1] = total[1] + (turn * cosine) * result[(top + k) * 8 : (top + k) * 8 + 8, :]
            total[1] = total[1] - (turn * sine) * result[k * 8 : k * 8 + 8, :]
        potential[z] = total[0]
        charge = jnp.concatenate([got[z, 0:8, :], got[z, 8:16, :]], axis=1)
        for d in range(3):
            line = jnp.sum(charge * total[1 + d], axis=0, keepdims=True) / edges[d]
            gradient[z, 2 * d : 2 * d + 1, :] = line[:, 0:128]
            gradient[z, 2 * d + 1 : 2 * d + 2, :] = line[:, 128:256]
        return carry

    lax.fori_loop(0, ranks, step, 0)


def pair_kernel(
    got, features, disp, marks, slope, listing, lines, first_high, first_low, second, embed_t,
    blend, energy, energy_t, energy_final, project, cells0, cells3, mid0, mid3, domain, direct,
    upstream, upper, lower, left, right, total, pulled,
):
    potential = got[0]
    for z in range(1, ranks):
        potential = potential + got[z]
    activation = dot3(energy_t[...], features[...])
    gate = 0.5 * jnp.tanh(0.5 * activation) + 0.5
    ramp = energy_final[...] * gate * (1.0 + activation * (1.0 - gate))
    change = dot3(energy[...], ramp) + dot3(project[...], potential)
    change = dot3(blend[...], change) * (1.0 / slots)
    for s in range(kinds):
        upstream[s] = dot3(second[...], embed_t[:, s : s + 1] * change)
    total[...] = jnp.zeros_like(total)
    pulled[...] = jnp.zeros_like(pulled)
    row_high = lax.broadcasted_iota(i32, (32, own), 0)
    row_low = lax.broadcasted_iota(i32, (128, own), 0)

    def step(j, carry):
        at = pl.ds(pl.multiple_of(j * chunk, chunk), chunk)
        offsets = [disp[d, at, :] for d in range(3)]
        mark = marks[at, :]
        for m in range(chunk):
            mine = jnp.broadcast_to(mark[m : m + 1, :], (hidden, own))
            chosen = jnp.zeros((hidden, own), f32)
            for s in range(kinds):
                chosen = jnp.where(mine == float(s), upstream[s], chosen)
            chosen = chosen * slope[j, m * hidden : (m + 1) * hidden, :]
            upper[m * hidden : (m + 1) * hidden, :], lower[m * hidden : (m + 1) * hidden, :] = (
                split(chosen)
            )
        back = dot_n(first_high[...], upper[...]) + (
            dot_n(first_low[...], upper[...]) + dot_n(first_high[...], lower[...])
        )
        squared = offsets[0] * offsets[0] + offsets[1] * offsets[1] + offsets[2] * offsets[2]
        radial = jnp.zeros((chunk, own), f32)
        for n, w in enumerate(radial_widths):
            lean = jnp.exp(squared * (-1.0 / (w * w))) * (-2.0 / (w * w))
            radial = radial + lean * back[n * chunk : (n + 1) * chunk, :]
        pulls = [radial * offset for offset in offsets]
        index = listing[at, :]
        low, high = index & 127, lax.shift_right_logical(index, 7)
        pieces = []
        for d in range(3):
            pulled[d] += pulls[d]
            main = pulls[d].astype(bf16).astype(f32)
            pieces.append((main, pulls[d] - main))
        for m in range(chunk):
            lanes = slice(m * own, (m + 1) * own)
            hit = jnp.broadcast_to(high[m : m + 1, :], (32, own)) == row_high
            for part in range(2):
                for d in range(3):
                    row = part * 96 + d * 32
                    left[row : row + 32, lanes] = jnp.where(
                        hit, pieces[d][part][m : m + 1, :], 0.0
                    ).astype(bf16)
            spot = jnp.broadcast_to(low[m : m + 1, :], (128, own)) == row_low
            right[:, lanes] = jnp.where(spot, 1.0, 0.0).astype(bf16)
        total[...] += dot_t(left[...], right[...])
        return carry

    lax.fori_loop(0, chunks, step, 0)
    scattered = total[0:96, :] + total[96:192, :]
    nothing = jnp.zeros((1, 128), f32)
    for u in range(4):
        for c in range(4):
            for ref, v in ((cells0, 0), (cells3, 3)):
                spot = c * 32 + 16 + u * 4 + v
                value = scattered[spot : spot + 1, :] if c < 3 else nothing
                ref[u * 4 + c : u * 4 + c + 1, :] = value
    for ref, u in ((mid0, 0), (mid3, 3)):
        for j in range(2):
            for c in range(4):
                spot = c * 32 + 16 + u * 4 + 1 + j
                value = scattered[spot : spot + 1, :] if c < 3 else nothing
                ref[j * 4 + c : j * 4 + c + 1, :] = value
    for z in range(ranks):
        for d in range(3):
            for half in range(2):
                spot, r = d * 32 + z * 2 + half, 2 * d + half
                domain[z, r : r + 1, :] = scattered[spot : spot + 1, :] + lines[z, r : r + 1, :]
        domain[z, 6:8, :] = jnp.zeros((2, 128), f32)
    for d in range(3):
        line = -jnp.sum(pulled[d], axis=0, keepdims=True)
        direct[2 * d : 2 * d + 1, :] = line[:, 0:128]
        direct[2 * d + 1 : 2 * d + 2, :] = line[:, 128:256]
    direct[6:8, :] = jnp.zeros((2, 128), f32)


def echo_kernel(above, below, mid0, mid3, send0, send3, inner0, inner1):
    for u, ref in ((0, send0), (1, inner0), (2, inner1), (3, send3)):
        both = jnp.concatenate([below[u * 4 : u * 4 + 4, :], above[u * 4 : u * 4 + 4, :]], axis=0)
        if u == 0:
            both = both + mid0[...]
        if u == 3:
            both = both + mid3[...]
        ref[...] = both


def border_back_kernel(inner0, inner1, from_left, from_right, rows, domain, out):
    cells = (inner0[...] + from_left[...], inner1[...] + from_right[...])
    row_high = lax.broadcasted_iota(i32, (16, 128), 0)
    row_low = lax.broadcasted_iota(i32, (128, 128), 0)
    total = jnp.zeros((96, 128), f32)
    for i in range(2):
        index = rows[i]
        low, high = index & 127, lax.shift_right_logical(index, 7)
        for j in range(2):
            hit = jnp.broadcast_to(high[j : j + 1, :], (16, 128)) == row_high
            spot = jnp.broadcast_to(low[j : j + 1, :], (128, 128)) == row_low
            left = []
            for part in range(2):
                for c in range(3):
                    value = cells[i][j * 4 + c : j * 4 + c + 1, :]
                    main = value.astype(bf16).astype(f32)
                    left.append(jnp.where(hit, main if part == 0 else value - main, 0.0))
            total = total + dot_t(
                jnp.concatenate(left, axis=0).astype(bf16),
                jnp.where(spot, 1.0, 0.0).astype(bf16),
            )
    total = total[0:48, :] + total[48:96, :]
    for z in range(ranks):
        lines = [total[d * 16 + z * 2 : d * 16 + z * 2 + 2, :] for d in range(3)]
        lines.append(jnp.zeros((2, 128), f32))
        out[z] = domain[z] + jnp.concatenate(lines, axis=0)


def step_kernel(edges, got, direct, place, speed, kind, kicks, force_out, place_out, speed_out):
    gradient = direct[...]
    for z in range(ranks):
        gradient = gradient + got[z]
    species = kind[...]
    mass = jnp.zeros((1, own), f32)
    for s in range(kinds):
        mass = jnp.where(species == s, masses_table[s], mass)
    retain = math.exp(-friction * time_step)
    spread = jnp.sqrt((1.0 - retain * retain) / mass)
    for d in range(3):
        row = slice(d, d + 1)
        force = -jnp.concatenate(
            [gradient[2 * d : 2 * d + 1, :], gradient[2 * d + 1 : 2 * d + 2, :]], axis=1
        )
        halfway = speed[row, :] + 0.5 * time_step * force / mass
        updated = retain * halfway + spread * kicks[row, :]
        force_out[row, :] = force
        speed_out[row, :] = updated
        place_out[row, :] = place[row, :] + 0.5 * time_step * (halfway + updated) / edges[d]


def shift(axis, by):
    count = lax.axis_size(axis)
    return [(i, (i + by) % count) for i in range(count)]


def partners():
    maps = (
        lambda x, yl, yh, c: (x, yl, yh, 1 - c),
        lambda x, yl, yh, c: (x, 1 - yl, yh, c),
        lambda x, yl, yh, c: (x, 1 - yl, 1 - yh, c),
        lambda x, yl, yh, c: (x ^ 1, yl, yh, c),
        lambda x, yl, yh, c: (3 - x, yl, yh, c),
    )
    places = [(x, a, b, c) for x in range(4) for a in range(2) for b in range(2) for c in range(2)]
    number = {p: (p[0] * 2 + p[1]) * 4 + p[2] * 2 + p[3] for p in places}
    return [[(number[p], number[m(*p)]) for p in places] for m in maps]


def body(
    fractional_placements,
    particle_speeds,
    element_kinds,
    adjacent_padded_indices,
    adjacent_valid_tally,
    border_particle_rows,
    reciprocal_integer_triples,
    cell_edge_sizes,
    friction_random_kicks,
    element_feature_vectors,
    distance_net_initial_weights,
    distance_net_final_weights,
    message_blend_matrix,
    energy_head_initial_weights,
    energy_head_final_weights,
    hidden_electric_projection,
):
    rank = lax.axis_index("ka").astype(i32).reshape(1)
    core = (lax.axis_index("gy") % 2).astype(i32).reshape(1)
    kind = element_kinds.reshape(1, own)
    tally = adjacent_valid_tally.reshape(1, own)
    listing = adjacent_padded_indices.T
    blocks = jnp.einsum(
        "nh,ml->mhnl", distance_net_initial_weights, jnp.eye(chunk, dtype=f32), precision="highest"
    ).reshape(chunk * hidden, 8 * chunk)
    blocks_high, blocks_low = split(blocks)
    first = jnp.concatenate([blocks_high, blocks_high, blocks_low], axis=1)
    embed_t = element_feature_vectors.T

    packed = call(pack_kernel, [((ranks, 8, 128), f32)], [vmem] * 2)(fractional_placements, kind)[0]
    table = lax.all_to_all(packed, "ka", 0, 0)
    cell0, cell1 = call(border_kernel, [((8, 128), f32)] * 2, [vmem] * 2)(
        table, border_particle_rows
    )
    left = lax.ppermute(cell1, "gx", shift("gx", 1))
    right = lax.ppermute(cell0, "gx", shift("gx", -1))
    head, tail = call(columns_kernel, [((16, 128), f32)] * 2, [vmem] * 4)(left, cell0, cell1, right)
    tail_in = lax.ppermute(tail, "gy", shift("gy", 1))
    head_in = lax.ppermute(head, "gy", shift("gy", -1))

    near = call(
        own_gather_kernel,
        [((4, slots, own), f32)],
        [vmem] * 2,
        cost=pl.CostEstimate(flops=20_000_000, bytes_accessed=400_000, transcendentals=0),
    )(table, listing)[0]
    high, low, waves_x = call(
        factor_kernel,
        [((waves, ranks * own), bf16), ((waves, ranks * own), bf16), ((2 * top, ranks * own), f32)],
        [smem, vmem],
        cost=pl.CostEstimate(flops=10_000_000, bytes_accessed=1_500_000, transcendentals=0),
    )(rank, table)
    counts = call(
        count_kernel,
        [((ranks, 40, 128), f32)],
        [vmem],
        cost=pl.CostEstimate(flops=10_000_000, bytes_accessed=200_000, transcendentals=0),
    )(reciprocal_integer_triples)[0]

    send, features, disp, marks, slope = call(
        message_kernel,
        [
            ((ranks, 56, 128), f32),
            ((128, own), f32),
            ((3, slots, own), f32),
            ((slots, own), f32),
            ((chunks, chunk * hidden, own), f32),
        ],
        [smem] + [vmem] * 15,
        [
            pltpu.VMEM((64, 128), f32),
            pltpu.VMEM((kinds * hidden, own), f32),
            pltpu.VMEM((chunk * hidden, own), f32),
        ],
    )(
        cell_edge_sizes, listing, near, left, right, tail_in, head_in, fractional_placements, kind,
        tally, counts, first, distance_net_final_weights.T, embed_t, message_blend_matrix.T,
        hidden_electric_projection.T,
    )
    got = lax.all_to_all(send, "ka", 0, 0)

    mine, other = call(
        structure_kernel,
        [((plane_rows + 8, own), f32)] * 2,
        [smem] + [vmem] * 4,
        [
            pltpu.VMEM((waves, own), f32),
            pltpu.VMEM((8, own), f32),
            pltpu.VMEM((own, own), bf16),
            pltpu.VMEM((own, own), bf16),
        ],
    )(core, got, waves_x, high, low)
    swaps = partners()
    both = ("gx", "gy")
    summed = mine + lax.ppermute(other, both, swaps[0])
    for swap in swaps[1:]:
        summed = summed + lax.ppermute(summed, both, swap)
    opposite = lax.ppermute(summed, both, swaps[0])

    potential, lines = call(
        potential_kernel,
        [((ranks, 8, own), f32), ((ranks, 8, 128), f32)],
        [smem] * 3 + [vmem] * 6,
        [
            pltpu.VMEM((waves, 896), f32),
            pltpu.VMEM((896, own), bf16),
            pltpu.VMEM((896, own), bf16),
            pltpu.VMEM((800, own), f32),
        ],
    )(rank, core, cell_edge_sizes, summed, opposite, got, waves_x, high, low)
    shares = lax.all_to_all(potential, "ka", 0, 0)

    cells0, cells3, mid0, mid3, domain, direct = call(
        pair_kernel,
        [
            ((16, 128), f32),
            ((16, 128), f32),
            ((8, 128), f32),
            ((8, 128), f32),
            ((ranks, 8, 128), f32),
            ((8, 128), f32),
        ],
        [vmem] * 16,
        [
            pltpu.VMEM((kinds, hidden, own), f32),
            pltpu.VMEM((chunk * hidden, own), bf16),
            pltpu.VMEM((chunk * hidden, own), bf16),
            pltpu.VMEM((192, chunk * own), bf16),
            pltpu.VMEM((128, chunk * own), bf16),
            pltpu.VMEM((192, 128), f32),
            pltpu.VMEM((3, chunk, own), f32),
        ],
    )(
        shares, features, disp, marks, slope, listing, lines, blocks_high.T, blocks_low.T,
        distance_net_final_weights, embed_t, message_blend_matrix, energy_head_initial_weights,
        energy_head_initial_weights.T, energy_head_final_weights.reshape(-1, 1),
        hidden_electric_projection,
    )
    above = lax.ppermute(cells0, "gy", shift("gy", -1))
    below = lax.ppermute(cells3, "gy", shift("gy", 1))
    send0, send3, inner0, inner1 = call(echo_kernel, [((8, 128), f32)] * 4, [vmem] * 4)(
        above, below, mid0, mid3
    )
    from_right = lax.ppermute(send0, "gx", shift("gx", -1))
    from_left = lax.ppermute(send3, "gx", shift("gx", 1))
    reaction = call(border_back_kernel, [((ranks, 8, 128), f32)], [vmem] * 6)(
        inner0, inner1, from_left, from_right, border_particle_rows, domain
    )[0]
    returned = lax.all_to_all(reaction, "ka", 0, 0)
    forces, places, speeds = call(
        step_kernel, [((3, own), f32)] * 3, [smem] + [vmem] * 6
    )(
        cell_edge_sizes, returned, direct, fractional_placements, particle_speeds, kind,
        friction_random_kicks,
    )
    return (forces, places, speeds)


def solution(mesh):
    atoms = ("gx", "gy", "ka")
    return jax.shard_map(
        body,
        mesh=mesh,
        in_specs=(
            P(None, atoms),
            P(None, atoms),
            P(atoms),
            P(atoms, None),
            P(atoms),
            P("gx", "gy", None),
            P(None, "ka"),
            P(),
            P(None, atoms),
            P(),
            P(),
            P(),
            P(),
            P(),
            P(),
            P(),
        ),
        out_specs=(P(None, atoms), P(None, atoms), P(None, atoms)),
        check_vma=False,
    )
```

time: 972 us -> 144 us (0.15)
  matrix products: 364 us -> 0 us
  waiting for transfers between devices: 300 us -> 57.9 us
  other arithmetic: 110 us -> 0.86 us
  local copies, waits for them, and re-layouts: 106 us -> 14.3 us
  blocking collectives: 55.4 us -> 10.4 us
  Pallas kernels: 0 us -> 32.4 us
  starting transfers between devices: 11.5 us -> 26 us
  between operations: 15 us -> 0.95 us
    dot_general x149 -> x0, matrix products: 364 us -> none  [product(): jnp.dot(left_side, right_side, precision=highest, preferred_element_type=...]
    psum x1 -> x0, waiting for transfers between devices: 255 us -> none  [body(): lax.psum(structure(fractional_placements, charges, reciprocal_real_triple...]
    scatter-add x2 -> x0, other arithmetic: 93.5 us -> none  [the longest x1 88.3 us: body(): scattered = jnp.zeros((3, surround.shape[1]), jnp.float32).at[:, adjacent...]
    gather x3 -> x0, local copies, waits for them, and re-layouts: 62 us -> none  [the longest x2 60.9 us: displacements(): nearby = extended[:, listing]]
    all_gather x2 -> x0, blocking collectives: 55.4 us -> none  [the longest x1 30.6 us: body(): domain_packed = lax.all_gather(packed, 'ka', axis=1, tiled=True)]
    unnamed x3 -> x0, waiting for transfers between devices: 39 us -> none
    pallas_call x0 -> x13, Pallas kernels: none -> 32.4 us  [the longest x1 8.52 us: body(): call(message_kernel, [((ranks, 56, 128), f32), ((128, own), f32), ((3, sl...]
    slice x138 -> x0, local copies, waits for them, and re-layouts: 29.9 us -> none  [the longest x32 26.3 us: one_step(): kblock[0][None] * second_part]
  transfers between devices with their start and end apart: 10 -> 17, of which waited for: 8 -> 15; matrix products, arithmetic and copies ran while one was open for 1% -> 3% of each run, Pallas kernels for 0% -> 3%
where the time goes in v1:
time: 144 us; the launch traced here: 143 us
  waiting for transfers between devices  57.9 us (40%)
  Pallas kernels  32.4 us (22%)
  starting transfers between devices  26 us (18%)
  local copies, waits for them, and re-layouts  14.3 us (10%)
  blocking collectives  10.4 us (7%)
    ppermute x4, waiting for transfers between devices, body(): summed = summed + lax.ppermute(summed, both, swap)  17.9 us
    unnamed x53, local copies, waits for them, and re-layouts  14 us
    all_to_all x1, blocking collectives, body(): returned = lax.all_to_all(reaction, 'ka', 0, 0)  10.4 us
    all_to_all x1, waiting for transfers between devices, body(): got = lax.all_to_all(send, 'ka', 0, 0)  9.71 us
    pallas_call x1, Pallas kernels, body(): call(message_kernel, [((ranks, 56, 128), f32), ((128, own), f32), ((3, sl...  8.52 us
    all_to_all x1, starting transfers between devices, body(): table = lax.all_to_all(packed, 'ka', 0, 0)  8.47 us
    pallas_call x1, Pallas kernels, body(): call(pair_kernel, [((16, 128), f32), ((16, 128), f32), ((8, 128), f32), (...  8.45 us
    all_to_all x1, waiting for transfers between devices, body(): shares = lax.all_to_all(potential, 'ka', 0, 0)  7.81 us
  transfers between devices with their start and end apart: 17, of which 15 were waited for; matrix products, arithmetic and copies ran while one was open for 3% of the time, Pallas kernels for 3%

profile of v1, /device:TPU:14, one launch (start us, length us, event | category | flops | bytes accessed | tf_op | source)
XLA Modules:
  0.0 142.8 jit_solution(10836167141694081591)
XLA Ops:
  0.7 0.7 copy-done.6
  1.3 0.7 copy-done.13
  2.0 0.6 shard_map.175
  2.6 8.5 %all-to-all-start = ((f32[8,8,128]{2,1,0:T(8,128)}), f32[8,8,128]{2,1,0:T(8,128)S(1)}, u32[]{:S(2)}, u32[]{:S(2)}) async-start(f32[8,8,128]{2,1,0:T(8,128)} %shard_map.175), calls=%async_computation | async-start | bytes 65536 | tf_op jit(solution)/shard_map/all_to_all | solution.py:597
  11.1 0.8 multiply_bitcast_fusion
  12.0 7.1 %all-to-all-done.table = f32[8,8,128]{2,1,0:T(8,128)S(1)} async-done(((f32[8,8,128]{2,1,0:T(8,128)}), f32[8,8,128]{2,1,0:T(8,128)S(1)}, u32[]{:S(2)}, u32[]{:S(2)}) %all-to-all-start) | async-done | bytes 32800 | tf_op jit(solution)/shard_map/all_to_all | solution.py:597
  19.1 0.7 copy-done.16
  20.4 1.7 %collective-permute-start.1 = (f32[8,128]{1,0:T(8,128)S(1)}, f32[8,128]{1,0:T(8,128)S(1)}, u32[]{:S(2)}, u32[]{:S(2)}) collective-permute-start(f32[8,128]{1,0:T(8,128)S(1)} %get-tuple-element.30.cell0), channel_id=1, source_target_pairs={{0,224},{32,0},{64,32},{96,64},{128,96},{160,128},{192,160},{224,1... | collective-permute-start | bytes 12296 | tf_op jit(solution)/shard_map/ppermute | solution.py:602
  22.2 1.5 %collective-permute-done.left = f32[8,128]{1,0:T(8,128)S(1)} collective-permute-done((f32[8,128]{1,0:T(8,128)S(1)}, f32[8,128]{1,0:T(8,128)S(1)}, u32[]{:S(2)}, u32[]{:S(2)}) %collective-permute-start) | collective-permute-done | bytes 4128 | tf_op jit(solution)/shard_map/ppermute | solution.py:601
  23.6 2.6 %collective-permute-done.1.right = f32[8,128]{1,0:T(8,128)S(1)} collective-permute-done((f32[8,128]{1,0:T(8,128)S(1)}, f32[8,128]{1,0:T(8,128)S(1)}, u32[]{:S(2)}, u32[]{:S(2)}) %collective-permute-start.1) | collective-permute-done | bytes 4128 | tf_op jit(solution)/shard_map/ppermute | solution.py:602
  26.2 3.2 %collective-permute-start.3 = (f32[16,128]{1,0:T(8,128)S(1)}, f32[16,128]{1,0:T(8,128)S(1)}, u32[]{:S(2)}, u32[]{:S(2)}) collective-permute-start(f32[16,128]{1,0:T(8,128)S(1)} %get-tuple-element.32), channel_id=1, source_target_pairs={{0,24},{8,0},{16,8},{24,16},{1,25},{9,1},{17,9},{25,17},{2,26},{10... | collective-permute-start | bytes 24584 | tf_op jit(solution)/shard_map/ppermute | solution.py:605
  29.6 0.8 copy.20
  30.4 0.8 copy.19
  31.3 0.9 copy.21
  32.2 0.8 copy-done.10
  33.0 1.6 %shard_map.179.counts = f32[8,40,128]{2,1,0:T(8,128)S(1)} custom-call(s32[3,2048]{1,0:T(4,128)S(1)} %copy-done.10), custom_call_target="tpu_custom_call" | custom-call | flops 10000000 | bytes 200000 | tf_op jit(solution)/shard_map/pallas_call | solution.py:619
  34.6 0.8 copy-done.2
  35.4 1.7 %shard_map.176.near = f32[4,64,256]{2,1,0:T(8,128)S(1)} custom-call(f32[8,8,128]{2,1,0:T(8,128)S(1)} %all-to-all-done.table, s32[64,256]{1,0:T(8,128)S(1)} %bitcast.21), custom_call_target="tpu_custom_call" | custom-call | flops 20000000 | bytes 400000 | tf_op jit(solution)/shard_map/pallas_call | solution.py:607
  37.1 0.7 copy-done.7
  37.8 0.7 copy-done.11
  38.5 0.7 copy-done.14
  39.2 0.7 copy-done.18
  39.8 0.7 copy-done.22
  40.5 8.5 %shard_map.180 = (f32[8,56,128]{2,1,0:T(8,128)}, f32[128,256]{1,0:T(8,128)S(1)}, f32[3,64,256]{2,1,0:T(8,128)S(1)}, f32[64,256]{1,0:T(8,128)S(1)}, f32[8,512,256]{2,1,0:T(8,128)S(1)}) custom-call(f32[3]{0:T(128)S(1)} %copy-done.18, s32[64,256]{1,0:T(8,128)S(1)} %bitcast.22, f32[4,64,256]{2,1,0:T(8,128)S(1)} %shard_map.176.near, ...), custom_call_target="tpu_custom_call" | custom-call | tf_op jit(solution)/shard_map/pallas_call | solution.py:626
  49.0 2.0 %copy-done = f32[8,512,256]{2,1,0:T(8,128)} copy-done((f32[8,512,256]{2,1,0:T(8,128)}, f32[8,512,256]{2,1,0:T(8,128)S(1)}, u32[]{:S(2)}) %copy-start) | copy-done | bytes 4194328
  51.0 3.4 %all-to-all-start.1 = ((f32[8,56,128]{2,1,0:T(8,128)}), f32[8,56,128]{2,1,0:T(8,128)S(1)}, u32[]{:S(2)}, u32[]{:S(2)}) async-start(f32[8,56,128]{2,1,0:T(8,128)} %get-tuple-element.33), calls=%async_computation.1 | async-start | bytes 458752 | tf_op jit(solution)/shard_map/all_to_all | solution.py:646
  54.4 1.3 shard_map.181
  55.7 9.7 %all-to-all-done.1.got = f32[8,56,128]{2,1,0:T(8,128)S(1)} async-done(((f32[8,56,128]{2,1,0:T(8,128)}), f32[8,56,128]{2,1,0:T(8,128)S(1)}, u32[]{:S(2)}, u32[]{:S(2)}) %all-to-all-start.1) | async-done | bytes 229408 | tf_op jit(solution)/shard_map/all_to_all | solution.py:646
  65.4 2.6 %shard_map.182 = (f32[80,256]{1,0:T(8,128)S(1)}, f32[80,256]{1,0:T(8,128)S(1)}) custom-call(s32[1]{0:T(128)} %bitcast.1.core, f32[8,56,128]{2,1,0:T(8,128)S(1)} %all-to-all-done.1.got, f32[32,2048]{1,0:T(8,128)S(1)} %get-tuple-element.34.waves_x, bf16[144,2048]{1,0:T(8,128)(2,1)S(1)} %get-tuple-element.35.high, bf16[144,2048]{1,0:T(8,128)(2,1)S(1)} %get-tuple-element.36.low), custom_call_target="tpu_custom_call" | custom-call | tf_op jit(solution)/shard_map/pallas_call | solution.py:648
  68.1 1.3 collective-permute-done.4
  69.5 4.5 %collective-permute-done.5 = f32[80,256]{1,0:T(8,128)S(1)} collective-permute-done((f32[80,256]{1,0:T(8,128)S(1)}, f32[80,256]{1,0:T(8,128)S(1)}, u32[]{:S(2)}, u32[]{:S(2)}) %collective-permute-start.5) | collective-permute-done | bytes 81952 | tf_op jit(solution)/shard_map/ppermute | solution.py:663
  74.6 4.0 %collective-permute-done.6 = f32[80,256]{1,0:T(8,128)S(1)} collective-permute-done((f32[80,256]{1,0:T(8,128)S(1)}, f32[80,256]{1,0:T(8,128)S(1)}, u32[]{:S(2)}, u32[]{:S(2)}) %collective-permute-start.6) | collective-permute-done | bytes 81952 | tf_op jit(solution)/shard_map/ppermute | solution.py:663
  79.0 4.1 %collective-permute-done.7 = f32[80,256]{1,0:T(8,128)S(1)} collective-permute-done((f32[80,256]{1,0:T(8,128)S(1)}, f32[80,256]{1,0:T(8,128)S(1)}, u32[]{:S(2)}, u32[]{:S(2)}) %collective-permute-start.7) | collective-permute-done | bytes 81952 | tf_op jit(solution)/shard_map/ppermute | solution.py:663
  83.5 5.4 %collective-permute-done.8 = f32[80,256]{1,0:T(8,128)S(1)} collective-permute-done((f32[80,256]{1,0:T(8,128)S(1)}, f32[80,256]{1,0:T(8,128)S(1)}, u32[]{:S(2)}, u32[]{:S(2)}) %collective-permute-start.8) | collective-permute-done | bytes 81952 | tf_op jit(solution)/shard_map/ppermute | solution.py:663
  88.9 1.3 collective-permute-done.9.other
  90.2 6.2 %shard_map.183 = (f32[8,8,256]{2,1,0:T(8,128)}, f32[8,8,128]{2,1,0:T(8,128)S(1)}) custom-call(s32[1]{0:T(128)} %bitcast.rank, s32[1]{0:T(128)} %bitcast.1.core, f32[3]{0:T(128)S(1)} %copy-done.19, f32[80,256]{1,0:T(8,128)S(1)} %add.24.mine, f32[80,256]{1,0:T(8,128)S(1)} %collective-permute-done.9.other, f32[8,56,128]{2,1,0:T(8,128)S(1)} %all-to-all-done.1.got, ...), custom_call_target="tpu_custom_call" | custom-call | tf_op jit(solution)/shard_map/pallas_call | solution.py:666
  96.4 3.5 %all-to-all-start.2 = ((f32[8,8,256]{2,1,0:T(8,128)}), f32[8,8,256]{2,1,0:T(8,128)S(1)}, u32[]{:S(2)}, u32[]{:S(2)}) async-start(f32[8,8,256]{2,1,0:T(8,128)} %get-tuple-element.39), calls=%async_computation.2 | async-start | bytes 131072 | tf_op jit(solution)/shard_map/all_to_all | solution.py:677
  100.3 7.8 %all-to-all-done.2.got = f32[8,8,256]{2,1,0:T(8,128)S(1)} async-done(((f32[8,8,256]{2,1,0:T(8,128)}), f32[8,8,256]{2,1,0:T(8,128)S(1)}, u32[]{:S(2)}, u32[]{:S(2)}) %all-to-all-start.2) | async-done | bytes 65568 | tf_op jit(solution)/shard_map/all_to_all | solution.py:677
  108.1 2.2 %copy-done.1 = f32[8,512,256]{2,1,0:T(8,128)S(1)} copy-done((f32[8,512,256]{2,1,0:T(8,128)S(1)}, f32[8,512,256]{2,1,0:T(8,128)}, u32[]{:S(2)}) %copy-start.1) | copy-done | bytes 4194328
  110.3 8.5 %shard_map.184 = (f32[16,128]{1,0:T(8,128)S(1)}, f32[16,128]{1,0:T(8,128)S(1)}, f32[8,128]{1,0:T(8,128)S(1)}, f32[8,128]{1,0:T(8,128)S(1)}, f32[8,8,128]{2,1,0:T(8,128)S(1)}, /*index=5*/f32[8,128]{1,0:T(8,128)S(1)}) custom-call(f32[8,8,256]{2,1,0:T(8,128)S(1)} %all-to-all-done.2.got, f32[128,256]{1,0:T(8,128)S(1)} %get-tuple-element.40.features, ...), custom_call_target="tpu_custom_call" | custom-call | tf_op jit(solution)/shard_map/pallas_call | solution.py:679
  118.7 1.5 %collective-permute-start.10 = (f32[16,128]{1,0:T(8,128)S(1)}, f32[16,128]{1,0:T(8,128)S(1)}, u32[]{:S(2)}, u32[]{:S(2)}) collective-permute-start(f32[16,128]{1,0:T(8,128)S(1)} %get-tuple-element.45), channel_id=1, source_target_pairs={{0,24},{8,0},{16,8},{24,16},{1,25},{9,1},{17,9},{25,17},{2,26},{10... | collective-permute-start | bytes 24584 | tf_op jit(solution)/shard_map/ppermute | solution.py:705
  120.2 1.4 collective-permute-done.10.above
  121.6 3.2 %collective-permute-done.11.below = f32[16,128]{1,0:T(8,128)S(1)} collective-permute-done((f32[16,128]{1,0:T(8,128)S(1)}, f32[16,128]{1,0:T(8,128)S(1)}, u32[]{:S(2)}, u32[]{:S(2)}) %collective-permute-start.11) | collective-permute-done | bytes 8224 | tf_op jit(solution)/shard_map/ppermute | solution.py:706
  125.3 1.5 %collective-permute-start.13 = (f32[8,128]{1,0:T(8,128)S(1)}, f32[8,128]{1,0:T(8,128)S(1)}, u32[]{:S(2)}, u32[]{:S(2)}) collective-permute-start(f32[8,128]{1,0:T(8,128)S(1)} %get-tuple-element.52), channel_id=1, source_target_pairs={{0,224},{32,0},{64,32},{96,64},{128,96},{160,128},{192,160},{224,1... | collective-permute-start | bytes 12296 | tf_op jit(solution)/shard_map/ppermute | solution.py:710
  126.8 1.6 %collective-permute-done.12.from_left = f32[8,128]{1,0:T(8,128)S(1)} collective-permute-done((f32[8,128]{1,0:T(8,128)S(1)}, f32[8,128]{1,0:T(8,128)S(1)}, u32[]{:S(2)}, u32[]{:S(2)}) %collective-permute-start.12) | collective-permute-done | bytes 4128 | tf_op jit(solution)/shard_map/ppermute | solution.py:711
  128.4 2.6 %collective-permute-done.13.from_right = f32[8,128]{1,0:T(8,128)S(1)} collective-permute-done((f32[8,128]{1,0:T(8,128)S(1)}, f32[8,128]{1,0:T(8,128)S(1)}, u32[]{:S(2)}, u32[]{:S(2)}) %collective-permute-start.13) | collective-permute-done | bytes 4128 | tf_op jit(solution)/shard_map/ppermute | solution.py:710
  131.2 10.4 %all_to_all.20.got = f32[8,8,128]{2,1,0:T(8,128)S(1)} all-to-all(f32[8,8,128]{2,1,0:T(8,128)S(1)} %shard_map.186), channel_id=1, replica_groups=mesh['gx'=8,'gy'=4,'ka'=8] {'ka'}, dimensions={0} | all-to-all | bytes 65536 | tf_op jit(solution)/shard_map/all_to_all | solution.py:715
  141.6 1.2 shard_map.187
  (65 shorter events, 3.7 us)
Async XLA Ops:
  0.6 89.6 %copy-start.19 = (f32[3]{0:T(128)S(1)}, f32[3]{0:T(128)}, u32[]{:S(2)}) copy-start(f32[3]{0:T(128)} %edges.5) | copy-start | bytes 40
  0.6 0.7 copy-start.6
  1.3 0.7 copy-start.13
  2.6 16.5 %all-to-all-start = ((f32[8,8,128]{2,1,0:T(8,128)}), f32[8,8,128]{2,1,0:T(8,128)S(1)}, u32[]{:S(2)}, u32[]{:S(2)}) async-start(f32[8,8,128]{2,1,0:T(8,128)} %shard_map.175), calls=%async_computation | async-start | bytes 65536 | tf_op jit(solution)/shard_map/all_to_all | solution.py:597
  12.0 88.0 %copy-start.12 = (f32[128,8]{0,1:T(8,128)S(1)}, f32[128,8]{0,1:T(8,128)}, u32[]{:S(2)}) copy-start(f32[128,8]{0,1:T(8,128)} %param.31) | copy-start | bytes 12292
  19.1 0.7 copy-start.16
  20.0 3.7 %collective-permute-start = (f32[8,128]{1,0:T(8,128)S(1)}, f32[8,128]{1,0:T(8,128)S(1)}, u32[]{:S(2)}, u32[]{:S(2)}) collective-permute-start(f32[8,128]{1,0:T(8,128)S(1)} %get-tuple-element.29.cell1), channel_id=1, source_target_pairs={{0,32},{32,64},{64,96},{96,128},{128,160},{160,192},{192,224},{224... | collective-permute-start | bytes 12296 | tf_op jit(solution)/shard_map/ppermute | solution.py:601
  20.4 79.7 %copy-start.9 = (f32[128,16]{0,1:T(8,128)S(1)}, f32[128,16]{0,1:T(8,128)}, u32[]{:S(2)}) copy-start(f32[128,16]{0,1:T(8,128)} %param.29) | copy-start | bytes 24580
  20.4 79.8 %copy-start.23 = (f32[16]{0:T(128)S(1)}, f32[16]{0:T(128)}, u32[]{:S(2)}) copy-start(f32[16]{0:T(128)} %param.30) | copy-start | bytes 196
  20.4 87.7 %copy-start.3 = (s32[256,64]{0,1:T(8,128)S(1)}, s32[256,64]{0,1:T(8,128)}, u32[]{:S(2)}) copy-start(s32[256,64]{0,1:T(8,128)} %param.19) | copy-start | bytes 196612
  20.4 87.7 %copy-start.4 = (f32[128,128]{1,0:T(8,128)S(1)}, f32[128,128]{1,0:T(8,128)}, u32[]{:S(2)}) copy-start(f32[128,128]{1,0:T(8,128)} %blend.1) | copy-start | bytes 196612
  20.4 87.7 %copy-start.5 = (f32[64,128]{1,0:T(8,128)S(1)}, f32[64,128]{1,0:T(8,128)}, u32[]{:S(2)}) copy-start(f32[64,128]{1,0:T(8,128)} %second.1) | copy-start | bytes 98308
  20.4 5.8 %collective-permute-start.1 = (f32[8,128]{1,0:T(8,128)S(1)}, f32[8,128]{1,0:T(8,128)S(1)}, u32[]{:S(2)}, u32[]{:S(2)}) collective-permute-start(f32[8,128]{1,0:T(8,128)S(1)} %get-tuple-element.30.cell0), channel_id=1, source_target_pairs={{0,224},{32,0},{64,32},{96,64},{128,96},{160,128},{192,160},{224,1... | collective-permute-start | bytes 12296 | tf_op jit(solution)/shard_map/ppermute | solution.py:602
  26.2 10.9 %collective-permute-start.2 = (f32[16,128]{1,0:T(8,128)S(1)}, f32[16,128]{1,0:T(8,128)S(1)}, u32[]{:S(2)}, u32[]{:S(2)}) collective-permute-start(f32[16,128]{1,0:T(8,128)S(1)} %get-tuple-element.31), channel_id=1, source_target_pairs={{0,8},{8,16},{16,24},{24,0},{1,9},{9,17},{17,25},{25,1},{2,10},{10... | collective-permute-start | bytes 24584 | tf_op jit(solution)/shard_map/ppermute | solution.py:604
  26.2 10.9 %collective-permute-start.3 = (f32[16,128]{1,0:T(8,128)S(1)}, f32[16,128]{1,0:T(8,128)S(1)}, u32[]{:S(2)}, u32[]{:S(2)}) collective-permute-start(f32[16,128]{1,0:T(8,128)S(1)} %get-tuple-element.32), channel_id=1, source_target_pairs={{0,24},{8,0},{16,8},{24,16},{1,25},{9,1},{17,9},{25,17},{2,26},{10... | collective-permute-start | bytes 24584 | tf_op jit(solution)/shard_map/ppermute | solution.py:605
  32.2 0.8 copy-start.10
  34.5 0.9 copy-start.2
  37.1 0.7 copy-start.7
  37.8 0.7 copy-start.11
  38.5 0.7 copy-start.14
  39.2 0.7 copy-start.18
  39.8 0.7 copy-start.22
  49.0 2.0 %copy-start = (f32[8,512,256]{2,1,0:T(8,128)}, f32[8,512,256]{2,1,0:T(8,128)S(1)}, u32[]{:S(2)}) copy-start(f32[8,512,256]{2,1,0:T(8,128)S(1)} %get-tuple-element.43.slope) | copy-start | bytes 12582916
  51.0 14.4 %all-to-all-start.1 = ((f32[8,56,128]{2,1,0:T(8,128)}), f32[8,56,128]{2,1,0:T(8,128)S(1)}, u32[]{:S(2)}, u32[]{:S(2)}) async-start(f32[8,56,128]{2,1,0:T(8,128)} %get-tuple-element.33), calls=%async_computation.1 | async-start | bytes 458752 | tf_op jit(solution)/shard_map/all_to_all | solution.py:646
  68.0 1.4 collective-permute-start.4
  69.3 61.7 %copy-start.17 = (s32[2,2,128]{2,1,0:T(2,128)S(1)}, s32[2,2,128]{2,1,0:T(2,128)}, u32[]{:S(2)}) copy-start(s32[2,2,128]{2,1,0:T(2,128)} %rows.3) | copy-start | bytes 6148
  69.4 72.3 %copy-start.8 = (f32[3,256]{1,0:T(4,128)S(1)}, f32[3,256]{1,0:T(4,128)}, u32[]{:S(2)}) copy-start(f32[3,256]{1,0:T(4,128)} %place.5) | copy-start | bytes 9220
  69.4 72.3 %copy-start.15 = (s32[256]{0:T(256)S(1)}, s32[256]{0:T(256)}, u32[]{:S(2)}) copy-start(s32[256]{0:T(256)} %param.18) | copy-start | bytes 3076
  69.4 72.3 %copy-start.20 = (f32[3,256]{1,0:T(4,128)S(1)}, f32[3,256]{1,0:T(4,128)}, u32[]{:S(2)}) copy-start(f32[3,256]{1,0:T(4,128)} %speed.1) | copy-start | bytes 9220
  69.4 72.2 %copy-start.21 = (f32[3,256]{1,0:T(4,128)S(1)}, f32[3,256]{1,0:T(4,128)}, u32[]{:S(2)}) copy-start(f32[3,256]{1,0:T(4,128)} %kicks.1) | copy-start | bytes 9220
  69.4 4.6 %collective-permute-start.5 = (f32[80,256]{1,0:T(8,128)S(1)}, f32[80,256]{1,0:T(8,128)S(1)}, u32[]{:S(2)}, u32[]{:S(2)}) collective-permute-start(f32[80,256]{1,0:T(8,128)S(1)} %add.20), channel_id=1, source_target_pairs={{0,32},{8,40},{16,48},{24,56},{32,0},{40,8},{48,16},{56,24},{64,96... | collective-permute-start | bytes 245768 | tf_op jit(solution)/shard_map/ppermute | solution.py:663
  74.0 4.5 %collective-permute-start.6 = (f32[80,256]{1,0:T(8,128)S(1)}, f32[80,256]{1,0:T(8,128)S(1)}, u32[]{:S(2)}, u32[]{:S(2)}) collective-permute-start(f32[80,256]{1,0:T(8,128)S(1)} %add.21), channel_id=1, source_target_pairs={{0,48},{8,56},{16,32},{24,40},{32,16},{40,24},{48,0},{56,8},{64,11... | collective-permute-start | bytes 245768 | tf_op jit(solution)/shard_map/ppermute | solution.py:663
  78.5 4.5 %collective-permute-start.7 = (f32[80,256]{1,0:T(8,128)S(1)}, f32[80,256]{1,0:T(8,128)S(1)}, u32[]{:S(2)}, u32[]{:S(2)}) collective-permute-start(f32[80,256]{1,0:T(8,128)S(1)} %add.22), channel_id=1, source_target_pairs={{0,64},{8,72},{16,80},{24,88},{32,96},{40,104},{48,112},{56,120},{... | collective-permute-start | bytes 245768 | tf_op jit(solution)/shard_map/ppermute | solution.py:663
  83.1 5.7 %collective-permute-start.8 = (f32[80,256]{1,0:T(8,128)S(1)}, f32[80,256]{1,0:T(8,128)S(1)}, u32[]{:S(2)}, u32[]{:S(2)}) collective-permute-start(f32[80,256]{1,0:T(8,128)S(1)} %add.23), channel_id=1, source_target_pairs={{0,192},{8,200},{16,208},{24,216},{32,224},{40,232},{48,240},{56,2... | collective-permute-start | bytes 245768 | tf_op jit(solution)/shard_map/ppermute | solution.py:663
  88.8 1.4 collective-permute-start.9
  96.4 11.7 %all-to-all-start.2 = ((f32[8,8,256]{2,1,0:T(8,128)}), f32[8,8,256]{2,1,0:T(8,128)S(1)}, u32[]{:S(2)}, u32[]{:S(2)}) async-start(f32[8,8,256]{2,1,0:T(8,128)} %get-tuple-element.39), calls=%async_computation.2 | async-start | bytes 131072 | tf_op jit(solution)/shard_map/all_to_all | solution.py:677
  108.1 2.2 %copy-start.1 = (f32[8,512,256]{2,1,0:T(8,128)S(1)}, f32[8,512,256]{2,1,0:T(8,128)}, u32[]{:S(2)}) copy-start(f32[8,512,256]{2,1,0:T(8,128)} %copy-done) | copy-start | bytes 12582916
  118.7 2.8 %collective-permute-start.10 = (f32[16,128]{1,0:T(8,128)S(1)}, f32[16,128]{1,0:T(8,128)S(1)}, u32[]{:S(2)}, u32[]{:S(2)}) collective-permute-start(f32[16,128]{1,0:T(8,128)S(1)} %get-tuple-element.45), channel_id=1, source_target_pairs={{0,24},{8,0},{16,8},{24,16},{1,25},{9,1},{17,9},{25,17},{2,26},{10... | collective-permute-start | bytes 24584 | tf_op jit(solution)/shard_map/ppermute | solution.py:705
  120.2 4.6 %collective-permute-start.11 = (f32[16,128]{1,0:T(8,128)S(1)}, f32[16,128]{1,0:T(8,128)S(1)}, u32[]{:S(2)}, u32[]{:S(2)}) collective-permute-start(f32[16,128]{1,0:T(8,128)S(1)} %get-tuple-element.46), channel_id=1, source_target_pairs={{0,8},{8,16},{16,24},{24,0},{1,9},{9,17},{17,25},{25,1},{2,10},{10... | collective-permute-start | bytes 24584 | tf_op jit(solution)/shard_map/ppermute | solution.py:706
  124.8 3.6 %collective-permute-start.12 = (f32[8,128]{1,0:T(8,128)S(1)}, f32[8,128]{1,0:T(8,128)S(1)}, u32[]{:S(2)}, u32[]{:S(2)}) collective-permute-start(f32[8,128]{1,0:T(8,128)S(1)} %get-tuple-element.51), channel_id=1, source_target_pairs={{0,32},{32,64},{64,96},{96,128},{128,160},{160,192},{192,224},{224... | collective-permute-start | bytes 12296 | tf_op jit(solution)/shard_map/ppermute | solution.py:711
  125.3 5.7 %collective-permute-start.13 = (f32[8,128]{1,0:T(8,128)S(1)}, f32[8,128]{1,0:T(8,128)S(1)}, u32[]{:S(2)}, u32[]{:S(2)}) collective-permute-start(f32[8,128]{1,0:T(8,128)S(1)} %get-tuple-element.52), channel_id=1, source_target_pairs={{0,224},{32,0},{64,32},{96,64},{128,96},{160,128},{192,160},{224,1... | collective-permute-start | bytes 12296 | tf_op jit(solution)/shard_map/ppermute | solution.py:710

commit v2 on v1

--- a/solution.py
+++ b/solution.py
@@ -32,7 +32,15 @@
 outer = [(u, v) for u in range(4) for v in range(4) if not (u in (1, 2) and v in (1, 2))]
 vmem = pl.BlockSpec(memory_space=pltpu.VMEM)
 smem = pl.BlockSpec(memory_space=pltpu.SMEM)
+far = pl.BlockSpec(memory_space=pltpu.HBM)
+anywhere = pl.BlockSpec(memory_space=pl.ANY)
 params = pltpu.CompilerParams(vmem_limit_bytes=24 * 1024 * 1024)
+
+
+def work(micros):
+    return pl.CostEstimate(
+        flops=int(micros * 5e8), bytes_accessed=int(micros * 2e6), transcendentals=0
+    )
 
 
 def call(kernel, outs, specs, scratch=(), cost=None):
@@ -62,6 +70,12 @@
     )
 
 
+def dot_h(a, b):
+    return lax.dot_general(
+        a, b, (((1,), (1,)), ((), ())), precision=lax.Precision.HIGHEST, preferred_element_type=f32
+    )
+
+
 def split(x):
     high = x.astype(bf16)
     return high, (x - high.astype(f32)).astype(bf16)
@@ -101,7 +115,15 @@
     return first, index - span * first
 
 
-def pack_kernel(place, kind, out):
+def pack_kernel(place_far, kind_far, out, place, kind, done):
+    copies = [
+        pltpu.make_async_copy(place_far, place, done.at[0]),
+        pltpu.make_async_copy(kind_far, kind, done.at[1]),
+    ]
+    for copy in copies:
+        copy.start()
+    for copy in copies:
+        copy.wait()
     rows = []
     for c in range(3):
         rows += [place[c : c + 1, 0:128], place[c : c + 1, 128:256]]
@@ -110,6 +132,84 @@
     tile = jnp.concatenate(rows, axis=0)
     for z in range(ranks):
         out[z] = tile
+
+
+def count_triples(triples, out):
+    kx, ky, kz = (triples[d : d + 1, :].astype(f32) for d in range(3))
+    code = span * ky + kz
+    flip = jnp.where(code < 0.0, -1.0, 1.0)
+    code = code * flip
+    kx = kx * flip
+    count = kx.shape[1]
+    row = lax.broadcasted_iota(i32, (48, count), 0).astype(f32)
+    wanted = jnp.where(row < top, row + 1.0, row - (top - 1.0))
+    sign = jnp.where(kx < 0.0, -1.0, 1.0)
+    value = jnp.where(row < top, 1.0, sign)
+    line = jnp.where(row < 2 * top, jnp.where(jnp.abs(kx) == wanted, value, 0.0), 0.0)
+    line = jnp.where((row == 2 * top) & (kx == 0.0), 1.0, line).astype(bf16)
+    place = lax.broadcasted_iota(i32, (128, count), 0).astype(f32)
+    valid = place < plane_own
+    for z in range(ranks):
+        hit = jnp.where(valid & (code == place + float(z * plane_own)), 1.0, 0.0).astype(bf16)
+        out[z] = dot_t(line, hit)[0:40, :]
+
+
+def prepare_kernel(
+    edges_far, listing_far, tally_far, rows_far, triples_far, initial_far, second_far, embed_far,
+    blend_far, energy_far, project_far, final_far,
+    edges_out, listing, tally, rows, counts, first, mixed_high, mixed_low, ball, base, final_out,
+    triples, initial, second, embed, blend, heads, final, edges, wide, done,
+):
+    embed[...] = jnp.zeros_like(embed)
+    far = (
+        (edges_far, edges), (listing_far, listing), (tally_far, tally), (rows_far, rows),
+        (triples_far, triples), (initial_far, initial), (second_far, second),
+        (embed_far, embed.at[0:kinds]), (blend_far, blend), (energy_far, heads.at[8:24]),
+        (project_far, heads.at[0:8]), (final_far, final),
+    )
+    copies = [pltpu.make_async_copy(a, b, done.at[n]) for n, (a, b) in enumerate(far)]
+    for copy in copies:
+        copy.start()
+    for copy in copies:
+        copy.wait()
+    for d in range(3):
+        edges_out[d : d + 1, :] = jnp.full((1, own), 1.0, f32) * edges[d]
+    edges_out[3:8, :] = jnp.zeros((5, own), f32)
+    lane = lax.broadcasted_iota(i32, (8, 64), 1)
+    pick = jnp.where(lax.shift_right_logical(lane, 3) == lax.broadcasted_iota(i32, (8, 64), 0), 1.0, 0.0)
+    repeated = dot_c(initial[...], pick)
+    lane = lax.broadcasted_iota(i32, (hidden, 64), 1) & 7
+    blocks = jnp.concatenate(
+        [jnp.where(lane == m, repeated, 0.0) for m in range(chunk)], axis=0
+    )
+    high, low = split(blocks)
+    first[:, 0:64], first[:, 64:128], first[:, 128:192] = high, high, low
+    through = dot_h(heads[...], blend[...])
+    base[...] = dot_h(heads[...], embed[...])
+    doubled = jnp.concatenate([second[...], second[...]], axis=0)
+    left = lax.broadcasted_iota(i32, (24, 128), 1) < hidden
+    slot = lax.broadcasted_iota(i32, (8, 128), 0)
+    group = lax.shift_right_logical(lax.broadcasted_iota(i32, (8, 128), 1), 6)
+    responses = []
+    for s in range(kinds):
+        response = dot_h(through * embed[s : s + 1, :], doubled) * (1.0 / slots)
+        responses.append(response)
+        for l in range(8):
+            line = jnp.broadcast_to(response[l : l + 1, :], (8, 128))
+            for t in range(4):
+                at = (l * kinds + s) * 8
+                wide[at : at + 8, t * 128 : (t + 1) * 128] = jnp.where(
+                    group + 2 * t == slot, line, 0.0
+                )
+    for t in range(kinds // 2):
+        ball[:, t * 128 : (t + 1) * 128] = jnp.where(left, responses[2 * t], responses[2 * t + 1])
+    mixed_high[...], mixed_low[...] = split(wide[...])
+    square = (16, 16)
+    same = lax.broadcasted_iota(i32, square, 0) == lax.broadcasted_iota(i32, square, 1)
+    final_out[...] = jnp.sum(
+        jnp.where(same, jnp.broadcast_to(final[...], square), 0.0), axis=1, keepdims=True
+    )
+    count_triples(triples, counts)
 
 
 def border_kernel(table, rows, cell0, cell1):
@@ -125,7 +225,7 @@
             cell1[j * 4 + c : j * 4 + c + 1, :] = found[2 + j : 3 + j]
 
 
-def columns_kernel(left, cell0, cell1, right, head, tail):
+def columns_kernel(left, cell0, cell1, right, after, head, tail):
     for u, ref in enumerate((left, cell0, cell1, right)):
         head[u * 4 : u * 4 + 4, :] = ref[0:4, :]
         tail[u * 4 : u * 4 + 4, :] = ref[4:8, :]
@@ -174,29 +274,9 @@
     lax.fori_loop(0, ranks, step, 0)
 
 
-def count_kernel(triples, out):
-    kx, ky, kz = (triples[d : d + 1, :].astype(f32) for d in range(3))
-    code = span * ky + kz
-    flip = jnp.where(code < 0.0, -1.0, 1.0)
-    code = code * flip
-    kx = kx * flip
-    count = kx.shape[1]
-    row = lax.broadcasted_iota(i32, (48, count), 0).astype(f32)
-    wanted = jnp.where(row < top, row + 1.0, row - (top - 1.0))
-    sign = jnp.where(kx < 0.0, -1.0, 1.0)
-    value = jnp.where(row < top, 1.0, sign)
-    line = jnp.where(row < 2 * top, jnp.where(jnp.abs(kx) == wanted, value, 0.0), 0.0)
-    line = jnp.where((row == 2 * top) & (kx == 0.0), 1.0, line).astype(bf16)
-    place = lax.broadcasted_iota(i32, (128, count), 0).astype(f32)
-    valid = place < plane_own
-    for z in range(ranks):
-        hit = jnp.where(valid & (code == place + float(z * plane_own)), 1.0, 0.0).astype(bf16)
-        out[z] = dot_t(line, hit)[0:40, :]
-
-
 def message_kernel(
-    edges, listing, near, left, right, head, tail, place, kind, tally, counts, first, second_t,
-    embed_t, blend_t, project_t, send, feature_out, disp_out, mark_out, slope_out,
+    edges, listing, near, left, right, head, tail, place, kind, tally, counts, first, ball, base,
+    after, send, activation, disp_out, mark_out,
     cells, pooled, active,
 ):
     for u in range(4):
@@ -230,7 +310,7 @@
         for d in range(3):
             offset = found[d] - place[d : d + 1, :]
             offset = offset - jnp.floor(offset + 0.5)
-            offset = offset * edges[d]
+            offset = offset * edges[d : d + 1, :]
             disp_out[d, at, :] = offset
             squared = squared + offset * offset
         slot = lax.broadcasted_iota(i32, (chunk, own), 0) + j * chunk
@@ -242,9 +322,7 @@
         upper, lower = split(basis)
         pre = dot_n(first[...], jnp.concatenate([upper, lower, upper], axis=0))
         gate = 0.5 * jnp.tanh(0.5 * pre) + 0.5
-        out = pre * gate
-        active[...] = out
-        slope_out[j] = gate + out * (1.0 - gate)
+        active[...] = pre * gate
         for s in range(kinds):
             total = pooled[s * hidden : (s + 1) * hidden, :]
             for m in range(chunk):
@@ -254,23 +332,67 @@
         return carry
 
     lax.fori_loop(0, chunks, step, 0)
-    message = jnp.zeros((128, own), f32)
-    features = jnp.zeros((128, own), f32)
+    answers = dot3(ball[...], pooled[...])
     for s in range(kinds):
-        message = message + embed_t[:, s : s + 1] * dot3(
-            second_t[...], pooled[s * hidden : (s + 1) * hidden, :]
-        )
-        features = features + embed_t[:, s : s + 1] * jnp.where(kind[...] == s, 1.0, 0.0)
-    features = features + dot3(blend_t[...], message * (1.0 / slots))
-    feature_out[...] = features
-    charges = dot3(project_t[...], features)
+        answers = answers + base[:, s : s + 1] * jnp.where(kind[...] == s, 1.0, 0.0)
+    activation[...] = answers[8:24]
+    charges = answers[0:8]
     for z in range(ranks):
         send[z, 0:8, :] = charges[:, 0:128]
         send[z, 8:16, :] = charges[:, 128:256]
         send[z, 16:56, :] = counts[z]
 
 
-def structure_kernel(core, got, waves_x, high, low, mine, other, total, extra, left_high, left_low):
+def response_kernel(
+    activation, final, disp, marks, first, mixed_high, mixed_low, ball, out, upstream, bend, upper,
+    lower,
+):
+    value = activation[...]
+    gate = 0.5 * jnp.tanh(0.5 * value) + 0.5
+    ramp = final[...] * gate * (1.0 + value * (1.0 - gate))
+    upstream[...] = dot_c(ball[8:24, :], ramp)
+
+    def step(j, carry):
+        at = pl.ds(pl.multiple_of(j * chunk, chunk), chunk)
+        mark = marks[at, :]
+        squared = disp[0, at, :] * disp[0, at, :]
+        squared = squared + disp[1, at, :] * disp[1, at, :] + disp[2, at, :] * disp[2, at, :]
+        basis = [jnp.exp(squared * (-1.0 / (w * w))) for w in radial_widths]
+        lean = [b * (-2.0 / (w * w)) for b, w in zip(basis, radial_widths)]
+        ah, al = split(jnp.concatenate(basis, axis=0))
+        bh, bl = split(jnp.concatenate(lean, axis=0))
+        pre = dot_n(first[...], jnp.concatenate([ah, al, ah], axis=0))
+        gate = 0.5 * jnp.tanh(0.5 * pre) + 0.5
+        bend[...] = (gate + pre * gate * (1.0 - gate)) * dot_n(
+            first[...], jnp.concatenate([bh, bl, bh], axis=0)
+        )
+        upper[...], lower[...] = split(bend[...])
+        mixed = dot_n(mixed_high[...], upper[...]) + (
+            dot_n(mixed_low[...], upper[...]) + dot_n(mixed_high[...], lower[...])
+        )
+        for l in range(8):
+            total = jnp.zeros((chunk, own), f32)
+            for s in range(kinds):
+                row = (l * kinds + s) * 8
+                total = jnp.where(mark == float(s), mixed[row : row + 8, :], total)
+            out[l, at, :] = total
+        for m in range(chunk):
+            mine = jnp.broadcast_to(mark[m : m + 1, :], (hidden, own))
+            chosen = jnp.zeros((hidden, own), f32)
+            for s in range(kinds):
+                chosen = jnp.where(
+                    mine == float(s), upstream[s * hidden : (s + 1) * hidden, :], chosen
+                )
+            line = jnp.sum(chosen * bend[m * hidden : (m + 1) * hidden, :], axis=0, keepdims=True)
+            out[8, pl.ds(j * chunk + m, 1), :] = line
+        return carry
+
+    lax.fori_loop(0, chunks, step, 0)
+
+
+def structure_kernel(
+    core, got, waves_x, high, low, after, mine, other, total, extra, left_high, left_low
+):
     total[...] = jnp.zeros_like(total)
     extra[...] = jnp.zeros_like(extra)
 
@@ -304,9 +426,42 @@
         ref[plane_rows : plane_rows + 8, 128:256] = jnp.zeros((8, 128), f32)
 
 
+def weight_kernel(rank, edges, got, out):
+    counts = got[0, 16:56, :]
+    for z in range(1, ranks):
+        counts = counts + got[z, 16:56, :]
+    lane = lax.broadcasted_iota(i32, (top, 128), 1)
+    spread = jnp.where(
+        lax.shift_right_logical(lane, 3) == lax.broadcasted_iota(i32, (top, 128), 0), 1.0, 0.0
+    )
+    flat = jnp.where(lax.broadcasted_iota(i32, (8, 128), 0) == 0, 1.0, 0.0)
+    both = dot_c(counts[0:top], spread)[0:plane_rows]
+    apart = dot_c(counts[top : 2 * top], spread)[0:plane_rows]
+    zero = dot_c(counts[2 * top : 2 * top + 8], flat)[0:plane_rows]
+    shape = (plane_rows, 128)
+    ky, kz = plane_of(rank[0], shape, 0)
+    kx = (lax.shift_right_logical(lax.broadcasted_iota(i32, shape, 1), 3) + 1).astype(f32)
+    qx, qy, qz = (tau * k / edges[d : d + 1, 0:128] for d, k in enumerate((kx, ky, kz)))
+    flat_square = qy * qy + qz * qz
+    square = qx * qx + flat_square
+
+    def weigh(q):
+        return (tau / atoms_all) * jnp.exp((-0.5 * gauss_width * gauss_width) * q) / q
+
+    weight = weigh(square)
+    out[0] = both * weight
+    out[1] = apart * weight
+    out[2] = zero * jnp.where(flat_square > 0.0, weigh(jnp.maximum(flat_square, 1e-6)), 0.0)
+
+
+def turn_table(table, blocks, table_high, table_low):
+    for block in range(blocks):
+        at = slice(block * 128, block * 128 + 128)
+        table_high[at, 0:waves], table_low[at, 0:waves] = split(jnp.transpose(table[:, at]))
+
+
 def potential_kernel(
-    rank, core, edges, mine, other, got, waves_x, high, low, potential, gradient,
-    table, table_high, table_low, result,
+    core, mine, other, weights, waves_x, high, low, potential, table, table_high, table_low, result
 ):
     first = core[0] == 0
     real = jnp.where(first, mine[0:plane_rows, :], other[0:plane_rows, :])
@@ -314,79 +469,80 @@
     tail = slice(plane_rows, plane_rows + 8)
     begin = jnp.where(first, mine[tail, 0:128], other[tail, 0:128])
     rest = jnp.where(first, other[tail, 0:128], mine[tail, 0:128])
-    counts = got[0, 16:56, :]
-    for z in range(1, ranks):
-        counts = counts + got[z, 16:56, :]
-    lane = lax.broadcasted_iota(i32, (top, 128), 1)
-    spread = jnp.where(
-        lax.shift_right_logical(lane, 3) == lax.broadcasted_iota(i32, (top, 128), 0), 1.0, 0.0
-    )
     lane = lax.broadcasted_iota(i32, (8, 128), 1)
-    line = lax.broadcasted_iota(i32, (8, 128), 0)
-    flat = jnp.where(line == 0, 1.0, 0.0)
-    repeat = jnp.where((lane & 7) == line, 1.0, 0.0)
-    both = dot_c(counts[0:top], spread)[0:plane_rows]
-    apart = dot_c(counts[top : 2 * top], spread)[0:plane_rows]
-    zero = dot_c(counts[2 * top : 2 * top + 8], flat)[0:plane_rows]
+    repeat = jnp.where((lane & 7) == lax.broadcasted_iota(i32, (8, 128), 0), 1.0, 0.0)
     lone = dot_c(jnp.concatenate([begin, rest], axis=1), repeat)
-    shape = (plane_rows, 128)
-    ky, kz = plane_of(rank[0], shape, 0)
-    lanes = lax.broadcasted_iota(i32, shape, 1)
-    kx = (lax.shift_right_logical(lanes, 3) + 1).astype(f32)
-    qx, qy, qz = tau * kx / edges[0], tau * ky / edges[1], tau * kz / edges[2]
-    flat_square = qy * qy + qz * qz
-    square = qx * qx + flat_square
-
-    def weigh(q):
-        return (tau / atoms_all) * jnp.exp((-0.5 * gauss_width * gauss_width) * q) / q
-
-    weight = weigh(square)
-    both, apart = both * weight, apart * weight
-    zero = zero * jnp.where(flat_square > 0.0, weigh(jnp.maximum(flat_square, 1e-6)), 0.0)
+    both, apart, zero = weights[0], weights[1], weights[2]
     real_c, real_s = real[:, 0:128], real[:, 128:256]
     imag_c, imag_s = imaginary[:, 0:128], imaginary[:, 128:256]
-    pair_c = (both * real_c - apart * imag_s, both * imag_c + apart * real_s)
-    pair_s = (both * real_s + apart * imag_c, both * imag_s - apart * real_c)
-    ty, tz = tau * ky, tau * kz
     upper, lower = slice(0, plane_rows), slice(plane_rows, waves)
-    for part, (re, im) in enumerate((pair_c, pair_s)):
-        for form, scale in enumerate((None, ty, tz)):
-            at = slice(form * 256 + part * 128, form * 256 + part * 128 + 128)
-            table[upper, at] = re if scale is None else scale * im
-            table[lower, at] = im if scale is None else -(scale * re)
-    re, im = zero * lone[0:plane_rows], zero * lone[plane_rows:waves]
-    group = lax.shift_right_logical(lanes, 3)
-    turn = jnp.where(group == 1, ty, tz)
-    at = slice(768, 896)
-    table[upper, at] = jnp.where(group == 0, re, turn * im)
-    table[lower, at] = jnp.where(group == 0, im, -(turn * re))
-    for block in range(7):
-        at = slice(block * 128, block * 128 + 128)
-        turned = jnp.transpose(table[:, at])
-        table_high[at, 0:waves], table_low[at, 0:waves] = split(turned)
+    table[upper, 0:128] = both * real_c - apart * imag_s
+    table[lower, 0:128] = both * imag_c + apart * real_s
+    table[upper, 128:256] = both * real_s + apart * imag_c
+    table[lower, 128:256] = both * imag_s - apart * real_c
+    table[upper, 256:384] = zero * lone[0:plane_rows]
+    table[lower, 256:384] = zero * lone[plane_rows:waves]
+    turn_table(table, 3, table_high, table_low)
 
     def step(z, carry):
         at = pl.ds(pl.multiple_of(z * own, own), own)
         plane_high, plane_low = high[:, at], low[:, at]
-        weights = table_high[0:800, 0:waves]
-        result[...] = dot_n(weights, plane_high) + (
-            dot_n(table_low[0:800, 0:waves], plane_high) + dot_n(weights, plane_low)
+        lines = table_high[0:272, 0:waves]
+        result[...] = dot_n(lines, plane_high) + (
+            dot_n(table_low[0:272, 0:waves], plane_high) + dot_n(lines, plane_low)
         )
-        total = [result[768:776, :], jnp.zeros((8, own), f32), result[776:784, :], result[784:792, :]]
+        total = result[256:264, :]
+        for f in range(2 * top):
+            total = total + waves_x[f : f + 1, at] * result[f * 8 : f * 8 + 8, :]
+        potential[z] = total
+        return carry
+
+    lax.fori_loop(0, ranks, step, 0)
+
+
+def gradient_kernel(
+    rank, edges, table, got, waves_x, high, low, gradient, wide, table_high, table_low, result
+):
+    shape = (plane_rows, 128)
+    ky, kz = plane_of(rank[0], shape, 0)
+    ty, tz = tau * ky, tau * kz
+    upper, lower = slice(0, plane_rows), slice(plane_rows, waves)
+    for part in range(2):
+        at = slice(part * 128, part * 128 + 128)
+        re, im = table[upper, at], table[lower, at]
+        wide[upper, at], wide[lower, at] = re, im
+        for form, scale in ((1, ty), (2, tz)):
+            at = slice(form * 256 + part * 128, form * 256 + part * 128 + 128)
+            wide[upper, at] = scale * im
+            wide[lower, at] = -(scale * re)
+    re, im = table[upper, 256:384], table[lower, 256:384]
+    group = lax.shift_right_logical(lax.broadcasted_iota(i32, shape, 1), 3)
+    turn = jnp.where(group == 0, ty, tz)
+    wide[upper, 768:896] = turn * im
+    wide[lower, 768:896] = -(turn * re)
+    turn_table(wide, 7, table_high, table_low)
+
+    def step(z, carry):
+        at = pl.ds(pl.multiple_of(z * own, own), own)
+        plane_high, plane_low = high[:, at], low[:, at]
+        lines = table_high[0:784, 0:waves]
+        result[...] = dot_n(lines, plane_high) + (
+            dot_n(table_low[0:784, 0:waves], plane_high) + dot_n(lines, plane_low)
+        )
+        total = [jnp.zeros((8, own), f32), result[768:776, :], result[776:784, :]]
         for f in range(2 * top):
             wave = waves_x[f : f + 1, at]
-            for form, slot in enumerate((0, 2, 3)):
-                lines = slice(form * 256 + f * 8, form * 256 + f * 8 + 8)
-                total[slot] = total[slot] + wave * result[lines, :]
+            for form in (1, 2):
+                row = form * 256 + f * 8
+                total[form] = total[form] + wave * result[row : row + 8, :]
         for k in range(top):
             cosine, sine = waves_x[k : k + 1, at], waves_x[top + k : top + k + 1, at]
             turn = tau * (k + 1)
-            total[1] = total[1] + (turn * cosine) * result[(top + k) * 8 : (top + k) * 8 + 8, :]
-            total[1] = total[1] - (turn * sine) * result[k * 8 : k * 8 + 8, :]
-        potential[z] = total[0]
+            total[0] = total[0] + (turn * cosine) * result[(top + k) * 8 : (top + k) * 8 + 8, :]
+            total[0] = total[0] - (turn * sine) * result[k * 8 : k * 8 + 8, :]
         charge = jnp.concatenate([got[z, 0:8, :], got[z, 8:16, :]], axis=1)
         for d in range(3):
-            line = jnp.sum(charge * total[1 + d], axis=0, keepdims=True) / edges[d]
+            line = jnp.sum(charge * total[d], axis=0, keepdims=True) / edges[d : d + 1, :]
             gradient[z, 2 * d : 2 * d + 1, :] = line[:, 0:128]
             gradient[z, 2 * d + 1 : 2 * d + 2, :] = line[:, 128:256]
         return carry
@@ -395,20 +551,12 @@
 
 
 def pair_kernel(
-    got, features, disp, marks, slope, listing, lines, first_high, first_low, second, embed_t,
-    blend, energy, energy_t, energy_final, project, cells0, cells3, mid0, mid3, domain, direct,
-    upstream, upper, lower, left, right, total, pulled,
+    got, response, disp, listing, lines, cells0, cells3, mid0, mid3, domain, direct, left, right,
+    total, pulled,
 ):
     potential = got[0]
     for z in range(1, ranks):
         potential = potential + got[z]
-    activation = dot3(energy_t[...], features[...])
-    gate = 0.5 * jnp.tanh(0.5 * activation) + 0.5
-    ramp = energy_final[...] * gate * (1.0 + activation * (1.0 - gate))
-    change = dot3(energy[...], ramp) + dot3(project[...], potential)
-    change = dot3(blend[...], change) * (1.0 / slots)
-    for s in range(kinds):
-        upstream[s] = dot3(second[...], embed_t[:, s : s + 1] * change)
     total[...] = jnp.zeros_like(total)
     pulled[...] = jnp.zeros_like(pulled)
     row_high = lax.broadcasted_iota(i32, (32, own), 0)
@@ -417,24 +565,9 @@
     def step(j, carry):
         at = pl.ds(pl.multiple_of(j * chunk, chunk), chunk)
         offsets = [disp[d, at, :] for d in range(3)]
-        mark = marks[at, :]
-        for m in range(chunk):
-            mine = jnp.broadcast_to(mark[m : m + 1, :], (hidden, own))
-            chosen = jnp.zeros((hidden, own), f32)
-            for s in range(kinds):
-                chosen = jnp.where(mine == float(s), upstream[s], chosen)
-            chosen = chosen * slope[j, m * hidden : (m + 1) * hidden, :]
-            upper[m * hidden : (m + 1) * hidden, :], lower[m * hidden : (m + 1) * hidden, :] = (
-                split(chosen)
-            )
-        back = dot_n(first_high[...], upper[...]) + (
-            dot_n(first_low[...], upper[...]) + dot_n(first_high[...], lower[...])
-        )
-        squared = offsets[0] * offsets[0] + offsets[1] * offsets[1] + offsets[2] * offsets[2]
-        radial = jnp.zeros((chunk, own), f32)
-        for n, w in enumerate(radial_widths):
-            lean = jnp.exp(squared * (-1.0 / (w * w))) * (-2.0 / (w * w))
-            radial = radial + lean * back[n * chunk : (n + 1) * chunk, :]
+        radial = response[8, at, :]
+        for l in range(8):
+            radial = radial + potential[l : l + 1, :] * response[l, at, :]
         pulls = [radial * offset for offset in offsets]
         index = listing[at, :]
         low, high = index & 127, lax.shift_right_logical(index, 7)
@@ -542,7 +675,7 @@
         updated = retain * halfway + spread * kicks[row, :]
         force_out[row, :] = force
         speed_out[row, :] = updated
-        place_out[row, :] = place[row, :] + 0.5 * time_step * (halfway + updated) / edges[d]
+        place_out[row, :] = place[row, :] + 0.5 * time_step * (halfway + updated) / edges[row, :]
 
 
 def shift(axis, by):
@@ -583,79 +716,112 @@
 ):
     rank = lax.axis_index("ka").astype(i32).reshape(1)
     core = (lax.axis_index("gy") % 2).astype(i32).reshape(1)
-    kind = element_kinds.reshape(1, own)
-    tally = adjacent_valid_tally.reshape(1, own)
-    listing = adjacent_padded_indices.T
-    blocks = jnp.einsum(
-        "nh,ml->mhnl", distance_net_initial_weights, jnp.eye(chunk, dtype=f32), precision="highest"
-    ).reshape(chunk * hidden, 8 * chunk)
-    blocks_high, blocks_low = split(blocks)
-    first = jnp.concatenate([blocks_high, blocks_high, blocks_low], axis=1)
-    embed_t = element_feature_vectors.T
-
-    packed = call(pack_kernel, [((ranks, 8, 128), f32)], [vmem] * 2)(fractional_placements, kind)[0]
+    packed, place, kind = call(
+        pack_kernel,
+        [((ranks, 8, 128), f32), ((3, own), f32), ((1, own), i32)],
+        [far] * 2,
+        [pltpu.SemaphoreType.DMA((2,))],
+    )(fractional_placements, element_kinds.reshape(1, own))
     table = lax.all_to_all(packed, "ka", 0, 0)
-    cell0, cell1 = call(border_kernel, [((8, 128), f32)] * 2, [vmem] * 2)(
-        table, border_particle_rows
-    )
+    edges, listing, tally, rows, counts, first, mixed_high, mixed_low, ball, base, final = call(
+        prepare_kernel,
+        [
+            ((8, own), f32),
+            ((slots, own), i32),
+            ((1, own), i32),
+            ((2, 2, 128), i32),
+            ((ranks, 40, 128), f32),
+            ((chunk * hidden, 192), bf16),
+            ((8 * 8 * kinds, chunk * hidden), bf16),
+            ((8 * 8 * kinds, chunk * hidden), bf16),
+            ((24, kinds * hidden), f32),
+            ((24, 8), f32),
+            ((16, 1), f32),
+        ],
+        [far] * 12,
+        [
+            pltpu.VMEM((3, reciprocal_integer_triples.shape[1]), i32),
+            pltpu.VMEM((8, hidden), f32),
+            pltpu.VMEM((hidden, 128), f32),
+            pltpu.VMEM((8, 128), f32),
+            pltpu.VMEM((128, 128), f32),
+            pltpu.VMEM((24, 128), f32),
+            pltpu.VMEM((1, 16), f32),
+            pltpu.SMEM((3,), f32),
+            pltpu.VMEM((8 * 8 * kinds, chunk * hidden), f32),
+            pltpu.SemaphoreType.DMA((12,)),
+        ],
+        cost=work(8),
+    )(
+        cell_edge_sizes, adjacent_padded_indices.T, adjacent_valid_tally.reshape(1, own),
+        border_particle_rows, reciprocal_integer_triples, distance_net_initial_weights,
+        distance_net_final_weights, element_feature_vectors, message_blend_matrix,
+        energy_head_initial_weights.T, hidden_electric_projection.T,
+        energy_head_final_weights.reshape(1, 16),
+    )
+    cell0, cell1 = call(border_kernel, [((8, 128), f32)] * 2, [vmem] * 2)(table, rows)
     left = lax.ppermute(cell1, "gx", shift("gx", 1))
     right = lax.ppermute(cell0, "gx", shift("gx", -1))
-    head, tail = call(columns_kernel, [((16, 128), f32)] * 2, [vmem] * 4)(left, cell0, cell1, right)
+    near = call(own_gather_kernel, [((4, slots, own), f32)], [vmem] * 2, cost=work(2))(
+        table, listing
+    )[0]
+    head, tail = call(columns_kernel, [((16, 128), f32)] * 2, [vmem] * 4 + [anywhere])(
+        left, cell0, cell1, right, near
+    )
     tail_in = lax.ppermute(tail, "gy", shift("gy", 1))
     head_in = lax.ppermute(head, "gy", shift("gy", -1))
-
-    near = call(
-        own_gather_kernel,
-        [((4, slots, own), f32)],
-        [vmem] * 2,
-        cost=pl.CostEstimate(flops=20_000_000, bytes_accessed=400_000, transcendentals=0),
-    )(table, listing)[0]
     high, low, waves_x = call(
         factor_kernel,
         [((waves, ranks * own), bf16), ((waves, ranks * own), bf16), ((2 * top, ranks * own), f32)],
         [smem, vmem],
-        cost=pl.CostEstimate(flops=10_000_000, bytes_accessed=1_500_000, transcendentals=0),
+        cost=work(2),
     )(rank, table)
-    counts = call(
-        count_kernel,
-        [((ranks, 40, 128), f32)],
-        [vmem],
-        cost=pl.CostEstimate(flops=10_000_000, bytes_accessed=200_000, transcendentals=0),
-    )(reciprocal_integer_triples)[0]
-
-    send, features, disp, marks, slope = call(
+
+    send, activation, disp, marks = call(
         message_kernel,
         [
             ((ranks, 56, 128), f32),
-            ((128, own), f32),
+            ((16, own), f32),
             ((3, slots, own), f32),
             ((slots, own), f32),
-            ((chunks, chunk * hidden, own), f32),
         ],
-        [smem] + [vmem] * 15,
+        [vmem] * 14 + [anywhere],
         [
             pltpu.VMEM((64, 128), f32),
             pltpu.VMEM((kinds * hidden, own), f32),
             pltpu.VMEM((chunk * hidden, own), f32),
         ],
+        cost=work(8),
     )(
-        cell_edge_sizes, listing, near, left, right, tail_in, head_in, fractional_placements, kind,
-        tally, counts, first, distance_net_final_weights.T, embed_t, message_blend_matrix.T,
-        hidden_electric_projection.T,
+        edges, listing, near, left, right, tail_in, head_in, place, kind, tally, counts, first,
+        ball, base, waves_x,
     )
     got = lax.all_to_all(send, "ka", 0, 0)
+    response = call(
+        response_kernel,
+        [((9, slots, own), f32)],
+        [vmem] * 8,
+        [
+            pltpu.VMEM((kinds * hidden, own), f32),
+            pltpu.VMEM((chunk * hidden, own), f32),
+            pltpu.VMEM((chunk * hidden, own), bf16),
+            pltpu.VMEM((chunk * hidden, own), bf16),
+        ],
+        cost=work(8),
+    )(activation, final, disp, marks, first, mixed_high, mixed_low, ball)[0]
 
     mine, other = call(
         structure_kernel,
         [((plane_rows + 8, own), f32)] * 2,
-        [smem] + [vmem] * 4,
+        [smem] + [vmem] * 4 + [anywhere],
         [
             pltpu.VMEM((waves, own), f32),
             pltpu.VMEM((8, own), f32),
             pltpu.VMEM((own, own), bf16),
             pltpu.VMEM((own, own), bf16),
         ],
-    )(core, got, waves_x, high, low)
+        cost=work(3),
+    )(core, got, waves_x, high, low, response)
     swaps = partners()
     both = ("gx", "gy")
     summed = mine + lax.ppermute(other, both, swaps[0])
@@ -663,19 +829,33 @@
         summed = summed + lax.ppermute(summed, both, swap)
     opposite = lax.ppermute(summed, both, swaps[0])
 
-    potential, lines = call(
+    weights = call(
+        weight_kernel, [((3, plane_rows, 128), f32)], [smem] + [vmem] * 2, cost=work(0.5)
+    )(rank, edges, got)[0]
+    potential, spectrum = call(
         potential_kernel,
-        [((ranks, 8, own), f32), ((ranks, 8, 128), f32)],
-        [smem] * 3 + [vmem] * 6,
+        [((ranks, 8, own), f32), ((waves, 384), f32)],
+        [smem] + [vmem] * 6,
+        [
+            pltpu.VMEM((384, own), bf16),
+            pltpu.VMEM((384, own), bf16),
+            pltpu.VMEM((272, own), f32),
+        ],
+        cost=work(2),
+    )(core, summed, opposite, weights, waves_x, high, low)
+    shares = lax.all_to_all(potential, "ka", 0, 0)
+    lines = call(
+        gradient_kernel,
+        [((ranks, 8, 128), f32)],
+        [smem] + [vmem] * 6,
         [
             pltpu.VMEM((waves, 896), f32),
             pltpu.VMEM((896, own), bf16),
             pltpu.VMEM((896, own), bf16),
-            pltpu.VMEM((800, own), f32),
+            pltpu.VMEM((784, own), f32),
         ],
-    )(rank, core, cell_edge_sizes, summed, opposite, got, waves_x, high, low)
-    shares = lax.all_to_all(potential, "ka", 0, 0)
-
+        cost=work(5),
+    )(rank, edges, spectrum, got, waves_x, high, low)[0]
     cells0, cells3, mid0, mid3, domain, direct = call(
         pair_kernel,
         [
@@ -686,22 +866,15 @@
             ((ranks, 8, 128), f32),
             ((8, 128), f32),
         ],
-        [vmem] * 16,
+        [vmem] * 5,
         [
-            pltpu.VMEM((kinds, hidden, own), f32),
-            pltpu.VMEM((chunk * hidden, own), bf16),
-            pltpu.VMEM((chunk * hidden, own), bf16),
             pltpu.VMEM((192, chunk * own), bf16),
             pltpu.VMEM((128, chunk * own), bf16),
             pltpu.VMEM((192, 128), f32),
             pltpu.VMEM((3, chunk, own), f32),
         ],
-    )(
-        shares, features, disp, marks, slope, listing, lines, blocks_high.T, blocks_low.T,
-        distance_net_final_weights, embed_t, message_blend_matrix, energy_head_initial_weights,
-        energy_head_initial_weights.T, energy_head_final_weights.reshape(-1, 1),
-        hidden_electric_projection,
-    )
+        cost=work(4),
+    )(shares, response, disp, listing, lines)
     above = lax.ppermute(cells0, "gy", shift("gy", -1))
     below = lax.ppermute(cells3, "gy", shift("gy", 1))
     send0, send3, inner0, inner1 = call(echo_kernel, [((8, 128), f32)] * 4, [vmem] * 4)(
@@ -710,14 +883,13 @@
     from_right = lax.ppermute(send0, "gx", shift("gx", -1))
     from_left = lax.ppermute(send3, "gx", shift("gx", 1))
     reaction = call(border_back_kernel, [((ranks, 8, 128), f32)], [vmem] * 6)(
-        inner0, inner1, from_left, from_right, border_particle_rows, domain
+        inner0, inner1, from_left, from_right, rows, domain
     )[0]
     returned = lax.all_to_all(reaction, "ka", 0, 0)
     forces, places, speeds = call(
-        step_kernel, [((3, own), f32)] * 3, [smem] + [vmem] * 6
+        step_kernel, [((3, own), f32)] * 3, [vmem] * 7
     )(
-        cell_edge_sizes, returned, direct, fractional_placements, particle_speeds, kind,
-        friction_random_kicks,
+        edges, returned, direct, place, particle_speeds, kind, friction_random_kicks,
     )
     return (forces, places, speeds)
 

time: 144 us -> 131 us (0.910)
  waiting for transfers between devices: 57.9 us -> 35.9 us
  starting transfers between devices: 26 us -> 35 us
  Pallas kernels: 32.4 us -> 38.2 us
  local copies, waits for them, and re-layouts: 14.3 us -> 8.81 us
    pallas_call x8 -> x11, Pallas kernels: 19.9 us -> 31 us  [the longest x1 9.4 us: body(): call(response_kernel, [((9, slots, own), f32)], [vmem] * 8, [pltpu.VMEM((...]
    all_to_all x1, waiting for transfers between devices: 9.71 us -> 0.46 us  [body(): got = lax.all_to_all(send, 'ka', 0, 0)]
    all_to_all x1, waiting for transfers between devices: 7.12 us -> 0.01 us  [body(): table = lax.all_to_all(packed, 'ka', 0, 0)]
    pallas_call x1, Pallas kernels: 8.45 us -> 3.07 us  [body(): call(pair_kernel, [((16, 128), f32), ((16, 128), f32), ((8, 128), f32), (...]
    unnamed x53 -> x36, local copies, waits for them, and re-layouts: 14 us -> 8.81 us
    all_to_all x1, waiting for transfers between devices: 7.81 us -> 3.83 us  [body(): shares = lax.all_to_all(potential, 'ka', 0, 0)]
    all_to_all x1, starting transfers between devices: 3.4 us -> 7.21 us  [body(): got = lax.all_to_all(send, 'ka', 0, 0)]
    all_to_all x1, starting transfers between devices: 3.53 us -> 6.93 us  [body(): shares = lax.all_to_all(potential, 'ka', 0, 0)]
  transfers between devices with their start and end apart: 17 -> 17, of which waited for: 15 -> 14; matrix products, arithmetic and copies ran while one was open for 3% -> 0% of each run, Pallas kernels for 3% -> 16%
where the time goes in v2:
time: 131 us; the launch traced here: 130 us
  Pallas kernels  38.2 us (29%)
  waiting for transfers between devices  35.9 us (27%)
  starting transfers between devices  35 us (27%)
  blocking collectives  11.2 us (9%)
  local copies, waits for them, and re-layouts  8.81 us (7%)
    ppermute x4, waiting for transfers between devices, body(): summed = summed + lax.ppermute(summed, both, swap)  17.5 us
    all_to_all x1, blocking collectives, body(): returned = lax.all_to_all(reaction, 'ka', 0, 0)  11.2 us
    pallas_call x1, Pallas kernels, body(): call(response_kernel, [((9, slots, own), f32)], [vmem] * 8, [pltpu.VMEM((...  9.4 us
    unnamed x36, local copies, waits for them, and re-layouts  8.81 us
    all_to_all x1, starting transfers between devices, body(): table = lax.all_to_all(packed, 'ka', 0, 0)  8.48 us
    all_to_all x1, starting transfers between devices, body(): got = lax.all_to_all(send, 'ka', 0, 0)  7.21 us
    pallas_call x1, Pallas kernels, body(): call(message_kernel, [((ranks, 56, 128), f32), ((16, own), f32), ((3, slo...  6.95 us
    all_to_all x1, starting transfers between devices, body(): shares = lax.all_to_all(potential, 'ka', 0, 0)  6.93 us
  transfers between devices with their start and end apart: 17, of which 14 were waited for; matrix products, arithmetic and copies ran while one was open for 0% of the time, Pallas kernels for 16%

profile of v2, /device:TPU:14, one launch (start us, length us, event | category | flops | bytes accessed | tf_op | source)
XLA Modules:
  0.0 130.0 jit_solution(7936242878210351243)
XLA Ops:
  0.7 0.7 copy-done.3
  1.3 0.7 copy-done.2
  2.0 0.6 shard_map.176
  2.7 8.5 %all-to-all-start = ((f32[8,8,128]{2,1,0:T(8,128)}), f32[8,8,128]{2,1,0:T(8,128)S(1)}, u32[]{:S(2)}, u32[]{:S(2)}) async-start(f32[8,8,128]{2,1,0:T(8,128)} %get-tuple-element.44), calls=%async_computation | async-start | bytes 65536 | tf_op jit(solution)/shard_map/all_to_all | solution.py:725
  11.2 0.7 copy-done.8
  11.8 0.8 copy-done.5
  12.7 0.8 copy-done.6
  13.4 0.8 copy-done.7
  14.2 0.7 copy-done.11
  14.9 0.7 copy-done.12
  15.6 0.7 copy-done.13
  16.2 0.7 copy-done.15
  16.9 3.2 %shard_map.175 = (f32[8,256]{1,0:T(8,128)S(1)}, s32[64,256]{1,0:T(8,128)S(1)}, s32[1,256]{1,0:T(1,128)S(1)}, s32[2,2,128]{2,1,0:T(2,128)S(1)}, f32[8,40,128]{2,1...) custom-call(f32[3]{0:T(128)S(1)} %copy-done.14, ...), custom_call_target="tpu_custom_call" | custom-call | flops 4000000000 | bytes 16000000 | tf_op jit(solution)/shard_map/pallas_call | solution.py:726
  20.2 0.7 copy-done.16
  21.0 0.4 collective-permute-start
  21.5 1.7 %collective-permute-start.1 = (f32[8,128]{1,0:T(8,128)S(1)}, f32[8,128]{1,0:T(8,128)S(1)}, u32[]{:S(2)}, u32[]{:S(2)}) collective-permute-start(f32[8,128]{1,0:T(8,128)S(1)} %get-tuple-element.47.cell0), channel_id=1, source_target_pairs={{0,224},{32,0},{64,32},{96,64},{128,96},{160,128},{192,160},{224,1... | collective-permute-start | bytes 12296 | tf_op jit(solution)/shard_map/ppermute | solution.py:764
  23.2 1.7 %shard_map.177.after.near = f32[4,64,256]{2,1,0:T(8,128)S(1)} custom-call(f32[8,8,128]{2,1,0:T(8,128)S(1)} %all-to-all-done.table, s32[64,256]{1,0:T(8,128)S(1)} %get-tuple-element.43.listing), custom_call_target="tpu_custom_call" | custom-call | flops 1000000000 | bytes 4000000 | tf_op jit(solution)/shard_map/pallas_call | solution.py:765
  24.8 2.4 %collective-permute-done.1.right = f32[8,128]{1,0:T(8,128)S(1)} collective-permute-done((f32[8,128]{1,0:T(8,128)S(1)}, f32[8,128]{1,0:T(8,128)S(1)}, u32[]{:S(2)}, u32[]{:S(2)}) %collective-permute-start.1) | collective-permute-done | bytes 4128 | tf_op jit(solution)/shard_map/ppermute | solution.py:764
  27.2 3.2 %collective-permute-start.3 = (f32[16,128]{1,0:T(8,128)S(1)}, f32[16,128]{1,0:T(8,128)S(1)}, u32[]{:S(2)}, u32[]{:S(2)}) collective-permute-start(f32[16,128]{1,0:T(8,128)S(1)} %get-tuple-element.49), channel_id=1, source_target_pairs={{0,24},{8,0},{16,8},{24,16},{1,25},{9,1},{17,9},{25,17},{2,26},{10... | collective-permute-start | bytes 24584 | tf_op jit(solution)/shard_map/ppermute | solution.py:772
  30.5 1.3 shard_map.180
  31.8 7.0 %shard_map.181 = (f32[8,56,128]{2,1,0:T(8,128)}, f32[16,256]{1,0:T(8,128)S(1)}, f32[3,64,256]{2,1,0:T(8,128)S(1)}, f32[64,256]{1,0:T(8,128)S(1)}) custom-call(f32[8,256]{1,0:T(8,128)S(1)} %get-tuple-element.42.edges, s32[64,256]{1,0:T(8,128)S(1)} %get-tuple-element.43.listing, f32[4,64,256]{2,1,0:T(8,128)S(1)} %shard_map.177.after.near, ...), custom_call_target="tpu_custom_call" | custom-call | flops 4000000000 | bytes 16000000 | tf_op jit(solution)/shard_map/pallas_call | solution.py:780
  38.8 7.2 %all-to-all-start.1 = ((f32[8,56,128]{2,1,0:T(8,128)}), f32[8,56,128]{2,1,0:T(8,128)S(1)}, u32[]{:S(2)}, u32[]{:S(2)}) async-start(f32[8,56,128]{2,1,0:T(8,128)} %get-tuple-element.58), calls=%async_computation.1 | async-start | bytes 458752 | tf_op jit(solution)/shard_map/all_to_all | solution.py:799
  46.0 1.0 copy-done.17
  47.0 9.4 %shard_map.182.after.response = f32[9,64,256]{2,1,0:T(8,128)S(1)} custom-call(f32[16,256]{1,0:T(8,128)S(1)} %get-tuple-element.61.activation, f32[16,1]{1,0:T(8,128)S(1)} %get-tuple-element.62.final, f32[3,64,256]{2,1,0:T(8,128)S(1)} %get-tuple-element.63.disp, f32[64,256]{1,0:T(8,128)S(1)} %get-tuple-element.64.marks, ...), custom_call_target="tpu_custom_call" | custom-call | flops 4000000000 | bytes 16000000 | tf_op jit(solution)/shard_map/pallas_call | solution.py:800
  56.4 0.5 all-to-all-done.1.got
  56.9 2.6 %shard_map.183 = (f32[80,256]{1,0:T(8,128)S(1)}, f32[80,256]{1,0:T(8,128)S(1)}) custom-call(s32[1]{0:T(128)} %bitcast.5.core, f32[8,56,128]{2,1,0:T(8,128)S(1)} %all-to-all-done.1.got, f32[32,2048]{1,0:T(8,128)S(1)} %get-tuple-element.57.after.waves_x, bf16[144,2048]{1,0:T(8,128)(2,1)S(1)} %get-tuple-element.59.high, ...), custom_call_target="tpu_custom_call" | custom-call | flops 1500000000 | bytes 6000000 | tf_op jit(solution)/shard_map/pallas_call | solution.py:813
  59.4 2.0 %collective-permute-start.4 = (f32[80,256]{1,0:T(8,128)S(1)}, f32[80,256]{1,0:T(8,128)S(1)}, u32[]{:S(2)}, u32[]{:S(2)}) collective-permute-start(f32[80,256]{1,0:T(8,128)S(1)} %get-tuple-element.68), channel_id=1, source_target_pairs={{0,8},{8,0},{16,24},{24,16},{32,40},{40,32},{48,56},{56,48},{64,72... | collective-permute-start | bytes 245768 | tf_op jit(solution)/shard_map/ppermute | solution.py:827
  61.5 0.9 collective-permute-done.4
  62.5 4.7 %collective-permute-done.5 = f32[80,256]{1,0:T(8,128)S(1)} collective-permute-done((f32[80,256]{1,0:T(8,128)S(1)}, f32[80,256]{1,0:T(8,128)S(1)}, u32[]{:S(2)}, u32[]{:S(2)}) %collective-permute-start.5) | collective-permute-done | bytes 81952 | tf_op jit(solution)/shard_map/ppermute | solution.py:829
  67.2 1.2 collective-permute-start.6
  68.4 3.3 %collective-permute-done.6 = f32[80,256]{1,0:T(8,128)S(1)} collective-permute-done((f32[80,256]{1,0:T(8,128)S(1)}, f32[80,256]{1,0:T(8,128)S(1)}, u32[]{:S(2)}, u32[]{:S(2)}) %collective-permute-start.6) | collective-permute-done | bytes 81952 | tf_op jit(solution)/shard_map/ppermute | solution.py:829
  71.8 0.4 collective-permute-start.7
  72.2 4.1 %collective-permute-done.7 = f32[80,256]{1,0:T(8,128)S(1)} collective-permute-done((f32[80,256]{1,0:T(8,128)S(1)}, f32[80,256]{1,0:T(8,128)S(1)}, u32[]{:S(2)}, u32[]{:S(2)}) %collective-permute-start.7) | collective-permute-done | bytes 81952 | tf_op jit(solution)/shard_map/ppermute | solution.py:829
  76.7 5.4 %collective-permute-done.8 = f32[80,256]{1,0:T(8,128)S(1)} collective-permute-done((f32[80,256]{1,0:T(8,128)S(1)}, f32[80,256]{1,0:T(8,128)S(1)}, u32[]{:S(2)}, u32[]{:S(2)}) %collective-permute-start.8) | collective-permute-done | bytes 81952 | tf_op jit(solution)/shard_map/ppermute | solution.py:829
  82.7 0.9 collective-permute-done.9.other
  83.6 3.5 %shard_map.185 = (f32[8,8,256]{2,1,0:T(8,128)}, f32[144,384]{1,0:T(8,128)S(1)}) custom-call(s32[1]{0:T(128)} %bitcast.5.core, f32[80,256]{1,0:T(8,128)S(1)} %add.24.mine, f32[80,256]{1,0:T(8,128)S(1)} %collective-permute-done.9.other, f32[3,72,128]{2,1,0:T(8,128)S(1)} %shard_map.184.weights, f32[32,2048]{1,0:T(8,128)S(1)} %get-tuple-element.57.after.waves_x, ...), custom_call_target="tpu_custom_call" | custom-call | flops 1000000000 | bytes 4000000 | tf_op jit(solution)/shard_map/pallas_call | solution.py:835
  87.1 6.9 %all-to-all-start.2 = ((f32[8,8,256]{2,1,0:T(8,128)}), f32[8,8,256]{2,1,0:T(8,128)S(1)}, u32[]{:S(2)}, u32[]{:S(2)}) async-start(f32[8,8,256]{2,1,0:T(8,128)} %get-tuple-element.69), calls=%async_computation.2 | async-start | bytes 131072 | tf_op jit(solution)/shard_map/all_to_all | solution.py:846
  94.0 4.5 %shard_map.186.lines = f32[8,8,128]{2,1,0:T(8,128)S(1)} custom-call(s32[1]{0:T(128)} %bitcast.7.rank, f32[8,256]{1,0:T(8,128)S(1)} %get-tuple-element.42.edges, f32[144,384]{1,0:T(8,128)S(1)} %get-tuple-element.70.table, f32[8,56,128]{2,1,0:T(8,128)S(1)} %all-to-all-done.1.got, f32[32,2048]{1,0:T(8,128)S(1)} %get-tuple-element.57.after.waves_x, ...), custom_call_target="tpu_custom_call" | custom-call | flops 2500000000 | bytes 10000000 | tf_op jit(solution)/shard_map/pallas_call | solution.py:847
  98.5 3.8 %all-to-all-done.2.got = f32[8,8,256]{2,1,0:T(8,128)S(1)} async-done(((f32[8,8,256]{2,1,0:T(8,128)}), f32[8,8,256]{2,1,0:T(8,128)S(1)}, u32[]{:S(2)}, u32[]{:S(2)}) %all-to-all-start.2) | async-done | bytes 65568 | tf_op jit(solution)/shard_map/all_to_all | solution.py:846
  102.4 3.1 %shard_map.187 = (f32[16,128]{1,0:T(8,128)S(1)}, f32[16,128]{1,0:T(8,128)S(1)}, f32[8,128]{1,0:T(8,128)S(1)}, f32[8,128]{1,0:T(8,128)S(1)}, f32[8,8,128]{2,1,0:T(8,128)S(1)}, /*index=5*/f32[8,128]{1,0:T(8,128)S(1)}) custom-call(f32[8,8,256]{2,1,0:T(8,128)S(1)} %all-to-all-done.2.got, f32[9,64,256]{2,1,0:T(8,128)S(1)} %shard_map.182.after.response, ...), custom_call_target="tpu_custom_call" | custom-call | flops 2000000000 | bytes 8000000 | tf_op jit(solution)/shard_map/pallas_call | solution.py:859
  105.5 0.6 collective-permute-start.10
  106.0 1.3 %collective-permute-done.10.above = f32[16,128]{1,0:T(8,128)S(1)} collective-permute-done((f32[16,128]{1,0:T(8,128)S(1)}, f32[16,128]{1,0:T(8,128)S(1)}, u32[]{:S(2)}, u32[]{:S(2)}) %collective-permute-start.10) | collective-permute-done | bytes 8224 | tf_op jit(solution)/shard_map/ppermute | solution.py:878
  107.4 3.2 %collective-permute-done.11.below = f32[16,128]{1,0:T(8,128)S(1)} collective-permute-done((f32[16,128]{1,0:T(8,128)S(1)}, f32[16,128]{1,0:T(8,128)S(1)}, u32[]{:S(2)}, u32[]{:S(2)}) %collective-permute-start.11) | collective-permute-done | bytes 8224 | tf_op jit(solution)/shard_map/ppermute | solution.py:879
  110.6 1.6 %collective-permute-start.12 = (f32[8,128]{1,0:T(8,128)S(1)}, f32[8,128]{1,0:T(8,128)S(1)}, u32[]{:S(2)}, u32[]{:S(2)}) collective-permute-start(f32[8,128]{1,0:T(8,128)S(1)} %get-tuple-element.77), channel_id=1, source_target_pairs={{0,32},{32,64},{64,96},{96,128},{128,160},{160,192},{192,224},{224... | collective-permute-start | bytes 12296 | tf_op jit(solution)/shard_map/ppermute | solution.py:884
  112.6 1.6 %collective-permute-done.12.from_left = f32[8,128]{1,0:T(8,128)S(1)} collective-permute-done((f32[8,128]{1,0:T(8,128)S(1)}, f32[8,128]{1,0:T(8,128)S(1)}, u32[]{:S(2)}, u32[]{:S(2)}) %collective-permute-start.12) | collective-permute-done | bytes 4128 | tf_op jit(solution)/shard_map/ppermute | solution.py:884
  114.2 3.7 %collective-permute-done.13.from_right = f32[8,128]{1,0:T(8,128)S(1)} collective-permute-done((f32[8,128]{1,0:T(8,128)S(1)}, f32[8,128]{1,0:T(8,128)S(1)}, u32[]{:S(2)}, u32[]{:S(2)}) %collective-permute-start.13) | collective-permute-done | bytes 4128 | tf_op jit(solution)/shard_map/ppermute | solution.py:883
  118.2 11.2 %all_to_all.20.got = f32[8,8,128]{2,1,0:T(8,128)S(1)} all-to-all(f32[8,8,128]{2,1,0:T(8,128)S(1)} %shard_map.189), channel_id=1, replica_groups=mesh['gx'=8,'gy'=4,'ka'=8] {'ka'}, dimensions={0} | all-to-all | bytes 65536 | tf_op jit(solution)/shard_map/all_to_all | solution.py:888
  129.4 0.6 shard_map.190
  (44 shorter events, 2.1 us)
Async XLA Ops:
  0.6 0.7 copy-start.3
  0.6 10.5 %copy-start.14 = (f32[3]{0:T(128)S(1)}, f32[3]{0:T(128)}, u32[]{:S(2)}) copy-start(f32[3]{0:T(128)} %edges_far.1) | copy-start | bytes 40
  1.3 0.7 copy-start.2
  2.0 9.2 %copy-start.4 = (s32[256,64]{0,1:T(8,128)S(1)}, s32[256,64]{0,1:T(8,128)}, u32[]{:S(2)}) copy-start(s32[256,64]{0,1:T(8,128)} %param.19) | copy-start | bytes 196612
  2.6 8.5 %copy-start.9 = (f32[8,64]{1,0:T(8,128)S(1)}, f32[8,64]{1,0:T(8,128)}, u32[]{:S(2)}) copy-start(f32[8,64]{1,0:T(8,128)} %initial_far.1) | copy-start | bytes 6148
  2.6 8.5 %copy-start.10 = (f32[6,128]{1,0:T(8,128)S(1)}, f32[6,128]{1,0:T(8,128)}, u32[]{:S(2)}) copy-start(f32[6,128]{1,0:T(8,128)} %embed_far.1) | copy-start | bytes 9220
  2.7 18.2 %all-to-all-start = ((f32[8,8,128]{2,1,0:T(8,128)}), f32[8,8,128]{2,1,0:T(8,128)S(1)}, u32[]{:S(2)}, u32[]{:S(2)}) async-start(f32[8,8,128]{2,1,0:T(8,128)} %get-tuple-element.44), calls=%async_computation | async-start | bytes 65536 | tf_op jit(solution)/shard_map/all_to_all | solution.py:725
  11.1 0.7 copy-start.8
  11.8 0.8 copy-start.5
  12.7 0.8 copy-start.6
  13.4 0.8 copy-start.7
  14.2 0.7 copy-start.11
  14.9 0.7 copy-start.12
  15.6 0.7 copy-start.13
  16.2 0.7 copy-start.15
  20.2 0.7 copy-start.16
  21.0 3.8 %collective-permute-start = (f32[8,128]{1,0:T(8,128)S(1)}, f32[8,128]{1,0:T(8,128)S(1)}, u32[]{:S(2)}, u32[]{:S(2)}) collective-permute-start(f32[8,128]{1,0:T(8,128)S(1)} %get-tuple-element.46.cell1), channel_id=1, source_target_pairs={{0,32},{32,64},{64,96},{96,128},{128,160},{160,192},{192,224},{224... | collective-permute-start | bytes 12296 | tf_op jit(solution)/shard_map/ppermute | solution.py:763
  21.5 5.7 %collective-permute-start.1 = (f32[8,128]{1,0:T(8,128)S(1)}, f32[8,128]{1,0:T(8,128)S(1)}, u32[]{:S(2)}, u32[]{:S(2)}) collective-permute-start(f32[8,128]{1,0:T(8,128)S(1)} %get-tuple-element.47.cell0), channel_id=1, source_target_pairs={{0,224},{32,0},{64,32},{96,64},{128,96},{160,128},{192,160},{224,1... | collective-permute-start | bytes 12296 | tf_op jit(solution)/shard_map/ppermute | solution.py:764
  27.2 4.6 %collective-permute-start.2 = (f32[16,128]{1,0:T(8,128)S(1)}, f32[16,128]{1,0:T(8,128)S(1)}, u32[]{:S(2)}, u32[]{:S(2)}) collective-permute-start(f32[16,128]{1,0:T(8,128)S(1)} %get-tuple-element.48), channel_id=1, source_target_pairs={{0,8},{8,16},{16,24},{24,0},{1,9},{9,17},{17,25},{25,1},{2,10},{10... | collective-permute-start | bytes 24584 | tf_op jit(solution)/shard_map/ppermute | solution.py:771
  27.2 4.6 %collective-permute-start.3 = (f32[16,128]{1,0:T(8,128)S(1)}, f32[16,128]{1,0:T(8,128)S(1)}, u32[]{:S(2)}, u32[]{:S(2)}) collective-permute-start(f32[16,128]{1,0:T(8,128)S(1)} %get-tuple-element.49), channel_id=1, source_target_pairs={{0,24},{8,0},{16,8},{24,16},{1,25},{9,1},{17,9},{25,17},{2,26},{10... | collective-permute-start | bytes 24584 | tf_op jit(solution)/shard_map/ppermute | solution.py:772
  38.8 18.1 %all-to-all-start.1 = ((f32[8,56,128]{2,1,0:T(8,128)}), f32[8,56,128]{2,1,0:T(8,128)S(1)}, u32[]{:S(2)}, u32[]{:S(2)}) async-start(f32[8,56,128]{2,1,0:T(8,128)} %get-tuple-element.58), calls=%async_computation.1 | async-start | bytes 458752 | tf_op jit(solution)/shard_map/all_to_all | solution.py:799
  46.0 1.0 copy-start.17
  59.4 3.0 %collective-permute-start.4 = (f32[80,256]{1,0:T(8,128)S(1)}, f32[80,256]{1,0:T(8,128)S(1)}, u32[]{:S(2)}, u32[]{:S(2)}) collective-permute-start(f32[80,256]{1,0:T(8,128)S(1)} %get-tuple-element.68), channel_id=1, source_target_pairs={{0,8},{8,0},{16,24},{24,16},{32,40},{40,32},{48,56},{56,48},{64,72... | collective-permute-start | bytes 245768 | tf_op jit(solution)/shard_map/ppermute | solution.py:827
  62.4 4.8 %collective-permute-start.5 = (f32[80,256]{1,0:T(8,128)S(1)}, f32[80,256]{1,0:T(8,128)S(1)}, u32[]{:S(2)}, u32[]{:S(2)}) collective-permute-start(f32[80,256]{1,0:T(8,128)S(1)} %add.20), channel_id=1, source_target_pairs={{0,32},{8,40},{16,48},{24,56},{32,0},{40,8},{48,16},{56,24},{64,96... | collective-permute-start | bytes 245768 | tf_op jit(solution)/shard_map/ppermute | solution.py:829
  67.2 4.5 %collective-permute-start.6 = (f32[80,256]{1,0:T(8,128)S(1)}, f32[80,256]{1,0:T(8,128)S(1)}, u32[]{:S(2)}, u32[]{:S(2)}) collective-permute-start(f32[80,256]{1,0:T(8,128)S(1)} %add.21), channel_id=1, source_target_pairs={{0,48},{8,56},{16,32},{24,40},{32,16},{40,24},{48,0},{56,8},{64,11... | collective-permute-start | bytes 245768 | tf_op jit(solution)/shard_map/ppermute | solution.py:829
  71.8 4.5 %collective-permute-start.7 = (f32[80,256]{1,0:T(8,128)S(1)}, f32[80,256]{1,0:T(8,128)S(1)}, u32[]{:S(2)}, u32[]{:S(2)}) collective-permute-start(f32[80,256]{1,0:T(8,128)S(1)} %add.22), channel_id=1, source_target_pairs={{0,64},{8,72},{16,80},{24,88},{32,96},{40,104},{48,112},{56,120},{... | collective-permute-start | bytes 245768 | tf_op jit(solution)/shard_map/ppermute | solution.py:829
  76.3 5.7 %collective-permute-start.8 = (f32[80,256]{1,0:T(8,128)S(1)}, f32[80,256]{1,0:T(8,128)S(1)}, u32[]{:S(2)}, u32[]{:S(2)}) collective-permute-start(f32[80,256]{1,0:T(8,128)S(1)} %add.23), channel_id=1, source_target_pairs={{0,192},{8,200},{16,208},{24,216},{32,224},{40,232},{48,240},{56,2... | collective-permute-start | bytes 245768 | tf_op jit(solution)/shard_map/ppermute | solution.py:829
  82.1 1.5 %collective-permute-start.9 = (f32[80,256]{1,0:T(8,128)S(1)}, f32[80,256]{1,0:T(8,128)S(1)}, u32[]{:S(2)}, u32[]{:S(2)}) collective-permute-start(f32[80,256]{1,0:T(8,128)S(1)} %add.24.mine), channel_id=1, source_target_pairs={{0,8},{8,0},{16,24},{24,16},{32,40},{40,32},{48,56},{56,48},{64,72... | collective-permute-start | bytes 245768 | tf_op jit(solution)/shard_map/ppermute | solution.py:830
  87.1 15.3 %all-to-all-start.2 = ((f32[8,8,256]{2,1,0:T(8,128)}), f32[8,8,256]{2,1,0:T(8,128)S(1)}, u32[]{:S(2)}, u32[]{:S(2)}) async-start(f32[8,8,256]{2,1,0:T(8,128)} %get-tuple-element.69), calls=%async_computation.2 | async-start | bytes 131072 | tf_op jit(solution)/shard_map/all_to_all | solution.py:846
  102.4 27.0 %copy-start = (f32[3,256]{1,0:T(4,128)S(1)}, f32[3,256]{1,0:T(4,128)}, u32[]{:S(2)}) copy-start(f32[3,256]{1,0:T(4,128)} %speed.1) | copy-start | bytes 9220
  102.4 27.0 %copy-start.1 = (f32[3,256]{1,0:T(4,128)S(1)}, f32[3,256]{1,0:T(4,128)}, u32[]{:S(2)}) copy-start(f32[3,256]{1,0:T(4,128)} %kicks.1) | copy-start | bytes 9220
  105.5 1.9 %collective-permute-start.10 = (f32[16,128]{1,0:T(8,128)S(1)}, f32[16,128]{1,0:T(8,128)S(1)}, u32[]{:S(2)}, u32[]{:S(2)}) collective-permute-start(f32[16,128]{1,0:T(8,128)S(1)} %get-tuple-element.71), channel_id=1, source_target_pairs={{0,24},{8,0},{16,8},{24,16},{1,25},{9,1},{17,9},{25,17},{2,26},{10... | collective-permute-start | bytes 24584 | tf_op jit(solution)/shard_map/ppermute | solution.py:878
  106.0 4.6 %collective-permute-start.11 = (f32[16,128]{1,0:T(8,128)S(1)}, f32[16,128]{1,0:T(8,128)S(1)}, u32[]{:S(2)}, u32[]{:S(2)}) collective-permute-start(f32[16,128]{1,0:T(8,128)S(1)} %get-tuple-element.72), channel_id=1, source_target_pairs={{0,8},{8,16},{16,24},{24,0},{1,9},{9,17},{17,25},{25,1},{2,10},{10... | collective-permute-start | bytes 24584 | tf_op jit(solution)/shard_map/ppermute | solution.py:879
  110.6 3.6 %collective-permute-start.12 = (f32[8,128]{1,0:T(8,128)S(1)}, f32[8,128]{1,0:T(8,128)S(1)}, u32[]{:S(2)}, u32[]{:S(2)}) collective-permute-start(f32[8,128]{1,0:T(8,128)S(1)} %get-tuple-element.77), channel_id=1, source_target_pairs={{0,32},{32,64},{64,96},{96,128},{128,160},{160,192},{192,224},{224... | collective-permute-start | bytes 12296 | tf_op jit(solution)/shard_map/ppermute | solution.py:884
  112.2 5.7 %collective-permute-start.13 = (f32[8,128]{1,0:T(8,128)S(1)}, f32[8,128]{1,0:T(8,128)S(1)}, u32[]{:S(2)}, u32[]{:S(2)}) collective-permute-start(f32[8,128]{1,0:T(8,128)S(1)} %get-tuple-element.78), channel_id=1, source_target_pairs={{0,224},{32,0},{64,32},{96,64},{128,96},{160,128},{192,160},{224,1... | collective-permute-start | bytes 12296 | tf_op jit(solution)/shard_map/ppermute | solution.py:883

commit v3 on v2

--- a/solution.py
+++ b/solution.py
@@ -1,3 +1,4 @@
+import functools
 import math
 
 import jax
@@ -277,7 +278,7 @@
 def message_kernel(
     edges, listing, near, left, right, head, tail, place, kind, tally, counts, first, ball, base,
     after, send, activation, disp_out, mark_out,
-    cells, pooled, active,
+    cells, pooled, actives,
 ):
     for u in range(4):
         for c in range(4):
@@ -290,7 +291,7 @@
                 cells[spot : spot + 1, :] = ref[j * 4 + c : j * 4 + c + 1, :]
     pooled[...] = jnp.zeros_like(pooled)
 
-    def step(j, carry):
+    def part(j, active):
         at = pl.ds(pl.multiple_of(j * chunk, chunk), chunk)
         halves = []
         for half in range(2):
@@ -329,9 +330,8 @@
                 hit = jnp.broadcast_to(mark[m : m + 1, :], (hidden, own)) == float(s)
                 total = total + jnp.where(hit, active[m * hidden : (m + 1) * hidden, :], 0.0)
             pooled[s * hidden : (s + 1) * hidden, :] = total
-        return carry
-
-    lax.fori_loop(0, chunks, step, 0)
+
+    paired(chunks, part, (actives,))
     answers = dot3(ball[...], pooled[...])
     for s in range(kinds):
         answers = answers + base[:, s : s + 1] * jnp.where(kind[...] == s, 1.0, 0.0)
@@ -343,17 +343,34 @@
         send[z, 16:56, :] = counts[z]
 
 
-def response_kernel(
-    activation, final, disp, marks, first, mixed_high, mixed_low, ball, out, upstream, bend, upper,
-    lower,
-):
+def response_start(activation, final, ball, upstream):
     value = activation[...]
     gate = 0.5 * jnp.tanh(0.5 * value) + 0.5
     ramp = final[...] * gate * (1.0 + value * (1.0 - gate))
     upstream[...] = dot_c(ball[8:24, :], ramp)
 
-    def step(j, carry):
-        at = pl.ds(pl.multiple_of(j * chunk, chunk), chunk)
+
+def paired(count, part, scratch):
+    def step(pair, carry):
+        for p in range(2):
+            part(pair * 2 + p, *[ref.at[p] for ref in scratch])
+        return carry
+
+    lax.fori_loop(0, count // 2, step, 0)
+
+
+def response_kernel(begin, count, first_part, *refs):
+    if first_part:
+        activation, final, ball, disp, marks, first, mixed_high, mixed_low = refs[:8]
+        out, upstream = refs[8:10]
+        response_start(activation, final, ball, upstream)
+    else:
+        upstream, disp, marks, first, mixed_high, mixed_low, out = refs[:7]
+    bends, uppers, lowers = refs[-3:]
+
+    def part(j, bend, upper, lower):
+        at = pl.ds(pl.multiple_of((j + begin) * chunk, chunk), chunk)
+        to = pl.ds(pl.multiple_of(j * chunk, chunk), chunk)
         mark = marks[at, :]
         squared = disp[0, at, :] * disp[0, at, :]
         squared = squared + disp[1, at, :] * disp[1, at, :] + disp[2, at, :] * disp[2, at, :]
@@ -375,7 +392,7 @@
             for s in range(kinds):
                 row = (l * kinds + s) * 8
                 total = jnp.where(mark == float(s), mixed[row : row + 8, :], total)
-            out[l, at, :] = total
+            out[l, to, :] = total
         for m in range(chunk):
             mine = jnp.broadcast_to(mark[m : m + 1, :], (hidden, own))
             chosen = jnp.zeros((hidden, own), f32)
@@ -385,18 +402,17 @@
                 )
             line = jnp.sum(chosen * bend[m * hidden : (m + 1) * hidden, :], axis=0, keepdims=True)
             out[8, pl.ds(j * chunk + m, 1), :] = line
-        return carry
-
-    lax.fori_loop(0, chunks, step, 0)
+
+    paired(count, part, (bends, uppers, lowers))
 
 
 def structure_kernel(
-    core, got, waves_x, high, low, after, mine, other, total, extra, left_high, left_low
+    core, got, waves_x, high, low, after, mine, other, total, extra, lefts_high, lefts_low
 ):
     total[...] = jnp.zeros_like(total)
     extra[...] = jnp.zeros_like(extra)
 
-    def step(z, carry):
+    def part(z, left_high, left_low):
         at = pl.ds(pl.multiple_of(z * own, own), own)
         charge = jnp.concatenate([got[z, 0:8, :], got[z, 8:16, :]], axis=1)
         for f in range(0, 2 * top, 2):
@@ -414,9 +430,8 @@
         extra[:, 0:waves] += dot_t(upper, plane_high) + (
             dot_t(lower, plane_high) + dot_t(upper, plane_low)
         )
-        return carry
-
-    lax.fori_loop(0, ranks, step, 0)
+
+    paired(ranks, part, (lefts_high, lefts_low))
     first = core[0] == 0
     real, imaginary = total[0:plane_rows, :], total[plane_rows:waves, :]
     begin, rest = extra[:, 0:128], extra[:, 128:256]
@@ -461,7 +476,7 @@
 
 
 def potential_kernel(
-    core, mine, other, weights, waves_x, high, low, potential, table, table_high, table_low, result
+    core, mine, other, weights, waves_x, high, low, potential, table, table_high, table_low, results
 ):
     first = core[0] == 0
     real = jnp.where(first, mine[0:plane_rows, :], other[0:plane_rows, :])
@@ -484,7 +499,7 @@
     table[lower, 256:384] = zero * lone[plane_rows:waves]
     turn_table(table, 3, table_high, table_low)
 
-    def step(z, carry):
+    def part(z, result):
         at = pl.ds(pl.multiple_of(z * own, own), own)
         plane_high, plane_low = high[:, at], low[:, at]
         lines = table_high[0:272, 0:waves]
@@ -495,13 +510,12 @@
         for f in range(2 * top):
             total = total + waves_x[f : f + 1, at] * result[f * 8 : f * 8 + 8, :]
         potential[z] = total
-        return carry
-
-    lax.fori_loop(0, ranks, step, 0)
+
+    paired(ranks, part, (results,))
 
 
 def gradient_kernel(
-    rank, edges, table, got, waves_x, high, low, gradient, wide, table_high, table_low, result
+    rank, edges, table, got, waves_x, high, low, gradient, wide, table_high, table_low, results
 ):
     shape = (plane_rows, 128)
     ky, kz = plane_of(rank[0], shape, 0)
@@ -522,7 +536,7 @@
     wide[lower, 768:896] = -(turn * re)
     turn_table(wide, 7, table_high, table_low)
 
-    def step(z, carry):
+    def part(z, result):
         at = pl.ds(pl.multiple_of(z * own, own), own)
         plane_high, plane_low = high[:, at], low[:, at]
         lines = table_high[0:784, 0:waves]
@@ -545,14 +559,13 @@
             line = jnp.sum(charge * total[d], axis=0, keepdims=True) / edges[d : d + 1, :]
             gradient[z, 2 * d : 2 * d + 1, :] = line[:, 0:128]
             gradient[z, 2 * d + 1 : 2 * d + 2, :] = line[:, 128:256]
-        return carry
-
-    lax.fori_loop(0, ranks, step, 0)
+
+    paired(ranks, part, (results,))
 
 
 def pair_kernel(
-    got, response, disp, listing, lines, cells0, cells3, mid0, mid3, domain, direct, left, right,
-    total, pulled,
+    got, response0, response1, response2, disp, listing, lines, cells0, cells3, mid0, mid3, domain,
+    direct, lefts, rights, total, pulled,
 ):
     potential = got[0]
     for z in range(1, ranks):
@@ -562,12 +575,13 @@
     row_high = lax.broadcasted_iota(i32, (32, own), 0)
     row_low = lax.broadcasted_iota(i32, (128, own), 0)
 
-    def step(j, carry):
-        at = pl.ds(pl.multiple_of(j * chunk, chunk), chunk)
+    def part(response, begin, j, left, right):
+        to = pl.ds(pl.multiple_of(j * chunk, chunk), chunk)
+        at = pl.ds(pl.multiple_of((j + begin) * chunk, chunk), chunk)
         offsets = [disp[d, at, :] for d in range(3)]
-        radial = response[8, at, :]
+        radial = response[8, to, :]
         for l in range(8):
-            radial = radial + potential[l : l + 1, :] * response[l, at, :]
+            radial = radial + potential[l : l + 1, :] * response[l, to, :]
         pulls = [radial * offset for offset in offsets]
         index = listing[at, :]
         low, high = index & 127, lax.shift_right_logical(index, 7)
@@ -588,9 +602,12 @@
             spot = jnp.broadcast_to(low[m : m + 1, :], (128, own)) == row_low
             right[:, lanes] = jnp.where(spot, 1.0, 0.0).astype(bf16)
         total[...] += dot_t(left[...], right[...])
-        return carry
-
-    lax.fori_loop(0, chunks, step, 0)
+
+    begin = 0
+    for response in (response0, response1, response2):
+        count = response.shape[1] // chunk
+        paired(count, functools.partial(part, response, begin), (lefts, rights))
+        begin += count
     scattered = total[0:96, :] + total[96:192, :]
     nothing = jnp.zeros((1, 128), f32)
     for u in range(4):
@@ -683,17 +700,25 @@
     return [(i, (i + by) % count) for i in range(count)]
 
 
+def add_kernel(after, *refs):
+    total = refs[0][...]
+    for ref in refs[1:-1]:
+        total = total + ref[...]
+    refs[-1][...] = total
+
+
 def partners():
-    maps = (
-        lambda x, yl, yh, c: (x, yl, yh, 1 - c),
-        lambda x, yl, yh, c: (x, 1 - yl, yh, c),
-        lambda x, yl, yh, c: (x, 1 - yl, 1 - yh, c),
-        lambda x, yl, yh, c: (x ^ 1, yl, yh, c),
-        lambda x, yl, yh, c: (3 - x, yl, yh, c),
-    )
-    places = [(x, a, b, c) for x in range(4) for a in range(2) for b in range(2) for c in range(2)]
-    number = {p: (p[0] * 2 + p[1]) * 4 + p[2] * 2 + p[3] for p in places}
-    return [[(number[p], number[m(*p)]) for p in places] for m in maps]
+    places = [(x, y, c) for x in range(4) for y in range(4) for c in range(2)]
+
+    def number(x, y, c):
+        return (x % 4 * 2 + y % 2) * 4 + y % 4 // 2 * 2 + c
+
+    swap = [(number(x, y, c), number(x, y, 1 - c)) for x, y, c in places]
+    rings = [
+        [[(number(x, y, c), number(x, y + d, c)) for x, y, c in places] for d in (1, 3, 2)],
+        [[(number(x, y, c), number(x + d, y, c)) for x, y, c in places] for d in (1, 3, 2)],
+    ]
+    return swap, rings
 
 
 def body(
@@ -716,12 +741,15 @@
 ):
     rank = lax.axis_index("ka").astype(i32).reshape(1)
     core = (lax.axis_index("gy") % 2).astype(i32).reshape(1)
+    def stay(array):
+        return pltpu.with_memory_space_constraint(array, pltpu.HBM)
+
     packed, place, kind = call(
         pack_kernel,
         [((ranks, 8, 128), f32), ((3, own), f32), ((1, own), i32)],
         [far] * 2,
         [pltpu.SemaphoreType.DMA((2,))],
-    )(fractional_placements, element_kinds.reshape(1, own))
+    )(stay(fractional_placements), stay(element_kinds.reshape(1, own)))
     table = lax.all_to_all(packed, "ka", 0, 0)
     edges, listing, tally, rows, counts, first, mixed_high, mixed_low, ball, base, final = call(
         prepare_kernel,
@@ -753,11 +781,23 @@
         ],
         cost=work(8),
     )(
-        cell_edge_sizes, adjacent_padded_indices.T, adjacent_valid_tally.reshape(1, own),
-        border_particle_rows, reciprocal_integer_triples, distance_net_initial_weights,
-        distance_net_final_weights, element_feature_vectors, message_blend_matrix,
-        energy_head_initial_weights.T, hidden_electric_projection.T,
-        energy_head_final_weights.reshape(1, 16),
+        *map(
+            stay,
+            (
+                cell_edge_sizes,
+                adjacent_padded_indices.T,
+                adjacent_valid_tally.reshape(1, own),
+                border_particle_rows,
+                reciprocal_integer_triples,
+                distance_net_initial_weights,
+                distance_net_final_weights,
+                element_feature_vectors,
+                message_blend_matrix,
+                energy_head_initial_weights.T,
+                hidden_electric_projection.T,
+                energy_head_final_weights.reshape(1, 16),
+            ),
+        )
     )
     cell0, cell1 = call(border_kernel, [((8, 128), f32)] * 2, [vmem] * 2)(table, rows)
     left = lax.ppermute(cell1, "gx", shift("gx", 1))
@@ -789,7 +829,7 @@
         [
             pltpu.VMEM((64, 128), f32),
             pltpu.VMEM((kinds * hidden, own), f32),
-            pltpu.VMEM((chunk * hidden, own), f32),
+            pltpu.VMEM((2, chunk * hidden, own), f32),
         ],
         cost=work(8),
     )(
@@ -797,18 +837,26 @@
         ball, base, waves_x,
     )
     got = lax.all_to_all(send, "ka", 0, 0)
-    response = call(
-        response_kernel,
-        [((9, slots, own), f32)],
-        [vmem] * 8,
-        [
-            pltpu.VMEM((kinds * hidden, own), f32),
-            pltpu.VMEM((chunk * hidden, own), f32),
-            pltpu.VMEM((chunk * hidden, own), bf16),
-            pltpu.VMEM((chunk * hidden, own), bf16),
-        ],
-        cost=work(8),
-    )(activation, final, disp, marks, first, mixed_high, mixed_low, ball)[0]
+    ready = (disp, marks, first, mixed_high, mixed_low)
+
+    def respond(begin, count, operands):
+        started = begin == 0
+        outs = [((9, count * chunk, own), f32)] + [((kinds * hidden, own), f32)] * started
+        return call(
+            functools.partial(response_kernel, begin, count, started),
+            outs,
+            [vmem] * len(operands),
+            [
+                pltpu.VMEM((2, chunk * hidden, own), f32),
+                pltpu.VMEM((2, chunk * hidden, own), bf16),
+                pltpu.VMEM((2, chunk * hidden, own), bf16),
+            ],
+            cost=work(count),
+        )(*operands)
+
+    response0, upstream = respond(0, 4, (activation, final, ball) + ready)
+    response1 = respond(4, 2, (upstream,) + ready)[0]
+    response2 = respond(6, 2, (upstream,) + ready)[0]
 
     mine, other = call(
         structure_kernel,
@@ -817,18 +865,23 @@
         [
             pltpu.VMEM((waves, own), f32),
             pltpu.VMEM((8, own), f32),
-            pltpu.VMEM((own, own), bf16),
-            pltpu.VMEM((own, own), bf16),
+            pltpu.VMEM((2, own, own), bf16),
+            pltpu.VMEM((2, own, own), bf16),
         ],
         cost=work(3),
-    )(core, got, waves_x, high, low, response)
-    swaps = partners()
+    )(core, got, waves_x, high, low, response0)
+    swap, rings = partners()
     both = ("gx", "gy")
-    summed = mine + lax.ppermute(other, both, swaps[0])
-    for swap in swaps[1:]:
-        summed = summed + lax.ppermute(summed, both, swap)
-    opposite = lax.ppermute(summed, both, swaps[0])
-
+
+    def add(after, *parts):
+        return call(
+            add_kernel, [((plane_rows + 8, own), f32)], [anywhere] + [vmem] * len(parts)
+        )(after, *parts)[0]
+
+    summed = mine + lax.ppermute(other, both, swap)
+    for ring, after in zip(rings, (response1, response2)):
+        summed = add(after, summed, *[lax.ppermute(summed, both, turn) for turn in ring])
+    opposite = lax.ppermute(summed, both, swap)
     weights = call(
         weight_kernel, [((3, plane_rows, 128), f32)], [smem] + [vmem] * 2, cost=work(0.5)
     )(rank, edges, got)[0]
@@ -839,7 +892,7 @@
         [
             pltpu.VMEM((384, own), bf16),
             pltpu.VMEM((384, own), bf16),
-            pltpu.VMEM((272, own), f32),
+            pltpu.VMEM((2, 272, own), f32),
         ],
         cost=work(2),
     )(core, summed, opposite, weights, waves_x, high, low)
@@ -852,7 +905,7 @@
             pltpu.VMEM((waves, 896), f32),
             pltpu.VMEM((896, own), bf16),
             pltpu.VMEM((896, own), bf16),
-            pltpu.VMEM((784, own), f32),
+            pltpu.VMEM((2, 784, own), f32),
         ],
         cost=work(5),
     )(rank, edges, spectrum, got, waves_x, high, low)[0]
@@ -866,15 +919,15 @@
             ((ranks, 8, 128), f32),
             ((8, 128), f32),
         ],
-        [vmem] * 5,
+        [vmem] * 7,
         [
-            pltpu.VMEM((192, chunk * own), bf16),
-            pltpu.VMEM((128, chunk * own), bf16),
+            pltpu.VMEM((2, 192, chunk * own), bf16),
+            pltpu.VMEM((2, 128, chunk * own), bf16),
             pltpu.VMEM((192, 128), f32),
             pltpu.VMEM((3, chunk, own), f32),
         ],
         cost=work(4),
-    )(shares, response, disp, listing, lines)
+    )(shares, response0, response1, response2, disp, listing, lines)
     above = lax.ppermute(cells0, "gy", shift("gy", -1))
     below = lax.ppermute(cells3, "gy", shift("gy", 1))
     send0, send3, inner0, inner1 = call(echo_kernel, [((8, 128), f32)] * 4, [vmem] * 4)(

time: 131 us -> 115 us (0.88)
  local copies, waits for them, and re-layouts: 8.81 us -> 1.73 us
  Pallas kernels: 38.2 us -> 33 us
  waiting for transfers between devices: 35.9 us -> 33.9 us
    ppermute x6 -> x8, waiting for transfers between devices: 19.3 us -> 6.92 us  [the longest x6 5.1 us: body(): lax.ppermute(summed, both, turn)]
    unnamed x36 -> x24, local copies, waits for them, and re-layouts: 8.81 us -> 1.73 us
    ppermute x6 -> x8, starting transfers between devices: 4.41 us -> 10.4 us  [the longest x6 8.53 us: body(): lax.ppermute(summed, both, turn)]
    all_to_all x1, waiting for transfers between devices: 0.46 us -> 5.81 us  [body(): got = lax.all_to_all(send, 'ka', 0, 0)]
    all_to_all x1, waiting for transfers between devices: 0.01 us -> 4.34 us  [body(): table = lax.all_to_all(packed, 'ka', 0, 0)]
    all_to_all x1, starting transfers between devices: 7.21 us -> 3.4 us  [body(): got = lax.all_to_all(send, 'ka', 0, 0)]
    all_to_all x1, starting transfers between devices: 6.93 us -> 3.35 us  [body(): shares = lax.all_to_all(potential, 'ka', 0, 0)]
    pallas_call x1 -> x5, Pallas kernels: 9.4 us -> 7.58 us  [the longest x3 7.55 us: respond(): call(functools.partial(response_kernel, begin, count, started), outs, [vm...]
  transfers between devices with their start and end apart: 17 -> 19, of which waited for: 14 -> 14; matrix products, arithmetic and copies ran while one was open for 0% -> 0% of each run, Pallas kernels for 16% -> 16%
where the time goes in v3:
time: 115 us
  waiting for transfers between devices  33.9 us (29%)
  starting transfers between devices  33.7 us (29%)
  Pallas kernels  33 us (29%)
  blocking collectives  11.4 us (10%)
  local copies, waits for them, and re-layouts  1.73 us (2%)
    all_to_all x1, blocking collectives, body(): returned = lax.all_to_all(reaction, 'ka', 0, 0)  11.4 us
    ppermute x6, starting transfers between devices, body(): lax.ppermute(summed, both, turn)  8.53 us
    all_to_all x1, starting transfers between devices, body(): table = lax.all_to_all(packed, 'ka', 0, 0)  8.48 us
    pallas_call x3, Pallas kernels, respond(): call(functools.partial(response_kernel, begin, count, started), outs, [vm...  7.55 us
    all_to_all x1, waiting for transfers between devices, body(): got = lax.all_to_all(send, 'ka', 0, 0)  5.81 us
    pallas_call x1, Pallas kernels, body(): call(message_kernel, [((ranks, 56, 128), f32), ((16, own), f32), ((3, slo...  5.27 us
    ppermute x6, waiting for transfers between devices, body(): lax.ppermute(summed, both, turn)  5.1 us
    all_to_all x1, waiting for transfers between devices, body(): table = lax.all_to_all(packed, 'ka', 0, 0)  4.34 us
  transfers between devices with their start and end apart: 19, of which 14 were waited for; matrix products, arithmetic and copies ran while one was open for 0% of the time, Pallas kernels for 16%

profile of v3, /device:TPU:14, one launch (start us, length us, event | category | flops | bytes accessed | tf_op | source)
XLA Modules:
  0.0 114.5 jit_solution(15383437570005120976)
XLA Ops:
  0.6 1.3 %shard_map.176 = (f32[8,8,128]{2,1,0:T(8,128)}, f32[3,256]{1,0:T(4,128)S(1)}, s32[1,256]{1,0:T(1,128)S(1)}) custom-call(f32[3,256]{1,0:T(4,128)} %place_far.1, s32[1,256]{1,0:T(1,128)} %bitcast.8), custom_call_target="tpu_custom_call" | custom-call | tf_op jit(solution)/shard_map/pallas_call | solution.py:747
  2.0 8.5 %all-to-all-start = ((f32[8,8,128]{2,1,0:T(8,128)}), f32[8,8,128]{2,1,0:T(8,128)S(1)}, u32[]{:S(2)}, u32[]{:S(2)}) async-start(f32[8,8,128]{2,1,0:T(8,128)} %get-tuple-element.46), calls=%async_computation | async-start | bytes 65536 | tf_op jit(solution)/shard_map/all_to_all | solution.py:753
  10.4 3.7 %shard_map.175 = (f32[8,256]{1,0:T(8,128)S(1)}, s32[64,256]{1,0:T(8,128)S(1)}, s32[1,256]{1,0:T(1,128)S(1)}, s32[2,2,128]{2,1,0:T(2,128)S(1)}, f32[8,40,128]{2,1...) custom-call(f32[3]{0:T(128)} %edges_far.1, ...), custom_call_target="tpu_custom_call" | custom-call | flops 4000000000 | bytes 16000000 | tf_op jit(solution)/shard_map/pallas_call | solution.py:754
  14.1 4.3 %all-to-all-done.table = f32[8,8,128]{2,1,0:T(8,128)S(1)} async-done(((f32[8,8,128]{2,1,0:T(8,128)}), f32[8,8,128]{2,1,0:T(8,128)S(1)}, u32[]{:S(2)}, u32[]{:S(2)}) %all-to-all-start) | async-done | bytes 32800 | tf_op jit(solution)/shard_map/all_to_all | solution.py:753
  18.5 0.1 shard_map.178
  18.6 0.4 collective-permute-start
  19.1 1.7 %collective-permute-start.1 = (f32[8,128]{1,0:T(8,128)S(1)}, f32[8,128]{1,0:T(8,128)S(1)}, u32[]{:S(2)}, u32[]{:S(2)}) collective-permute-start(f32[8,128]{1,0:T(8,128)S(1)} %get-tuple-element.49.cell0), channel_id=1, source_target_pairs={{0,224},{32,0},{64,32},{96,64},{128,96},{160,128},{192,160},{224,1... | collective-permute-start | bytes 12296 | tf_op jit(solution)/shard_map/ppermute | solution.py:804
  20.7 1.7 %shard_map.177.after.near = f32[4,64,256]{2,1,0:T(8,128)S(1)} custom-call(f32[8,8,128]{2,1,0:T(8,128)S(1)} %all-to-all-done.table, s32[64,256]{1,0:T(8,128)S(1)} %get-tuple-element.45.listing), custom_call_target="tpu_custom_call" | custom-call | flops 1000000000 | bytes 4000000 | tf_op jit(solution)/shard_map/pallas_call | solution.py:805
  22.4 2.4 %collective-permute-done.1.right = f32[8,128]{1,0:T(8,128)S(1)} collective-permute-done((f32[8,128]{1,0:T(8,128)S(1)}, f32[8,128]{1,0:T(8,128)S(1)}, u32[]{:S(2)}, u32[]{:S(2)}) %collective-permute-start.1) | collective-permute-done | bytes 4128 | tf_op jit(solution)/shard_map/ppermute | solution.py:804
  24.8 3.2 %collective-permute-start.3 = (f32[16,128]{1,0:T(8,128)S(1)}, f32[16,128]{1,0:T(8,128)S(1)}, u32[]{:S(2)}, u32[]{:S(2)}) collective-permute-start(f32[16,128]{1,0:T(8,128)S(1)} %get-tuple-element.51), channel_id=1, source_target_pairs={{0,24},{8,0},{16,8},{24,16},{1,25},{9,1},{17,9},{25,17},{2,26},{10... | collective-permute-start | bytes 24584 | tf_op jit(solution)/shard_map/ppermute | solution.py:812
  28.0 1.3 %shard_map.180 = (bf16[144,2048]{1,0:T(8,128)(2,1)S(1)}, bf16[144,2048]{1,0:T(8,128)(2,1)S(1)}, f32[32,2048]{1,0:T(8,128)S(1)}) custom-call(s32[1]{0:T(128)} %bitcast.7.rank, f32[8,8,128]{2,1,0:T(8,128)S(1)} %all-to-all-done.table), custom_call_target="tpu_custom_call" | custom-call | flops 1000000000 | bytes 4000000 | tf_op jit(solution)/shard_map/pallas_call | solution.py:813
  29.4 5.3 %shard_map.181 = (f32[8,56,128]{2,1,0:T(8,128)}, f32[16,256]{1,0:T(8,128)S(1)}, f32[3,64,256]{2,1,0:T(8,128)S(1)}, f32[64,256]{1,0:T(8,128)S(1)}) custom-call(f32[8,256]{1,0:T(8,128)S(1)} %get-tuple-element.44.edges, s32[64,256]{1,0:T(8,128)S(1)} %get-tuple-element.45.listing, f32[4,64,256]{2,1,0:T(8,128)S(1)} %shard_map.177.after.near, ...), custom_call_target="tpu_custom_call" | custom-call | flops 4000000000 | bytes 16000000 | tf_op jit(solution)/shard_map/pallas_call | solution.py:820
  34.7 3.4 %all-to-all-start.1 = ((f32[8,56,128]{2,1,0:T(8,128)}), f32[8,56,128]{2,1,0:T(8,128)S(1)}, u32[]{:S(2)}, u32[]{:S(2)}) async-start(f32[8,56,128]{2,1,0:T(8,128)} %get-tuple-element.67), calls=%async_computation.1 | async-start | bytes 458752 | tf_op jit(solution)/shard_map/all_to_all | solution.py:839
  38.1 4.0 %shard_map.182 = (f32[9,32,256]{2,1,0:T(8,128)S(1)}, f32[384,256]{1,0:T(8,128)S(1)}) custom-call(f32[16,256]{1,0:T(8,128)S(1)} %get-tuple-element.60.refs_0_, f32[16,1]{1,0:T(8,128)S(1)} %get-tuple-element.61.refs_1_, f32[24,384]{1,0:T(8,128)S(1)} %get-tuple-element.57.ball.refs_2_, f32[3,64,256]{2,1,0:T(8,128)S(1)} %get-tuple-element.62.refs_3_.refs_1_.disp, ...), custom_call_target="tpu_custom_call" | custom-call | flops 2000000000 | bytes 8000000 | tf_op jit(solution)/shard_map/pallas_call | solution.py:845
  42.1 0.7 copy-done.5
  42.9 5.8 %all-to-all-done.1.got = f32[8,56,128]{2,1,0:T(8,128)S(1)} async-done(((f32[8,56,128]{2,1,0:T(8,128)}), f32[8,56,128]{2,1,0:T(8,128)S(1)}, u32[]{:S(2)}, u32[]{:S(2)}) %all-to-all-start.1) | async-done | bytes 229408 | tf_op jit(solution)/shard_map/all_to_all | solution.py:839
  48.7 1.0 copy-done.6
  49.6 2.0 %shard_map.185 = (f32[80,256]{1,0:T(8,128)S(1)}, f32[80,256]{1,0:T(8,128)S(1)}) custom-call(s32[1]{0:T(128)} %bitcast.5.core, f32[8,56,128]{2,1,0:T(8,128)S(1)} %all-to-all-done.1.got, f32[32,2048]{1,0:T(8,128)S(1)} %get-tuple-element.59.after.waves_x, bf16[144,2048]{1,0:T(8,128)(2,1)S(1)} %get-tuple-element.68.high, ...), custom_call_target="tpu_custom_call" | custom-call | flops 1500000000 | bytes 6000000 | tf_op jit(solution)/shard_map/pallas_call | solution.py:861
  51.6 1.8 %collective-permute-start.4 = (f32[80,256]{1,0:T(8,128)S(1)}, f32[80,256]{1,0:T(8,128)S(1)}, u32[]{:S(2)}, u32[]{:S(2)}) collective-permute-start(f32[80,256]{1,0:T(8,128)S(1)} %get-tuple-element.72), channel_id=1, source_target_pairs={{0,8},{8,0},{32,40},{40,32},{16,24},{24,16},{48,56},{56,48},{64,72... | collective-permute-start | bytes 245768 | tf_op jit(solution)/shard_map/ppermute | solution.py:881
  53.5 0.9 collective-permute-done.4
  54.4 0.7 collective-permute-start.5
  55.1 1.4 %collective-permute-start.6 = (f32[80,256]{1,0:T(8,128)S(1)}, f32[80,256]{1,0:T(8,128)S(1)}, u32[]{:S(2)}, u32[]{:S(2)}) collective-permute-start(f32[80,256]{1,0:T(8,128)S(1)} %add.8.refs_0_), channel_id=1, source_target_pairs={{0,48},{8,56},{32,0},{40,8},{16,32},{24,40},{48,16},{56,24},{64,11... | collective-permute-start | bytes 245768 | tf_op jit(solution)/shard_map/ppermute | solution.py:883
  56.5 3.1 %collective-permute-start.7 = (f32[80,256]{1,0:T(8,128)S(1)}, f32[80,256]{1,0:T(8,128)S(1)}, u32[]{:S(2)}, u32[]{:S(2)}) collective-permute-start(f32[80,256]{1,0:T(8,128)S(1)} %add.8.refs_0_), channel_id=1, source_target_pairs={{0,16},{8,24},{32,48},{40,56},{16,0},{24,8},{48,32},{56,40},{64,80... | collective-permute-start | bytes 245768 | tf_op jit(solution)/shard_map/ppermute | solution.py:883
  59.6 1.8 %shard_map.184.after.response1 = f32[9,16,256]{2,1,0:T(8,128)S(1)} custom-call(f32[384,256]{1,0:T(8,128)S(1)} %get-tuple-element.66.refs_0_, f32[3,64,256]{2,1,0:T(8,128)S(1)} %get-tuple-element.62.refs_3_.refs_1_.disp, f32[64,256]{1,0:T(8,128)S(1)} %copy-done.9, bf16[512,192]{1,0:T(8,128)(2,1)S(1)} %get-tuple-element.56.first.refs_5_.refs_3_, ...), custom_call_target="tpu_custom_call" | custom-call | flops 1000000000 | bytes 4000000 | tf_op jit(solution)/shard_map/pallas_call | solution.py:845
  61.4 2.1 %collective-permute-done.7.refs_3_ = f32[80,256]{1,0:T(8,128)S(1)} collective-permute-done((f32[80,256]{1,0:T(8,128)S(1)}, f32[80,256]{1,0:T(8,128)S(1)}, u32[]{:S(2)}, u32[]{:S(2)}) %collective-permute-start.7) | collective-permute-done | bytes 81952 | tf_op jit(solution)/shard_map/ppermute | solution.py:883
  63.6 0.4 collective-permute-start.8
  64.0 1.7 %collective-permute-start.9 = (f32[80,256]{1,0:T(8,128)S(1)}, f32[80,256]{1,0:T(8,128)S(1)}, u32[]{:S(2)}, u32[]{:S(2)}) collective-permute-start(f32[80,256]{1,0:T(8,128)S(1)} %shard_map.186.refs_0_), channel_id=1, source_target_pairs={{0,192},{8,200},{32,224},{40,232},{16,208},{24,216},{48,240},{56,2... | collective-permute-start | bytes 245768 | tf_op jit(solution)/shard_map/ppermute | solution.py:883
  65.7 1.2 %collective-permute-start.10 = (f32[80,256]{1,0:T(8,128)S(1)}, f32[80,256]{1,0:T(8,128)S(1)}, u32[]{:S(2)}, u32[]{:S(2)}) collective-permute-start(f32[80,256]{1,0:T(8,128)S(1)} %shard_map.186.refs_0_), channel_id=1, source_target_pairs={{0,128},{8,136},{32,160},{40,168},{16,144},{24,152},{48,176},{56,1... | collective-permute-start | bytes 245768 | tf_op jit(solution)/shard_map/ppermute | solution.py:883
  66.9 1.8 %shard_map.183.after.response2 = f32[9,16,256]{2,1,0:T(8,128)S(1)} custom-call(f32[384,256]{1,0:T(8,128)S(1)} %get-tuple-element.66.refs_0_, f32[3,64,256]{2,1,0:T(8,128)S(1)} %copy-done.3, f32[64,256]{1,0:T(8,128)S(1)} %copy-done.9, bf16[512,192]{1,0:T(8,128)(2,1)S(1)} %get-tuple-element.56.first.refs_5_.refs_3_, ...), custom_call_target="tpu_custom_call" | custom-call | flops 1000000000 | bytes 4000000 | tf_op jit(solution)/shard_map/pallas_call | solution.py:845
  68.7 1.2 %collective-permute-done.9.refs_2_ = f32[80,256]{1,0:T(8,128)S(1)} collective-permute-done((f32[80,256]{1,0:T(8,128)S(1)}, f32[80,256]{1,0:T(8,128)S(1)}, u32[]{:S(2)}, u32[]{:S(2)}) %collective-permute-start.9) | collective-permute-done | bytes 81952 | tf_op jit(solution)/shard_map/ppermute | solution.py:883
  69.9 1.8 %collective-permute-done.10.refs_3_ = f32[80,256]{1,0:T(8,128)S(1)} collective-permute-done((f32[80,256]{1,0:T(8,128)S(1)}, f32[80,256]{1,0:T(8,128)S(1)}, u32[]{:S(2)}, u32[]{:S(2)}) %collective-permute-start.10) | collective-permute-done | bytes 81952 | tf_op jit(solution)/shard_map/ppermute | solution.py:883
  71.8 0.4 shard_map.188.weights
  72.1 0.9 collective-permute-done.11.other
  73.0 2.7 %shard_map.189 = (f32[8,8,256]{2,1,0:T(8,128)}, f32[144,384]{1,0:T(8,128)S(1)}) custom-call(s32[1]{0:T(128)} %bitcast.5.core, f32[80,256]{1,0:T(8,128)S(1)} %shard_map.187.mine, f32[80,256]{1,0:T(8,128)S(1)} %collective-permute-done.11.other, f32[3,72,128]{2,1,0:T(8,128)S(1)} %shard_map.188.weights, f32[32,2048]{1,0:T(8,128)S(1)} %get-tuple-element.59.after.waves_x, ...), custom_call_target="tpu_custom_call" | custom-call | flops 1000000000 | bytes 4000000 | tf_op jit(solution)/shard_map/pallas_call | solution.py:888
  75.8 3.3 %all-to-all-start.2 = ((f32[8,8,256]{2,1,0:T(8,128)}), f32[8,8,256]{2,1,0:T(8,128)S(1)}, u32[]{:S(2)}, u32[]{:S(2)}) async-start(f32[8,8,256]{2,1,0:T(8,128)} %get-tuple-element.73), calls=%async_computation.2 | async-start | bytes 131072 | tf_op jit(solution)/shard_map/all_to_all | solution.py:899
  79.1 3.9 %shard_map.190.lines = f32[8,8,128]{2,1,0:T(8,128)S(1)} custom-call(s32[1]{0:T(128)} %bitcast.7.rank, f32[8,256]{1,0:T(8,128)S(1)} %get-tuple-element.44.edges, f32[144,384]{1,0:T(8,128)S(1)} %get-tuple-element.74.table, f32[8,56,128]{2,1,0:T(8,128)S(1)} %all-to-all-done.1.got, f32[32,2048]{1,0:T(8,128)S(1)} %get-tuple-element.59.after.waves_x, ...), custom_call_target="tpu_custom_call" | custom-call | flops 2500000000 | bytes 10000000 | tf_op jit(solution)/shard_map/pallas_call | solution.py:900
  83.1 4.3 %all-to-all-done.2.got = f32[8,8,256]{2,1,0:T(8,128)S(1)} async-done(((f32[8,8,256]{2,1,0:T(8,128)}), f32[8,8,256]{2,1,0:T(8,128)S(1)}, u32[]{:S(2)}, u32[]{:S(2)}) %all-to-all-start.2) | async-done | bytes 65568 | tf_op jit(solution)/shard_map/all_to_all | solution.py:899
  87.4 2.2 %shard_map.191 = (f32[16,128]{1,0:T(8,128)S(1)}, f32[16,128]{1,0:T(8,128)S(1)}, f32[8,128]{1,0:T(8,128)S(1)}, f32[8,128]{1,0:T(8,128)S(1)}, f32[8,8,128]{2,1,0:T(8,128)S(1)}, /*index=5*/f32[8,128]{1,0:T(8,128)S(1)}) custom-call(f32[8,8,256]{2,1,0:T(8,128)S(1)} %all-to-all-done.2.got, f32[9,32,256]{2,1,0:T(8,128)S(1)} %copy-done.7, ...), custom_call_target="tpu_custom_call" | custom-call | flops 2000000000 | bytes 8000000 | tf_op jit(solution)/shard_map/pallas_call | solution.py:912
  89.6 0.6 collective-permute-start.12
  90.2 1.4 %collective-permute-done.12.above = f32[16,128]{1,0:T(8,128)S(1)} collective-permute-done((f32[16,128]{1,0:T(8,128)S(1)}, f32[16,128]{1,0:T(8,128)S(1)}, u32[]{:S(2)}, u32[]{:S(2)}) %collective-permute-start.12) | collective-permute-done | bytes 8224 | tf_op jit(solution)/shard_map/ppermute | solution.py:931
  91.6 3.2 %collective-permute-done.13.below = f32[16,128]{1,0:T(8,128)S(1)} collective-permute-done((f32[16,128]{1,0:T(8,128)S(1)}, f32[16,128]{1,0:T(8,128)S(1)}, u32[]{:S(2)}, u32[]{:S(2)}) %collective-permute-start.13) | collective-permute-done | bytes 8224 | tf_op jit(solution)/shard_map/ppermute | solution.py:932
  94.8 1.7 %collective-permute-start.14 = (f32[8,128]{1,0:T(8,128)S(1)}, f32[8,128]{1,0:T(8,128)S(1)}, u32[]{:S(2)}, u32[]{:S(2)}) collective-permute-start(f32[8,128]{1,0:T(8,128)S(1)} %get-tuple-element.81), channel_id=1, source_target_pairs={{0,32},{32,64},{64,96},{96,128},{128,160},{160,192},{192,224},{224... | collective-permute-start | bytes 12296 | tf_op jit(solution)/shard_map/ppermute | solution.py:937
  96.6 0.3 collective-permute-start.15
  96.9 1.6 %collective-permute-done.14.from_left = f32[8,128]{1,0:T(8,128)S(1)} collective-permute-done((f32[8,128]{1,0:T(8,128)S(1)}, f32[8,128]{1,0:T(8,128)S(1)}, u32[]{:S(2)}, u32[]{:S(2)}) %collective-permute-start.14) | collective-permute-done | bytes 4128 | tf_op jit(solution)/shard_map/ppermute | solution.py:937
  98.4 3.8 %collective-permute-done.15.from_right = f32[8,128]{1,0:T(8,128)S(1)} collective-permute-done((f32[8,128]{1,0:T(8,128)S(1)}, f32[8,128]{1,0:T(8,128)S(1)}, u32[]{:S(2)}, u32[]{:S(2)}) %collective-permute-start.15) | collective-permute-done | bytes 4128 | tf_op jit(solution)/shard_map/ppermute | solution.py:936
  102.3 0.2 shard_map.193
  102.5 11.4 %all_to_all.20.got = f32[8,8,128]{2,1,0:T(8,128)S(1)} all-to-all(f32[8,8,128]{2,1,0:T(8,128)S(1)} %shard_map.193), channel_id=1, replica_groups=mesh['gx'=8,'gy'=4,'ka'=8] {'ka'}, dimensions={0} | all-to-all | bytes 65536 | tf_op jit(solution)/shard_map/all_to_all | solution.py:941
  113.9 0.6 shard_map.194
  (36 shorter events, 0.3 us)
Async XLA Ops:
  2.0 16.5 %all-to-all-start = ((f32[8,8,128]{2,1,0:T(8,128)}), f32[8,8,128]{2,1,0:T(8,128)S(1)}, u32[]{:S(2)}, u32[]{:S(2)}) async-start(f32[8,8,128]{2,1,0:T(8,128)} %get-tuple-element.46), calls=%async_computation | async-start | bytes 65536 | tf_op jit(solution)/shard_map/all_to_all | solution.py:753
  14.1 15.3 %copy-start.10 = (s32[64,256]{1,0:T(8,128)}, s32[64,256]{1,0:T(8,128)S(1)}, u32[]{:S(2)}) copy-start(s32[64,256]{1,0:T(8,128)S(1)} %get-tuple-element.45.listing) | copy-start | bytes 196612
  18.6 3.8 %collective-permute-start = (f32[8,128]{1,0:T(8,128)S(1)}, f32[8,128]{1,0:T(8,128)S(1)}, u32[]{:S(2)}, u32[]{:S(2)}) collective-permute-start(f32[8,128]{1,0:T(8,128)S(1)} %get-tuple-element.48.cell1), channel_id=1, source_target_pairs={{0,32},{32,64},{64,96},{96,128},{128,160},{160,192},{192,224},{224... | collective-permute-start | bytes 12296 | tf_op jit(solution)/shard_map/ppermute | solution.py:803
  19.1 5.7 %collective-permute-start.1 = (f32[8,128]{1,0:T(8,128)S(1)}, f32[8,128]{1,0:T(8,128)S(1)}, u32[]{:S(2)}, u32[]{:S(2)}) collective-permute-start(f32[8,128]{1,0:T(8,128)S(1)} %get-tuple-element.49.cell0), channel_id=1, source_target_pairs={{0,224},{32,0},{64,32},{96,64},{128,96},{160,128},{192,160},{224,1... | collective-permute-start | bytes 12296 | tf_op jit(solution)/shard_map/ppermute | solution.py:804
  24.8 4.6 %collective-permute-start.2 = (f32[16,128]{1,0:T(8,128)S(1)}, f32[16,128]{1,0:T(8,128)S(1)}, u32[]{:S(2)}, u32[]{:S(2)}) collective-permute-start(f32[16,128]{1,0:T(8,128)S(1)} %get-tuple-element.50), channel_id=1, source_target_pairs={{0,8},{8,16},{16,24},{24,0},{1,9},{9,17},{17,25},{25,1},{2,10},{10... | collective-permute-start | bytes 24584 | tf_op jit(solution)/shard_map/ppermute | solution.py:811
  24.8 4.6 %collective-permute-start.3 = (f32[16,128]{1,0:T(8,128)S(1)}, f32[16,128]{1,0:T(8,128)S(1)}, u32[]{:S(2)}, u32[]{:S(2)}) collective-permute-start(f32[16,128]{1,0:T(8,128)S(1)} %get-tuple-element.51), channel_id=1, source_target_pairs={{0,24},{8,0},{16,8},{24,16},{1,25},{9,1},{17,9},{25,17},{2,26},{10... | collective-permute-start | bytes 24584 | tf_op jit(solution)/shard_map/ppermute | solution.py:812
  34.7 3.4 %copy-start.8 = (f32[64,256]{1,0:T(8,128)}, f32[64,256]{1,0:T(8,128)S(1)}, u32[]{:S(2)}) copy-start(f32[64,256]{1,0:T(8,128)S(1)} %get-tuple-element.63.refs_4_.refs_2_) | copy-start | bytes 196612
  34.7 24.9 %copy-start.2 = (f32[3,64,256]{2,1,0:T(8,128)}, f32[3,64,256]{2,1,0:T(8,128)S(1)}, u32[]{:S(2)}) copy-start(f32[3,64,256]{2,1,0:T(8,128)S(1)} %get-tuple-element.62.refs_3_.refs_1_.disp) | copy-start | bytes 589828
  34.7 14.0 %all-to-all-start.1 = ((f32[8,56,128]{2,1,0:T(8,128)}), f32[8,56,128]{2,1,0:T(8,128)S(1)}, u32[]{:S(2)}, u32[]{:S(2)}) async-start(f32[8,56,128]{2,1,0:T(8,128)} %get-tuple-element.67), calls=%async_computation.1 | async-start | bytes 458752 | tf_op jit(solution)/shard_map/all_to_all | solution.py:839
  42.1 0.7 copy-start.5
  48.7 1.0 copy-start.6
  51.6 2.7 %collective-permute-start.4 = (f32[80,256]{1,0:T(8,128)S(1)}, f32[80,256]{1,0:T(8,128)S(1)}, u32[]{:S(2)}, u32[]{:S(2)}) collective-permute-start(f32[80,256]{1,0:T(8,128)S(1)} %get-tuple-element.72), channel_id=1, source_target_pairs={{0,8},{8,0},{32,40},{40,32},{16,24},{24,16},{48,56},{56,48},{64,72... | collective-permute-start | bytes 245768 | tf_op jit(solution)/shard_map/ppermute | solution.py:881
  54.4 5.2 %copy-start.9 = (f32[64,256]{1,0:T(8,128)S(1)}, f32[64,256]{1,0:T(8,128)}, u32[]{:S(2)}) copy-start(f32[64,256]{1,0:T(8,128)} %copy-done.8) | copy-start | bytes 196612
  54.4 7.0 %collective-permute-start.5 = (f32[80,256]{1,0:T(8,128)S(1)}, f32[80,256]{1,0:T(8,128)S(1)}, u32[]{:S(2)}, u32[]{:S(2)}) collective-permute-start(f32[80,256]{1,0:T(8,128)S(1)} %add.8.refs_0_), channel_id=1, source_target_pairs={{0,32},{8,40},{32,16},{40,24},{16,48},{24,56},{48,0},{56,8},{64,96... | collective-permute-start | bytes 245768 | tf_op jit(solution)/shard_map/ppermute | solution.py:883
  55.1 6.3 %collective-permute-start.6 = (f32[80,256]{1,0:T(8,128)S(1)}, f32[80,256]{1,0:T(8,128)S(1)}, u32[]{:S(2)}, u32[]{:S(2)}) collective-permute-start(f32[80,256]{1,0:T(8,128)S(1)} %add.8.refs_0_), channel_id=1, source_target_pairs={{0,48},{8,56},{32,0},{40,8},{16,32},{24,40},{48,16},{56,24},{64,11... | collective-permute-start | bytes 245768 | tf_op jit(solution)/shard_map/ppermute | solution.py:883
  56.5 7.1 %collective-permute-start.7 = (f32[80,256]{1,0:T(8,128)S(1)}, f32[80,256]{1,0:T(8,128)S(1)}, u32[]{:S(2)}, u32[]{:S(2)}) collective-permute-start(f32[80,256]{1,0:T(8,128)S(1)} %add.8.refs_0_), channel_id=1, source_target_pairs={{0,16},{8,24},{32,48},{40,56},{16,0},{24,8},{48,32},{56,40},{64,80... | collective-permute-start | bytes 245768 | tf_op jit(solution)/shard_map/ppermute | solution.py:883
  61.4 5.5 %copy-start.3 = (f32[3,64,256]{2,1,0:T(8,128)S(1)}, f32[3,64,256]{2,1,0:T(8,128)}, u32[]{:S(2)}) copy-start(f32[3,64,256]{2,1,0:T(8,128)} %copy-done.2) | copy-start | bytes 589828
  63.6 5.1 %collective-permute-start.8 = (f32[80,256]{1,0:T(8,128)S(1)}, f32[80,256]{1,0:T(8,128)S(1)}, u32[]{:S(2)}, u32[]{:S(2)}) collective-permute-start(f32[80,256]{1,0:T(8,128)S(1)} %shard_map.186.refs_0_), channel_id=1, source_target_pairs={{0,64},{8,72},{32,96},{40,104},{16,80},{24,88},{48,112},{56,120},{... | collective-permute-start | bytes 245768 | tf_op jit(solution)/shard_map/ppermute | solution.py:883
  64.0 5.9 %collective-permute-start.9 = (f32[80,256]{1,0:T(8,128)S(1)}, f32[80,256]{1,0:T(8,128)S(1)}, u32[]{:S(2)}, u32[]{:S(2)}) collective-permute-start(f32[80,256]{1,0:T(8,128)S(1)} %shard_map.186.refs_0_), channel_id=1, source_target_pairs={{0,192},{8,200},{32,224},{40,232},{16,208},{24,216},{48,240},{56,2... | collective-permute-start | bytes 245768 | tf_op jit(solution)/shard_map/ppermute | solution.py:883
  65.7 5.9 %collective-permute-start.10 = (f32[80,256]{1,0:T(8,128)S(1)}, f32[80,256]{1,0:T(8,128)S(1)}, u32[]{:S(2)}, u32[]{:S(2)}) collective-permute-start(f32[80,256]{1,0:T(8,128)S(1)} %shard_map.186.refs_0_), channel_id=1, source_target_pairs={{0,128},{8,136},{32,160},{40,168},{16,144},{24,152},{48,176},{56,1... | collective-permute-start | bytes 245768 | tf_op jit(solution)/shard_map/ppermute | solution.py:883
  71.7 1.4 %collective-permute-start.11 = (f32[80,256]{1,0:T(8,128)S(1)}, f32[80,256]{1,0:T(8,128)S(1)}, u32[]{:S(2)}, u32[]{:S(2)}) collective-permute-start(f32[80,256]{1,0:T(8,128)S(1)} %shard_map.187.mine), channel_id=1, source_target_pairs={{0,8},{8,0},{32,40},{40,32},{16,24},{24,16},{48,56},{56,48},{64,72... | collective-permute-start | bytes 245768 | tf_op jit(solution)/shard_map/ppermute | solution.py:884
  75.8 11.7 %all-to-all-start.2 = ((f32[8,8,256]{2,1,0:T(8,128)}), f32[8,8,256]{2,1,0:T(8,128)S(1)}, u32[]{:S(2)}, u32[]{:S(2)}) async-start(f32[8,8,256]{2,1,0:T(8,128)} %get-tuple-element.73), calls=%async_computation.2 | async-start | bytes 131072 | tf_op jit(solution)/shard_map/all_to_all | solution.py:899
  79.1 8.3 %copy-start.4 = (f32[3,64,256]{2,1,0:T(8,128)S(1)}, f32[3,64,256]{2,1,0:T(8,128)}, u32[]{:S(2)}) copy-start(f32[3,64,256]{2,1,0:T(8,128)} %copy-done.2) | copy-start | bytes 589828
  79.1 8.3 %copy-start.7 = (f32[9,32,256]{2,1,0:T(8,128)S(1)}, f32[9,32,256]{2,1,0:T(8,128)}, u32[]{:S(2)}) copy-start(f32[9,32,256]{2,1,0:T(8,128)} %copy-done.5) | copy-start | bytes 884740
  79.1 8.3 %copy-start.11 = (s32[64,256]{1,0:T(8,128)S(1)}, s32[64,256]{1,0:T(8,128)}, u32[]{:S(2)}) copy-start(s32[64,256]{1,0:T(8,128)} %copy-done.10) | copy-start | bytes 196612
  87.4 26.5 %copy-start = (f32[3,256]{1,0:T(4,128)S(1)}, f32[3,256]{1,0:T(4,128)}, u32[]{:S(2)}) copy-start(f32[3,256]{1,0:T(4,128)} %speed.1) | copy-start | bytes 9220
  87.4 26.5 %copy-start.1 = (f32[3,256]{1,0:T(4,128)S(1)}, f32[3,256]{1,0:T(4,128)}, u32[]{:S(2)}) copy-start(f32[3,256]{1,0:T(4,128)} %kicks.1) | copy-start | bytes 9220
  89.6 2.0 %collective-permute-start.12 = (f32[16,128]{1,0:T(8,128)S(1)}, f32[16,128]{1,0:T(8,128)S(1)}, u32[]{:S(2)}, u32[]{:S(2)}) collective-permute-start(f32[16,128]{1,0:T(8,128)S(1)} %get-tuple-element.75), channel_id=1, source_target_pairs={{0,24},{8,0},{16,8},{24,16},{1,25},{9,1},{17,9},{25,17},{2,26},{10... | collective-permute-start | bytes 24584 | tf_op jit(solution)/shard_map/ppermute | solution.py:931
  90.2 4.6 %collective-permute-start.13 = (f32[16,128]{1,0:T(8,128)S(1)}, f32[16,128]{1,0:T(8,128)S(1)}, u32[]{:S(2)}, u32[]{:S(2)}) collective-permute-start(f32[16,128]{1,0:T(8,128)S(1)} %get-tuple-element.76), channel_id=1, source_target_pairs={{0,8},{8,16},{16,24},{24,0},{1,9},{9,17},{17,25},{25,1},{2,10},{10... | collective-permute-start | bytes 24584 | tf_op jit(solution)/shard_map/ppermute | solution.py:932
  94.8 3.6 %collective-permute-start.14 = (f32[8,128]{1,0:T(8,128)S(1)}, f32[8,128]{1,0:T(8,128)S(1)}, u32[]{:S(2)}, u32[]{:S(2)}) collective-permute-start(f32[8,128]{1,0:T(8,128)S(1)} %get-tuple-element.81), channel_id=1, source_target_pairs={{0,32},{32,64},{64,96},{96,128},{128,160},{160,192},{192,224},{224... | collective-permute-start | bytes 12296 | tf_op jit(solution)/shard_map/ppermute | solution.py:937
  96.6 5.7 %collective-permute-start.15 = (f32[8,128]{1,0:T(8,128)S(1)}, f32[8,128]{1,0:T(8,128)S(1)}, u32[]{:S(2)}, u32[]{:S(2)}) collective-permute-start(f32[8,128]{1,0:T(8,128)S(1)} %get-tuple-element.82), channel_id=1, source_target_pairs={{0,224},{32,0},{64,32},{96,64},{128,96},{160,128},{192,160},{224,1... | collective-permute-start | bytes 12296 | tf_op jit(solution)/shard_map/ppermute | solution.py:936

commit v4 on v3

--- a/solution.py
+++ b/solution.py
@@ -77,6 +77,12 @@
     )
 
 
+def dot_x(a, b):
+    return lax.dot_general(
+        a, b, (((1,), (0,)), ((), ())), precision=lax.Precision.HIGHEST, preferred_element_type=f32
+    )
+
+
 def split(x):
     high = x.astype(bf16)
     return high, (x - high.astype(f32)).astype(bf16)
@@ -148,11 +154,18 @@
     value = jnp.where(row < top, 1.0, sign)
     line = jnp.where(row < 2 * top, jnp.where(jnp.abs(kx) == wanted, value, 0.0), 0.0)
     line = jnp.where((row == 2 * top) & (kx == 0.0), 1.0, line).astype(bf16)
-    place = lax.broadcasted_iota(i32, (128, count), 0).astype(f32)
-    valid = place < plane_own
+    place = (lax.broadcasted_iota(i32, (128, count), 0) & 63).astype(f32)
+    spill = (lax.broadcasted_iota(i32, (16, count), 0) + 64).astype(f32)
+    left = lax.broadcasted_iota(i32, (16, 128), 1) < 64
     for z in range(ranks):
-        hit = jnp.where(valid & (code == place + float(z * plane_own)), 1.0, 0.0).astype(bf16)
-        out[z] = dot_t(line, hit)[0:40, :]
+        begin = float(z * plane_own)
+        hit = jnp.where(code == place + begin, 1.0, 0.0).astype(bf16)
+        both = dot_t(line, hit)
+        out[z, 0:16, :] = jnp.where(left, both[0:16], both[16:32])
+        hit = jnp.where((code == spill + begin) & (spill < plane_own), 1.0, 0.0).astype(bf16)
+        out[z, 16:24, :] = jnp.zeros((8, 128), f32)
+        out[z, 16:21, 0:48] = dot_t(hit, line)[0:5]
+        out[z, 21:22, 0:64] = both[32:33, 0:64]
 
 
 def prepare_kernel(
@@ -178,7 +191,7 @@
     edges_out[3:8, :] = jnp.zeros((5, own), f32)
     lane = lax.broadcasted_iota(i32, (8, 64), 1)
     pick = jnp.where(lax.shift_right_logical(lane, 3) == lax.broadcasted_iota(i32, (8, 64), 0), 1.0, 0.0)
-    repeated = dot_c(initial[...], pick)
+    repeated = 0.5 * dot_c(initial[...], pick)
     lane = lax.broadcasted_iota(i32, (hidden, 64), 1) & 7
     blocks = jnp.concatenate(
         [jnp.where(lane == m, repeated, 0.0) for m in range(chunk)], axis=0
@@ -221,15 +234,15 @@
         for h in range(16):
             row = table[h // 2, 2 * c + h % 2 : 2 * c + h % 2 + 1, :]
             found = jnp.where(high == h, lane_pick(row, low), found)
-        for j in range(2):
-            cell0[j * 4 + c : j * 4 + c + 1, :] = found[j : j + 1]
-            cell1[j * 4 + c : j * 4 + c + 1, :] = found[2 + j : 3 + j]
-
-
-def columns_kernel(left, cell0, cell1, right, after, head, tail):
-    for u, ref in enumerate((left, cell0, cell1, right)):
-        head[u * 4 : u * 4 + 4, :] = ref[0:4, :]
-        tail[u * 4 : u * 4 + 4, :] = ref[4:8, :]
+        for i in range(2):
+            cell0[i * 4 + c : i * 4 + c + 1, :] = found[2 * i : 2 * i + 1]
+            cell1[i * 4 + c : i * 4 + c + 1, :] = found[2 * i + 1 : 2 * i + 2]
+
+
+def columns_kernel(below, cell0, cell1, above, after, head, tail):
+    for v, ref in enumerate((below, cell0, cell1, above)):
+        head[v * 4 : v * 4 + 4, :] = ref[0:4, :]
+        tail[v * 4 : v * 4 + 4, :] = ref[4:8, :]
 
 
 def own_gather_kernel(table, listing, near):
@@ -276,19 +289,20 @@
 
 
 def message_kernel(
-    edges, listing, near, left, right, head, tail, place, kind, tally, counts, first, ball, base,
+    edges, listing, near, below, above, left, right, place, kind, tally, counts, first, ball, base,
     after, send, activation, disp_out, mark_out,
     cells, pooled, actives,
 ):
-    for u in range(4):
-        for c in range(4):
-            cells[c * 16 + u * 4 : c * 16 + u * 4 + 1, :] = head[u * 4 + c : u * 4 + c + 1, :]
-            cells[c * 16 + u * 4 + 3 : c * 16 + u * 4 + 4, :] = tail[u * 4 + c : u * 4 + c + 1, :]
     for u, ref in ((0, left), (3, right)):
-        for j in range(2):
+        for v in range(4):
             for c in range(4):
-                spot = c * 16 + u * 4 + 1 + j
-                cells[spot : spot + 1, :] = ref[j * 4 + c : j * 4 + c + 1, :]
+                spot = c * 16 + u * 4 + v
+                cells[spot : spot + 1, :] = ref[v * 4 + c : v * 4 + c + 1, :]
+    for v, ref in ((0, below), (3, above)):
+        for i in range(2):
+            for c in range(4):
+                spot = c * 16 + (1 + i) * 4 + v
+                cells[spot : spot + 1, :] = ref[i * 4 + c : i * 4 + c + 1, :]
     pooled[...] = jnp.zeros_like(pooled)
 
     def part(j, active):
@@ -321,15 +335,17 @@
             [jnp.exp(squared * (-1.0 / (w * w))) for w in radial_widths], axis=0
         )
         upper, lower = split(basis)
-        pre = dot_n(first[...], jnp.concatenate([upper, lower, upper], axis=0))
-        gate = 0.5 * jnp.tanh(0.5 * pre) + 0.5
-        active[...] = pre * gate
+        half_pre = dot_n(first[...], jnp.concatenate([upper, lower, upper], axis=0))
+        active[...] = half_pre + half_pre * jnp.tanh(half_pre)
         for s in range(kinds):
-            total = pooled[s * hidden : (s + 1) * hidden, :]
+            total = [pooled[s * hidden + b : s * hidden + b + 8, :] for b in range(0, hidden, 8)]
             for m in range(chunk):
-                hit = jnp.broadcast_to(mark[m : m + 1, :], (hidden, own)) == float(s)
-                total = total + jnp.where(hit, active[m * hidden : (m + 1) * hidden, :], 0.0)
-            pooled[s * hidden : (s + 1) * hidden, :] = total
+                hit = jnp.broadcast_to(mark[m : m + 1, :], (8, own)) == float(s)
+                for n in range(hidden // 8):
+                    row = m * hidden + n * 8
+                    total[n] = total[n] + jnp.where(hit, active[row : row + 8, :], 0.0)
+            for n in range(hidden // 8):
+                pooled[s * hidden + n * 8 : s * hidden + n * 8 + 8, :] = total[n]
 
     paired(chunks, part, (actives,))
     answers = dot3(ball[...], pooled[...])
@@ -340,7 +356,7 @@
     for z in range(ranks):
         send[z, 0:8, :] = charges[:, 0:128]
         send[z, 8:16, :] = charges[:, 128:256]
-        send[z, 16:56, :] = counts[z]
+        send[z, 16:40, :] = counts[z]
 
 
 def response_start(activation, final, ball, upstream):
@@ -362,10 +378,11 @@
 def response_kernel(begin, count, first_part, *refs):
     if first_part:
         activation, final, ball, disp, marks, first, mixed_high, mixed_low = refs[:8]
-        out, upstream = refs[8:10]
+        out, token, upstream = refs[8:11]
         response_start(activation, final, ball, upstream)
     else:
-        upstream, disp, marks, first, mixed_high, mixed_low, out = refs[:7]
+        upstream, disp, marks, first, mixed_high, mixed_low, out, token = refs[:8]
+    token[...] = jnp.zeros_like(token)
     bends, uppers, lowers = refs[-3:]
 
     def part(j, bend, upper, lower):
@@ -378,10 +395,12 @@
         lean = [b * (-2.0 / (w * w)) for b, w in zip(basis, radial_widths)]
         ah, al = split(jnp.concatenate(basis, axis=0))
         bh, bl = split(jnp.concatenate(lean, axis=0))
-        pre = dot_n(first[...], jnp.concatenate([ah, al, ah], axis=0))
-        gate = 0.5 * jnp.tanh(0.5 * pre) + 0.5
-        bend[...] = (gate + pre * gate * (1.0 - gate)) * dot_n(
-            first[...], jnp.concatenate([bh, bl, bh], axis=0)
+        half_pre = dot_n(first[...], jnp.concatenate([ah, al, ah], axis=0))
+        bent = jnp.tanh(half_pre)
+        bend[...] = (
+            (1.0 + bent)
+            * (1.0 + half_pre * (1.0 - bent))
+            * dot_n(first[...], jnp.concatenate([bh, bl, bh], axis=0))
         )
         upper[...], lower[...] = split(bend[...])
         mixed = dot_n(mixed_high[...], upper[...]) + (
@@ -394,13 +413,16 @@
                 total = jnp.where(mark == float(s), mixed[row : row + 8, :], total)
             out[l, to, :] = total
         for m in range(chunk):
-            mine = jnp.broadcast_to(mark[m : m + 1, :], (hidden, own))
-            chosen = jnp.zeros((hidden, own), f32)
-            for s in range(kinds):
-                chosen = jnp.where(
-                    mine == float(s), upstream[s * hidden : (s + 1) * hidden, :], chosen
-                )
-            line = jnp.sum(chosen * bend[m * hidden : (m + 1) * hidden, :], axis=0, keepdims=True)
+            mine = jnp.broadcast_to(mark[m : m + 1, :], (8, own))
+            hits = [mine == float(s) for s in range(kinds)]
+            total = jnp.zeros((8, own), f32)
+            for n in range(0, hidden, 8):
+                chosen = jnp.zeros((8, own), f32)
+                for s in range(kinds):
+                    row = s * hidden + n
+                    chosen = jnp.where(hits[s], upstream[row : row + 8, :], chosen)
+                total = total + chosen * bend[m * hidden + n : m * hidden + n + 8, :]
+            line = jnp.sum(total, axis=0, keepdims=True)
             out[8, pl.ds(j * chunk + m, 1), :] = line
 
     paired(count, part, (bends, uppers, lowers))
@@ -441,18 +463,25 @@
         ref[plane_rows : plane_rows + 8, 128:256] = jnp.zeros((8, 128), f32)
 
 
-def weight_kernel(rank, edges, got, out):
-    counts = got[0, 16:56, :]
+def weight_kernel(rank, edges, got, out, lone_out):
+    counts = got[0, 16:40, :]
     for z in range(1, ranks):
-        counts = counts + got[z, 16:56, :]
-    lane = lax.broadcasted_iota(i32, (top, 128), 1)
-    spread = jnp.where(
-        lax.shift_right_logical(lane, 3) == lax.broadcasted_iota(i32, (top, 128), 0), 1.0, 0.0
-    )
-    flat = jnp.where(lax.broadcasted_iota(i32, (8, 128), 0) == 0, 1.0, 0.0)
-    both = dot_c(counts[0:top], spread)[0:plane_rows]
-    apart = dot_c(counts[top : 2 * top], spread)[0:plane_rows]
-    zero = dot_c(counts[2 * top : 2 * top + 8], flat)[0:plane_rows]
+        counts = counts + got[z, 16:40, :]
+    main, rest = counts[0:16], counts[16:24]
+    line = lax.broadcasted_iota(i32, (8, 128), 0)
+    lane = lax.broadcasted_iota(i32, (8, 128), 1)
+    spill = jnp.where(line < 5, rest, 0.0)
+    flat = jnp.where(line == 5, 1.0, 0.0)
+    row = lax.broadcasted_iota(i32, (128, 128), 0)
+    wave = lax.shift_right_logical(lax.broadcasted_iota(i32, (128, 128), 1), 3)
+
+    def pick(where):
+        return jnp.where(where, 1.0, 0.0)
+
+    halves = dot_c(main, pick(row == wave)[0:16])
+    both = jnp.concatenate([halves[0:64], dot_x(spill, pick(row == wave))], axis=0)
+    apart = jnp.concatenate([halves[64:128], dot_x(spill, pick(row == wave + 16))], axis=0)
+    zero = jnp.concatenate([dot_c(rest, flat)[0:64], dot_x(spill, pick(row == 32))], axis=0)
     shape = (plane_rows, 128)
     ky, kz = plane_of(rank[0], shape, 0)
     kx = (lax.shift_right_logical(lax.broadcasted_iota(i32, shape, 1), 3) + 1).astype(f32)
@@ -466,7 +495,12 @@
     weight = weigh(square)
     out[0] = both * weight
     out[1] = apart * weight
-    out[2] = zero * jnp.where(flat_square > 0.0, weigh(jnp.maximum(flat_square, 1e-6)), 0.0)
+    zero = zero * jnp.where(flat_square > 0.0, weigh(jnp.maximum(flat_square, 1e-6)), 0.0)
+    out[2] = zero
+    lane = lax.broadcasted_iota(i32, (plane_rows, own), 1)
+    row = lax.broadcasted_iota(i32, (plane_rows, own), 0)
+    twice = jnp.where((lane == row) | (lane == row + plane_rows), 1.0, 0.0)
+    lone_out[...] = dot_c(zero[:, 0:8], twice)
 
 
 def turn_table(table, blocks, table_high, table_low):
@@ -475,19 +509,22 @@
         table_high[at, 0:waves], table_low[at, 0:waves] = split(jnp.transpose(table[:, at]))
 
 
-def potential_kernel(
-    core, mine, other, weights, waves_x, high, low, potential, table, table_high, table_low, results
-):
+def halves_of(core, mine, other):
     first = core[0] == 0
     real = jnp.where(first, mine[0:plane_rows, :], other[0:plane_rows, :])
     imaginary = jnp.where(first, other[0:plane_rows, :], mine[0:plane_rows, :])
     tail = slice(plane_rows, plane_rows + 8)
     begin = jnp.where(first, mine[tail, 0:128], other[tail, 0:128])
     rest = jnp.where(first, other[tail, 0:128], mine[tail, 0:128])
-    lane = lax.broadcasted_iota(i32, (8, 128), 1)
-    repeat = jnp.where((lane & 7) == lax.broadcasted_iota(i32, (8, 128), 0), 1.0, 0.0)
-    lone = dot_c(jnp.concatenate([begin, rest], axis=1), repeat)
-    both, apart, zero = weights[0], weights[1], weights[2]
+    return real, imaginary, jnp.concatenate([begin, rest], axis=1)
+
+
+def potential_kernel(
+    core, mine, other, weights, lone_weights, waves_x, high, low, potential, table, table_high,
+    table_low, results
+):
+    real, imaginary, lone = halves_of(core, mine, other)
+    both, apart = weights[0], weights[1]
     real_c, real_s = real[:, 0:128], real[:, 128:256]
     imag_c, imag_s = imaginary[:, 0:128], imaginary[:, 128:256]
     upper, lower = slice(0, plane_rows), slice(plane_rows, waves)
@@ -495,9 +532,10 @@
     table[lower, 0:128] = both * imag_c + apart * real_s
     table[upper, 128:256] = both * real_s + apart * imag_c
     table[lower, 128:256] = both * imag_s - apart * real_c
-    table[upper, 256:384] = zero * lone[0:plane_rows]
-    table[lower, 256:384] = zero * lone[plane_rows:waves]
-    turn_table(table, 3, table_high, table_low)
+    turn_table(table, 2, table_high, table_low)
+    lone = (lone * lone_weights[...])[:, 0:waves]
+    lone = jnp.concatenate([lone, jnp.zeros_like(lone)], axis=0)
+    table_high[256:272, 0:waves], table_low[256:272, 0:waves] = split(lone)
 
     def part(z, result):
         at = pl.ds(pl.multiple_of(z * own, own), own)
@@ -515,8 +553,14 @@
 
 
 def gradient_kernel(
-    rank, edges, table, got, waves_x, high, low, gradient, wide, table_high, table_low, results
+    rank, core, edges, mine, other, weights, table, got, waves_x, high, low, gradient, wide,
+    table_high, table_low, results
 ):
+    _, _, lone = halves_of(core, mine, other)
+    lane = lax.broadcasted_iota(i32, (8, 128), 1)
+    repeat = jnp.where((lane & 7) == lax.broadcasted_iota(i32, (8, 128), 0), 1.0, 0.0)
+    lone = dot_c(lone, repeat)
+    zero = weights[2]
     shape = (plane_rows, 128)
     ky, kz = plane_of(rank[0], shape, 0)
     ty, tz = tau * ky, tau * kz
@@ -529,7 +573,7 @@
             at = slice(form * 256 + part * 128, form * 256 + part * 128 + 128)
             wide[upper, at] = scale * im
             wide[lower, at] = -(scale * re)
-    re, im = table[upper, 256:384], table[lower, 256:384]
+    re, im = zero * lone[0:plane_rows], zero * lone[plane_rows:waves]
     group = lax.shift_right_logical(lax.broadcasted_iota(i32, shape, 1), 3)
     turn = jnp.where(group == 0, ty, tz)
     wide[upper, 768:896] = turn * im
@@ -563,41 +607,39 @@
     paired(ranks, part, (results,))
 
 
-def pair_kernel(
-    got, response0, response1, response2, disp, listing, lines, cells0, cells3, mid0, mid3, domain,
-    direct, lefts, rights, total, pulled,
-):
+def pair_kernel(ghosts, got, response0, response1, response2, disp, listing, *refs):
     potential = got[0]
     for z in range(1, ranks):
         potential = potential + got[z]
+    lefts, rights, total, pulled = refs[-4:]
     total[...] = jnp.zeros_like(total)
     pulled[...] = jnp.zeros_like(pulled)
-    row_high = lax.broadcasted_iota(i32, (32, own), 0)
+    row_high = lax.broadcasted_iota(i32, (16, own), 0) + (16 if ghosts else 0)
     row_low = lax.broadcasted_iota(i32, (128, own), 0)
 
     def part(response, begin, j, left, right):
         to = pl.ds(pl.multiple_of(j * chunk, chunk), chunk)
         at = pl.ds(pl.multiple_of((j + begin) * chunk, chunk), chunk)
-        offsets = [disp[d, at, :] for d in range(3)]
         radial = response[8, to, :]
         for l in range(8):
             radial = radial + potential[l : l + 1, :] * response[l, to, :]
-        pulls = [radial * offset for offset in offsets]
+        pulls = [radial * disp[d, at, :] for d in range(3)]
         index = listing[at, :]
         low, high = index & 127, lax.shift_right_logical(index, 7)
         pieces = []
         for d in range(3):
-            pulled[d] += pulls[d]
+            if not ghosts:
+                pulled[d] += pulls[d]
             main = pulls[d].astype(bf16).astype(f32)
             pieces.append((main, pulls[d] - main))
         for m in range(chunk):
             lanes = slice(m * own, (m + 1) * own)
-            hit = jnp.broadcast_to(high[m : m + 1, :], (32, own)) == row_high
-            for part in range(2):
+            hit = jnp.broadcast_to(high[m : m + 1, :], (16, own)) == row_high
+            for piece in range(2):
                 for d in range(3):
-                    row = part * 96 + d * 32
-                    left[row : row + 32, lanes] = jnp.where(
-                        hit, pieces[d][part][m : m + 1, :], 0.0
+                    row = piece * 48 + d * 16
+                    left[row : row + 16, lanes] = jnp.where(
+                        hit, pieces[d][piece][m : m + 1, :], 0.0
                     ).astype(bf16)
             spot = jnp.broadcast_to(low[m : m + 1, :], (128, own)) == row_low
             right[:, lanes] = jnp.where(spot, 1.0, 0.0).astype(bf16)
@@ -608,24 +650,28 @@
         count = response.shape[1] // chunk
         paired(count, functools.partial(part, response, begin), (lefts, rights))
         begin += count
-    scattered = total[0:96, :] + total[96:192, :]
-    nothing = jnp.zeros((1, 128), f32)
-    for u in range(4):
-        for c in range(4):
-            for ref, v in ((cells0, 0), (cells3, 3)):
-                spot = c * 32 + 16 + u * 4 + v
-                value = scattered[spot : spot + 1, :] if c < 3 else nothing
-                ref[u * 4 + c : u * 4 + c + 1, :] = value
-    for ref, u in ((mid0, 0), (mid3, 3)):
-        for j in range(2):
+    scattered = total[0:48, :] + total[48:96, :]
+    if ghosts:
+        cells0, cells3, mid0, mid3 = refs[:4]
+        nothing = jnp.zeros((1, 128), f32)
+        for u in range(4):
             for c in range(4):
-                spot = c * 32 + 16 + u * 4 + 1 + j
-                value = scattered[spot : spot + 1, :] if c < 3 else nothing
-                ref[j * 4 + c : j * 4 + c + 1, :] = value
+                for ref, v in ((cells0, 0), (cells3, 3)):
+                    spot = c * 16 + u * 4 + v
+                    value = scattered[spot : spot + 1, :] if c < 3 else nothing
+                    ref[u * 4 + c : u * 4 + c + 1, :] = value
+        for ref, u in ((mid0, 0), (mid3, 3)):
+            for j in range(2):
+                for c in range(4):
+                    spot = c * 16 + u * 4 + 1 + j
+                    value = scattered[spot : spot + 1, :] if c < 3 else nothing
+                    ref[j * 4 + c : j * 4 + c + 1, :] = value
+        return
+    lines, domain, direct = refs[:3]
     for z in range(ranks):
         for d in range(3):
             for half in range(2):
-                spot, r = d * 32 + z * 2 + half, 2 * d + half
+                spot, r = d * 16 + z * 2 + half, 2 * d + half
                 domain[z, r : r + 1, :] = scattered[spot : spot + 1, :] + lines[z, r : r + 1, :]
         domain[z, 6:8, :] = jnp.zeros((2, 128), f32)
     for d in range(3):
@@ -635,7 +681,7 @@
     direct[6:8, :] = jnp.zeros((2, 128), f32)
 
 
-def echo_kernel(above, below, mid0, mid3, send0, send3, inner0, inner1):
+def echo_kernel(above, below, mid0, mid3, after, send0, send3, inner0, inner1):
     for u, ref in ((0, send0), (1, inner0), (2, inner1), (3, send3)):
         both = jnp.concatenate([below[u * 4 : u * 4 + 4, :], above[u * 4 : u * 4 + 4, :]], axis=0)
         if u == 0:
@@ -758,7 +804,7 @@
             ((slots, own), i32),
             ((1, own), i32),
             ((2, 2, 128), i32),
-            ((ranks, 40, 128), f32),
+            ((ranks, 24, 128), f32),
             ((chunk * hidden, 192), bf16),
             ((8 * 8 * kinds, chunk * hidden), bf16),
             ((8 * 8 * kinds, chunk * hidden), bf16),
@@ -800,16 +846,16 @@
         )
     )
     cell0, cell1 = call(border_kernel, [((8, 128), f32)] * 2, [vmem] * 2)(table, rows)
-    left = lax.ppermute(cell1, "gx", shift("gx", 1))
-    right = lax.ppermute(cell0, "gx", shift("gx", -1))
+    below = lax.ppermute(cell1, "gy", shift("gy", 1))
+    above = lax.ppermute(cell0, "gy", shift("gy", -1))
     near = call(own_gather_kernel, [((4, slots, own), f32)], [vmem] * 2, cost=work(2))(
         table, listing
     )[0]
     head, tail = call(columns_kernel, [((16, 128), f32)] * 2, [vmem] * 4 + [anywhere])(
-        left, cell0, cell1, right, near
-    )
-    tail_in = lax.ppermute(tail, "gy", shift("gy", 1))
-    head_in = lax.ppermute(head, "gy", shift("gy", -1))
+        below, cell0, cell1, above, near
+    )
+    left = lax.ppermute(tail, "gx", shift("gx", 1))
+    right = lax.ppermute(head, "gx", shift("gx", -1))
     high, low, waves_x = call(
         factor_kernel,
         [((waves, ranks * own), bf16), ((waves, ranks * own), bf16), ((2 * top, ranks * own), f32)],
@@ -820,7 +866,7 @@
     send, activation, disp, marks = call(
         message_kernel,
         [
-            ((ranks, 56, 128), f32),
+            ((ranks, 40, 128), f32),
             ((16, own), f32),
             ((3, slots, own), f32),
             ((slots, own), f32),
@@ -833,15 +879,18 @@
         ],
         cost=work(8),
     )(
-        edges, listing, near, left, right, tail_in, head_in, place, kind, tally, counts, first,
+        edges, listing, near, below, above, left, right, place, kind, tally, counts, first,
         ball, base, waves_x,
     )
     got = lax.all_to_all(send, "ka", 0, 0)
-    ready = (disp, marks, first, mixed_high, mixed_low)
+    ready = (disp, marks, first) + tuple(
+        pltpu.with_memory_space_constraint(part, pltpu.VMEM) for part in (mixed_high, mixed_low)
+    )
 
     def respond(begin, count, operands):
         started = begin == 0
-        outs = [((9, count * chunk, own), f32)] + [((kinds * hidden, own), f32)] * started
+        outs = [((9, count * chunk, own), f32), ((8, 128), f32)]
+        outs += [((kinds * hidden, own), f32)] * started
         return call(
             functools.partial(response_kernel, begin, count, started),
             outs,
@@ -854,9 +903,9 @@
             cost=work(count),
         )(*operands)
 
-    response0, upstream = respond(0, 4, (activation, final, ball) + ready)
-    response1 = respond(4, 2, (upstream,) + ready)[0]
-    response2 = respond(6, 2, (upstream,) + ready)[0]
+    response0, token0, upstream = respond(0, 4, (activation, final, ball) + ready)
+    response1, token1 = respond(4, 2, (upstream,) + ready)
+    response2, token2 = respond(6, 2, (upstream,) + ready)
 
     mine, other = call(
         structure_kernel,
@@ -869,7 +918,7 @@
             pltpu.VMEM((2, own, own), bf16),
         ],
         cost=work(3),
-    )(core, got, waves_x, high, low, response0)
+    )(core, got, waves_x, high, low, token0)
     swap, rings = partners()
     both = ("gx", "gy")
 
@@ -879,28 +928,31 @@
         )(after, *parts)[0]
 
     summed = mine + lax.ppermute(other, both, swap)
-    for ring, after in zip(rings, (response1, response2)):
+    for ring, after in zip(rings, (token1, token2)):
         summed = add(after, summed, *[lax.ppermute(summed, both, turn) for turn in ring])
     opposite = lax.ppermute(summed, both, swap)
-    weights = call(
-        weight_kernel, [((3, plane_rows, 128), f32)], [smem] + [vmem] * 2, cost=work(0.5)
-    )(rank, edges, got)[0]
+    weights, lone_weights = call(
+        weight_kernel,
+        [((3, plane_rows, 128), f32), ((8, own), f32)],
+        [smem] + [vmem] * 2,
+        cost=work(0.5),
+    )(rank, edges, got)
     potential, spectrum = call(
         potential_kernel,
-        [((ranks, 8, own), f32), ((waves, 384), f32)],
-        [smem] + [vmem] * 6,
+        [((ranks, 8, own), f32), ((waves, 256), f32)],
+        [smem] + [vmem] * 7,
         [
-            pltpu.VMEM((384, own), bf16),
-            pltpu.VMEM((384, own), bf16),
+            pltpu.VMEM((272, own), bf16),
+            pltpu.VMEM((272, own), bf16),
             pltpu.VMEM((2, 272, own), f32),
         ],
         cost=work(2),
-    )(core, summed, opposite, weights, waves_x, high, low)
+    )(core, summed, opposite, weights, lone_weights, waves_x, high, low)
     shares = lax.all_to_all(potential, "ka", 0, 0)
     lines = call(
         gradient_kernel,
         [((ranks, 8, 128), f32)],
-        [smem] + [vmem] * 6,
+        [smem] * 2 + [vmem] * 9,
         [
             pltpu.VMEM((waves, 896), f32),
             pltpu.VMEM((896, own), bf16),
@@ -908,31 +960,32 @@
             pltpu.VMEM((2, 784, own), f32),
         ],
         cost=work(5),
-    )(rank, edges, spectrum, got, waves_x, high, low)[0]
-    cells0, cells3, mid0, mid3, domain, direct = call(
-        pair_kernel,
-        [
-            ((16, 128), f32),
-            ((16, 128), f32),
-            ((8, 128), f32),
-            ((8, 128), f32),
-            ((ranks, 8, 128), f32),
-            ((8, 128), f32),
-        ],
-        [vmem] * 7,
-        [
-            pltpu.VMEM((2, 192, chunk * own), bf16),
-            pltpu.VMEM((2, 128, chunk * own), bf16),
-            pltpu.VMEM((192, 128), f32),
-            pltpu.VMEM((3, chunk, own), f32),
-        ],
-        cost=work(4),
-    )(shares, response0, response1, response2, disp, listing, lines)
-    above = lax.ppermute(cells0, "gy", shift("gy", -1))
-    below = lax.ppermute(cells3, "gy", shift("gy", 1))
-    send0, send3, inner0, inner1 = call(echo_kernel, [((8, 128), f32)] * 4, [vmem] * 4)(
-        above, below, mid0, mid3
-    )
+    )(rank, core, edges, summed, opposite, weights, spectrum, got, waves_x, high, low)[0]
+    pairs = (shares, response0, response1, response2, disp, listing)
+
+    def pull(ghosts, outs, operands):
+        return call(
+            functools.partial(pair_kernel, ghosts),
+            outs,
+            [vmem] * len(operands),
+            [
+                pltpu.VMEM((2, 96, chunk * own), bf16),
+                pltpu.VMEM((2, 128, chunk * own), bf16),
+                pltpu.VMEM((96, 128), f32),
+                pltpu.VMEM((3, chunk, own), f32),
+            ],
+            cost=work(2),
+        )(*operands)
+
+    cells0, cells3, mid0, mid3 = pull(
+        True, [((16, 128), f32), ((16, 128), f32), ((8, 128), f32), ((8, 128), f32)], pairs
+    )
+    domain, direct = pull(False, [((ranks, 8, 128), f32), ((8, 128), f32)], pairs + (lines,))
+    from_above = lax.ppermute(cells0, "gy", shift("gy", -1))
+    from_below = lax.ppermute(cells3, "gy", shift("gy", 1))
+    send0, send3, inner0, inner1 = call(
+        echo_kernel, [((8, 128), f32)] * 4, [vmem] * 4 + [anywhere]
+    )(from_above, from_below, mid0, mid3, domain)
     from_right = lax.ppermute(send0, "gx", shift("gx", -1))
     from_left = lax.ppermute(send3, "gx", shift("gx", 1))
     reaction = call(border_back_kernel, [((ranks, 8, 128), f32)], [vmem] * 6)(

time: 115 us -> 112 us (0.974)
  starting transfers between devices: 33.7 us -> 30.9 us
  waiting for transfers between devices: 33.9 us -> 31.4 us
  local copies, waits for them, and re-layouts: 1.73 us -> 2.99 us
    ppermute x6, starting transfers between devices: 8.53 us -> 6.78 us  [body(): lax.ppermute(summed, both, turn)]
    ppermute x6, waiting for transfers between devices: 7.04 us -> 5.49 us  [the longest x1 2.65 us: body(): from_below = lax.ppermute(cells3, 'gy', shift('gy', 1))]
    unnamed x24, local copies, waits for them, and re-layouts: 1.73 us -> 2.99 us
    ppermute x1, starting transfers between devices: 1.82 us -> 0.58 us  [body(): summed = mine + lax.ppermute(other, both, swap)]
    pallas_call x6 -> x7, Pallas kernels: 14.5 us -> 15.3 us  [the longest x1 4.9 us: body(): call(message_kernel, [((ranks, 40, 128), f32), ((16, own), f32), ((3, slo...]
  transfers between devices with their start and end apart: 19 -> 19, of which waited for: 14 -> 13; matrix products, arithmetic and copies ran while one was open for 0% -> 0% of each run, Pallas kernels for 16% -> 18%
where the time goes in v4:
time: 112 us; the launch traced here: 111 us
  Pallas kernels  33.6 us (30%)
  waiting for transfers between devices  31.4 us (28%)
  starting transfers between devices  30.9 us (28%)
  blocking collectives  11.3 us (10%)
  local copies, waits for them, and re-layouts  2.99 us (3%)
    all_to_all x1, blocking collectives, body(): returned = lax.all_to_all(reaction, 'ka', 0, 0)  11.3 us
    all_to_all x1, starting transfers between devices, body(): table = lax.all_to_all(packed, 'ka', 0, 0)  8.48 us
    pallas_call x3, Pallas kernels, respond(): call(functools.partial(response_kernel, begin, count, started), outs, [vm...  7.03 us
    ppermute x6, starting transfers between devices, body(): lax.ppermute(summed, both, turn)  6.78 us
    ppermute x6, waiting for transfers between devices, body(): lax.ppermute(summed, both, turn)  5.32 us
    all_to_all x1, waiting for transfers between devices, body(): got = lax.all_to_all(send, 'ka', 0, 0)  5.02 us
    pallas_call x1, Pallas kernels, body(): call(message_kernel, [((ranks, 40, 128), f32), ((16, own), f32), ((3, slo...  4.9 us
    ppermute x1, waiting for transfers between devices, body(): from_right = lax.ppermute(send0, 'gx', shift('gx', -1))  4.34 us
  transfers between devices with their start and end apart: 19, of which 13 were waited for; matrix products, arithmetic and copies ran while one was open for 0% of the time, Pallas kernels for 18%

profile of v4, /device:TPU:14, one launch (start us, length us, event | category | flops | bytes accessed | tf_op | source)
XLA Modules:
  0.0 111.2 jit_solution(12033345283132713904)
XLA Ops:
  0.6 1.3 %shard_map.176 = (f32[8,8,128]{2,1,0:T(8,128)}, f32[3,256]{1,0:T(4,128)S(1)}, s32[1,256]{1,0:T(1,128)S(1)}) custom-call(f32[3,256]{1,0:T(4,128)} %place_far.1, s32[1,256]{1,0:T(1,128)} %bitcast.8), custom_call_target="tpu_custom_call" | custom-call | tf_op jit(solution)/shard_map/pallas_call | solution.py:793
  2.0 8.5 %all-to-all-start = ((f32[8,8,128]{2,1,0:T(8,128)}), f32[8,8,128]{2,1,0:T(8,128)S(1)}, u32[]{:S(2)}, u32[]{:S(2)}) async-start(f32[8,8,128]{2,1,0:T(8,128)} %get-tuple-element.53), calls=%async_computation | async-start | bytes 65536 | tf_op jit(solution)/shard_map/all_to_all | solution.py:799
  10.4 4.0 %shard_map.175 = (f32[8,256]{1,0:T(8,128)S(1)}, s32[64,256]{1,0:T(8,128)S(1)}, s32[1,256]{1,0:T(1,128)S(1)}, s32[2,2,128]{2,1,0:T(2,128)S(1)}, f32[8,24,128]{2,1...) custom-call(f32[3]{0:T(128)} %edges_far.1, ...), custom_call_target="tpu_custom_call" | custom-call | flops 4000000000 | bytes 16000000 | tf_op jit(solution)/shard_map/pallas_call | solution.py:800
  14.4 4.1 %all-to-all-done.table = f32[8,8,128]{2,1,0:T(8,128)S(1)} async-done(((f32[8,8,128]{2,1,0:T(8,128)}), f32[8,8,128]{2,1,0:T(8,128)S(1)}, u32[]{:S(2)}, u32[]{:S(2)}) %all-to-all-start) | async-done | bytes 32800 | tf_op jit(solution)/shard_map/all_to_all | solution.py:799
  18.7 3.2 %collective-permute-start.1 = (f32[8,128]{1,0:T(8,128)S(1)}, f32[8,128]{1,0:T(8,128)S(1)}, u32[]{:S(2)}, u32[]{:S(2)}) collective-permute-start(f32[8,128]{1,0:T(8,128)S(1)} %get-tuple-element.56.cell0), channel_id=1, source_target_pairs={{0,24},{8,0},{16,8},{24,16},{1,25},{9,1},{17,9},{25,17},{2,26},{10... | collective-permute-start | bytes 12296 | tf_op jit(solution)/shard_map/ppermute | solution.py:850
  21.9 1.7 %shard_map.177.after.near = f32[4,64,256]{2,1,0:T(8,128)S(1)} custom-call(f32[8,8,128]{2,1,0:T(8,128)S(1)} %all-to-all-done.table, s32[64,256]{1,0:T(8,128)S(1)} %get-tuple-element.52.listing), custom_call_target="tpu_custom_call" | custom-call | flops 1000000000 | bytes 4000000 | tf_op jit(solution)/shard_map/pallas_call | solution.py:851
  23.7 0.4 collective-permute-start.2
  24.1 1.7 %collective-permute-start.3 = (f32[16,128]{1,0:T(8,128)S(1)}, f32[16,128]{1,0:T(8,128)S(1)}, u32[]{:S(2)}, u32[]{:S(2)}) collective-permute-start(f32[16,128]{1,0:T(8,128)S(1)} %get-tuple-element.58), channel_id=1, source_target_pairs={{0,224},{32,0},{64,32},{96,64},{128,96},{160,128},{192,160},{224,1... | collective-permute-start | bytes 24584 | tf_op jit(solution)/shard_map/ppermute | solution.py:858
  25.8 1.3 %shard_map.180 = (bf16[144,2048]{1,0:T(8,128)(2,1)S(1)}, bf16[144,2048]{1,0:T(8,128)(2,1)S(1)}, f32[32,2048]{1,0:T(8,128)S(1)}) custom-call(s32[1]{0:T(128)} %bitcast.7.rank, f32[8,8,128]{2,1,0:T(8,128)S(1)} %all-to-all-done.table), custom_call_target="tpu_custom_call" | custom-call | flops 1000000000 | bytes 4000000 | tf_op jit(solution)/shard_map/pallas_call | solution.py:859
  27.0 0.4 collective-permute-done.2.left
  27.4 2.5 %collective-permute-done.3.right = f32[16,128]{1,0:T(8,128)S(1)} collective-permute-done((f32[16,128]{1,0:T(8,128)S(1)}, f32[16,128]{1,0:T(8,128)S(1)}, u32[]{:S(2)}, u32[]{:S(2)}) %collective-permute-start.3) | collective-permute-done | bytes 8224 | tf_op jit(solution)/shard_map/ppermute | solution.py:858
  29.9 4.9 %shard_map.181 = (f32[8,40,128]{2,1,0:T(8,128)}, f32[16,256]{1,0:T(8,128)S(1)}, f32[3,64,256]{2,1,0:T(8,128)S(1)}, f32[64,256]{1,0:T(8,128)S(1)}) custom-call(f32[8,256]{1,0:T(8,128)S(1)} %get-tuple-element.51.edges, s32[64,256]{1,0:T(8,128)S(1)} %get-tuple-element.52.listing, f32[4,64,256]{2,1,0:T(8,128)S(1)} %shard_map.177.after.near, ...), custom_call_target="tpu_custom_call" | custom-call | flops 4000000000 | bytes 16000000 | tf_op jit(solution)/shard_map/pallas_call | solution.py:866
  34.8 0.7 copy-done.2
  35.4 3.4 %all-to-all-start.1 = ((f32[8,40,128]{2,1,0:T(8,128)}), f32[8,40,128]{2,1,0:T(8,128)S(1)}, u32[]{:S(2)}, u32[]{:S(2)}) async-start(f32[8,40,128]{2,1,0:T(8,128)} %get-tuple-element.76), calls=%async_computation.1 | async-start | bytes 327680 | tf_op jit(solution)/shard_map/all_to_all | solution.py:885
  38.9 0.9 copy-done.3
  39.8 3.8 %shard_map.182 = (f32[9,32,256]{2,1,0:T(8,128)S(1)}, f32[8,128]{1,0:T(8,128)S(1)}, f32[384,256]{1,0:T(8,128)S(1)}) custom-call(f32[16,256]{1,0:T(8,128)S(1)} %get-tuple-element.67.refs_0_, f32[16,1]{1,0:T(8,128)S(1)} %get-tuple-element.68.refs_1_, f32[24,384]{1,0:T(8,128)S(1)} %get-tuple-element.64.ball.refs_2_, f32[3,64,256]{2,1,0:T(8,128)S(1)} %copy-done.3, ...), custom_call_target="tpu_custom_call" | custom-call | flops 2000000000 | bytes 8000000 | tf_op jit(solution)/shard_map/pallas_call | solution.py:894
  43.5 0.7 copy-done.6
  44.2 5.0 %all-to-all-done.1.got = f32[8,40,128]{2,1,0:T(8,128)S(1)} async-done(((f32[8,40,128]{2,1,0:T(8,128)}), f32[8,40,128]{2,1,0:T(8,128)S(1)}, u32[]{:S(2)}, u32[]{:S(2)}) %all-to-all-start.1) | async-done | bytes 163872 | tf_op jit(solution)/shard_map/all_to_all | solution.py:885
  49.3 2.0 %shard_map.185 = (f32[80,256]{1,0:T(8,128)S(1)}, f32[80,256]{1,0:T(8,128)S(1)}) custom-call(s32[1]{0:T(128)} %bitcast.5.core, f32[8,40,128]{2,1,0:T(8,128)S(1)} %all-to-all-done.1.got, f32[32,2048]{1,0:T(8,128)S(1)} %get-tuple-element.66.after.waves_x, bf16[144,2048]{1,0:T(8,128)(2,1)S(1)} %get-tuple-element.77.high, ...), custom_call_target="tpu_custom_call" | custom-call | flops 1500000000 | bytes 6000000 | tf_op jit(solution)/shard_map/pallas_call | solution.py:910
  51.3 0.6 collective-permute-start.4
  51.9 0.9 collective-permute-done.4
  52.9 2.0 %collective-permute-start.6 = (f32[80,256]{1,0:T(8,128)S(1)}, f32[80,256]{1,0:T(8,128)S(1)}, u32[]{:S(2)}, u32[]{:S(2)}) collective-permute-start(f32[80,256]{1,0:T(8,128)S(1)} %add.8.refs_0_), channel_id=1, source_target_pairs={{0,48},{8,56},{32,0},{40,8},{16,32},{24,40},{48,16},{56,24},{64,11... | collective-permute-start | bytes 245768 | tf_op jit(solution)/shard_map/ppermute | solution.py:932
  54.9 1.4 %collective-permute-start.7 = (f32[80,256]{1,0:T(8,128)S(1)}, f32[80,256]{1,0:T(8,128)S(1)}, u32[]{:S(2)}, u32[]{:S(2)}) collective-permute-start(f32[80,256]{1,0:T(8,128)S(1)} %add.8.refs_0_), channel_id=1, source_target_pairs={{0,16},{8,24},{32,48},{40,56},{16,0},{24,8},{48,32},{56,40},{64,80... | collective-permute-start | bytes 245768 | tf_op jit(solution)/shard_map/ppermute | solution.py:932
  56.3 1.6 %shard_map.184 = (f32[9,16,256]{2,1,0:T(8,128)S(1)}, f32[8,128]{1,0:T(8,128)S(1)}) custom-call(f32[384,256]{1,0:T(8,128)S(1)} %get-tuple-element.73.refs_0_, f32[3,64,256]{2,1,0:T(8,128)S(1)} %copy-done.4, f32[64,256]{1,0:T(8,128)S(1)} %get-tuple-element.70.refs_4_.refs_2_, bf16[512,192]{1,0:T(8,128)(2,1)S(1)} %get-tuple-element.63.first.refs_5_.refs_3_, ...), custom_call_target="tpu_custom_call" | custom-call | flops 1000000000 | bytes 4000000 | tf_op jit(solution)/shard_map/pallas_call | solution.py:894
  57.9 2.9 %collective-permute-done.7.refs_3_ = f32[80,256]{1,0:T(8,128)S(1)} collective-permute-done((f32[80,256]{1,0:T(8,128)S(1)}, f32[80,256]{1,0:T(8,128)S(1)}, u32[]{:S(2)}, u32[]{:S(2)}) %collective-permute-start.7) | collective-permute-done | bytes 81952 | tf_op jit(solution)/shard_map/ppermute | solution.py:932
  60.9 0.4 collective-permute-start.8
  61.2 1.7 %collective-permute-start.9 = (f32[80,256]{1,0:T(8,128)S(1)}, f32[80,256]{1,0:T(8,128)S(1)}, u32[]{:S(2)}, u32[]{:S(2)}) collective-permute-start(f32[80,256]{1,0:T(8,128)S(1)} %shard_map.186.refs_0_), channel_id=1, source_target_pairs={{0,192},{8,200},{32,224},{40,232},{16,208},{24,216},{48,240},{56,2... | collective-permute-start | bytes 245768 | tf_op jit(solution)/shard_map/ppermute | solution.py:932
  63.0 1.2 %collective-permute-start.10 = (f32[80,256]{1,0:T(8,128)S(1)}, f32[80,256]{1,0:T(8,128)S(1)}, u32[]{:S(2)}, u32[]{:S(2)}) collective-permute-start(f32[80,256]{1,0:T(8,128)S(1)} %shard_map.186.refs_0_), channel_id=1, source_target_pairs={{0,128},{8,136},{32,160},{40,168},{16,144},{24,152},{48,176},{56,1... | collective-permute-start | bytes 245768 | tf_op jit(solution)/shard_map/ppermute | solution.py:932
  64.2 1.6 %shard_map.183 = (f32[9,16,256]{2,1,0:T(8,128)S(1)}, f32[8,128]{1,0:T(8,128)S(1)}) custom-call(f32[384,256]{1,0:T(8,128)S(1)} %get-tuple-element.73.refs_0_, f32[3,64,256]{2,1,0:T(8,128)S(1)} %copy-done.4, f32[64,256]{1,0:T(8,128)S(1)} %get-tuple-element.70.refs_4_.refs_2_, bf16[512,192]{1,0:T(8,128)(2,1)S(1)} %get-tuple-element.63.first.refs_5_.refs_3_, ...), custom_call_target="tpu_custom_call" | custom-call | flops 1000000000 | bytes 4000000 | tf_op jit(solution)/shard_map/pallas_call | solution.py:894
  65.8 0.7 copy-done.8
  66.5 0.6 collective-permute-done.9.refs_2_
  67.1 1.8 %collective-permute-done.10.refs_3_ = f32[80,256]{1,0:T(8,128)S(1)} collective-permute-done((f32[80,256]{1,0:T(8,128)S(1)}, f32[80,256]{1,0:T(8,128)S(1)}, u32[]{:S(2)}, u32[]{:S(2)}) %collective-permute-start.10) | collective-permute-done | bytes 81952 | tf_op jit(solution)/shard_map/ppermute | solution.py:932
  69.0 0.6 shard_map.188
  69.6 0.7 collective-permute-done.11.other
  70.3 2.4 %shard_map.189 = (f32[8,8,256]{2,1,0:T(8,128)}, f32[144,256]{1,0:T(8,128)S(1)}) custom-call(s32[1]{0:T(128)} %bitcast.5.core, f32[80,256]{1,0:T(8,128)S(1)} %shard_map.187.mine, f32[80,256]{1,0:T(8,128)S(1)} %collective-permute-done.11.other, f32[3,72,128]{2,1,0:T(8,128)S(1)} %get-tuple-element.82.weights, f32[8,256]{1,0:T(8,128)S(1)} %get-tuple-element.83.lone_weights, ...), custom_call_target="tpu_custom_call" | custom-call | flops 1000000000 | bytes 4000000 | tf_op jit(solution)/shard_map/pallas_call | solution.py:940
  72.7 3.3 %all-to-all-start.2 = ((f32[8,8,256]{2,1,0:T(8,128)}), f32[8,8,256]{2,1,0:T(8,128)S(1)}, u32[]{:S(2)}, u32[]{:S(2)}) async-start(f32[8,8,256]{2,1,0:T(8,128)} %get-tuple-element.84), calls=%async_computation.2 | async-start | bytes 131072 | tf_op jit(solution)/shard_map/all_to_all | solution.py:951
  76.1 4.0 %shard_map.191.refs_0_ = f32[8,8,128]{2,1,0:T(8,128)S(1)} custom-call(s32[1]{0:T(128)} %bitcast.7.rank, s32[1]{0:T(128)} %bitcast.5.core, f32[8,256]{1,0:T(8,128)S(1)} %get-tuple-element.51.edges, f32[80,256]{1,0:T(8,128)S(1)} %shard_map.187.mine, f32[80,256]{1,0:T(8,128)S(1)} %collective-permute-done.11.other, f32[3,72,128]{2,1,0:T(8,128)S(1)} %get-tuple-element.82.weights, ...), custom_call_target="tpu_custom_call" | custom-call | flops 2500000000 | bytes 10000000 | tf_op jit(solution)/shard_map/pallas_call | solution.py:952
  80.2 4.2 %all-to-all-done.2.got = f32[8,8,256]{2,1,0:T(8,128)S(1)} async-done(((f32[8,8,256]{2,1,0:T(8,128)}), f32[8,8,256]{2,1,0:T(8,128)S(1)}, u32[]{:S(2)}, u32[]{:S(2)}) %all-to-all-start.2) | async-done | bytes 65568 | tf_op jit(solution)/shard_map/all_to_all | solution.py:951
  84.4 1.7 %shard_map.190 = (f32[16,128]{1,0:T(8,128)S(1)}, f32[16,128]{1,0:T(8,128)S(1)}, f32[8,128]{1,0:T(8,128)S(1)}, f32[8,128]{1,0:T(8,128)S(1)}) custom-call(f32[8,8,256]{2,1,0:T(8,128)S(1)} %all-to-all-done.2.got, f32[9,32,256]{2,1,0:T(8,128)S(1)} %copy-done.7, f32[9,16,256]{2,1,0:T(8,128)S(1)} %get-tuple-element.86.response1, f32[9,16,256]{2,1,0:T(8,128)S(1)} %copy-done.9, ...), custom_call_target="tpu_custom_call" | custom-call | flops 1000000000 | bytes 4000000 | tf_op jit(solution)/shard_map/pallas_call | solution.py:967
  86.1 0.4 collective-permute-start.12
  86.5 0.2 collective-permute-start.13
  86.7 1.7 %shard_map.192 = (f32[8,8,128]{2,1,0:T(8,128)S(1)}, f32[8,128]{1,0:T(8,128)S(1)}) custom-call(f32[8,8,256]{2,1,0:T(8,128)S(1)} %all-to-all-done.2.got, f32[9,32,256]{2,1,0:T(8,128)S(1)} %copy-done.7, f32[9,16,256]{2,1,0:T(8,128)S(1)} %get-tuple-element.86.response1, f32[9,16,256]{2,1,0:T(8,128)S(1)} %copy-done.9, f32[3,64,256]{2,1,0:T(8,128)S(1)} %copy-done.5, ...), custom_call_target="tpu_custom_call" | custom-call | flops 1000000000 | bytes 4000000 | tf_op jit(solution)/shard_map/pallas_call | solution.py:967
  88.4 2.6 %collective-permute-done.13.below = f32[16,128]{1,0:T(8,128)S(1)} collective-permute-done((f32[16,128]{1,0:T(8,128)S(1)}, f32[16,128]{1,0:T(8,128)S(1)}, u32[]{:S(2)}, u32[]{:S(2)}) %collective-permute-start.13) | collective-permute-done | bytes 8224 | tf_op jit(solution)/shard_map/ppermute | solution.py:985
  91.1 2.2 %collective-permute-start.14 = (f32[8,128]{1,0:T(8,128)S(1)}, f32[8,128]{1,0:T(8,128)S(1)}, u32[]{:S(2)}, u32[]{:S(2)}) collective-permute-start(f32[8,128]{1,0:T(8,128)S(1)} %get-tuple-element.96), channel_id=1, source_target_pairs={{0,32},{32,64},{64,96},{96,128},{128,160},{160,192},{192,224},{224... | collective-permute-start | bytes 12296 | tf_op jit(solution)/shard_map/ppermute | solution.py:990
  93.3 1.4 %collective-permute-done.14.from_left = f32[8,128]{1,0:T(8,128)S(1)} collective-permute-done((f32[8,128]{1,0:T(8,128)S(1)}, f32[8,128]{1,0:T(8,128)S(1)}, u32[]{:S(2)}, u32[]{:S(2)}) %collective-permute-start.14) | collective-permute-done | bytes 4128 | tf_op jit(solution)/shard_map/ppermute | solution.py:990
  94.7 4.3 %collective-permute-done.15.from_right = f32[8,128]{1,0:T(8,128)S(1)} collective-permute-done((f32[8,128]{1,0:T(8,128)S(1)}, f32[8,128]{1,0:T(8,128)S(1)}, u32[]{:S(2)}, u32[]{:S(2)}) %collective-permute-start.15) | collective-permute-done | bytes 4128 | tf_op jit(solution)/shard_map/ppermute | solution.py:989
  99.3 11.3 %all_to_all.20.got = f32[8,8,128]{2,1,0:T(8,128)S(1)} all-to-all(f32[8,8,128]{2,1,0:T(8,128)S(1)} %shard_map.194), channel_id=1, replica_groups=mesh['gx'=8,'gy'=4,'ka'=8] {'ka'}, dimensions={0} | all-to-all | bytes 65536 | tf_op jit(solution)/shard_map/all_to_all | solution.py:994
  110.6 0.6 shard_map.195
  (37 shorter events, 0.7 us)
Async XLA Ops:
  2.0 16.5 %all-to-all-start = ((f32[8,8,128]{2,1,0:T(8,128)}), f32[8,8,128]{2,1,0:T(8,128)S(1)}, u32[]{:S(2)}, u32[]{:S(2)}) async-start(f32[8,8,128]{2,1,0:T(8,128)} %get-tuple-element.53), calls=%async_computation | async-start | bytes 65536 | tf_op jit(solution)/shard_map/all_to_all | solution.py:799
  14.4 15.5 %copy-start.10 = (s32[64,256]{1,0:T(8,128)}, s32[64,256]{1,0:T(8,128)S(1)}, u32[]{:S(2)}) copy-start(s32[64,256]{1,0:T(8,128)S(1)} %get-tuple-element.52.listing) | copy-start | bytes 196612
  18.6 5.0 %collective-permute-start = (f32[8,128]{1,0:T(8,128)S(1)}, f32[8,128]{1,0:T(8,128)S(1)}, u32[]{:S(2)}, u32[]{:S(2)}) collective-permute-start(f32[8,128]{1,0:T(8,128)S(1)} %get-tuple-element.55.cell1), channel_id=1, source_target_pairs={{0,8},{8,16},{16,24},{24,0},{1,9},{9,17},{17,25},{25,1},{2,10},{10... | collective-permute-start | bytes 12296 | tf_op jit(solution)/shard_map/ppermute | solution.py:849
  18.7 4.9 %collective-permute-start.1 = (f32[8,128]{1,0:T(8,128)S(1)}, f32[8,128]{1,0:T(8,128)S(1)}, u32[]{:S(2)}, u32[]{:S(2)}) collective-permute-start(f32[8,128]{1,0:T(8,128)S(1)} %get-tuple-element.56.cell0), channel_id=1, source_target_pairs={{0,24},{8,0},{16,8},{24,16},{1,25},{9,1},{17,9},{25,17},{2,26},{10... | collective-permute-start | bytes 12296 | tf_op jit(solution)/shard_map/ppermute | solution.py:850
  23.7 3.7 %collective-permute-start.2 = (f32[16,128]{1,0:T(8,128)S(1)}, f32[16,128]{1,0:T(8,128)S(1)}, u32[]{:S(2)}, u32[]{:S(2)}) collective-permute-start(f32[16,128]{1,0:T(8,128)S(1)} %get-tuple-element.57), channel_id=1, source_target_pairs={{0,32},{32,64},{64,96},{96,128},{128,160},{160,192},{192,224},{224... | collective-permute-start | bytes 24584 | tf_op jit(solution)/shard_map/ppermute | solution.py:857
  24.1 5.8 %collective-permute-start.3 = (f32[16,128]{1,0:T(8,128)S(1)}, f32[16,128]{1,0:T(8,128)S(1)}, u32[]{:S(2)}, u32[]{:S(2)}) collective-permute-start(f32[16,128]{1,0:T(8,128)S(1)} %get-tuple-element.58), channel_id=1, source_target_pairs={{0,224},{32,0},{64,32},{96,64},{128,96},{160,128},{192,160},{224,1... | collective-permute-start | bytes 24584 | tf_op jit(solution)/shard_map/ppermute | solution.py:858
  34.8 0.7 copy-start.2
  35.4 13.8 %all-to-all-start.1 = ((f32[8,40,128]{2,1,0:T(8,128)}), f32[8,40,128]{2,1,0:T(8,128)S(1)}, u32[]{:S(2)}, u32[]{:S(2)}) async-start(f32[8,40,128]{2,1,0:T(8,128)} %get-tuple-element.76), calls=%async_computation.1 | async-start | bytes 327680 | tf_op jit(solution)/shard_map/all_to_all | solution.py:885
  38.8 0.9 copy-start.3
  43.5 0.7 copy-start.6
  51.3 5.0 %copy-start.4 = (f32[3,64,256]{2,1,0:T(8,128)S(1)}, f32[3,64,256]{2,1,0:T(8,128)}, u32[]{:S(2)}) copy-start(f32[3,64,256]{2,1,0:T(8,128)} %copy-done.2) | copy-start | bytes 589828
  51.3 1.5 %collective-permute-start.4 = (f32[80,256]{1,0:T(8,128)S(1)}, f32[80,256]{1,0:T(8,128)S(1)}, u32[]{:S(2)}, u32[]{:S(2)}) collective-permute-start(f32[80,256]{1,0:T(8,128)S(1)} %get-tuple-element.81), channel_id=1, source_target_pairs={{0,8},{8,0},{32,40},{40,32},{16,24},{24,16},{48,56},{56,48},{64,72... | collective-permute-start | bytes 245768 | tf_op jit(solution)/shard_map/ppermute | solution.py:930
  52.8 5.1 %collective-permute-start.5 = (f32[80,256]{1,0:T(8,128)S(1)}, f32[80,256]{1,0:T(8,128)S(1)}, u32[]{:S(2)}, u32[]{:S(2)}) collective-permute-start(f32[80,256]{1,0:T(8,128)S(1)} %add.8.refs_0_), channel_id=1, source_target_pairs={{0,32},{8,40},{32,16},{40,24},{16,48},{24,56},{48,0},{56,8},{64,96... | collective-permute-start | bytes 245768 | tf_op jit(solution)/shard_map/ppermute | solution.py:932
  52.9 5.0 %collective-permute-start.6 = (f32[80,256]{1,0:T(8,128)S(1)}, f32[80,256]{1,0:T(8,128)S(1)}, u32[]{:S(2)}, u32[]{:S(2)}) collective-permute-start(f32[80,256]{1,0:T(8,128)S(1)} %add.8.refs_0_), channel_id=1, source_target_pairs={{0,48},{8,56},{32,0},{40,8},{16,32},{24,40},{48,16},{56,24},{64,11... | collective-permute-start | bytes 245768 | tf_op jit(solution)/shard_map/ppermute | solution.py:932
  54.9 5.9 %collective-permute-start.7 = (f32[80,256]{1,0:T(8,128)S(1)}, f32[80,256]{1,0:T(8,128)S(1)}, u32[]{:S(2)}, u32[]{:S(2)}) collective-permute-start(f32[80,256]{1,0:T(8,128)S(1)} %add.8.refs_0_), channel_id=1, source_target_pairs={{0,16},{8,24},{32,48},{40,56},{16,0},{24,8},{48,32},{56,40},{64,80... | collective-permute-start | bytes 245768 | tf_op jit(solution)/shard_map/ppermute | solution.py:932
  60.9 5.6 %collective-permute-start.8 = (f32[80,256]{1,0:T(8,128)S(1)}, f32[80,256]{1,0:T(8,128)S(1)}, u32[]{:S(2)}, u32[]{:S(2)}) collective-permute-start(f32[80,256]{1,0:T(8,128)S(1)} %shard_map.186.refs_0_), channel_id=1, source_target_pairs={{0,64},{8,72},{32,96},{40,104},{16,80},{24,88},{48,112},{56,120},{... | collective-permute-start | bytes 245768 | tf_op jit(solution)/shard_map/ppermute | solution.py:932
  61.2 5.9 %collective-permute-start.9 = (f32[80,256]{1,0:T(8,128)S(1)}, f32[80,256]{1,0:T(8,128)S(1)}, u32[]{:S(2)}, u32[]{:S(2)}) collective-permute-start(f32[80,256]{1,0:T(8,128)S(1)} %shard_map.186.refs_0_), channel_id=1, source_target_pairs={{0,192},{8,200},{32,224},{40,232},{16,208},{24,216},{48,240},{56,2... | collective-permute-start | bytes 245768 | tf_op jit(solution)/shard_map/ppermute | solution.py:932
  63.0 5.9 %collective-permute-start.10 = (f32[80,256]{1,0:T(8,128)S(1)}, f32[80,256]{1,0:T(8,128)S(1)}, u32[]{:S(2)}, u32[]{:S(2)}) collective-permute-start(f32[80,256]{1,0:T(8,128)S(1)} %shard_map.186.refs_0_), channel_id=1, source_target_pairs={{0,128},{8,136},{32,160},{40,168},{16,144},{24,152},{48,176},{56,1... | collective-permute-start | bytes 245768 | tf_op jit(solution)/shard_map/ppermute | solution.py:932
  65.8 0.7 copy-start.8
  68.9 1.4 %collective-permute-start.11 = (f32[80,256]{1,0:T(8,128)S(1)}, f32[80,256]{1,0:T(8,128)S(1)}, u32[]{:S(2)}, u32[]{:S(2)}) collective-permute-start(f32[80,256]{1,0:T(8,128)S(1)} %shard_map.187.mine), channel_id=1, source_target_pairs={{0,8},{8,0},{32,40},{40,32},{16,24},{24,16},{48,56},{56,48},{64,72... | collective-permute-start | bytes 245768 | tf_op jit(solution)/shard_map/ppermute | solution.py:933
  72.7 11.7 %all-to-all-start.2 = ((f32[8,8,256]{2,1,0:T(8,128)}), f32[8,8,256]{2,1,0:T(8,128)S(1)}, u32[]{:S(2)}, u32[]{:S(2)}) async-start(f32[8,8,256]{2,1,0:T(8,128)} %get-tuple-element.84), calls=%async_computation.2 | async-start | bytes 131072 | tf_op jit(solution)/shard_map/all_to_all | solution.py:951
  76.1 8.3 %copy-start.5 = (f32[3,64,256]{2,1,0:T(8,128)S(1)}, f32[3,64,256]{2,1,0:T(8,128)}, u32[]{:S(2)}) copy-start(f32[3,64,256]{2,1,0:T(8,128)} %copy-done.2) | copy-start | bytes 589828
  76.1 8.3 %copy-start.7 = (f32[9,32,256]{2,1,0:T(8,128)S(1)}, f32[9,32,256]{2,1,0:T(8,128)}, u32[]{:S(2)}) copy-start(f32[9,32,256]{2,1,0:T(8,128)} %copy-done.6) | copy-start | bytes 884740
  76.1 8.3 %copy-start.9 = (f32[9,16,256]{2,1,0:T(8,128)S(1)}, f32[9,16,256]{2,1,0:T(8,128)}, u32[]{:S(2)}) copy-start(f32[9,16,256]{2,1,0:T(8,128)} %copy-done.8) | copy-start | bytes 442372
  76.1 8.3 %copy-start.11 = (s32[64,256]{1,0:T(8,128)S(1)}, s32[64,256]{1,0:T(8,128)}, u32[]{:S(2)}) copy-start(s32[64,256]{1,0:T(8,128)} %copy-done.10) | copy-start | bytes 196612
  86.1 2.3 %collective-permute-start.12 = (f32[16,128]{1,0:T(8,128)S(1)}, f32[16,128]{1,0:T(8,128)S(1)}, u32[]{:S(2)}, u32[]{:S(2)}) collective-permute-start(f32[16,128]{1,0:T(8,128)S(1)} %get-tuple-element.88), channel_id=1, source_target_pairs={{0,24},{8,0},{16,8},{24,16},{1,25},{9,1},{17,9},{25,17},{2,26},{10... | collective-permute-start | bytes 24584 | tf_op jit(solution)/shard_map/ppermute | solution.py:984
  86.5 4.6 %collective-permute-start.13 = (f32[16,128]{1,0:T(8,128)S(1)}, f32[16,128]{1,0:T(8,128)S(1)}, u32[]{:S(2)}, u32[]{:S(2)}) collective-permute-start(f32[16,128]{1,0:T(8,128)S(1)} %get-tuple-element.89), channel_id=1, source_target_pairs={{0,8},{8,16},{16,24},{24,0},{1,9},{9,17},{17,25},{25,1},{2,10},{10... | collective-permute-start | bytes 24584 | tf_op jit(solution)/shard_map/ppermute | solution.py:985
  86.7 23.8 %copy-start = (f32[3,256]{1,0:T(4,128)S(1)}, f32[3,256]{1,0:T(4,128)}, u32[]{:S(2)}) copy-start(f32[3,256]{1,0:T(4,128)} %speed.1) | copy-start | bytes 9220
  86.7 23.8 %copy-start.1 = (f32[3,256]{1,0:T(4,128)S(1)}, f32[3,256]{1,0:T(4,128)}, u32[]{:S(2)}) copy-start(f32[3,256]{1,0:T(4,128)} %kicks.1) | copy-start | bytes 9220
  91.1 3.6 %collective-permute-start.14 = (f32[8,128]{1,0:T(8,128)S(1)}, f32[8,128]{1,0:T(8,128)S(1)}, u32[]{:S(2)}, u32[]{:S(2)}) collective-permute-start(f32[8,128]{1,0:T(8,128)S(1)} %get-tuple-element.96), channel_id=1, source_target_pairs={{0,32},{32,64},{64,96},{96,128},{128,160},{160,192},{192,224},{224... | collective-permute-start | bytes 12296 | tf_op jit(solution)/shard_map/ppermute | solution.py:990
  93.3 5.7 %collective-permute-start.15 = (f32[8,128]{1,0:T(8,128)S(1)}, f32[8,128]{1,0:T(8,128)S(1)}, u32[]{:S(2)}, u32[]{:S(2)}) collective-permute-start(f32[8,128]{1,0:T(8,128)S(1)} %get-tuple-element.97), channel_id=1, source_target_pairs={{0,224},{32,0},{64,32},{96,64},{128,96},{160,128},{192,160},{224,1... | collective-permute-start | bytes 12296 | tf_op jit(solution)/shard_map/ppermute | solution.py:989

commit v5 on v4

--- a/solution.py
+++ b/solution.py
@@ -171,8 +171,8 @@
 def prepare_kernel(
     edges_far, listing_far, tally_far, rows_far, triples_far, initial_far, second_far, embed_far,
     blend_far, energy_far, project_far, final_far,
-    edges_out, listing, tally, rows, counts, first, mixed_high, mixed_low, ball, base, final_out,
-    triples, initial, second, embed, blend, heads, final, edges, wide, done,
+    edges_out, listing, tally, rows, counts, first, mixed, ball, base, final_out, triples, initial,
+    second, embed, blend, heads, final, edges, done,
 ):
     embed[...] = jnp.zeros_like(embed)
     far = (
@@ -202,22 +202,14 @@
     base[...] = dot_h(heads[...], embed[...])
     doubled = jnp.concatenate([second[...], second[...]], axis=0)
     left = lax.broadcasted_iota(i32, (24, 128), 1) < hidden
-    slot = lax.broadcasted_iota(i32, (8, 128), 0)
-    group = lax.shift_right_logical(lax.broadcasted_iota(i32, (8, 128), 1), 6)
     responses = []
     for s in range(kinds):
         response = dot_h(through * embed[s : s + 1, :], doubled) * (1.0 / slots)
         responses.append(response)
-        for l in range(8):
-            line = jnp.broadcast_to(response[l : l + 1, :], (8, 128))
-            for t in range(4):
-                at = (l * kinds + s) * 8
-                wide[at : at + 8, t * 128 : (t + 1) * 128] = jnp.where(
-                    group + 2 * t == slot, line, 0.0
-                )
     for t in range(kinds // 2):
         ball[:, t * 128 : (t + 1) * 128] = jnp.where(left, responses[2 * t], responses[2 * t + 1])
-    mixed_high[...], mixed_low[...] = split(wide[...])
+    high, low = split(jnp.concatenate([r[0:8, 0:hidden] for r in responses], axis=0))
+    mixed[0:48, :], mixed[48:96, :] = high, low
     square = (16, 16)
     same = lax.broadcasted_iota(i32, square, 0) == lax.broadcasted_iota(i32, square, 1)
     final_out[...] = jnp.sum(
@@ -347,7 +339,7 @@
             for n in range(hidden // 8):
                 pooled[s * hidden + n * 8 : s * hidden + n * 8 + 8, :] = total[n]
 
-    paired(chunks, part, (actives,))
+    paired(chunks, part, (actives,), 8)
     answers = dot3(ball[...], pooled[...])
     for s in range(kinds):
         answers = answers + base[:, s : s + 1] * jnp.where(kind[...] == s, 1.0, 0.0)
@@ -366,28 +358,27 @@
     upstream[...] = dot_c(ball[8:24, :], ramp)
 
 
-def paired(count, part, scratch):
-    def step(pair, carry):
-        for p in range(2):
-            part(pair * 2 + p, *[ref.at[p] for ref in scratch])
+def paired(count, part, scratch, width=2):
+    def step(group, carry):
+        for p in range(width):
+            part(group * width + p, *[ref.at[p] for ref in scratch])
         return carry
 
-    lax.fori_loop(0, count // 2, step, 0)
+    lax.fori_loop(0, count // width, step, 0)
 
 
 def response_kernel(begin, count, first_part, *refs):
     if first_part:
-        activation, final, ball, disp, marks, first, mixed_high, mixed_low = refs[:8]
-        out, token, upstream = refs[8:11]
+        activation, final, ball, disp, marks, first, mixed = refs[:7]
+        out, site, token, upstream = refs[7:11]
         response_start(activation, final, ball, upstream)
     else:
-        upstream, disp, marks, first, mixed_high, mixed_low, out, token = refs[:8]
+        upstream, disp, marks, first, mixed, out, site, token = refs[:8]
     token[...] = jnp.zeros_like(token)
     bends, uppers, lowers = refs[-3:]
 
     def part(j, bend, upper, lower):
         at = pl.ds(pl.multiple_of((j + begin) * chunk, chunk), chunk)
-        to = pl.ds(pl.multiple_of(j * chunk, chunk), chunk)
         mark = marks[at, :]
         squared = disp[0, at, :] * disp[0, at, :]
         squared = squared + disp[1, at, :] * disp[1, at, :] + disp[2, at, :] * disp[2, at, :]
@@ -403,18 +394,16 @@
             * dot_n(first[...], jnp.concatenate([bh, bl, bh], axis=0))
         )
         upper[...], lower[...] = split(bend[...])
-        mixed = dot_n(mixed_high[...], upper[...]) + (
-            dot_n(mixed_low[...], upper[...]) + dot_n(mixed_high[...], lower[...])
-        )
-        for l in range(8):
-            total = jnp.zeros((chunk, own), f32)
-            for s in range(kinds):
-                row = (l * kinds + s) * 8
-                total = jnp.where(mark == float(s), mixed[row : row + 8, :], total)
-            out[l, to, :] = total
         for m in range(chunk):
             mine = jnp.broadcast_to(mark[m : m + 1, :], (8, own))
             hits = [mine == float(s) for s in range(kinds)]
+            lines = slice(m * hidden, (m + 1) * hidden)
+            wide = dot_n(mixed[...], upper[lines, :])
+            wide = wide[0:48] + (wide[48:96] + dot_n(mixed[0:48, :], lower[lines, :]))
+            total = jnp.zeros((8, own), f32)
+            for s in range(kinds):
+                total = jnp.where(hits[s], wide[s * 8 : s * 8 + 8], total)
+            out[j * chunk + m] = total
             total = jnp.zeros((8, own), f32)
             for n in range(0, hidden, 8):
                 chosen = jnp.zeros((8, own), f32)
@@ -423,7 +412,7 @@
                     chosen = jnp.where(hits[s], upstream[row : row + 8, :], chosen)
                 total = total + chosen * bend[m * hidden + n : m * hidden + n + 8, :]
             line = jnp.sum(total, axis=0, keepdims=True)
-            out[8, pl.ds(j * chunk + m, 1), :] = line
+            site[pl.ds(j * chunk + m, 1), :] = line
 
     paired(count, part, (bends, uppers, lowers))
 
@@ -453,7 +442,7 @@
             dot_t(lower, plane_high) + dot_t(upper, plane_low)
         )
 
-    paired(ranks, part, (lefts_high, lefts_low))
+    paired(ranks, part, (lefts_high, lefts_low), 8)
     first = core[0] == 0
     real, imaginary = total[0:plane_rows, :], total[plane_rows:waves, :]
     begin, rest = extra[:, 0:128], extra[:, 128:256]
@@ -549,7 +538,7 @@
             total = total + waves_x[f : f + 1, at] * result[f * 8 : f * 8 + 8, :]
         potential[z] = total
 
-    paired(ranks, part, (results,))
+    paired(ranks, part, (results,), 8)
 
 
 def gradient_kernel(
@@ -607,7 +596,7 @@
     paired(ranks, part, (results,))
 
 
-def pair_kernel(ghosts, got, response0, response1, response2, disp, listing, *refs):
+def pair_kernel(ghosts, got, r0, e0, r1, e1, r2, e2, disp, listing, *refs):
     potential = got[0]
     for z in range(1, ranks):
         potential = potential + got[z]
@@ -617,12 +606,14 @@
     row_high = lax.broadcasted_iota(i32, (16, own), 0) + (16 if ghosts else 0)
     row_low = lax.broadcasted_iota(i32, (128, own), 0)
 
-    def part(response, begin, j, left, right):
+    def part(response, site, begin, j, left, right):
         to = pl.ds(pl.multiple_of(j * chunk, chunk), chunk)
         at = pl.ds(pl.multiple_of((j + begin) * chunk, chunk), chunk)
-        radial = response[8, to, :]
-        for l in range(8):
-            radial = radial + potential[l : l + 1, :] * response[l, to, :]
+        lines = [
+            jnp.sum(potential * response[j * chunk + m], axis=0, keepdims=True)
+            for m in range(chunk)
+        ]
+        radial = site[to, :] + jnp.concatenate(lines, axis=0)
         pulls = [radial * disp[d, at, :] for d in range(3)]
         index = listing[at, :]
         low, high = index & 127, lax.shift_right_logical(index, 7)
@@ -646,9 +637,9 @@
         total[...] += dot_t(left[...], right[...])
 
     begin = 0
-    for response in (response0, response1, response2):
-        count = response.shape[1] // chunk
-        paired(count, functools.partial(part, response, begin), (lefts, rights))
+    for response, site in ((r0, e0), (r1, e1), (r2, e2)):
+        count = response.shape[0] // chunk
+        paired(count, functools.partial(part, response, site, begin), (lefts, rights), count)
         begin += count
     scattered = total[0:48, :] + total[48:96, :]
     if ghosts:
@@ -797,7 +788,7 @@
         [pltpu.SemaphoreType.DMA((2,))],
     )(stay(fractional_placements), stay(element_kinds.reshape(1, own)))
     table = lax.all_to_all(packed, "ka", 0, 0)
-    edges, listing, tally, rows, counts, first, mixed_high, mixed_low, ball, base, final = call(
+    edges, listing, tally, rows, counts, first, mixed, ball, base, final = call(
         prepare_kernel,
         [
             ((8, own), f32),
@@ -806,8 +797,7 @@
             ((2, 2, 128), i32),
             ((ranks, 24, 128), f32),
             ((chunk * hidden, 192), bf16),
-            ((8 * 8 * kinds, chunk * hidden), bf16),
-            ((8 * 8 * kinds, chunk * hidden), bf16),
+            ((2 * 8 * kinds, hidden), bf16),
             ((24, kinds * hidden), f32),
             ((24, 8), f32),
             ((16, 1), f32),
@@ -822,7 +812,6 @@
             pltpu.VMEM((24, 128), f32),
             pltpu.VMEM((1, 16), f32),
             pltpu.SMEM((3,), f32),
-            pltpu.VMEM((8 * 8 * kinds, chunk * hidden), f32),
             pltpu.SemaphoreType.DMA((12,)),
         ],
         cost=work(8),
@@ -875,7 +864,7 @@
         [
             pltpu.VMEM((64, 128), f32),
             pltpu.VMEM((kinds * hidden, own), f32),
-            pltpu.VMEM((2, chunk * hidden, own), f32),
+            pltpu.VMEM((8, chunk * hidden, own), f32),
         ],
         cost=work(8),
     )(
@@ -883,13 +872,11 @@
         ball, base, waves_x,
     )
     got = lax.all_to_all(send, "ka", 0, 0)
-    ready = (disp, marks, first) + tuple(
-        pltpu.with_memory_space_constraint(part, pltpu.VMEM) for part in (mixed_high, mixed_low)
-    )
+    ready = (disp, marks, first, mixed)
 
     def respond(begin, count, operands):
         started = begin == 0
-        outs = [((9, count * chunk, own), f32), ((8, 128), f32)]
+        outs = [((count * chunk, 8, own), f32), ((count * chunk, own), f32), ((8, 128), f32)]
         outs += [((kinds * hidden, own), f32)] * started
         return call(
             functools.partial(response_kernel, begin, count, started),
@@ -903,9 +890,9 @@
             cost=work(count),
         )(*operands)
 
-    response0, token0, upstream = respond(0, 4, (activation, final, ball) + ready)
-    response1, token1 = respond(4, 2, (upstream,) + ready)
-    response2, token2 = respond(6, 2, (upstream,) + ready)
+    *response0, token0, upstream = respond(0, 4, (activation, final, ball) + ready)
+    *response1, token1 = respond(4, 2, (upstream,) + ready)
+    *response2, token2 = respond(6, 2, (upstream,) + ready)
 
     mine, other = call(
         structure_kernel,
@@ -914,8 +901,8 @@
         [
             pltpu.VMEM((waves, own), f32),
             pltpu.VMEM((8, own), f32),
-            pltpu.VMEM((2, own, own), bf16),
-            pltpu.VMEM((2, own, own), bf16),
+            pltpu.VMEM((8, own, own), bf16),
+            pltpu.VMEM((8, own, own), bf16),
         ],
         cost=work(3),
     )(core, got, waves_x, high, low, token0)
@@ -944,7 +931,7 @@
         [
             pltpu.VMEM((272, own), bf16),
             pltpu.VMEM((272, own), bf16),
-            pltpu.VMEM((2, 272, own), f32),
+            pltpu.VMEM((8, 272, own), f32),
         ],
         cost=work(2),
     )(core, summed, opposite, weights, lone_weights, waves_x, high, low)
@@ -957,11 +944,11 @@
             pltpu.VMEM((waves, 896), f32),
             pltpu.VMEM((896, own), bf16),
             pltpu.VMEM((896, own), bf16),
-            pltpu.VMEM((2, 784, own), f32),
+            pltpu.VMEM((8, 784, own), f32),
         ],
         cost=work(5),
     )(rank, core, edges, summed, opposite, weights, spectrum, got, waves_x, high, low)[0]
-    pairs = (shares, response0, response1, response2, disp, listing)
+    pairs = (shares, *response0, *response1, *response2, disp, listing)
 
     def pull(ghosts, outs, operands):
         return call(
@@ -969,8 +956,8 @@
             outs,
             [vmem] * len(operands),
             [
-                pltpu.VMEM((2, 96, chunk * own), bf16),
-                pltpu.VMEM((2, 128, chunk * own), bf16),
+                pltpu.VMEM((4, 96, chunk * own), bf16),
+                pltpu.VMEM((4, 128, chunk * own), bf16),
                 pltpu.VMEM((96, 128), f32),
                 pltpu.VMEM((3, chunk, own), f32),
             ],

time: 112 us -> 109 us (0.973)
  waiting for transfers between devices: 31.4 us -> 35.9 us
  Pallas kernels: 33.6 us -> 29.6 us
  local copies, waits for them, and re-layouts: 2.99 us -> 0.01 us
    unnamed x24 -> x4, local copies, waits for them, and re-layouts: 2.99 us -> 0.01 us
    all_to_all x1, waiting for transfers between devices: 5.02 us -> 7.52 us  [body(): got = lax.all_to_all(send, 'ka', 0, 0)]
    pallas_call x3, Pallas kernels: 7.03 us -> 5.2 us  [respond(): call(functools.partial(response_kernel, begin, count, started), outs, [vm...]
    ppermute x6, waiting for transfers between devices: 5.32 us -> 7 us  [body(): lax.ppermute(summed, both, turn)]
  transfers between devices with their start and end apart: 19 -> 19, of which waited for: 13 -> 16; matrix products, arithmetic and copies ran while one was open for 0% -> 0% of each run, Pallas kernels for 18% -> 17%
where the time goes in v5:
time: 109 us
  waiting for transfers between devices  35.9 us (33%)
  starting transfers between devices  31.3 us (29%)
  Pallas kernels  29.6 us (27%)
  blocking collectives  11 us (10%)
    all_to_all x1, blocking collectives, body(): returned = lax.all_to_all(reaction, 'ka', 0, 0)  11 us
    all_to_all x1, starting transfers between devices, body(): table = lax.all_to_all(packed, 'ka', 0, 0)  8.48 us
    all_to_all x1, waiting for transfers between devices, body(): got = lax.all_to_all(send, 'ka', 0, 0)  7.52 us
    ppermute x6, waiting for transfers between devices, body(): lax.ppermute(summed, both, turn)  7 us
    ppermute x6, starting transfers between devices, body(): lax.ppermute(summed, both, turn)  6.77 us
    pallas_call x3, Pallas kernels, respond(): call(functools.partial(response_kernel, begin, count, started), outs, [vm...  5.2 us
    ppermute x1, waiting for transfers between devices, body(): from_right = lax.ppermute(send0, 'gx', shift('gx', -1))  4.39 us
    all_to_all x1, waiting for transfers between devices, body(): shares = lax.all_to_all(potential, 'ka', 0, 0)  4.27 us
  transfers between devices with their start and end apart: 19, of which 16 were waited for; matrix products, arithmetic and copies ran while one was open for 0% of the time, Pallas kernels for 17%

profile of v5, /device:TPU:14, one launch (start us, length us, event | category | flops | bytes accessed | tf_op | source)
XLA Modules:
  0.0 108.7 jit_solution(12405905340334293912)
XLA Ops:
  0.6 1.3 %shard_map.176 = (f32[8,8,128]{2,1,0:T(8,128)}, f32[3,256]{1,0:T(4,128)S(1)}, s32[1,256]{1,0:T(1,128)S(1)}) custom-call(f32[3,256]{1,0:T(4,128)} %place_far.1, s32[1,256]{1,0:T(1,128)} %bitcast.8), custom_call_target="tpu_custom_call" | custom-call | tf_op jit(solution)/shard_map/pallas_call | solution.py:784
  2.0 8.5 %all-to-all-start = ((f32[8,8,128]{2,1,0:T(8,128)}), f32[8,8,128]{2,1,0:T(8,128)S(1)}, u32[]{:S(2)}, u32[]{:S(2)}) async-start(f32[8,8,128]{2,1,0:T(8,128)} %get-tuple-element.55), calls=%async_computation | async-start | bytes 65536 | tf_op jit(solution)/shard_map/all_to_all | solution.py:790
  10.4 3.9 %shard_map.175 = (f32[8,256]{1,0:T(8,128)S(1)}, s32[64,256]{1,0:T(8,128)S(1)}, s32[1,256]{1,0:T(1,128)S(1)}, s32[2,2,128]{2,1,0:T(2,128)S(1)}, f32[8,24,128]{2,1...) custom-call(f32[3]{0:T(128)} %edges_far.1, ...), custom_call_target="tpu_custom_call" | custom-call | flops 4000000000 | bytes 16000000 | tf_op jit(solution)/shard_map/pallas_call | solution.py:791
  14.4 4.1 %all-to-all-done.table = f32[8,8,128]{2,1,0:T(8,128)S(1)} async-done(((f32[8,8,128]{2,1,0:T(8,128)}), f32[8,8,128]{2,1,0:T(8,128)S(1)}, u32[]{:S(2)}, u32[]{:S(2)}) %all-to-all-start) | async-done | bytes 32800 | tf_op jit(solution)/shard_map/all_to_all | solution.py:790
  18.7 3.2 %collective-permute-start.1 = (f32[8,128]{1,0:T(8,128)S(1)}, f32[8,128]{1,0:T(8,128)S(1)}, u32[]{:S(2)}, u32[]{:S(2)}) collective-permute-start(f32[8,128]{1,0:T(8,128)S(1)} %get-tuple-element.58.cell0), channel_id=1, source_target_pairs={{0,24},{8,0},{16,8},{24,16},{1,25},{9,1},{17,9},{25,17},{2,26},{10... | collective-permute-start | bytes 12296 | tf_op jit(solution)/shard_map/ppermute | solution.py:839
  21.9 1.7 %shard_map.177.after.near = f32[4,64,256]{2,1,0:T(8,128)S(1)} custom-call(f32[8,8,128]{2,1,0:T(8,128)S(1)} %all-to-all-done.table, s32[64,256]{1,0:T(8,128)S(1)} %get-tuple-element.54.listing), custom_call_target="tpu_custom_call" | custom-call | flops 1000000000 | bytes 4000000 | tf_op jit(solution)/shard_map/pallas_call | solution.py:840
  23.7 0.4 collective-permute-start.2
  24.1 1.7 %collective-permute-start.3 = (f32[16,128]{1,0:T(8,128)S(1)}, f32[16,128]{1,0:T(8,128)S(1)}, u32[]{:S(2)}, u32[]{:S(2)}) collective-permute-start(f32[16,128]{1,0:T(8,128)S(1)} %get-tuple-element.60), channel_id=1, source_target_pairs={{0,224},{32,0},{64,32},{96,64},{128,96},{160,128},{192,160},{224,1... | collective-permute-start | bytes 24584 | tf_op jit(solution)/shard_map/ppermute | solution.py:847
  25.8 1.3 %shard_map.180 = (bf16[144,2048]{1,0:T(8,128)(2,1)S(1)}, bf16[144,2048]{1,0:T(8,128)(2,1)S(1)}, f32[32,2048]{1,0:T(8,128)S(1)}) custom-call(s32[1]{0:T(128)} %bitcast.7.rank, f32[8,8,128]{2,1,0:T(8,128)S(1)} %all-to-all-done.table), custom_call_target="tpu_custom_call" | custom-call | flops 1000000000 | bytes 4000000 | tf_op jit(solution)/shard_map/pallas_call | solution.py:848
  27.0 0.4 collective-permute-done.2.left
  27.4 2.5 %collective-permute-done.3.right = f32[16,128]{1,0:T(8,128)S(1)} collective-permute-done((f32[16,128]{1,0:T(8,128)S(1)}, f32[16,128]{1,0:T(8,128)S(1)}, u32[]{:S(2)}, u32[]{:S(2)}) %collective-permute-start.3) | collective-permute-done | bytes 8224 | tf_op jit(solution)/shard_map/ppermute | solution.py:847
  29.9 4.2 %shard_map.181 = (f32[8,40,128]{2,1,0:T(8,128)}, f32[16,256]{1,0:T(8,128)S(1)}, f32[3,64,256]{2,1,0:T(8,128)S(1)}, f32[64,256]{1,0:T(8,128)S(1)}) custom-call(f32[8,256]{1,0:T(8,128)S(1)} %get-tuple-element.53.edges, s32[64,256]{1,0:T(8,128)S(1)} %get-tuple-element.54.listing, f32[4,64,256]{2,1,0:T(8,128)S(1)} %shard_map.177.after.near, ...), custom_call_target="tpu_custom_call" | custom-call | flops 4000000000 | bytes 16000000 | tf_op jit(solution)/shard_map/pallas_call | solution.py:855
  34.1 3.4 %all-to-all-start.1 = ((f32[8,40,128]{2,1,0:T(8,128)}), f32[8,40,128]{2,1,0:T(8,128)S(1)}, u32[]{:S(2)}, u32[]{:S(2)}) async-start(f32[8,40,128]{2,1,0:T(8,128)} %get-tuple-element.77), calls=%async_computation.1 | async-start | bytes 327680 | tf_op jit(solution)/shard_map/all_to_all | solution.py:874
  37.5 2.9 %shard_map.182 = (f32[32,8,256]{2,1,0:T(8,128)S(1)}, f32[32,256]{1,0:T(8,128)S(1)}, f32[8,128]{1,0:T(8,128)S(1)}, f32[384,256]{1,0:T(8,128)S(1)}) custom-call(f32[16,256]{1,0:T(8,128)S(1)} %get-tuple-element.69.refs_0_, f32[16,1]{1,0:T(8,128)S(1)} %get-tuple-element.70.refs_1_, f32[24,384]{1,0:T(8,128)S(1)} %get-tuple-element.66.ball.refs_2_, ...), custom_call_target="tpu_custom_call" | custom-call | flops 2000000000 | bytes 8000000 | tf_op jit(solution)/shard_map/pallas_call | solution.py:881
  40.3 7.5 %all-to-all-done.1.got = f32[8,40,128]{2,1,0:T(8,128)S(1)} async-done(((f32[8,40,128]{2,1,0:T(8,128)}), f32[8,40,128]{2,1,0:T(8,128)S(1)}, u32[]{:S(2)}, u32[]{:S(2)}) %all-to-all-start.1) | async-done | bytes 163872 | tf_op jit(solution)/shard_map/all_to_all | solution.py:874
  47.9 1.6 %shard_map.185 = (f32[80,256]{1,0:T(8,128)S(1)}, f32[80,256]{1,0:T(8,128)S(1)}) custom-call(s32[1]{0:T(128)} %bitcast.5.core, f32[8,40,128]{2,1,0:T(8,128)S(1)} %all-to-all-done.1.got, f32[32,2048]{1,0:T(8,128)S(1)} %get-tuple-element.68.after.waves_x, bf16[144,2048]{1,0:T(8,128)(2,1)S(1)} %get-tuple-element.78.high, ...), custom_call_target="tpu_custom_call" | custom-call | flops 1500000000 | bytes 6000000 | tf_op jit(solution)/shard_map/pallas_call | solution.py:897
  49.4 0.8 collective-permute-start.4
  50.2 0.9 collective-permute-done.4
  51.2 2.0 %collective-permute-start.6 = (f32[80,256]{1,0:T(8,128)S(1)}, f32[80,256]{1,0:T(8,128)S(1)}, u32[]{:S(2)}, u32[]{:S(2)}) collective-permute-start(f32[80,256]{1,0:T(8,128)S(1)} %add.8.refs_0_), channel_id=1, source_target_pairs={{0,48},{8,56},{32,0},{40,8},{16,32},{24,40},{48,16},{56,24},{64,11... | collective-permute-start | bytes 245768 | tf_op jit(solution)/shard_map/ppermute | solution.py:919
  53.2 1.4 %collective-permute-start.7 = (f32[80,256]{1,0:T(8,128)S(1)}, f32[80,256]{1,0:T(8,128)S(1)}, u32[]{:S(2)}, u32[]{:S(2)}) collective-permute-start(f32[80,256]{1,0:T(8,128)S(1)} %add.8.refs_0_), channel_id=1, source_target_pairs={{0,16},{8,24},{32,48},{40,56},{16,0},{24,8},{48,32},{56,40},{64,80... | collective-permute-start | bytes 245768 | tf_op jit(solution)/shard_map/ppermute | solution.py:919
  54.6 1.2 %shard_map.184 = (f32[16,8,256]{2,1,0:T(8,128)S(1)}, f32[16,256]{1,0:T(8,128)S(1)}, f32[8,128]{1,0:T(8,128)S(1)}) custom-call(f32[384,256]{1,0:T(8,128)S(1)} %get-tuple-element.74.refs_0_, f32[3,64,256]{2,1,0:T(8,128)S(1)} %get-tuple-element.71.refs_3_.refs_1_.disp, f32[64,256]{1,0:T(8,128)S(1)} %get-tuple-element.72.refs_4_.refs_2_, ...), custom_call_target="tpu_custom_call" | custom-call | flops 1000000000 | bytes 4000000 | tf_op jit(solution)/shard_map/pallas_call | solution.py:881
  55.8 0.1 collective-permute-done.5.refs_1_
  55.9 0.2 collective-permute-done.6.refs_2_
  56.1 3.1 %collective-permute-done.7.refs_3_ = f32[80,256]{1,0:T(8,128)S(1)} collective-permute-done((f32[80,256]{1,0:T(8,128)S(1)}, f32[80,256]{1,0:T(8,128)S(1)}, u32[]{:S(2)}, u32[]{:S(2)}) %collective-permute-start.7) | collective-permute-done | bytes 81952 | tf_op jit(solution)/shard_map/ppermute | solution.py:919
  59.2 0.4 collective-permute-start.8
  59.6 1.7 %collective-permute-start.9 = (f32[80,256]{1,0:T(8,128)S(1)}, f32[80,256]{1,0:T(8,128)S(1)}, u32[]{:S(2)}, u32[]{:S(2)}) collective-permute-start(f32[80,256]{1,0:T(8,128)S(1)} %shard_map.186.refs_0_), channel_id=1, source_target_pairs={{0,192},{8,200},{32,224},{40,232},{16,208},{24,216},{48,240},{56,2... | collective-permute-start | bytes 245768 | tf_op jit(solution)/shard_map/ppermute | solution.py:919
  61.3 1.2 %collective-permute-start.10 = (f32[80,256]{1,0:T(8,128)S(1)}, f32[80,256]{1,0:T(8,128)S(1)}, u32[]{:S(2)}, u32[]{:S(2)}) collective-permute-start(f32[80,256]{1,0:T(8,128)S(1)} %shard_map.186.refs_0_), channel_id=1, source_target_pairs={{0,128},{8,136},{32,160},{40,168},{16,144},{24,152},{48,176},{56,1... | collective-permute-start | bytes 245768 | tf_op jit(solution)/shard_map/ppermute | solution.py:919
  62.5 1.2 %shard_map.183 = (f32[16,8,256]{2,1,0:T(8,128)S(1)}, f32[16,256]{1,0:T(8,128)S(1)}, f32[8,128]{1,0:T(8,128)S(1)}) custom-call(f32[384,256]{1,0:T(8,128)S(1)} %get-tuple-element.74.refs_0_, f32[3,64,256]{2,1,0:T(8,128)S(1)} %get-tuple-element.71.refs_3_.refs_1_.disp, f32[64,256]{1,0:T(8,128)S(1)} %get-tuple-element.72.refs_4_.refs_2_, ...), custom_call_target="tpu_custom_call" | custom-call | flops 1000000000 | bytes 4000000 | tf_op jit(solution)/shard_map/pallas_call | solution.py:881
  63.7 0.5 collective-permute-done.8.refs_1_
  64.2 1.3 %collective-permute-done.9.refs_2_ = f32[80,256]{1,0:T(8,128)S(1)} collective-permute-done((f32[80,256]{1,0:T(8,128)S(1)}, f32[80,256]{1,0:T(8,128)S(1)}, u32[]{:S(2)}, u32[]{:S(2)}) %collective-permute-start.9) | collective-permute-done | bytes 81952 | tf_op jit(solution)/shard_map/ppermute | solution.py:919
  65.4 1.8 %collective-permute-done.10.refs_3_ = f32[80,256]{1,0:T(8,128)S(1)} collective-permute-done((f32[80,256]{1,0:T(8,128)S(1)}, f32[80,256]{1,0:T(8,128)S(1)}, u32[]{:S(2)}, u32[]{:S(2)}) %collective-permute-start.10) | collective-permute-done | bytes 81952 | tf_op jit(solution)/shard_map/ppermute | solution.py:919
  67.4 0.6 shard_map.188
  68.0 0.7 collective-permute-done.11.other
  68.7 1.8 %shard_map.189 = (f32[8,8,256]{2,1,0:T(8,128)}, f32[144,256]{1,0:T(8,128)S(1)}) custom-call(s32[1]{0:T(128)} %bitcast.5.core, f32[80,256]{1,0:T(8,128)S(1)} %shard_map.187.mine, f32[80,256]{1,0:T(8,128)S(1)} %collective-permute-done.11.other, f32[3,72,128]{2,1,0:T(8,128)S(1)} %get-tuple-element.83.weights, f32[8,256]{1,0:T(8,128)S(1)} %get-tuple-element.84.lone_weights, ...), custom_call_target="tpu_custom_call" | custom-call | flops 1000000000 | bytes 4000000 | tf_op jit(solution)/shard_map/pallas_call | solution.py:927
  70.4 3.3 %all-to-all-start.2 = ((f32[8,8,256]{2,1,0:T(8,128)}), f32[8,8,256]{2,1,0:T(8,128)S(1)}, u32[]{:S(2)}, u32[]{:S(2)}) async-start(f32[8,8,256]{2,1,0:T(8,128)} %get-tuple-element.85), calls=%async_computation.2 | async-start | bytes 131072 | tf_op jit(solution)/shard_map/all_to_all | solution.py:938
  73.8 4.0 %shard_map.191.refs_0_ = f32[8,8,128]{2,1,0:T(8,128)S(1)} custom-call(s32[1]{0:T(128)} %bitcast.7.rank, s32[1]{0:T(128)} %bitcast.5.core, f32[8,256]{1,0:T(8,128)S(1)} %get-tuple-element.53.edges, f32[80,256]{1,0:T(8,128)S(1)} %shard_map.187.mine, f32[80,256]{1,0:T(8,128)S(1)} %collective-permute-done.11.other, f32[3,72,128]{2,1,0:T(8,128)S(1)} %get-tuple-element.83.weights, ...), custom_call_target="tpu_custom_call" | custom-call | flops 2500000000 | bytes 10000000 | tf_op jit(solution)/shard_map/pallas_call | solution.py:939
  77.8 4.3 %all-to-all-done.2.got = f32[8,8,256]{2,1,0:T(8,128)S(1)} async-done(((f32[8,8,256]{2,1,0:T(8,128)}), f32[8,8,256]{2,1,0:T(8,128)S(1)}, u32[]{:S(2)}, u32[]{:S(2)}) %all-to-all-start.2) | async-done | bytes 65568 | tf_op jit(solution)/shard_map/all_to_all | solution.py:938
  82.1 1.6 %shard_map.190 = (f32[16,128]{1,0:T(8,128)S(1)}, f32[16,128]{1,0:T(8,128)S(1)}, f32[8,128]{1,0:T(8,128)S(1)}, f32[8,128]{1,0:T(8,128)S(1)}) custom-call(f32[8,8,256]{2,1,0:T(8,128)S(1)} %all-to-all-done.2.got, f32[32,8,256]{2,1,0:T(8,128)S(1)} %get-tuple-element.86.r0, f32[32,256]{1,0:T(8,128)S(1)} %get-tuple-element.87.e0, ...), custom_call_target="tpu_custom_call" | custom-call | flops 1000000000 | bytes 4000000 | tf_op jit(solution)/shard_map/pallas_call | solution.py:954
  83.6 0.4 collective-permute-start.12
  84.0 0.2 collective-permute-start.13
  84.2 1.5 %shard_map.192 = (f32[8,8,128]{2,1,0:T(8,128)S(1)}, f32[8,128]{1,0:T(8,128)S(1)}) custom-call(f32[8,8,256]{2,1,0:T(8,128)S(1)} %all-to-all-done.2.got, f32[32,8,256]{2,1,0:T(8,128)S(1)} %get-tuple-element.86.r0, f32[32,256]{1,0:T(8,128)S(1)} %get-tuple-element.87.e0, f32[16,8,256]{2,1,0:T(8,128)S(1)} %get-tuple-element.88.r1, ...), custom_call_target="tpu_custom_call" | custom-call | flops 1000000000 | bytes 4000000 | tf_op jit(solution)/shard_map/pallas_call | solution.py:954
  85.8 2.8 %collective-permute-done.13.below = f32[16,128]{1,0:T(8,128)S(1)} collective-permute-done((f32[16,128]{1,0:T(8,128)S(1)}, f32[16,128]{1,0:T(8,128)S(1)}, u32[]{:S(2)}, u32[]{:S(2)}) %collective-permute-start.13) | collective-permute-done | bytes 8224 | tf_op jit(solution)/shard_map/ppermute | solution.py:972
  88.6 2.4 %collective-permute-start.14 = (f32[8,128]{1,0:T(8,128)S(1)}, f32[8,128]{1,0:T(8,128)S(1)}, u32[]{:S(2)}, u32[]{:S(2)}) collective-permute-start(f32[8,128]{1,0:T(8,128)S(1)} %get-tuple-element.100), channel_id=1, source_target_pairs={{0,32},{32,64},{64,96},{96,128},{128,160},{160,192},{192,224},{224... | collective-permute-start | bytes 12296 | tf_op jit(solution)/shard_map/ppermute | solution.py:977
  91.0 1.3 %collective-permute-done.14.from_left = f32[8,128]{1,0:T(8,128)S(1)} collective-permute-done((f32[8,128]{1,0:T(8,128)S(1)}, f32[8,128]{1,0:T(8,128)S(1)}, u32[]{:S(2)}, u32[]{:S(2)}) %collective-permute-start.14) | collective-permute-done | bytes 4128 | tf_op jit(solution)/shard_map/ppermute | solution.py:977
  92.4 4.4 %collective-permute-done.15.from_right = f32[8,128]{1,0:T(8,128)S(1)} collective-permute-done((f32[8,128]{1,0:T(8,128)S(1)}, f32[8,128]{1,0:T(8,128)S(1)}, u32[]{:S(2)}, u32[]{:S(2)}) %collective-permute-start.15) | collective-permute-done | bytes 4128 | tf_op jit(solution)/shard_map/ppermute | solution.py:976
  96.8 0.2 shard_map.194
  97.0 11.0 %all_to_all.20.got = f32[8,8,128]{2,1,0:T(8,128)S(1)} all-to-all(f32[8,8,128]{2,1,0:T(8,128)S(1)} %shard_map.194), channel_id=1, replica_groups=mesh['gx'=8,'gy'=4,'ka'=8] {'ka'}, dimensions={0} | all-to-all | bytes 65536 | tf_op jit(solution)/shard_map/all_to_all | solution.py:981
  108.0 0.6 shard_map.195
  (17 shorter events, 0.5 us)
Async XLA Ops:
  2.0 16.5 %all-to-all-start = ((f32[8,8,128]{2,1,0:T(8,128)}), f32[8,8,128]{2,1,0:T(8,128)S(1)}, u32[]{:S(2)}, u32[]{:S(2)}) async-start(f32[8,8,128]{2,1,0:T(8,128)} %get-tuple-element.55), calls=%async_computation | async-start | bytes 65536 | tf_op jit(solution)/shard_map/all_to_all | solution.py:790
  18.6 5.0 %collective-permute-start = (f32[8,128]{1,0:T(8,128)S(1)}, f32[8,128]{1,0:T(8,128)S(1)}, u32[]{:S(2)}, u32[]{:S(2)}) collective-permute-start(f32[8,128]{1,0:T(8,128)S(1)} %get-tuple-element.57.cell1), channel_id=1, source_target_pairs={{0,8},{8,16},{16,24},{24,0},{1,9},{9,17},{17,25},{25,1},{2,10},{10... | collective-permute-start | bytes 12296 | tf_op jit(solution)/shard_map/ppermute | solution.py:838
  18.7 4.9 %collective-permute-start.1 = (f32[8,128]{1,0:T(8,128)S(1)}, f32[8,128]{1,0:T(8,128)S(1)}, u32[]{:S(2)}, u32[]{:S(2)}) collective-permute-start(f32[8,128]{1,0:T(8,128)S(1)} %get-tuple-element.58.cell0), channel_id=1, source_target_pairs={{0,24},{8,0},{16,8},{24,16},{1,25},{9,1},{17,9},{25,17},{2,26},{10... | collective-permute-start | bytes 12296 | tf_op jit(solution)/shard_map/ppermute | solution.py:839
  23.7 3.7 %collective-permute-start.2 = (f32[16,128]{1,0:T(8,128)S(1)}, f32[16,128]{1,0:T(8,128)S(1)}, u32[]{:S(2)}, u32[]{:S(2)}) collective-permute-start(f32[16,128]{1,0:T(8,128)S(1)} %get-tuple-element.59), channel_id=1, source_target_pairs={{0,32},{32,64},{64,96},{96,128},{128,160},{160,192},{192,224},{224... | collective-permute-start | bytes 24584 | tf_op jit(solution)/shard_map/ppermute | solution.py:846
  24.1 5.8 %collective-permute-start.3 = (f32[16,128]{1,0:T(8,128)S(1)}, f32[16,128]{1,0:T(8,128)S(1)}, u32[]{:S(2)}, u32[]{:S(2)}) collective-permute-start(f32[16,128]{1,0:T(8,128)S(1)} %get-tuple-element.60), channel_id=1, source_target_pairs={{0,224},{32,0},{64,32},{96,64},{128,96},{160,128},{192,160},{224,1... | collective-permute-start | bytes 24584 | tf_op jit(solution)/shard_map/ppermute | solution.py:847
  34.1 13.8 %all-to-all-start.1 = ((f32[8,40,128]{2,1,0:T(8,128)}), f32[8,40,128]{2,1,0:T(8,128)S(1)}, u32[]{:S(2)}, u32[]{:S(2)}) async-start(f32[8,40,128]{2,1,0:T(8,128)} %get-tuple-element.77), calls=%async_computation.1 | async-start | bytes 327680 | tf_op jit(solution)/shard_map/all_to_all | solution.py:874
  49.4 1.7 %collective-permute-start.4 = (f32[80,256]{1,0:T(8,128)S(1)}, f32[80,256]{1,0:T(8,128)S(1)}, u32[]{:S(2)}, u32[]{:S(2)}) collective-permute-start(f32[80,256]{1,0:T(8,128)S(1)} %get-tuple-element.82), channel_id=1, source_target_pairs={{0,8},{8,0},{32,40},{40,32},{16,24},{24,16},{48,56},{56,48},{64,72... | collective-permute-start | bytes 245768 | tf_op jit(solution)/shard_map/ppermute | solution.py:917
  51.1 4.8 %collective-permute-start.5 = (f32[80,256]{1,0:T(8,128)S(1)}, f32[80,256]{1,0:T(8,128)S(1)}, u32[]{:S(2)}, u32[]{:S(2)}) collective-permute-start(f32[80,256]{1,0:T(8,128)S(1)} %add.8.refs_0_), channel_id=1, source_target_pairs={{0,32},{8,40},{32,16},{40,24},{16,48},{24,56},{48,0},{56,8},{64,96... | collective-permute-start | bytes 245768 | tf_op jit(solution)/shard_map/ppermute | solution.py:919
  51.2 4.8 %collective-permute-start.6 = (f32[80,256]{1,0:T(8,128)S(1)}, f32[80,256]{1,0:T(8,128)S(1)}, u32[]{:S(2)}, u32[]{:S(2)}) collective-permute-start(f32[80,256]{1,0:T(8,128)S(1)} %add.8.refs_0_), channel_id=1, source_target_pairs={{0,48},{8,56},{32,0},{40,8},{16,32},{24,40},{48,16},{56,24},{64,11... | collective-permute-start | bytes 245768 | tf_op jit(solution)/shard_map/ppermute | solution.py:919
  53.2 5.9 %collective-permute-start.7 = (f32[80,256]{1,0:T(8,128)S(1)}, f32[80,256]{1,0:T(8,128)S(1)}, u32[]{:S(2)}, u32[]{:S(2)}) collective-permute-start(f32[80,256]{1,0:T(8,128)S(1)} %add.8.refs_0_), channel_id=1, source_target_pairs={{0,16},{8,24},{32,48},{40,56},{16,0},{24,8},{48,32},{56,40},{64,80... | collective-permute-start | bytes 245768 | tf_op jit(solution)/shard_map/ppermute | solution.py:919
  59.2 5.0 %collective-permute-start.8 = (f32[80,256]{1,0:T(8,128)S(1)}, f32[80,256]{1,0:T(8,128)S(1)}, u32[]{:S(2)}, u32[]{:S(2)}) collective-permute-start(f32[80,256]{1,0:T(8,128)S(1)} %shard_map.186.refs_0_), channel_id=1, source_target_pairs={{0,64},{8,72},{32,96},{40,104},{16,80},{24,88},{48,112},{56,120},{... | collective-permute-start | bytes 245768 | tf_op jit(solution)/shard_map/ppermute | solution.py:919
  59.6 5.9 %collective-permute-start.9 = (f32[80,256]{1,0:T(8,128)S(1)}, f32[80,256]{1,0:T(8,128)S(1)}, u32[]{:S(2)}, u32[]{:S(2)}) collective-permute-start(f32[80,256]{1,0:T(8,128)S(1)} %shard_map.186.refs_0_), channel_id=1, source_target_pairs={{0,192},{8,200},{32,224},{40,232},{16,208},{24,216},{48,240},{56,2... | collective-permute-start | bytes 245768 | tf_op jit(solution)/shard_map/ppermute | solution.py:919
  61.3 5.9 %collective-permute-start.10 = (f32[80,256]{1,0:T(8,128)S(1)}, f32[80,256]{1,0:T(8,128)S(1)}, u32[]{:S(2)}, u32[]{:S(2)}) collective-permute-start(f32[80,256]{1,0:T(8,128)S(1)} %shard_map.186.refs_0_), channel_id=1, source_target_pairs={{0,128},{8,136},{32,160},{40,168},{16,144},{24,152},{48,176},{56,1... | collective-permute-start | bytes 245768 | tf_op jit(solution)/shard_map/ppermute | solution.py:919
  67.3 1.4 %collective-permute-start.11 = (f32[80,256]{1,0:T(8,128)S(1)}, f32[80,256]{1,0:T(8,128)S(1)}, u32[]{:S(2)}, u32[]{:S(2)}) collective-permute-start(f32[80,256]{1,0:T(8,128)S(1)} %shard_map.187.mine), channel_id=1, source_target_pairs={{0,8},{8,0},{32,40},{40,32},{16,24},{24,16},{48,56},{56,48},{64,72... | collective-permute-start | bytes 245768 | tf_op jit(solution)/shard_map/ppermute | solution.py:920
  70.4 11.7 %all-to-all-start.2 = ((f32[8,8,256]{2,1,0:T(8,128)}), f32[8,8,256]{2,1,0:T(8,128)S(1)}, u32[]{:S(2)}, u32[]{:S(2)}) async-start(f32[8,8,256]{2,1,0:T(8,128)} %get-tuple-element.85), calls=%async_computation.2 | async-start | bytes 131072 | tf_op jit(solution)/shard_map/all_to_all | solution.py:938
  83.6 2.1 %collective-permute-start.12 = (f32[16,128]{1,0:T(8,128)S(1)}, f32[16,128]{1,0:T(8,128)S(1)}, u32[]{:S(2)}, u32[]{:S(2)}) collective-permute-start(f32[16,128]{1,0:T(8,128)S(1)} %get-tuple-element.92), channel_id=1, source_target_pairs={{0,24},{8,0},{16,8},{24,16},{1,25},{9,1},{17,9},{25,17},{2,26},{10... | collective-permute-start | bytes 24584 | tf_op jit(solution)/shard_map/ppermute | solution.py:971
  84.0 4.6 %collective-permute-start.13 = (f32[16,128]{1,0:T(8,128)S(1)}, f32[16,128]{1,0:T(8,128)S(1)}, u32[]{:S(2)}, u32[]{:S(2)}) collective-permute-start(f32[16,128]{1,0:T(8,128)S(1)} %get-tuple-element.93), channel_id=1, source_target_pairs={{0,8},{8,16},{16,24},{24,0},{1,9},{9,17},{17,25},{25,1},{2,10},{10... | collective-permute-start | bytes 24584 | tf_op jit(solution)/shard_map/ppermute | solution.py:972
  84.2 23.8 %copy-start = (f32[3,256]{1,0:T(4,128)S(1)}, f32[3,256]{1,0:T(4,128)}, u32[]{:S(2)}) copy-start(f32[3,256]{1,0:T(4,128)} %speed.1) | copy-start | bytes 9220
  84.2 23.8 %copy-start.1 = (f32[3,256]{1,0:T(4,128)S(1)}, f32[3,256]{1,0:T(4,128)}, u32[]{:S(2)}) copy-start(f32[3,256]{1,0:T(4,128)} %kicks.1) | copy-start | bytes 9220
  88.6 3.7 %collective-permute-start.14 = (f32[8,128]{1,0:T(8,128)S(1)}, f32[8,128]{1,0:T(8,128)S(1)}, u32[]{:S(2)}, u32[]{:S(2)}) collective-permute-start(f32[8,128]{1,0:T(8,128)S(1)} %get-tuple-element.100), channel_id=1, source_target_pairs={{0,32},{32,64},{64,96},{96,128},{128,160},{160,192},{192,224},{224... | collective-permute-start | bytes 12296 | tf_op jit(solution)/shard_map/ppermute | solution.py:977
  91.0 5.7 %collective-permute-start.15 = (f32[8,128]{1,0:T(8,128)S(1)}, f32[8,128]{1,0:T(8,128)S(1)}, u32[]{:S(2)}, u32[]{:S(2)}) collective-permute-start(f32[8,128]{1,0:T(8,128)S(1)} %get-tuple-element.101), channel_id=1, source_target_pairs={{0,224},{32,0},{64,32},{96,64},{128,96},{160,128},{192,160},{224,1... | collective-permute-start | bytes 12296 | tf_op jit(solution)/shard_map/ppermute | solution.py:976

commit v6 on v5

--- a/solution.py
+++ b/solution.py
@@ -26,7 +26,6 @@
 atoms_all = 65536
 top = 16
 span = 2 * top + 1
-plane_own = 69
 plane_rows = 72
 waves = 2 * plane_rows
 tau = 2.0 * math.pi
@@ -117,7 +116,8 @@
 
 
 def plane_of(rank, shape, axis):
-    index = (lax.broadcasted_iota(i32, shape, axis) + rank * plane_own).astype(f32)
+    row = lax.broadcasted_iota(i32, shape, axis)
+    index = jnp.where(row < 64, row + rank * 64, row + (448 + rank * 5)).astype(f32)
     first = jnp.floor((index + (top + 0.5)) * (1.0 / span))
     return first, index - span * first
 
@@ -153,18 +153,22 @@
     sign = jnp.where(kx < 0.0, -1.0, 1.0)
     value = jnp.where(row < top, 1.0, sign)
     line = jnp.where(row < 2 * top, jnp.where(jnp.abs(kx) == wanted, value, 0.0), 0.0)
-    line = jnp.where((row == 2 * top) & (kx == 0.0), 1.0, line).astype(bf16)
-    place = (lax.broadcasted_iota(i32, (128, count), 0) & 63).astype(f32)
-    spill = (lax.broadcasted_iota(i32, (16, count), 0) + 64).astype(f32)
+    line = jnp.where((row == 2 * top) & (kx == 0.0), 1.0, line)
+    number = code.astype(i32)
+    owner, within = lax.shift_right_logical(number, 6), number & 63
+    hit = (lax.broadcasted_iota(i32, (128, count), 0) & 63) == within
+    stack = [jnp.where(owner == z, line, 0.0).astype(bf16) for z in range(ranks)]
+    main = dot_t(jnp.concatenate(stack, axis=0), jnp.where(hit, 1.0, 0.0).astype(bf16))
+    row = lax.broadcasted_iota(i32, (64, count), 0)
+    place = row & 7
+    hit = (number == 512 + 5 * lax.shift_right_logical(row, 3) + place) & (place < 5)
+    rest = dot_t(jnp.where(hit, 1.0, 0.0).astype(bf16), line.astype(bf16))
     left = lax.broadcasted_iota(i32, (16, 128), 1) < 64
     for z in range(ranks):
-        begin = float(z * plane_own)
-        hit = jnp.where(code == place + begin, 1.0, 0.0).astype(bf16)
-        both = dot_t(line, hit)
+        both = main[z * 48 : z * 48 + 48]
         out[z, 0:16, :] = jnp.where(left, both[0:16], both[16:32])
-        hit = jnp.where((code == spill + begin) & (spill < plane_own), 1.0, 0.0).astype(bf16)
         out[z, 16:24, :] = jnp.zeros((8, 128), f32)
-        out[z, 16:21, 0:48] = dot_t(hit, line)[0:5]
+        out[z, 16:24, 0:48] = rest[z * 8 : z * 8 + 8]
         out[z, 21:22, 0:64] = both[32:33, 0:64]
 
 
@@ -238,7 +242,7 @@
 
 
 def own_gather_kernel(table, listing, near):
-    def step(j, carry):
+    def part(j):
         at = pl.ds(pl.multiple_of(j * chunk, chunk), chunk)
         for half in range(2):
             lanes = slice(half * 128, half * 128 + 128)
@@ -253,31 +257,29 @@
                     found[c] = jnp.where(hit, lane_pick(row, low), found[c])
             for c in range(4):
                 near[c, at, lanes] = found[c]
-        return carry
-
-    lax.fori_loop(0, chunks, step, 0)
-
-
-def factor_kernel(rank, table, high, low, waves_x):
+
+    paired(chunks, part, (), 4)
+
+
+def factor_kernel(rank, table, planes, waves_x):
     shape = (plane_rows, 128)
     ky, kz = plane_of(rank[0], shape, 0)
     kx = (lax.broadcasted_iota(i32, (top, 128), 0) + 1).astype(f32)
 
-    def step(z, carry):
+    def part(z):
         for half in range(2):
             at = pl.ds(pl.multiple_of(z * own + half * 128, 128), 128)
             x, y, w = (table[z, 2 * c + half : 2 * c + half + 1, :] for c in range(3))
             cosine, sine = circle(ky * y + kz * w)
             both = jnp.concatenate([cosine, sine], axis=0)
             upper, lower = split(both)
-            high[:, at] = upper
-            low[:, at] = lower
+            planes[0:waves, at] = upper
+            planes[waves : 2 * waves, at] = lower
             cosine, sine = circle(kx * x)
             waves_x[0:top, at] = cosine
             waves_x[top : 2 * top, at] = sine
-        return carry
-
-    lax.fori_loop(0, ranks, step, 0)
+
+    paired(ranks, part, (), 2)
 
 
 def message_kernel(
@@ -418,7 +420,7 @@
 
 
 def structure_kernel(
-    core, got, waves_x, high, low, after, mine, other, total, extra, lefts_high, lefts_low
+    core, got, waves_x, planes, after, mine, other, total, extra, lefts_high, lefts_low
 ):
     total[...] = jnp.zeros_like(total)
     extra[...] = jnp.zeros_like(extra)
@@ -433,7 +435,7 @@
             upper, lower = split(pair)
             left_high[f * 8 : f * 8 + 16, :] = upper
             left_low[f * 8 : f * 8 + 16, :] = lower
-        plane_high, plane_low = high[:, at], low[:, at]
+        plane_high, plane_low = planes[0:waves, at], planes[waves : 2 * waves, at]
         total[...] += dot_t(plane_high, left_high[...]) + (
             dot_t(plane_low, left_high[...]) + dot_t(plane_high, left_low[...])
         )
@@ -492,10 +494,15 @@
     lone_out[...] = dot_c(zero[:, 0:8], twice)
 
 
-def turn_table(table, blocks, table_high, table_low):
+def threefold(x):
+    main = x.astype(bf16).astype(f32)
+    return jnp.concatenate([main, main, x - main], axis=1).astype(bf16)
+
+
+def turn_table(table, blocks, lines):
     for block in range(blocks):
         at = slice(block * 128, block * 128 + 128)
-        table_high[at, 0:waves], table_low[at, 0:waves] = split(jnp.transpose(table[:, at]))
+        lines[at, 0 : 3 * waves] = threefold(jnp.transpose(table[:, at]))
 
 
 def halves_of(core, mine, other):
@@ -509,8 +516,8 @@
 
 
 def potential_kernel(
-    core, mine, other, weights, lone_weights, waves_x, high, low, potential, table, table_high,
-    table_low, results
+    core, mine, other, weights, lone_weights, waves_x, planes, potential, table, lines_high, lines_low,
+    results
 ):
     real, imaginary, lone = halves_of(core, mine, other)
     both, apart = weights[0], weights[1]
@@ -521,17 +528,20 @@
     table[lower, 0:128] = both * imag_c + apart * real_s
     table[upper, 128:256] = both * real_s + apart * imag_c
     table[lower, 128:256] = both * imag_s - apart * real_c
-    turn_table(table, 2, table_high, table_low)
+    for block in range(2):
+        at = slice(block * 128, block * 128 + 128)
+        lines_high[at, 0:waves], lines_low[at, 0:waves] = split(jnp.transpose(table[:, at]))
     lone = (lone * lone_weights[...])[:, 0:waves]
     lone = jnp.concatenate([lone, jnp.zeros_like(lone)], axis=0)
-    table_high[256:272, 0:waves], table_low[256:272, 0:waves] = split(lone)
+    lines_high[256:272, 0:waves], lines_low[256:272, 0:waves] = split(lone)
 
     def part(z, result):
         at = pl.ds(pl.multiple_of(z * own, own), own)
-        plane_high, plane_low = high[:, at], low[:, at]
-        lines = table_high[0:272, 0:waves]
+        plane_high = planes[0:waves, at]
+        lines = lines_high[0:272, 0:waves]
         result[...] = dot_n(lines, plane_high) + (
-            dot_n(table_low[0:272, 0:waves], plane_high) + dot_n(lines, plane_low)
+            dot_n(lines_low[0:272, 0:waves], plane_high)
+            + dot_n(lines, planes[waves : 2 * waves, at])
         )
         total = result[256:264, :]
         for f in range(2 * top):
@@ -542,8 +552,8 @@
 
 
 def gradient_kernel(
-    rank, core, edges, mine, other, weights, table, got, waves_x, high, low, gradient, wide,
-    table_high, table_low, results
+    rank, core, edges, mine, other, weights, table, got, waves_x, planes, gradient, wide, lines,
+    tall, results
 ):
     _, _, lone = halves_of(core, mine, other)
     lane = lax.broadcasted_iota(i32, (8, 128), 1)
@@ -567,15 +577,13 @@
     turn = jnp.where(group == 0, ty, tz)
     wide[upper, 768:896] = turn * im
     wide[lower, 768:896] = -(turn * re)
-    turn_table(wide, 7, table_high, table_low)
+    turn_table(wide, 7, lines)
+    tall[0 : 2 * waves, :] = planes[...]
+    tall[2 * waves : 3 * waves, :] = planes[0:waves, :]
 
     def part(z, result):
         at = pl.ds(pl.multiple_of(z * own, own), own)
-        plane_high, plane_low = high[:, at], low[:, at]
-        lines = table_high[0:784, 0:waves]
-        result[...] = dot_n(lines, plane_high) + (
-            dot_n(table_low[0:784, 0:waves], plane_high) + dot_n(lines, plane_low)
-        )
+        result[...] = dot_n(lines[0:784, 0 : 3 * waves], tall[:, at])
         total = [jnp.zeros((8, own), f32), result[768:776, :], result[776:784, :]]
         for f in range(2 * top):
             wave = waves_x[f : f + 1, at]
@@ -603,7 +611,13 @@
     lefts, rights, total, pulled = refs[-4:]
     total[...] = jnp.zeros_like(total)
     pulled[...] = jnp.zeros_like(pulled)
-    row_high = lax.broadcasted_iota(i32, (16, own), 0) + (16 if ghosts else 0)
+    height = 8 if ghosts else 24
+    row = lax.broadcasted_iota(i32, (height, own), 0)
+    if ghosts:
+        row_high = 16 + 4 * lax.shift_right_logical(row, 1) + 3 * (row & 1)
+    else:
+        middle = 17 + 12 * lax.shift_right_logical(row - 16, 1) + (row & 1)
+        row_high = jnp.where(row < 16, row, jnp.where(row < 20, middle, -1))
     row_low = lax.broadcasted_iota(i32, (128, own), 0)
 
     def part(response, site, begin, j, left, right):
@@ -625,44 +639,48 @@
             pieces.append((main, pulls[d] - main))
         for m in range(chunk):
             lanes = slice(m * own, (m + 1) * own)
-            hit = jnp.broadcast_to(high[m : m + 1, :], (16, own)) == row_high
-            for piece in range(2):
-                for d in range(3):
-                    row = piece * 48 + d * 16
-                    left[row : row + 16, lanes] = jnp.where(
-                        hit, pieces[d][piece][m : m + 1, :], 0.0
-                    ).astype(bf16)
+            hit = jnp.broadcast_to(high[m : m + 1, :], (height, own)) == row_high
+            blocks = [
+                jnp.where(hit, pieces[d][piece][m : m + 1, :], 0.0)
+                for piece in range(2)
+                for d in range(3)
+            ]
+            left[:, lanes] = jnp.concatenate(blocks, axis=0).astype(bf16)
             spot = jnp.broadcast_to(low[m : m + 1, :], (128, own)) == row_low
             right[:, lanes] = jnp.where(spot, 1.0, 0.0).astype(bf16)
-        total[...] += dot_t(left[...], right[...])
+        if ghosts:
+            total[...] += dot_t(right[...], left[...])
+        else:
+            total[...] += dot_t(left[...], right[...])
 
     begin = 0
     for response, site in ((r0, e0), (r1, e1), (r2, e2)):
         count = response.shape[0] // chunk
         paired(count, functools.partial(part, response, site, begin), (lefts, rights), count)
         begin += count
-    scattered = total[0:48, :] + total[48:96, :]
+    whole = jnp.transpose(total[...]) if ghosts else total[...]
+    scattered = whole[0 : 3 * height, :] + whole[3 * height : 6 * height, :]
+    nothing = jnp.zeros((1, 128), f32)
     if ghosts:
-        cells0, cells3, mid0, mid3 = refs[:4]
-        nothing = jnp.zeros((1, 128), f32)
+        cells0, cells3 = refs[:2]
         for u in range(4):
             for c in range(4):
-                for ref, v in ((cells0, 0), (cells3, 3)):
-                    spot = c * 16 + u * 4 + v
+                for side, ref in ((0, cells0), (1, cells3)):
+                    spot = c * 8 + u * 2 + side
                     value = scattered[spot : spot + 1, :] if c < 3 else nothing
                     ref[u * 4 + c : u * 4 + c + 1, :] = value
-        for ref, u in ((mid0, 0), (mid3, 3)):
-            for j in range(2):
-                for c in range(4):
-                    spot = c * 16 + u * 4 + 1 + j
-                    value = scattered[spot : spot + 1, :] if c < 3 else nothing
-                    ref[j * 4 + c : j * 4 + c + 1, :] = value
         return
-    lines, domain, direct = refs[:3]
+    lines, domain, direct, mid0, mid3 = refs[:5]
+    for side, ref in ((0, mid0), (1, mid3)):
+        for j in range(2):
+            for c in range(4):
+                spot = c * 24 + 16 + side * 2 + j
+                value = scattered[spot : spot + 1, :] if c < 3 else nothing
+                ref[j * 4 + c : j * 4 + c + 1, :] = value
     for z in range(ranks):
         for d in range(3):
             for half in range(2):
-                spot, r = d * 16 + z * 2 + half, 2 * d + half
+                spot, r = d * 24 + z * 2 + half, 2 * d + half
                 domain[z, r : r + 1, :] = scattered[spot : spot + 1, :] + lines[z, r : r + 1, :]
         domain[z, 6:8, :] = jnp.zeros((2, 128), f32)
     for d in range(3):
@@ -672,7 +690,7 @@
     direct[6:8, :] = jnp.zeros((2, 128), f32)
 
 
-def echo_kernel(above, below, mid0, mid3, after, send0, send3, inner0, inner1):
+def echo_kernel(above, below, mid0, mid3, send0, send3, inner0, inner1):
     for u, ref in ((0, send0), (1, inner0), (2, inner1), (3, send3)):
         both = jnp.concatenate([below[u * 4 : u * 4 + 4, :], above[u * 4 : u * 4 + 4, :]], axis=0)
         if u == 0:
@@ -845,9 +863,9 @@
     )
     left = lax.ppermute(tail, "gx", shift("gx", 1))
     right = lax.ppermute(head, "gx", shift("gx", -1))
-    high, low, waves_x = call(
+    planes, waves_x = call(
         factor_kernel,
-        [((waves, ranks * own), bf16), ((waves, ranks * own), bf16), ((2 * top, ranks * own), f32)],
+        [((2 * waves, ranks * own), bf16), ((2 * top, ranks * own), f32)],
         [smem, vmem],
         cost=work(2),
     )(rank, table)
@@ -897,7 +915,7 @@
     mine, other = call(
         structure_kernel,
         [((plane_rows + 8, own), f32)] * 2,
-        [smem] + [vmem] * 4 + [anywhere],
+        [smem] + [vmem] * 3 + [anywhere],
         [
             pltpu.VMEM((waves, own), f32),
             pltpu.VMEM((8, own), f32),
@@ -905,7 +923,7 @@
             pltpu.VMEM((8, own, own), bf16),
         ],
         cost=work(3),
-    )(core, got, waves_x, high, low, token0)
+    )(core, got, waves_x, planes, token0)
     swap, rings = partners()
     both = ("gx", "gy")
 
@@ -927,27 +945,27 @@
     potential, spectrum = call(
         potential_kernel,
         [((ranks, 8, own), f32), ((waves, 256), f32)],
-        [smem] + [vmem] * 7,
+        [smem] + [vmem] * 6,
         [
             pltpu.VMEM((272, own), bf16),
             pltpu.VMEM((272, own), bf16),
             pltpu.VMEM((8, 272, own), f32),
         ],
         cost=work(2),
-    )(core, summed, opposite, weights, lone_weights, waves_x, high, low)
+    )(core, summed, opposite, weights, lone_weights, waves_x, planes)
     shares = lax.all_to_all(potential, "ka", 0, 0)
     lines = call(
         gradient_kernel,
         [((ranks, 8, 128), f32)],
-        [smem] * 2 + [vmem] * 9,
+        [smem] * 2 + [vmem] * 8,
         [
             pltpu.VMEM((waves, 896), f32),
-            pltpu.VMEM((896, own), bf16),
-            pltpu.VMEM((896, own), bf16),
+            pltpu.VMEM((896, 512), bf16),
+            pltpu.VMEM((3 * waves, ranks * own), bf16),
             pltpu.VMEM((8, 784, own), f32),
         ],
         cost=work(5),
-    )(rank, core, edges, summed, opposite, weights, spectrum, got, waves_x, high, low)[0]
+    )(rank, core, edges, summed, opposite, weights, spectrum, got, waves_x, planes)[0]
     pairs = (shares, *response0, *response1, *response2, disp, listing)
 
     def pull(ghosts, outs, operands):
@@ -956,23 +974,23 @@
             outs,
             [vmem] * len(operands),
             [
-                pltpu.VMEM((4, 96, chunk * own), bf16),
+                pltpu.VMEM((4, 48 if ghosts else 144, chunk * own), bf16),
                 pltpu.VMEM((4, 128, chunk * own), bf16),
-                pltpu.VMEM((96, 128), f32),
+                pltpu.VMEM((128, 48) if ghosts else (144, 128), f32),
                 pltpu.VMEM((3, chunk, own), f32),
             ],
             cost=work(2),
         )(*operands)
 
-    cells0, cells3, mid0, mid3 = pull(
-        True, [((16, 128), f32), ((16, 128), f32), ((8, 128), f32), ((8, 128), f32)], pairs
-    )
-    domain, direct = pull(False, [((ranks, 8, 128), f32), ((8, 128), f32)], pairs + (lines,))
+    cells0, cells3 = pull(True, [((16, 128), f32)] * 2, pairs)
+    domain, direct, mid0, mid3 = pull(
+        False, [((ranks, 8, 128), f32)] + [((8, 128), f32)] * 3, pairs + (lines,)
+    )
     from_above = lax.ppermute(cells0, "gy", shift("gy", -1))
     from_below = lax.ppermute(cells3, "gy", shift("gy", 1))
     send0, send3, inner0, inner1 = call(
-        echo_kernel, [((8, 128), f32)] * 4, [vmem] * 4 + [anywhere]
-    )(from_above, from_below, mid0, mid3, domain)
+        echo_kernel, [((8, 128), f32)] * 4, [vmem] * 4
+    )(from_above, from_below, mid0, mid3)
     from_right = lax.ppermute(send0, "gx", shift("gx", -1))
     from_left = lax.ppermute(send3, "gx", shift("gx", 1))
     reaction = call(border_back_kernel, [((ranks, 8, 128), f32)], [vmem] * 6)(

time: 109 us -> 109 us (level)
  Pallas kernels: 29.6 us -> 27.5 us
    all_to_all x1, waiting for transfers between devices: 4.11 us -> 5.23 us  [body(): table = lax.all_to_all(packed, 'ka', 0, 0)]
    pallas_call x1, Pallas kernels: 3.9 us -> 2.78 us  [body(): call(prepare_kernel, [((8, own), f32), ((slots, own), i32), ((1, own), i3...]
  transfers between devices with their start and end apart: 19 -> 19, of which waited for: 16 -> 14; matrix products, arithmetic and copies ran while one was open for 0% -> 0% of each run, Pallas kernels for 17% -> 15%
where the time goes in v6:
time: 109 us; the launch traced here: 108 us
  waiting for transfers between devices  36.8 us (34%)
  starting transfers between devices  31.9 us (29%)
  Pallas kernels  27.5 us (25%)
  blocking collectives  11 us (10%)
    all_to_all x1, blocking collectives, body(): returned = lax.all_to_all(reaction, 'ka', 0, 0)  11 us
    all_to_all x1, starting transfers between devices, body(): table = lax.all_to_all(packed, 'ka', 0, 0)  8.48 us
    ppermute x6, starting transfers between devices, body(): lax.ppermute(summed, both, turn)  7.26 us
    all_to_all x1, waiting for transfers between devices, body(): got = lax.all_to_all(send, 'ka', 0, 0)  7.14 us
    ppermute x6, waiting for transfers between devices, body(): lax.ppermute(summed, both, turn)  6.67 us
    all_to_all x1, waiting for transfers between devices, body(): table = lax.all_to_all(packed, 'ka', 0, 0)  5.23 us
    pallas_call x3, Pallas kernels, respond(): call(functools.partial(response_kernel, begin, count, started), outs, [vm...  5.2 us
    all_to_all x1, waiting for transfers between devices, body(): shares = lax.all_to_all(potential, 'ka', 0, 0)  4.7 us
  transfers between devices with their start and end apart: 19, of which 14 were waited for; matrix products, arithmetic and copies ran while one was open for 0% of the time, Pallas kernels for 15%

profile of v6, /device:TPU:14, one launch (start us, length us, event | category | flops | bytes accessed | tf_op | source)
XLA Modules:
  0.0 108.1 jit_solution(6904010214144838570)
XLA Ops:
  0.6 1.3 %shard_map.176 = (f32[8,8,128]{2,1,0:T(8,128)}, f32[3,256]{1,0:T(4,128)S(1)}, s32[1,256]{1,0:T(1,128)S(1)}) custom-call(f32[3,256]{1,0:T(4,128)} %place_far.1, s32[1,256]{1,0:T(1,128)} %bitcast.8), custom_call_target="tpu_custom_call" | custom-call | tf_op jit(solution)/shard_map/pallas_call | solution.py:802
  2.0 8.5 %all-to-all-start = ((f32[8,8,128]{2,1,0:T(8,128)}), f32[8,8,128]{2,1,0:T(8,128)S(1)}, u32[]{:S(2)}, u32[]{:S(2)}) async-start(f32[8,8,128]{2,1,0:T(8,128)} %get-tuple-element.54), calls=%async_computation | async-start | bytes 65536 | tf_op jit(solution)/shard_map/all_to_all | solution.py:808
  10.4 2.8 %shard_map.175 = (f32[8,256]{1,0:T(8,128)S(1)}, s32[64,256]{1,0:T(8,128)S(1)}, s32[1,256]{1,0:T(1,128)S(1)}, s32[2,2,128]{2,1,0:T(2,128)S(1)}, f32[8,24,128]{2,1...) custom-call(f32[3]{0:T(128)} %edges_far.1, ...), custom_call_target="tpu_custom_call" | custom-call | flops 4000000000 | bytes 16000000 | tf_op jit(solution)/shard_map/pallas_call | solution.py:809
  13.2 5.2 %all-to-all-done.table = f32[8,8,128]{2,1,0:T(8,128)S(1)} async-done(((f32[8,8,128]{2,1,0:T(8,128)}), f32[8,8,128]{2,1,0:T(8,128)S(1)}, u32[]{:S(2)}, u32[]{:S(2)}) %all-to-all-start) | async-done | bytes 32800 | tf_op jit(solution)/shard_map/all_to_all | solution.py:808
  18.5 0.1 shard_map.178
  18.7 3.2 %collective-permute-start.1 = (f32[8,128]{1,0:T(8,128)S(1)}, f32[8,128]{1,0:T(8,128)S(1)}, u32[]{:S(2)}, u32[]{:S(2)}) collective-permute-start(f32[8,128]{1,0:T(8,128)S(1)} %get-tuple-element.57.cell0), channel_id=1, source_target_pairs={{0,24},{8,0},{16,8},{24,16},{1,25},{9,1},{17,9},{25,17},{2,26},{10... | collective-permute-start | bytes 12296 | tf_op jit(solution)/shard_map/ppermute | solution.py:857
  21.9 1.3 %shard_map.177.after.near = f32[4,64,256]{2,1,0:T(8,128)S(1)} custom-call(f32[8,8,128]{2,1,0:T(8,128)S(1)} %all-to-all-done.table, s32[64,256]{1,0:T(8,128)S(1)} %get-tuple-element.53.listing), custom_call_target="tpu_custom_call" | custom-call | flops 1000000000 | bytes 4000000 | tf_op jit(solution)/shard_map/pallas_call | solution.py:858
  23.3 0.4 collective-permute-start.2
  23.7 1.7 %collective-permute-start.3 = (f32[16,128]{1,0:T(8,128)S(1)}, f32[16,128]{1,0:T(8,128)S(1)}, u32[]{:S(2)}, u32[]{:S(2)}) collective-permute-start(f32[16,128]{1,0:T(8,128)S(1)} %get-tuple-element.59), channel_id=1, source_target_pairs={{0,224},{32,0},{64,32},{96,64},{128,96},{160,128},{192,160},{224,1... | collective-permute-start | bytes 24584 | tf_op jit(solution)/shard_map/ppermute | solution.py:865
  25.3 1.3 %shard_map.180 = (bf16[288,2048]{1,0:T(8,128)(2,1)S(1)}, f32[32,2048]{1,0:T(8,128)S(1)}) custom-call(s32[1]{0:T(128)} %bitcast.7.rank, f32[8,8,128]{2,1,0:T(8,128)S(1)} %all-to-all-done.table), custom_call_target="tpu_custom_call" | custom-call | flops 1000000000 | bytes 4000000 | tf_op jit(solution)/shard_map/pallas_call | solution.py:866
  26.6 0.3 collective-permute-done.2.left
  27.0 2.5 %collective-permute-done.3.right = f32[16,128]{1,0:T(8,128)S(1)} collective-permute-done((f32[16,128]{1,0:T(8,128)S(1)}, f32[16,128]{1,0:T(8,128)S(1)}, u32[]{:S(2)}, u32[]{:S(2)}) %collective-permute-start.3) | collective-permute-done | bytes 8224 | tf_op jit(solution)/shard_map/ppermute | solution.py:865
  29.4 4.2 %shard_map.181 = (f32[8,40,128]{2,1,0:T(8,128)}, f32[16,256]{1,0:T(8,128)S(1)}, f32[3,64,256]{2,1,0:T(8,128)S(1)}, f32[64,256]{1,0:T(8,128)S(1)}) custom-call(f32[8,256]{1,0:T(8,128)S(1)} %get-tuple-element.52.edges, s32[64,256]{1,0:T(8,128)S(1)} %get-tuple-element.53.listing, f32[4,64,256]{2,1,0:T(8,128)S(1)} %shard_map.177.after.near, ...), custom_call_target="tpu_custom_call" | custom-call | flops 4000000000 | bytes 16000000 | tf_op jit(solution)/shard_map/pallas_call | solution.py:873
  33.6 3.4 %all-to-all-start.1 = ((f32[8,40,128]{2,1,0:T(8,128)}), f32[8,40,128]{2,1,0:T(8,128)S(1)}, u32[]{:S(2)}, u32[]{:S(2)}) async-start(f32[8,40,128]{2,1,0:T(8,128)} %get-tuple-element.76), calls=%async_computation.1 | async-start | bytes 327680 | tf_op jit(solution)/shard_map/all_to_all | solution.py:892
  37.0 2.9 %shard_map.182 = (f32[32,8,256]{2,1,0:T(8,128)S(1)}, f32[32,256]{1,0:T(8,128)S(1)}, f32[8,128]{1,0:T(8,128)S(1)}, f32[384,256]{1,0:T(8,128)S(1)}) custom-call(f32[16,256]{1,0:T(8,128)S(1)} %get-tuple-element.68.refs_0_, f32[16,1]{1,0:T(8,128)S(1)} %get-tuple-element.69.refs_1_, f32[24,384]{1,0:T(8,128)S(1)} %get-tuple-element.65.ball.refs_2_, ...), custom_call_target="tpu_custom_call" | custom-call | flops 2000000000 | bytes 8000000 | tf_op jit(solution)/shard_map/pallas_call | solution.py:899
  39.9 7.1 %all-to-all-done.1.got = f32[8,40,128]{2,1,0:T(8,128)S(1)} async-done(((f32[8,40,128]{2,1,0:T(8,128)}), f32[8,40,128]{2,1,0:T(8,128)S(1)}, u32[]{:S(2)}, u32[]{:S(2)}) %all-to-all-start.1) | async-done | bytes 163872 | tf_op jit(solution)/shard_map/all_to_all | solution.py:892
  47.1 1.6 %shard_map.185 = (f32[80,256]{1,0:T(8,128)S(1)}, f32[80,256]{1,0:T(8,128)S(1)}) custom-call(s32[1]{0:T(128)} %bitcast.5.core, f32[8,40,128]{2,1,0:T(8,128)S(1)} %all-to-all-done.1.got, f32[32,2048]{1,0:T(8,128)S(1)} %get-tuple-element.67.after.waves_x, bf16[288,2048]{1,0:T(8,128)(2,1)S(1)} %get-tuple-element.77.planes, f32[8,128]{1,0:T(8,128)S(1)} %get-tuple-element.78.after), custom_call_target="tpu_custom_call" | custom-call | flops 1500000000 | bytes 6000000 | tf_op jit(solution)/shard_map/pallas_call | solution.py:915
  48.6 1.0 collective-permute-start.4
  49.6 0.9 collective-permute-done.4
  50.5 0.4 collective-permute-start.5
  50.9 1.9 %collective-permute-start.6 = (f32[80,256]{1,0:T(8,128)S(1)}, f32[80,256]{1,0:T(8,128)S(1)}, u32[]{:S(2)}, u32[]{:S(2)}) collective-permute-start(f32[80,256]{1,0:T(8,128)S(1)} %add.8.refs_0_), channel_id=1, source_target_pairs={{0,48},{8,56},{32,0},{40,8},{16,32},{24,40},{48,16},{56,24},{64,11... | collective-permute-start | bytes 245768 | tf_op jit(solution)/shard_map/ppermute | solution.py:937
  52.8 1.7 %collective-permute-start.7 = (f32[80,256]{1,0:T(8,128)S(1)}, f32[80,256]{1,0:T(8,128)S(1)}, u32[]{:S(2)}, u32[]{:S(2)}) collective-permute-start(f32[80,256]{1,0:T(8,128)S(1)} %add.8.refs_0_), channel_id=1, source_target_pairs={{0,16},{8,24},{32,48},{40,56},{16,0},{24,8},{48,32},{56,40},{64,80... | collective-permute-start | bytes 245768 | tf_op jit(solution)/shard_map/ppermute | solution.py:937
  54.5 1.2 %shard_map.184 = (f32[16,8,256]{2,1,0:T(8,128)S(1)}, f32[16,256]{1,0:T(8,128)S(1)}, f32[8,128]{1,0:T(8,128)S(1)}) custom-call(f32[384,256]{1,0:T(8,128)S(1)} %get-tuple-element.73.refs_0_, f32[3,64,256]{2,1,0:T(8,128)S(1)} %get-tuple-element.70.refs_3_.refs_1_.disp, f32[64,256]{1,0:T(8,128)S(1)} %get-tuple-element.71.refs_4_.refs_2_, ...), custom_call_target="tpu_custom_call" | custom-call | flops 1000000000 | bytes 4000000 | tf_op jit(solution)/shard_map/pallas_call | solution.py:899
  55.7 3.1 %collective-permute-done.7.refs_3_ = f32[80,256]{1,0:T(8,128)S(1)} collective-permute-done((f32[80,256]{1,0:T(8,128)S(1)}, f32[80,256]{1,0:T(8,128)S(1)}, u32[]{:S(2)}, u32[]{:S(2)}) %collective-permute-start.7) | collective-permute-done | bytes 81952 | tf_op jit(solution)/shard_map/ppermute | solution.py:937
  58.8 0.4 collective-permute-start.8
  59.2 1.7 %collective-permute-start.9 = (f32[80,256]{1,0:T(8,128)S(1)}, f32[80,256]{1,0:T(8,128)S(1)}, u32[]{:S(2)}, u32[]{:S(2)}) collective-permute-start(f32[80,256]{1,0:T(8,128)S(1)} %shard_map.186.refs_0_), channel_id=1, source_target_pairs={{0,192},{8,200},{32,224},{40,232},{16,208},{24,216},{48,240},{56,2... | collective-permute-start | bytes 245768 | tf_op jit(solution)/shard_map/ppermute | solution.py:937
  60.9 1.2 %collective-permute-start.10 = (f32[80,256]{1,0:T(8,128)S(1)}, f32[80,256]{1,0:T(8,128)S(1)}, u32[]{:S(2)}, u32[]{:S(2)}) collective-permute-start(f32[80,256]{1,0:T(8,128)S(1)} %shard_map.186.refs_0_), channel_id=1, source_target_pairs={{0,128},{8,136},{32,160},{40,168},{16,144},{24,152},{48,176},{56,1... | collective-permute-start | bytes 245768 | tf_op jit(solution)/shard_map/ppermute | solution.py:937
  62.1 1.2 %shard_map.183 = (f32[16,8,256]{2,1,0:T(8,128)S(1)}, f32[16,256]{1,0:T(8,128)S(1)}, f32[8,128]{1,0:T(8,128)S(1)}) custom-call(f32[384,256]{1,0:T(8,128)S(1)} %get-tuple-element.73.refs_0_, f32[3,64,256]{2,1,0:T(8,128)S(1)} %get-tuple-element.70.refs_3_.refs_1_.disp, f32[64,256]{1,0:T(8,128)S(1)} %get-tuple-element.71.refs_4_.refs_2_, ...), custom_call_target="tpu_custom_call" | custom-call | flops 1000000000 | bytes 4000000 | tf_op jit(solution)/shard_map/pallas_call | solution.py:899
  63.3 0.7 collective-permute-done.8.refs_1_
  63.9 1.3 %collective-permute-done.9.refs_2_ = f32[80,256]{1,0:T(8,128)S(1)} collective-permute-done((f32[80,256]{1,0:T(8,128)S(1)}, f32[80,256]{1,0:T(8,128)S(1)}, u32[]{:S(2)}, u32[]{:S(2)}) %collective-permute-start.9) | collective-permute-done | bytes 81952 | tf_op jit(solution)/shard_map/ppermute | solution.py:937
  65.2 1.6 %collective-permute-done.10.refs_3_ = f32[80,256]{1,0:T(8,128)S(1)} collective-permute-done((f32[80,256]{1,0:T(8,128)S(1)}, f32[80,256]{1,0:T(8,128)S(1)}, u32[]{:S(2)}, u32[]{:S(2)}) %collective-permute-start.10) | collective-permute-done | bytes 81952 | tf_op jit(solution)/shard_map/ppermute | solution.py:937
  67.0 0.6 shard_map.188
  67.5 0.7 collective-permute-done.11.other
  68.2 1.8 %shard_map.189 = (f32[8,8,256]{2,1,0:T(8,128)}, f32[144,256]{1,0:T(8,128)S(1)}) custom-call(s32[1]{0:T(128)} %bitcast.5.core, f32[80,256]{1,0:T(8,128)S(1)} %shard_map.187.mine, f32[80,256]{1,0:T(8,128)S(1)} %collective-permute-done.11.other, f32[3,72,128]{2,1,0:T(8,128)S(1)} %get-tuple-element.81.weights, f32[8,256]{1,0:T(8,128)S(1)} %get-tuple-element.82.lone_weights, ...), custom_call_target="tpu_custom_call" | custom-call | flops 1000000000 | bytes 4000000 | tf_op jit(solution)/shard_map/pallas_call | solution.py:945
  70.0 3.3 %all-to-all-start.2 = ((f32[8,8,256]{2,1,0:T(8,128)}), f32[8,8,256]{2,1,0:T(8,128)S(1)}, u32[]{:S(2)}, u32[]{:S(2)}) async-start(f32[8,8,256]{2,1,0:T(8,128)} %get-tuple-element.83), calls=%async_computation.2 | async-start | bytes 131072 | tf_op jit(solution)/shard_map/all_to_all | solution.py:956
  73.4 3.6 %shard_map.191.refs_0_ = f32[8,8,128]{2,1,0:T(8,128)S(1)} custom-call(s32[1]{0:T(128)} %bitcast.7.rank, s32[1]{0:T(128)} %bitcast.5.core, f32[8,256]{1,0:T(8,128)S(1)} %get-tuple-element.52.edges, f32[80,256]{1,0:T(8,128)S(1)} %shard_map.187.mine, f32[80,256]{1,0:T(8,128)S(1)} %collective-permute-done.11.other, f32[3,72,128]{2,1,0:T(8,128)S(1)} %get-tuple-element.81.weights, ...), custom_call_target="tpu_custom_call" | custom-call | flops 2500000000 | bytes 10000000 | tf_op jit(solution)/shard_map/pallas_call | solution.py:957
  77.0 4.7 %all-to-all-done.2.got = f32[8,8,256]{2,1,0:T(8,128)S(1)} async-done(((f32[8,8,256]{2,1,0:T(8,128)}), f32[8,8,256]{2,1,0:T(8,128)S(1)}, u32[]{:S(2)}, u32[]{:S(2)}) %all-to-all-start.2) | async-done | bytes 65568 | tf_op jit(solution)/shard_map/all_to_all | solution.py:956
  81.7 1.4 %shard_map.190 = (f32[16,128]{1,0:T(8,128)S(1)}, f32[16,128]{1,0:T(8,128)S(1)}) custom-call(f32[8,8,256]{2,1,0:T(8,128)S(1)} %all-to-all-done.2.got, f32[32,8,256]{2,1,0:T(8,128)S(1)} %get-tuple-element.84.r0, f32[32,256]{1,0:T(8,128)S(1)} %get-tuple-element.85.e0, f32[16,8,256]{2,1,0:T(8,128)S(1)} %get-tuple-element.86.r1, ...), custom_call_target="tpu_custom_call" | custom-call | flops 1000000000 | bytes 4000000 | tf_op jit(solution)/shard_map/pallas_call | solution.py:972
  83.1 0.3 collective-permute-start.12
  83.4 0.2 collective-permute-start.13
  83.7 1.5 %shard_map.192 = (f32[8,8,128]{2,1,0:T(8,128)S(1)}, f32[8,128]{1,0:T(8,128)S(1)}, f32[8,128]{1,0:T(8,128)S(1)}, f32[8,128]{1,0:T(8,128)S(1)}) custom-call(f32[8,8,256]{2,1,0:T(8,128)S(1)} %all-to-all-done.2.got, f32[32,8,256]{2,1,0:T(8,128)S(1)} %get-tuple-element.84.r0, f32[32,256]{1,0:T(8,128)S(1)} %get-tuple-element.85.e0, ...), custom_call_target="tpu_custom_call" | custom-call | flops 1000000000 | bytes 4000000 | tf_op jit(solution)/shard_map/pallas_call | solution.py:972
  85.2 2.9 %collective-permute-done.13.below = f32[16,128]{1,0:T(8,128)S(1)} collective-permute-done((f32[16,128]{1,0:T(8,128)S(1)}, f32[16,128]{1,0:T(8,128)S(1)}, u32[]{:S(2)}, u32[]{:S(2)}) %collective-permute-start.13) | collective-permute-done | bytes 8224 | tf_op jit(solution)/shard_map/ppermute | solution.py:990
  88.1 2.4 %collective-permute-start.14 = (f32[8,128]{1,0:T(8,128)S(1)}, f32[8,128]{1,0:T(8,128)S(1)}, u32[]{:S(2)}, u32[]{:S(2)}) collective-permute-start(f32[8,128]{1,0:T(8,128)S(1)} %get-tuple-element.97), channel_id=1, source_target_pairs={{0,32},{32,64},{64,96},{96,128},{128,160},{160,192},{192,224},{224... | collective-permute-start | bytes 12296 | tf_op jit(solution)/shard_map/ppermute | solution.py:995
  90.5 1.3 %collective-permute-done.14.from_left = f32[8,128]{1,0:T(8,128)S(1)} collective-permute-done((f32[8,128]{1,0:T(8,128)S(1)}, f32[8,128]{1,0:T(8,128)S(1)}, u32[]{:S(2)}, u32[]{:S(2)}) %collective-permute-start.14) | collective-permute-done | bytes 4128 | tf_op jit(solution)/shard_map/ppermute | solution.py:995
  91.8 4.4 %collective-permute-done.15.from_right = f32[8,128]{1,0:T(8,128)S(1)} collective-permute-done((f32[8,128]{1,0:T(8,128)S(1)}, f32[8,128]{1,0:T(8,128)S(1)}, u32[]{:S(2)}, u32[]{:S(2)}) %collective-permute-start.15) | collective-permute-done | bytes 4128 | tf_op jit(solution)/shard_map/ppermute | solution.py:994
  96.2 0.2 shard_map.194
  96.5 11.0 %all_to_all.20.got = f32[8,8,128]{2,1,0:T(8,128)S(1)} all-to-all(f32[8,8,128]{2,1,0:T(8,128)S(1)} %shard_map.194), channel_id=1, replica_groups=mesh['gx'=8,'gy'=4,'ka'=8] {'ka'}, dimensions={0} | all-to-all | bytes 65536 | tf_op jit(solution)/shard_map/all_to_all | solution.py:999
  107.5 0.6 shard_map.195
  (17 shorter events, 0.3 us)
Async XLA Ops:
  2.0 16.5 %all-to-all-start = ((f32[8,8,128]{2,1,0:T(8,128)}), f32[8,8,128]{2,1,0:T(8,128)S(1)}, u32[]{:S(2)}, u32[]{:S(2)}) async-start(f32[8,8,128]{2,1,0:T(8,128)} %get-tuple-element.54), calls=%async_computation | async-start | bytes 65536 | tf_op jit(solution)/shard_map/all_to_all | solution.py:808
  18.6 4.6 %collective-permute-start = (f32[8,128]{1,0:T(8,128)S(1)}, f32[8,128]{1,0:T(8,128)S(1)}, u32[]{:S(2)}, u32[]{:S(2)}) collective-permute-start(f32[8,128]{1,0:T(8,128)S(1)} %get-tuple-element.56.cell1), channel_id=1, source_target_pairs={{0,8},{8,16},{16,24},{24,0},{1,9},{9,17},{17,25},{25,1},{2,10},{10... | collective-permute-start | bytes 12296 | tf_op jit(solution)/shard_map/ppermute | solution.py:856
  18.7 4.6 %collective-permute-start.1 = (f32[8,128]{1,0:T(8,128)S(1)}, f32[8,128]{1,0:T(8,128)S(1)}, u32[]{:S(2)}, u32[]{:S(2)}) collective-permute-start(f32[8,128]{1,0:T(8,128)S(1)} %get-tuple-element.57.cell0), channel_id=1, source_target_pairs={{0,24},{8,0},{16,8},{24,16},{1,25},{9,1},{17,9},{25,17},{2,26},{10... | collective-permute-start | bytes 12296 | tf_op jit(solution)/shard_map/ppermute | solution.py:857
  23.3 3.7 %collective-permute-start.2 = (f32[16,128]{1,0:T(8,128)S(1)}, f32[16,128]{1,0:T(8,128)S(1)}, u32[]{:S(2)}, u32[]{:S(2)}) collective-permute-start(f32[16,128]{1,0:T(8,128)S(1)} %get-tuple-element.58), channel_id=1, source_target_pairs={{0,32},{32,64},{64,96},{96,128},{128,160},{160,192},{192,224},{224... | collective-permute-start | bytes 24584 | tf_op jit(solution)/shard_map/ppermute | solution.py:864
  23.7 5.8 %collective-permute-start.3 = (f32[16,128]{1,0:T(8,128)S(1)}, f32[16,128]{1,0:T(8,128)S(1)}, u32[]{:S(2)}, u32[]{:S(2)}) collective-permute-start(f32[16,128]{1,0:T(8,128)S(1)} %get-tuple-element.59), channel_id=1, source_target_pairs={{0,224},{32,0},{64,32},{96,64},{128,96},{160,128},{192,160},{224,1... | collective-permute-start | bytes 24584 | tf_op jit(solution)/shard_map/ppermute | solution.py:865
  33.6 13.4 %all-to-all-start.1 = ((f32[8,40,128]{2,1,0:T(8,128)}), f32[8,40,128]{2,1,0:T(8,128)S(1)}, u32[]{:S(2)}, u32[]{:S(2)}) async-start(f32[8,40,128]{2,1,0:T(8,128)} %get-tuple-element.76), calls=%async_computation.1 | async-start | bytes 327680 | tf_op jit(solution)/shard_map/all_to_all | solution.py:892
  48.6 1.9 %collective-permute-start.4 = (f32[80,256]{1,0:T(8,128)S(1)}, f32[80,256]{1,0:T(8,128)S(1)}, u32[]{:S(2)}, u32[]{:S(2)}) collective-permute-start(f32[80,256]{1,0:T(8,128)S(1)} %get-tuple-element.80), channel_id=1, source_target_pairs={{0,8},{8,0},{32,40},{40,32},{16,24},{24,16},{48,56},{56,48},{64,72... | collective-permute-start | bytes 245768 | tf_op jit(solution)/shard_map/ppermute | solution.py:935
  50.5 5.1 %collective-permute-start.5 = (f32[80,256]{1,0:T(8,128)S(1)}, f32[80,256]{1,0:T(8,128)S(1)}, u32[]{:S(2)}, u32[]{:S(2)}) collective-permute-start(f32[80,256]{1,0:T(8,128)S(1)} %add.8.refs_0_), channel_id=1, source_target_pairs={{0,32},{8,40},{32,16},{40,24},{16,48},{24,56},{48,0},{56,8},{64,96... | collective-permute-start | bytes 245768 | tf_op jit(solution)/shard_map/ppermute | solution.py:937
  50.9 4.8 %collective-permute-start.6 = (f32[80,256]{1,0:T(8,128)S(1)}, f32[80,256]{1,0:T(8,128)S(1)}, u32[]{:S(2)}, u32[]{:S(2)}) collective-permute-start(f32[80,256]{1,0:T(8,128)S(1)} %add.8.refs_0_), channel_id=1, source_target_pairs={{0,48},{8,56},{32,0},{40,8},{16,32},{24,40},{48,16},{56,24},{64,11... | collective-permute-start | bytes 245768 | tf_op jit(solution)/shard_map/ppermute | solution.py:937
  52.8 5.9 %collective-permute-start.7 = (f32[80,256]{1,0:T(8,128)S(1)}, f32[80,256]{1,0:T(8,128)S(1)}, u32[]{:S(2)}, u32[]{:S(2)}) collective-permute-start(f32[80,256]{1,0:T(8,128)S(1)} %add.8.refs_0_), channel_id=1, source_target_pairs={{0,16},{8,24},{32,48},{40,56},{16,0},{24,8},{48,32},{56,40},{64,80... | collective-permute-start | bytes 245768 | tf_op jit(solution)/shard_map/ppermute | solution.py:937
  58.8 5.1 %collective-permute-start.8 = (f32[80,256]{1,0:T(8,128)S(1)}, f32[80,256]{1,0:T(8,128)S(1)}, u32[]{:S(2)}, u32[]{:S(2)}) collective-permute-start(f32[80,256]{1,0:T(8,128)S(1)} %shard_map.186.refs_0_), channel_id=1, source_target_pairs={{0,64},{8,72},{32,96},{40,104},{16,80},{24,88},{48,112},{56,120},{... | collective-permute-start | bytes 245768 | tf_op jit(solution)/shard_map/ppermute | solution.py:937
  59.2 6.1 %collective-permute-start.9 = (f32[80,256]{1,0:T(8,128)S(1)}, f32[80,256]{1,0:T(8,128)S(1)}, u32[]{:S(2)}, u32[]{:S(2)}) collective-permute-start(f32[80,256]{1,0:T(8,128)S(1)} %shard_map.186.refs_0_), channel_id=1, source_target_pairs={{0,192},{8,200},{32,224},{40,232},{16,208},{24,216},{48,240},{56,2... | collective-permute-start | bytes 245768 | tf_op jit(solution)/shard_map/ppermute | solution.py:937
  60.9 5.9 %collective-permute-start.10 = (f32[80,256]{1,0:T(8,128)S(1)}, f32[80,256]{1,0:T(8,128)S(1)}, u32[]{:S(2)}, u32[]{:S(2)}) collective-permute-start(f32[80,256]{1,0:T(8,128)S(1)} %shard_map.186.refs_0_), channel_id=1, source_target_pairs={{0,128},{8,136},{32,160},{40,168},{16,144},{24,152},{48,176},{56,1... | collective-permute-start | bytes 245768 | tf_op jit(solution)/shard_map/ppermute | solution.py:937
  66.9 1.4 %collective-permute-start.11 = (f32[80,256]{1,0:T(8,128)S(1)}, f32[80,256]{1,0:T(8,128)S(1)}, u32[]{:S(2)}, u32[]{:S(2)}) collective-permute-start(f32[80,256]{1,0:T(8,128)S(1)} %shard_map.187.mine), channel_id=1, source_target_pairs={{0,8},{8,0},{32,40},{40,32},{16,24},{24,16},{48,56},{56,48},{64,72... | collective-permute-start | bytes 245768 | tf_op jit(solution)/shard_map/ppermute | solution.py:938
  70.0 11.7 %all-to-all-start.2 = ((f32[8,8,256]{2,1,0:T(8,128)}), f32[8,8,256]{2,1,0:T(8,128)S(1)}, u32[]{:S(2)}, u32[]{:S(2)}) async-start(f32[8,8,256]{2,1,0:T(8,128)} %get-tuple-element.83), calls=%async_computation.2 | async-start | bytes 131072 | tf_op jit(solution)/shard_map/all_to_all | solution.py:956
  83.1 2.1 %collective-permute-start.12 = (f32[16,128]{1,0:T(8,128)S(1)}, f32[16,128]{1,0:T(8,128)S(1)}, u32[]{:S(2)}, u32[]{:S(2)}) collective-permute-start(f32[16,128]{1,0:T(8,128)S(1)} %get-tuple-element.90), channel_id=1, source_target_pairs={{0,24},{8,0},{16,8},{24,16},{1,25},{9,1},{17,9},{25,17},{2,26},{10... | collective-permute-start | bytes 24584 | tf_op jit(solution)/shard_map/ppermute | solution.py:989
  83.4 24.0 %copy-start = (f32[3,256]{1,0:T(4,128)S(1)}, f32[3,256]{1,0:T(4,128)}, u32[]{:S(2)}) copy-start(f32[3,256]{1,0:T(4,128)} %speed.1) | copy-start | bytes 9220
  83.4 24.0 %copy-start.1 = (f32[3,256]{1,0:T(4,128)S(1)}, f32[3,256]{1,0:T(4,128)}, u32[]{:S(2)}) copy-start(f32[3,256]{1,0:T(4,128)} %kicks.1) | copy-start | bytes 9220
  83.4 4.6 %collective-permute-start.13 = (f32[16,128]{1,0:T(8,128)S(1)}, f32[16,128]{1,0:T(8,128)S(1)}, u32[]{:S(2)}, u32[]{:S(2)}) collective-permute-start(f32[16,128]{1,0:T(8,128)S(1)} %get-tuple-element.91), channel_id=1, source_target_pairs={{0,8},{8,16},{16,24},{24,0},{1,9},{9,17},{17,25},{25,1},{2,10},{10... | collective-permute-start | bytes 24584 | tf_op jit(solution)/shard_map/ppermute | solution.py:990
  88.1 3.8 %collective-permute-start.14 = (f32[8,128]{1,0:T(8,128)S(1)}, f32[8,128]{1,0:T(8,128)S(1)}, u32[]{:S(2)}, u32[]{:S(2)}) collective-permute-start(f32[8,128]{1,0:T(8,128)S(1)} %get-tuple-element.97), channel_id=1, source_target_pairs={{0,32},{32,64},{64,96},{96,128},{128,160},{160,192},{192,224},{224... | collective-permute-start | bytes 12296 | tf_op jit(solution)/shard_map/ppermute | solution.py:995
  90.5 5.7 %collective-permute-start.15 = (f32[8,128]{1,0:T(8,128)S(1)}, f32[8,128]{1,0:T(8,128)S(1)}, u32[]{:S(2)}, u32[]{:S(2)}) collective-permute-start(f32[8,128]{1,0:T(8,128)S(1)} %get-tuple-element.98), channel_id=1, source_target_pairs={{0,224},{32,0},{64,32},{96,64},{128,96},{160,128},{192,160},{224,1... | collective-permute-start | bytes 12296 | tf_op jit(solution)/shard_map/ppermute | solution.py:994

commit v7 on v6

--- a/solution.py
+++ b/solution.py
@@ -330,7 +330,9 @@
         )
         upper, lower = split(basis)
         half_pre = dot_n(first[...], jnp.concatenate([upper, lower, upper], axis=0))
-        active[...] = half_pre + half_pre * jnp.tanh(half_pre)
+        below = 1.0 + jnp.exp(-2.0 * half_pre)
+        guess = pl.reciprocal(below, approx=True)
+        active[...] = (2.0 * half_pre) * (guess * (2.0 - below * guess))
         for s in range(kinds):
             total = [pooled[s * hidden + b : s * hidden + b + 8, :] for b in range(0, hidden, 8)]
             for m in range(chunk):

time: 109 us -> 109 us (level)
  Pallas kernels: 27.5 us -> 28.6 us
where the time goes in v7:
time: 109 us
  waiting for transfers between devices  36.4 us (33%)
  starting transfers between devices  31.9 us (29%)
  Pallas kernels  28.6 us (26%)
  blocking collectives  11.2 us (10%)
    all_to_all x1, blocking collectives, body(): returned = lax.all_to_all(reaction, 'ka', 0, 0)  11.2 us
    all_to_all x1, starting transfers between devices, body(): table = lax.all_to_all(packed, 'ka', 0, 0)  8.48 us
    ppermute x6, starting transfers between devices, body(): lax.ppermute(summed, both, turn)  7.1 us
    all_to_all x1, waiting for transfers between devices, body(): got = lax.all_to_all(send, 'ka', 0, 0)  7.04 us
    ppermute x6, waiting for transfers between devices, body(): lax.ppermute(summed, both, turn)  6.65 us
    pallas_call x1, Pallas kernels, body(): call(message_kernel, [((ranks, 40, 128), f32), ((16, own), f32), ((3, slo...  5.25 us
    all_to_all x1, waiting for transfers between devices, body(): table = lax.all_to_all(packed, 'ka', 0, 0)  5.23 us
    pallas_call x3, Pallas kernels, respond(): call(functools.partial(response_kernel, begin, count, started), outs, [vm...  5.2 us
  transfers between devices with their start and end apart: 19, of which 14 were waited for; matrix products, arithmetic and copies ran while one was open for 0% of the time, Pallas kernels for 15%

profile of v7, /device:TPU:14, one launch (start us, length us, event | category | flops | bytes accessed | tf_op | source)
XLA Modules:
  0.0 109.0 jit_solution(18080989540776039685)
XLA Ops:
  0.6 1.3 %shard_map.176 = (f32[8,8,128]{2,1,0:T(8,128)}, f32[3,256]{1,0:T(4,128)S(1)}, s32[1,256]{1,0:T(1,128)S(1)}) custom-call(f32[3,256]{1,0:T(4,128)} %place_far.1, s32[1,256]{1,0:T(1,128)} %bitcast.8), custom_call_target="tpu_custom_call" | custom-call | tf_op jit(solution)/shard_map/pallas_call | solution.py:804
  2.0 8.5 %all-to-all-start = ((f32[8,8,128]{2,1,0:T(8,128)}), f32[8,8,128]{2,1,0:T(8,128)S(1)}, u32[]{:S(2)}, u32[]{:S(2)}) async-start(f32[8,8,128]{2,1,0:T(8,128)} %get-tuple-element.54), calls=%async_computation | async-start | bytes 65536 | tf_op jit(solution)/shard_map/all_to_all | solution.py:810
  10.4 2.8 %shard_map.175 = (f32[8,256]{1,0:T(8,128)S(1)}, s32[64,256]{1,0:T(8,128)S(1)}, s32[1,256]{1,0:T(1,128)S(1)}, s32[2,2,128]{2,1,0:T(2,128)S(1)}, f32[8,24,128]{2,1...) custom-call(f32[3]{0:T(128)} %edges_far.1, ...), custom_call_target="tpu_custom_call" | custom-call | flops 4000000000 | bytes 16000000 | tf_op jit(solution)/shard_map/pallas_call | solution.py:811
  13.2 5.2 %all-to-all-done.table = f32[8,8,128]{2,1,0:T(8,128)S(1)} async-done(((f32[8,8,128]{2,1,0:T(8,128)}), f32[8,8,128]{2,1,0:T(8,128)S(1)}, u32[]{:S(2)}, u32[]{:S(2)}) %all-to-all-start) | async-done | bytes 32800 | tf_op jit(solution)/shard_map/all_to_all | solution.py:810
  18.5 0.1 shard_map.178
  18.7 3.2 %collective-permute-start.1 = (f32[8,128]{1,0:T(8,128)S(1)}, f32[8,128]{1,0:T(8,128)S(1)}, u32[]{:S(2)}, u32[]{:S(2)}) collective-permute-start(f32[8,128]{1,0:T(8,128)S(1)} %get-tuple-element.57.cell0), channel_id=1, source_target_pairs={{0,24},{8,0},{16,8},{24,16},{1,25},{9,1},{17,9},{25,17},{2,26},{10... | collective-permute-start | bytes 12296 | tf_op jit(solution)/shard_map/ppermute | solution.py:859
  21.9 1.3 %shard_map.177.after.near = f32[4,64,256]{2,1,0:T(8,128)S(1)} custom-call(f32[8,8,128]{2,1,0:T(8,128)S(1)} %all-to-all-done.table, s32[64,256]{1,0:T(8,128)S(1)} %get-tuple-element.53.listing), custom_call_target="tpu_custom_call" | custom-call | flops 1000000000 | bytes 4000000 | tf_op jit(solution)/shard_map/pallas_call | solution.py:860
  23.3 0.4 collective-permute-start.2
  23.7 1.7 %collective-permute-start.3 = (f32[16,128]{1,0:T(8,128)S(1)}, f32[16,128]{1,0:T(8,128)S(1)}, u32[]{:S(2)}, u32[]{:S(2)}) collective-permute-start(f32[16,128]{1,0:T(8,128)S(1)} %get-tuple-element.59), channel_id=1, source_target_pairs={{0,224},{32,0},{64,32},{96,64},{128,96},{160,128},{192,160},{224,1... | collective-permute-start | bytes 24584 | tf_op jit(solution)/shard_map/ppermute | solution.py:867
  25.3 1.3 %shard_map.180 = (bf16[288,2048]{1,0:T(8,128)(2,1)S(1)}, f32[32,2048]{1,0:T(8,128)S(1)}) custom-call(s32[1]{0:T(128)} %bitcast.7.rank, f32[8,8,128]{2,1,0:T(8,128)S(1)} %all-to-all-done.table), custom_call_target="tpu_custom_call" | custom-call | flops 1000000000 | bytes 4000000 | tf_op jit(solution)/shard_map/pallas_call | solution.py:868
  26.6 0.3 collective-permute-done.2.left
  27.0 2.5 %collective-permute-done.3.right = f32[16,128]{1,0:T(8,128)S(1)} collective-permute-done((f32[16,128]{1,0:T(8,128)S(1)}, f32[16,128]{1,0:T(8,128)S(1)}, u32[]{:S(2)}, u32[]{:S(2)}) %collective-permute-start.3) | collective-permute-done | bytes 8224 | tf_op jit(solution)/shard_map/ppermute | solution.py:867
  29.4 5.2 %shard_map.181 = (f32[8,40,128]{2,1,0:T(8,128)}, f32[16,256]{1,0:T(8,128)S(1)}, f32[3,64,256]{2,1,0:T(8,128)S(1)}, f32[64,256]{1,0:T(8,128)S(1)}) custom-call(f32[8,256]{1,0:T(8,128)S(1)} %get-tuple-element.52.edges, s32[64,256]{1,0:T(8,128)S(1)} %get-tuple-element.53.listing, f32[4,64,256]{2,1,0:T(8,128)S(1)} %shard_map.177.after.near, ...), custom_call_target="tpu_custom_call" | custom-call | flops 4000000000 | bytes 16000000 | tf_op jit(solution)/shard_map/pallas_call | solution.py:875
  34.7 3.6 %all-to-all-start.1 = ((f32[8,40,128]{2,1,0:T(8,128)}), f32[8,40,128]{2,1,0:T(8,128)S(1)}, u32[]{:S(2)}, u32[]{:S(2)}) async-start(f32[8,40,128]{2,1,0:T(8,128)} %get-tuple-element.76), calls=%async_computation.1 | async-start | bytes 327680 | tf_op jit(solution)/shard_map/all_to_all | solution.py:894
  38.3 2.9 %shard_map.182 = (f32[32,8,256]{2,1,0:T(8,128)S(1)}, f32[32,256]{1,0:T(8,128)S(1)}, f32[8,128]{1,0:T(8,128)S(1)}, f32[384,256]{1,0:T(8,128)S(1)}) custom-call(f32[16,256]{1,0:T(8,128)S(1)} %get-tuple-element.68.refs_0_, f32[16,1]{1,0:T(8,128)S(1)} %get-tuple-element.69.refs_1_, f32[24,384]{1,0:T(8,128)S(1)} %get-tuple-element.65.ball.refs_2_, ...), custom_call_target="tpu_custom_call" | custom-call | flops 2000000000 | bytes 8000000 | tf_op jit(solution)/shard_map/pallas_call | solution.py:901
  41.2 7.0 %all-to-all-done.1.got = f32[8,40,128]{2,1,0:T(8,128)S(1)} async-done(((f32[8,40,128]{2,1,0:T(8,128)}), f32[8,40,128]{2,1,0:T(8,128)S(1)}, u32[]{:S(2)}, u32[]{:S(2)}) %all-to-all-start.1) | async-done | bytes 163872 | tf_op jit(solution)/shard_map/all_to_all | solution.py:894
  48.2 1.6 %shard_map.185 = (f32[80,256]{1,0:T(8,128)S(1)}, f32[80,256]{1,0:T(8,128)S(1)}) custom-call(s32[1]{0:T(128)} %bitcast.5.core, f32[8,40,128]{2,1,0:T(8,128)S(1)} %all-to-all-done.1.got, f32[32,2048]{1,0:T(8,128)S(1)} %get-tuple-element.67.after.waves_x, bf16[288,2048]{1,0:T(8,128)(2,1)S(1)} %get-tuple-element.77.planes, f32[8,128]{1,0:T(8,128)S(1)} %get-tuple-element.78.after), custom_call_target="tpu_custom_call" | custom-call | flops 1500000000 | bytes 6000000 | tf_op jit(solution)/shard_map/pallas_call | solution.py:917
  49.8 0.9 collective-permute-start.4
  50.6 0.9 collective-permute-done.4
  51.6 0.2 collective-permute-start.5
  51.8 1.9 %collective-permute-start.6 = (f32[80,256]{1,0:T(8,128)S(1)}, f32[80,256]{1,0:T(8,128)S(1)}, u32[]{:S(2)}, u32[]{:S(2)}) collective-permute-start(f32[80,256]{1,0:T(8,128)S(1)} %add.8.refs_0_), channel_id=1, source_target_pairs={{0,48},{8,56},{32,0},{40,8},{16,32},{24,40},{48,16},{56,24},{64,11... | collective-permute-start | bytes 245768 | tf_op jit(solution)/shard_map/ppermute | solution.py:939
  53.7 1.7 %collective-permute-start.7 = (f32[80,256]{1,0:T(8,128)S(1)}, f32[80,256]{1,0:T(8,128)S(1)}, u32[]{:S(2)}, u32[]{:S(2)}) collective-permute-start(f32[80,256]{1,0:T(8,128)S(1)} %add.8.refs_0_), channel_id=1, source_target_pairs={{0,16},{8,24},{32,48},{40,56},{16,0},{24,8},{48,32},{56,40},{64,80... | collective-permute-start | bytes 245768 | tf_op jit(solution)/shard_map/ppermute | solution.py:939
  55.4 1.2 %shard_map.184 = (f32[16,8,256]{2,1,0:T(8,128)S(1)}, f32[16,256]{1,0:T(8,128)S(1)}, f32[8,128]{1,0:T(8,128)S(1)}) custom-call(f32[384,256]{1,0:T(8,128)S(1)} %get-tuple-element.73.refs_0_, f32[3,64,256]{2,1,0:T(8,128)S(1)} %get-tuple-element.70.refs_3_.refs_1_.disp, f32[64,256]{1,0:T(8,128)S(1)} %get-tuple-element.71.refs_4_.refs_2_, ...), custom_call_target="tpu_custom_call" | custom-call | flops 1000000000 | bytes 4000000 | tf_op jit(solution)/shard_map/pallas_call | solution.py:901
  56.6 3.1 %collective-permute-done.7.refs_3_ = f32[80,256]{1,0:T(8,128)S(1)} collective-permute-done((f32[80,256]{1,0:T(8,128)S(1)}, f32[80,256]{1,0:T(8,128)S(1)}, u32[]{:S(2)}, u32[]{:S(2)}) %collective-permute-start.7) | collective-permute-done | bytes 81952 | tf_op jit(solution)/shard_map/ppermute | solution.py:939
  59.7 0.4 collective-permute-start.8
  60.0 1.7 %collective-permute-start.9 = (f32[80,256]{1,0:T(8,128)S(1)}, f32[80,256]{1,0:T(8,128)S(1)}, u32[]{:S(2)}, u32[]{:S(2)}) collective-permute-start(f32[80,256]{1,0:T(8,128)S(1)} %shard_map.186.refs_0_), channel_id=1, source_target_pairs={{0,192},{8,200},{32,224},{40,232},{16,208},{24,216},{48,240},{56,2... | collective-permute-start | bytes 245768 | tf_op jit(solution)/shard_map/ppermute | solution.py:939
  61.8 1.2 %collective-permute-start.10 = (f32[80,256]{1,0:T(8,128)S(1)}, f32[80,256]{1,0:T(8,128)S(1)}, u32[]{:S(2)}, u32[]{:S(2)}) collective-permute-start(f32[80,256]{1,0:T(8,128)S(1)} %shard_map.186.refs_0_), channel_id=1, source_target_pairs={{0,128},{8,136},{32,160},{40,168},{16,144},{24,152},{48,176},{56,1... | collective-permute-start | bytes 245768 | tf_op jit(solution)/shard_map/ppermute | solution.py:939
  63.0 1.2 %shard_map.183 = (f32[16,8,256]{2,1,0:T(8,128)S(1)}, f32[16,256]{1,0:T(8,128)S(1)}, f32[8,128]{1,0:T(8,128)S(1)}) custom-call(f32[384,256]{1,0:T(8,128)S(1)} %get-tuple-element.73.refs_0_, f32[3,64,256]{2,1,0:T(8,128)S(1)} %get-tuple-element.70.refs_3_.refs_1_.disp, f32[64,256]{1,0:T(8,128)S(1)} %get-tuple-element.71.refs_4_.refs_2_, ...), custom_call_target="tpu_custom_call" | custom-call | flops 1000000000 | bytes 4000000 | tf_op jit(solution)/shard_map/pallas_call | solution.py:901
  64.1 0.7 collective-permute-done.8.refs_1_
  64.8 1.3 %collective-permute-done.9.refs_2_ = f32[80,256]{1,0:T(8,128)S(1)} collective-permute-done((f32[80,256]{1,0:T(8,128)S(1)}, f32[80,256]{1,0:T(8,128)S(1)}, u32[]{:S(2)}, u32[]{:S(2)}) %collective-permute-start.9) | collective-permute-done | bytes 81952 | tf_op jit(solution)/shard_map/ppermute | solution.py:939
  66.1 1.6 %collective-permute-done.10.refs_3_ = f32[80,256]{1,0:T(8,128)S(1)} collective-permute-done((f32[80,256]{1,0:T(8,128)S(1)}, f32[80,256]{1,0:T(8,128)S(1)}, u32[]{:S(2)}, u32[]{:S(2)}) %collective-permute-start.10) | collective-permute-done | bytes 81952 | tf_op jit(solution)/shard_map/ppermute | solution.py:939
  67.8 0.6 shard_map.188
  68.4 0.7 collective-permute-done.11.other
  69.1 1.8 %shard_map.189 = (f32[8,8,256]{2,1,0:T(8,128)}, f32[144,256]{1,0:T(8,128)S(1)}) custom-call(s32[1]{0:T(128)} %bitcast.5.core, f32[80,256]{1,0:T(8,128)S(1)} %shard_map.187.mine, f32[80,256]{1,0:T(8,128)S(1)} %collective-permute-done.11.other, f32[3,72,128]{2,1,0:T(8,128)S(1)} %get-tuple-element.81.weights, f32[8,256]{1,0:T(8,128)S(1)} %get-tuple-element.82.lone_weights, ...), custom_call_target="tpu_custom_call" | custom-call | flops 1000000000 | bytes 4000000 | tf_op jit(solution)/shard_map/pallas_call | solution.py:947
  70.9 3.6 %all-to-all-start.2 = ((f32[8,8,256]{2,1,0:T(8,128)}), f32[8,8,256]{2,1,0:T(8,128)S(1)}, u32[]{:S(2)}, u32[]{:S(2)}) async-start(f32[8,8,256]{2,1,0:T(8,128)} %get-tuple-element.83), calls=%async_computation.2 | async-start | bytes 131072 | tf_op jit(solution)/shard_map/all_to_all | solution.py:958
  74.5 3.6 %shard_map.191.refs_0_ = f32[8,8,128]{2,1,0:T(8,128)S(1)} custom-call(s32[1]{0:T(128)} %bitcast.7.rank, s32[1]{0:T(128)} %bitcast.5.core, f32[8,256]{1,0:T(8,128)S(1)} %get-tuple-element.52.edges, f32[80,256]{1,0:T(8,128)S(1)} %shard_map.187.mine, f32[80,256]{1,0:T(8,128)S(1)} %collective-permute-done.11.other, f32[3,72,128]{2,1,0:T(8,128)S(1)} %get-tuple-element.81.weights, ...), custom_call_target="tpu_custom_call" | custom-call | flops 2500000000 | bytes 10000000 | tf_op jit(solution)/shard_map/pallas_call | solution.py:959
  78.1 4.5 %all-to-all-done.2.got = f32[8,8,256]{2,1,0:T(8,128)S(1)} async-done(((f32[8,8,256]{2,1,0:T(8,128)}), f32[8,8,256]{2,1,0:T(8,128)S(1)}, u32[]{:S(2)}, u32[]{:S(2)}) %all-to-all-start.2) | async-done | bytes 65568 | tf_op jit(solution)/shard_map/all_to_all | solution.py:958
  82.6 1.4 %shard_map.190 = (f32[16,128]{1,0:T(8,128)S(1)}, f32[16,128]{1,0:T(8,128)S(1)}) custom-call(f32[8,8,256]{2,1,0:T(8,128)S(1)} %all-to-all-done.2.got, f32[32,8,256]{2,1,0:T(8,128)S(1)} %get-tuple-element.84.r0, f32[32,256]{1,0:T(8,128)S(1)} %get-tuple-element.85.e0, f32[16,8,256]{2,1,0:T(8,128)S(1)} %get-tuple-element.86.r1, ...), custom_call_target="tpu_custom_call" | custom-call | flops 1000000000 | bytes 4000000 | tf_op jit(solution)/shard_map/pallas_call | solution.py:974
  84.0 0.3 collective-permute-start.12
  84.3 0.2 collective-permute-start.13
  84.5 1.5 %shard_map.192 = (f32[8,8,128]{2,1,0:T(8,128)S(1)}, f32[8,128]{1,0:T(8,128)S(1)}, f32[8,128]{1,0:T(8,128)S(1)}, f32[8,128]{1,0:T(8,128)S(1)}) custom-call(f32[8,8,256]{2,1,0:T(8,128)S(1)} %all-to-all-done.2.got, f32[32,8,256]{2,1,0:T(8,128)S(1)} %get-tuple-element.84.r0, f32[32,256]{1,0:T(8,128)S(1)} %get-tuple-element.85.e0, ...), custom_call_target="tpu_custom_call" | custom-call | flops 1000000000 | bytes 4000000 | tf_op jit(solution)/shard_map/pallas_call | solution.py:974
  86.1 2.8 %collective-permute-done.13.below = f32[16,128]{1,0:T(8,128)S(1)} collective-permute-done((f32[16,128]{1,0:T(8,128)S(1)}, f32[16,128]{1,0:T(8,128)S(1)}, u32[]{:S(2)}, u32[]{:S(2)}) %collective-permute-start.13) | collective-permute-done | bytes 8224 | tf_op jit(solution)/shard_map/ppermute | solution.py:992
  88.9 2.3 %collective-permute-start.14 = (f32[8,128]{1,0:T(8,128)S(1)}, f32[8,128]{1,0:T(8,128)S(1)}, u32[]{:S(2)}, u32[]{:S(2)}) collective-permute-start(f32[8,128]{1,0:T(8,128)S(1)} %get-tuple-element.97), channel_id=1, source_target_pairs={{0,32},{32,64},{64,96},{96,128},{128,160},{160,192},{192,224},{224... | collective-permute-start | bytes 12296 | tf_op jit(solution)/shard_map/ppermute | solution.py:997
  91.2 1.3 %collective-permute-done.14.from_left = f32[8,128]{1,0:T(8,128)S(1)} collective-permute-done((f32[8,128]{1,0:T(8,128)S(1)}, f32[8,128]{1,0:T(8,128)S(1)}, u32[]{:S(2)}, u32[]{:S(2)}) %collective-permute-start.14) | collective-permute-done | bytes 4128 | tf_op jit(solution)/shard_map/ppermute | solution.py:997
  92.5 4.4 %collective-permute-done.15.from_right = f32[8,128]{1,0:T(8,128)S(1)} collective-permute-done((f32[8,128]{1,0:T(8,128)S(1)}, f32[8,128]{1,0:T(8,128)S(1)}, u32[]{:S(2)}, u32[]{:S(2)}) %collective-permute-start.15) | collective-permute-done | bytes 4128 | tf_op jit(solution)/shard_map/ppermute | solution.py:996
  96.9 0.2 shard_map.194
  97.1 11.2 %all_to_all.20.got = f32[8,8,128]{2,1,0:T(8,128)S(1)} all-to-all(f32[8,8,128]{2,1,0:T(8,128)S(1)} %shard_map.194), channel_id=1, replica_groups=mesh['gx'=8,'gy'=4,'ka'=8] {'ka'}, dimensions={0} | all-to-all | bytes 65536 | tf_op jit(solution)/shard_map/all_to_all | solution.py:1001
  108.4 0.6 shard_map.195
  (17 shorter events, 0.3 us)
Async XLA Ops:
  2.0 16.5 %all-to-all-start = ((f32[8,8,128]{2,1,0:T(8,128)}), f32[8,8,128]{2,1,0:T(8,128)S(1)}, u32[]{:S(2)}, u32[]{:S(2)}) async-start(f32[8,8,128]{2,1,0:T(8,128)} %get-tuple-element.54), calls=%async_computation | async-start | bytes 65536 | tf_op jit(solution)/shard_map/all_to_all | solution.py:810
  18.6 4.6 %collective-permute-start = (f32[8,128]{1,0:T(8,128)S(1)}, f32[8,128]{1,0:T(8,128)S(1)}, u32[]{:S(2)}, u32[]{:S(2)}) collective-permute-start(f32[8,128]{1,0:T(8,128)S(1)} %get-tuple-element.56.cell1), channel_id=1, source_target_pairs={{0,8},{8,16},{16,24},{24,0},{1,9},{9,17},{17,25},{25,1},{2,10},{10... | collective-permute-start | bytes 12296 | tf_op jit(solution)/shard_map/ppermute | solution.py:858
  18.7 4.6 %collective-permute-start.1 = (f32[8,128]{1,0:T(8,128)S(1)}, f32[8,128]{1,0:T(8,128)S(1)}, u32[]{:S(2)}, u32[]{:S(2)}) collective-permute-start(f32[8,128]{1,0:T(8,128)S(1)} %get-tuple-element.57.cell0), channel_id=1, source_target_pairs={{0,24},{8,0},{16,8},{24,16},{1,25},{9,1},{17,9},{25,17},{2,26},{10... | collective-permute-start | bytes 12296 | tf_op jit(solution)/shard_map/ppermute | solution.py:859
  23.3 3.7 %collective-permute-start.2 = (f32[16,128]{1,0:T(8,128)S(1)}, f32[16,128]{1,0:T(8,128)S(1)}, u32[]{:S(2)}, u32[]{:S(2)}) collective-permute-start(f32[16,128]{1,0:T(8,128)S(1)} %get-tuple-element.58), channel_id=1, source_target_pairs={{0,32},{32,64},{64,96},{96,128},{128,160},{160,192},{192,224},{224... | collective-permute-start | bytes 24584 | tf_op jit(solution)/shard_map/ppermute | solution.py:866
  23.7 5.8 %collective-permute-start.3 = (f32[16,128]{1,0:T(8,128)S(1)}, f32[16,128]{1,0:T(8,128)S(1)}, u32[]{:S(2)}, u32[]{:S(2)}) collective-permute-start(f32[16,128]{1,0:T(8,128)S(1)} %get-tuple-element.59), channel_id=1, source_target_pairs={{0,224},{32,0},{64,32},{96,64},{128,96},{160,128},{192,160},{224,1... | collective-permute-start | bytes 24584 | tf_op jit(solution)/shard_map/ppermute | solution.py:867
  34.7 13.5 %all-to-all-start.1 = ((f32[8,40,128]{2,1,0:T(8,128)}), f32[8,40,128]{2,1,0:T(8,128)S(1)}, u32[]{:S(2)}, u32[]{:S(2)}) async-start(f32[8,40,128]{2,1,0:T(8,128)} %get-tuple-element.76), calls=%async_computation.1 | async-start | bytes 327680 | tf_op jit(solution)/shard_map/all_to_all | solution.py:894
  49.8 1.8 %collective-permute-start.4 = (f32[80,256]{1,0:T(8,128)S(1)}, f32[80,256]{1,0:T(8,128)S(1)}, u32[]{:S(2)}, u32[]{:S(2)}) collective-permute-start(f32[80,256]{1,0:T(8,128)S(1)} %get-tuple-element.80), channel_id=1, source_target_pairs={{0,8},{8,0},{32,40},{40,32},{16,24},{24,16},{48,56},{56,48},{64,72... | collective-permute-start | bytes 245768 | tf_op jit(solution)/shard_map/ppermute | solution.py:937
  51.6 5.0 %collective-permute-start.5 = (f32[80,256]{1,0:T(8,128)S(1)}, f32[80,256]{1,0:T(8,128)S(1)}, u32[]{:S(2)}, u32[]{:S(2)}) collective-permute-start(f32[80,256]{1,0:T(8,128)S(1)} %add.8.refs_0_), channel_id=1, source_target_pairs={{0,32},{8,40},{32,16},{40,24},{16,48},{24,56},{48,0},{56,8},{64,96... | collective-permute-start | bytes 245768 | tf_op jit(solution)/shard_map/ppermute | solution.py:939
  51.8 4.7 %collective-permute-start.6 = (f32[80,256]{1,0:T(8,128)S(1)}, f32[80,256]{1,0:T(8,128)S(1)}, u32[]{:S(2)}, u32[]{:S(2)}) collective-permute-start(f32[80,256]{1,0:T(8,128)S(1)} %add.8.refs_0_), channel_id=1, source_target_pairs={{0,48},{8,56},{32,0},{40,8},{16,32},{24,40},{48,16},{56,24},{64,11... | collective-permute-start | bytes 245768 | tf_op jit(solution)/shard_map/ppermute | solution.py:939
  53.7 5.9 %collective-permute-start.7 = (f32[80,256]{1,0:T(8,128)S(1)}, f32[80,256]{1,0:T(8,128)S(1)}, u32[]{:S(2)}, u32[]{:S(2)}) collective-permute-start(f32[80,256]{1,0:T(8,128)S(1)} %add.8.refs_0_), channel_id=1, source_target_pairs={{0,16},{8,24},{32,48},{40,56},{16,0},{24,8},{48,32},{56,40},{64,80... | collective-permute-start | bytes 245768 | tf_op jit(solution)/shard_map/ppermute | solution.py:939
  59.7 5.2 %collective-permute-start.8 = (f32[80,256]{1,0:T(8,128)S(1)}, f32[80,256]{1,0:T(8,128)S(1)}, u32[]{:S(2)}, u32[]{:S(2)}) collective-permute-start(f32[80,256]{1,0:T(8,128)S(1)} %shard_map.186.refs_0_), channel_id=1, source_target_pairs={{0,64},{8,72},{32,96},{40,104},{16,80},{24,88},{48,112},{56,120},{... | collective-permute-start | bytes 245768 | tf_op jit(solution)/shard_map/ppermute | solution.py:939
  60.0 6.1 %collective-permute-start.9 = (f32[80,256]{1,0:T(8,128)S(1)}, f32[80,256]{1,0:T(8,128)S(1)}, u32[]{:S(2)}, u32[]{:S(2)}) collective-permute-start(f32[80,256]{1,0:T(8,128)S(1)} %shard_map.186.refs_0_), channel_id=1, source_target_pairs={{0,192},{8,200},{32,224},{40,232},{16,208},{24,216},{48,240},{56,2... | collective-permute-start | bytes 245768 | tf_op jit(solution)/shard_map/ppermute | solution.py:939
  61.8 5.9 %collective-permute-start.10 = (f32[80,256]{1,0:T(8,128)S(1)}, f32[80,256]{1,0:T(8,128)S(1)}, u32[]{:S(2)}, u32[]{:S(2)}) collective-permute-start(f32[80,256]{1,0:T(8,128)S(1)} %shard_map.186.refs_0_), channel_id=1, source_target_pairs={{0,128},{8,136},{32,160},{40,168},{16,144},{24,152},{48,176},{56,1... | collective-permute-start | bytes 245768 | tf_op jit(solution)/shard_map/ppermute | solution.py:939
  67.7 1.4 %collective-permute-start.11 = (f32[80,256]{1,0:T(8,128)S(1)}, f32[80,256]{1,0:T(8,128)S(1)}, u32[]{:S(2)}, u32[]{:S(2)}) collective-permute-start(f32[80,256]{1,0:T(8,128)S(1)} %shard_map.187.mine), channel_id=1, source_target_pairs={{0,8},{8,0},{32,40},{40,32},{16,24},{24,16},{48,56},{56,48},{64,72... | collective-permute-start | bytes 245768 | tf_op jit(solution)/shard_map/ppermute | solution.py:940
  70.9 11.7 %all-to-all-start.2 = ((f32[8,8,256]{2,1,0:T(8,128)}), f32[8,8,256]{2,1,0:T(8,128)S(1)}, u32[]{:S(2)}, u32[]{:S(2)}) async-start(f32[8,8,256]{2,1,0:T(8,128)} %get-tuple-element.83), calls=%async_computation.2 | async-start | bytes 131072 | tf_op jit(solution)/shard_map/all_to_all | solution.py:958
  84.0 2.1 %collective-permute-start.12 = (f32[16,128]{1,0:T(8,128)S(1)}, f32[16,128]{1,0:T(8,128)S(1)}, u32[]{:S(2)}, u32[]{:S(2)}) collective-permute-start(f32[16,128]{1,0:T(8,128)S(1)} %get-tuple-element.90), channel_id=1, source_target_pairs={{0,24},{8,0},{16,8},{24,16},{1,25},{9,1},{17,9},{25,17},{2,26},{10... | collective-permute-start | bytes 24584 | tf_op jit(solution)/shard_map/ppermute | solution.py:991
  84.3 24.1 %copy-start = (f32[3,256]{1,0:T(4,128)S(1)}, f32[3,256]{1,0:T(4,128)}, u32[]{:S(2)}) copy-start(f32[3,256]{1,0:T(4,128)} %speed.1) | copy-start | bytes 9220
  84.3 24.1 %copy-start.1 = (f32[3,256]{1,0:T(4,128)S(1)}, f32[3,256]{1,0:T(4,128)}, u32[]{:S(2)}) copy-start(f32[3,256]{1,0:T(4,128)} %kicks.1) | copy-start | bytes 9220
  84.3 4.6 %collective-permute-start.13 = (f32[16,128]{1,0:T(8,128)S(1)}, f32[16,128]{1,0:T(8,128)S(1)}, u32[]{:S(2)}, u32[]{:S(2)}) collective-permute-start(f32[16,128]{1,0:T(8,128)S(1)} %get-tuple-element.91), channel_id=1, source_target_pairs={{0,8},{8,16},{16,24},{24,0},{1,9},{9,17},{17,25},{25,1},{2,10},{10... | collective-permute-start | bytes 24584 | tf_op jit(solution)/shard_map/ppermute | solution.py:992
  88.9 3.6 %collective-permute-start.14 = (f32[8,128]{1,0:T(8,128)S(1)}, f32[8,128]{1,0:T(8,128)S(1)}, u32[]{:S(2)}, u32[]{:S(2)}) collective-permute-start(f32[8,128]{1,0:T(8,128)S(1)} %get-tuple-element.97), channel_id=1, source_target_pairs={{0,32},{32,64},{64,96},{96,128},{128,160},{160,192},{192,224},{224... | collective-permute-start | bytes 12296 | tf_op jit(solution)/shard_map/ppermute | solution.py:997
  91.2 5.7 %collective-permute-start.15 = (f32[8,128]{1,0:T(8,128)S(1)}, f32[8,128]{1,0:T(8,128)S(1)}, u32[]{:S(2)}, u32[]{:S(2)}) collective-permute-start(f32[8,128]{1,0:T(8,128)S(1)} %get-tuple-element.98), channel_id=1, source_target_pairs={{0,224},{32,0},{64,32},{96,64},{128,96},{160,128},{192,160},{224,1... | collective-permute-start | bytes 12296 | tf_op jit(solution)/shard_map/ppermute | solution.py:996
